TPU v7x, 32 devices: a whole 2x2x4 slice. The times are simulated.
32 devices in a mesh: gz: 2 (over x), bx: 2 (over y), by: 8 (over z, core).
Axes of the slice: x: 2, y: 2, z: 4, core: 2. Of those that a mesh axis runs over, the one named last changes fastest.
Arguments:
- observed: float32 [64, 128, 1024], P('gz', 'bx', 'by'), may hold values from 0.02 to 50.2
- psf_z: float32 [65], replicated, may hold values from 0.003 to 1.11
- psf_x: float32 [65], replicated, may hold values from 0.003 to 1.11
- psf_y: float32 [65], replicated, may hold values from 0.003 to 1.11
Outputs:
- estimate: float32 [64, 128, 1024], P('gz', 'bx', 'by')
All inputs are finite; a program needn't handle non-finite values.
Results may differ from a plain program's by a relative error of at most 0.00002.
Values sent between devices are 32-bit elements; how exact they have to be, the bound alone decides.
No kernel may reach another device: no remote copies, remote signals or barrier semaphores. Data moves between devices by JAX's collectives and lax.ppermute only.
A program may use at most 64 MiB of HBM per device.

v0:
```python
import jax
import jax.numpy as jnp
from jax import lax
from jax.sharding import PartitionSpec as P

ITERS = 2


def extended_2(block, sides, width):
    for axis, dim in sides:
        count = lax.axis_size(axis)
        forward = [(i, i + 1) for i in range(count - 1)]
        backward = [(target, source) for source, target in forward]
        low = lax.ppermute(
            lax.slice_in_dim(block, block.shape[dim] - width, None, axis=dim), axis, forward
        )
        high = lax.ppermute(lax.slice_in_dim(block, 0, width, axis=dim), axis, backward)
        block = jnp.concatenate([low, block, high], axis=dim)
    return block


def pass_axis(extended, kernel, axis_dim, length):
    result = kernel[0] * lax.slice_in_dim(extended, 0, length, axis=axis_dim)
    for offset in range(1, kernel.shape[0]):
        result = result + kernel[offset] * lax.slice_in_dim(
            extended, offset, offset + length, axis=axis_dim
        )
    return result


def blur(field, kernel_z, kernel_x, kernel_y):
    radius = kernel_z.shape[0] // 2
    planes, rows, columns = field.shape
    extended = extended_2(field, (("gz", 0),), radius)
    field = pass_axis(extended, kernel_z, 0, planes)
    extended = extended_2(field, (("bx", 1),), radius)
    field = pass_axis(extended, kernel_x, 1, rows)
    extended = extended_2(field, (("by", 2),), radius)
    field = pass_axis(extended, kernel_y, 2, columns)
    return field


def per_device(observed, psf_z, psf_x, psf_y):
    kernel_z = psf_z / jnp.sum(psf_z)
    kernel_x = psf_x / jnp.sum(psf_x)
    kernel_y = psf_y / jnp.sum(psf_y)
    estimate = observed
    for sweep in range(ITERS):
        blurred = blur(estimate, kernel_z, kernel_x, kernel_y)
        quotient = observed / blurred
        estimate = estimate * blur(quotient, kernel_z[::-1], kernel_x[::-1], kernel_y[::-1])
    return estimate


def solution(mesh):
    placed = (P("gz", "bx", "by"), P(), P(), P())
    return jax.shard_map(
        per_device, mesh=mesh, in_specs=placed, out_specs=P("gz", "bx", "by"), check_vma=False
    )
```

profile of v0, /device:TPU:1, one launch (start us, length us, event | category | flops | bytes accessed | tf_op | source)
XLA Modules:
  0.0 1036.3 jit_solution(12547806464578839189)
XLA Ops:
  0.0 4.1 collective-permute-start
  18.6 7.6 collective-permute-done
  30.9 50.9 %fusion.2083 = f32[32,64,128]{2,1,0:T(8,128)S(1)} fusion(f32[64,64,128]{2,1,0:T(8,128)S(1)} %constant_dynamic-update-slice_fusion.2, f32[64,64,128]{2,1,0:T(8,128)S(1)} %get-tuple-element.21, f32[32,64,128]{2,1,0:T(8,128)} %copy-done.3, f32[32,64,128]{2,1,0:T(8,128)S(1)} %copy-done, f32[32,64,128]{2,1,0:T(8,128)S(1)} %collective-permute-done, f32[]{:T(128)} %bitcast.69, ...), kind=kLoop, calls=%fused_computation.3458 | loop fusion | flops 33816576 | bytes 69206272 | tf_op jit(solution)/shard_map/add | solution.py:25
  83.2 4.0 collective-permute-start.2
  90.1 5.3 collective-permute-done.3
  97.1 61.3 %fusion.567 = f32[32,64,128]{2,1,0:T(8,128)S(1)} fusion(f32[32,64,128]{2,1,0:T(8,128)S(1)} %fusion.2083, f32[32,32,128]{2,1,0:T(8,128)} %copy-done.8, f32[32,32,128]{2,1,0:T(8,128)} %copy-done.9, f32[]{:T(128)} %bitcast.133, f32[]{:T(128)} %bitcast.132, f32[]{:T(128)} %bitcast.131, f32[]{:T(128)} %bitcast.130, f32[]{:T(128)} %bitcast.129, f32[]{:T(128)} %bitcast.128, ...), kind=kLoop, calls=%fused_computation.1919 | loop fusion | flops 50593792 | bytes 3145988 | tf_op jit(solution)/shard_map/add | solution.py:25
  162.2 5.0 collective-permute-start.5
  180.1 82.8 %fusion.1875 = f32[32,64,128]{2,1,0:T(8,128)S(1)} fusion(f32[32,64,128]{2,1,0:T(8,128)S(1)} %copy-done, f32[32,64,128]{2,1,0:T(8,128)S(1)} %fusion.567, f32[32,64,32]{2,1,0:T(8,128)S(1)} %copy.17, f32[32,64,32]{2,1,0:T(8,128)} %copy.15, f32[]{:T(128)} %bitcast.197, f32[]{:T(128)} %bitcast.196, f32[]{:T(128)} %bitcast.195, f32[]{:T(128)} %bitcast.194, ...), kind=kLoop, calls=%fused_computation.3227 | loop fusion | flops 50855936 | bytes 3670276 | tf_op jit(solution)/shard_map/div | solution.py:50
  264.2 4.1 collective-permute-start.6
  271.2 16.4 %collective-permute-done.7 = f32[32,64,128]{2,1,0:T(8,128)S(1)} collective-permute-done((f32[32,64,128]{2,1,0:T(8,128)S(1)}, f32[32,64,128]{2,1,0:T(8,128)S(1)}, u32[]{:S(2)}, u32[]{:S(2)}) %collective-permute-start.7) | collective-permute-done | bytes 1048608 | tf_op jit(solution)/shard_map/ppermute | solution.py:17
  290.4 56.4 %fusion.1124 = f32[32,64,128]{2,1,0:T(8,128)S(1)} fusion(f32[32,64,128]{2,1,0:T(8,128)S(1)} %fusion.1875, f32[32,64,128]{2,1,0:T(8,128)S(1)} %collective-permute-done.7, f32[32,64,128]{2,1,0:T(8,128)} %copy-done.4, f32[]{:T(128)} %bitcast.261, f32[]{:T(128)} %bitcast.260, f32[]{:T(128)} %bitcast.259, f32[]{:T(128)} %bitcast.258, f32[]{:T(128)} %bitcast.257, ...), kind=kLoop, calls=%fused_computation.2476 | loop fusion | flops 50069504 | bytes 4194564 | tf_op jit(solution)/shard_map/add | solution.py:25
  348.2 4.6 collective-permute-start.8
  356.4 5.0 collective-permute-done.9
  364.0 61.3 %fusion.379 = f32[32,64,128]{2,1,0:T(8,128)S(1)} fusion(f32[32,64,128]{2,1,0:T(8,128)S(1)} %fusion.1124, f32[32,32,128]{2,1,0:T(8,128)} %copy-done.5, f32[32,32,128]{2,1,0:T(8,128)} %copy-done.6, f32[]{:T(128)} %bitcast.325, f32[]{:T(128)} %bitcast.324, f32[]{:T(128)} %bitcast.323, f32[]{:T(128)} %bitcast.322, f32[]{:T(128)} %bitcast.321, f32[]{:T(128)} %bitcast.320, ...), kind=kLoop, calls=%fused_computation.1731 | loop fusion | flops 50593792 | bytes 3145988 | tf_op jit(solution)/shard_map/add | solution.py:25
  432.0 4.1 collective-permute-start.10
  444.9 82.4 %fusion.1686 = f32[32,64,128]{2,1,0:T(8,128)S(1)} fusion(f32[32,64,128]{2,1,0:T(8,128)S(1)} %copy-done, f32[32,64,128]{2,1,0:T(8,128)S(1)} %fusion.379, f32[32,64,32]{2,1,0:T(8,128)S(1)} %copy.21, f32[32,64,32]{2,1,0:T(8,128)} %copy.19, f32[]{:T(128)} %bitcast.389, f32[]{:T(128)} %bitcast.388, f32[]{:T(128)} %bitcast.387, f32[]{:T(128)} %bitcast.386, ...), kind=kLoop, calls=%fused_computation.3038 | loop fusion | flops 50855936 | bytes 3670276 | tf_op jit(solution)/shard_map/mul | solution.py:51
  528.7 5.4 collective-permute-start.12
  534.0 16.8 %collective-permute-done.13 = f32[32,64,128]{2,1,0:T(8,128)S(1)} collective-permute-done((f32[32,64,128]{2,1,0:T(8,128)S(1)}, f32[32,64,128]{2,1,0:T(8,128)S(1)}, u32[]{:S(2)}, u32[]{:S(2)}) %collective-permute-start.13) | collective-permute-done | bytes 1048608 | tf_op jit(solution)/shard_map/ppermute | solution.py:17
  552.6 57.3 %fusion.940 = f32[32,64,128]{2,1,0:T(8,128)S(1)} fusion(f32[32,64,128]{2,1,0:T(8,128)S(1)} %fusion.1686, f32[32,64,128]{2,1,0:T(8,128)S(1)} %collective-permute-done.13, f32[32,64,128]{2,1,0:T(8,128)} %collective-permute-done.12, f32[]{:T(128)} %bitcast.69, f32[]{:T(128)} %bitcast.68, f32[]{:T(128)} %bitcast.67, f32[]{:T(128)} %bitcast.66, f32[]{:T(128)} %bitcast.65, ...), kind=kLoop, calls=%fused_computation.2292 | loop fusion | flops 50069504 | bytes 4194564 | tf_op jit(solution)/shard_map/add | solution.py:25
  611.3 4.8 collective-permute-start.14
  616.2 7.0 collective-permute-done.15
  625.0 61.4 %fusion.191 = f32[32,64,128]{2,1,0:T(8,128)S(1)} fusion(f32[32,64,128]{2,1,0:T(8,128)S(1)} %fusion.940, f32[32,32,128]{2,1,0:T(8,128)} %copy-done.7, f32[32,32,128]{2,1,0:T(8,128)} %collective-permute-done.14, f32[]{:T(128)} %bitcast.133, f32[]{:T(128)} %bitcast.132, f32[]{:T(128)} %bitcast.131, f32[]{:T(128)} %bitcast.130, f32[]{:T(128)} %bitcast.129, ...), kind=kLoop, calls=%fused_computation.1543 | loop fusion | flops 50593792 | bytes 3145988 | tf_op jit(solution)/shard_map/add | solution.py:25
  693.2 6.9 collective-permute-start.16
  700.1 4.1 collective-permute-done.17
  709.0 83.1 %fusion.1497 = f32[32,64,128]{2,1,0:T(8,128)S(1)} fusion(f32[32,64,128]{2,1,0:T(8,128)S(1)} %copy-done, f32[32,64,128]{2,1,0:T(8,128)S(1)} %fusion.191, f32[32,64,32]{2,1,0:T(8,128)S(1)} %copy.25, f32[32,64,32]{2,1,0:T(8,128)} %copy.23, f32[]{:T(128)} %bitcast.197, f32[]{:T(128)} %bitcast.196, f32[]{:T(128)} %bitcast.195, f32[]{:T(128)} %bitcast.194, ...), kind=kLoop, calls=%fused_computation.2849 | loop fusion | flops 50855936 | bytes 3670276 | tf_op jit(solution)/shard_map/div | solution.py:50
  793.4 4.3 collective-permute-start.18
  797.8 12.9 %collective-permute-done.19 = f32[32,64,128]{2,1,0:T(8,128)S(1)} collective-permute-done((f32[32,64,128]{2,1,0:T(8,128)S(1)}, f32[32,64,128]{2,1,0:T(8,128)S(1)}, u32[]{:S(2)}, u32[]{:S(2)}) %collective-permute-start.19) | collective-permute-done | bytes 1048608 | tf_op jit(solution)/shard_map/ppermute | solution.py:17
  812.5 50.8 %fusion.756 = f32[32,64,128]{2,1,0:T(8,128)S(1)} fusion(f32[32,64,128]{2,1,0:T(8,128)S(1)} %fusion.1497, f32[32,64,128]{2,1,0:T(8,128)S(1)} %collective-permute-done.19, f32[32,64,128]{2,1,0:T(8,128)S(1)} %collective-permute-done.18, f32[]{:T(128)} %bitcast.261, f32[]{:T(128)} %bitcast.260, f32[]{:T(128)} %bitcast.259, f32[]{:T(128)} %bitcast.258, ...), kind=kLoop, calls=%fused_computation.2108 | loop fusion | flops 50069504 | bytes 4194564 | tf_op jit(solution)/shard_map/add | solution.py:25
  868.8 4.6 collective-permute-done.21
  874.9 51.1 %fusion.3 = f32[32,64,128]{2,1,0:T(8,128)S(1)} fusion(f32[32,64,128]{2,1,0:T(8,128)S(1)} %fusion.756, f32[32,32,128]{2,1,0:T(8,128)S(1)} %collective-permute-done.21, f32[32,32,128]{2,1,0:T(8,128)S(1)} %collective-permute-done.20, f32[]{:T(128)} %bitcast.325, f32[]{:T(128)} %bitcast.324, f32[]{:T(128)} %bitcast.323, f32[]{:T(128)} %bitcast.322, ...), kind=kLoop, calls=%fused_computation.1355 | loop fusion | flops 50593792 | bytes 3145988 | tf_op jit(solution)/shard_map/add | solution.py:25
  930.6 13.4 %collective-permute-start.22 = (f32[32,64,32]{1,2,0:T(8,128)}, f32[32,64,32]{1,2,0:T(8,128)}, u32[]{:S(2)}, u32[]{:S(2)}) collective-permute-start(f32[32,64,32]{1,2,0:T(8,128)} %copy.26), channel_id=1, source_target_pairs={{0,1},{1,2},{2,3},{3,4},{4,5},{5,6},{6,7},{8,9},{9,10},{10,11},{11... | collective-permute-start | bytes 786440 | tf_op jit(solution)/shard_map/ppermute | solution.py:14
  952.6 83.4 %fusion.1308 = f32[32,64,128]{2,1,0:T(8,128)} fusion(f32[32,64,128]{2,1,0:T(8,128)S(1)} %copy-done.2, f32[32,64,128]{2,1,0:T(8,128)S(1)} %fusion.3, f32[32,64,32]{2,1,0:T(8,128)S(1)} %copy.29, f32[32,64,32]{2,1,0:T(8,128)} %copy.27, f32[]{:T(128)} %bitcast.389, f32[]{:T(128)} %bitcast.388, f32[]{:T(128)} %bitcast.387, f32[]{:T(128)} %bitcast.386, ...), kind=kLoop, calls=%fused_computation.2660 | loop fusion | flops 50855936 | bytes 3670276 | tf_op jit(solution)/shard_map/mul | solution.py:51
  (110 shorter events, 112.7 us)
Async XLA Ops:
  0.0 26.3 %copy-start = (f32[32,64,128]{2,1,0:T(8,128)S(1)}, f32[32,64,128]{2,1,0:T(8,128)}, u32[]{:S(2)}) copy-start(f32[32,64,128]{2,1,0:T(8,128)} %param.4) | copy-start | bytes 3145732
  0.0 26.2 %collective-permute-start = (f32[32,64,128]{2,1,0:T(8,128)}, f32[32,64,128]{2,1,0:T(8,128)S(1)}, u32[]{:S(2)}, u32[]{:S(2)}) collective-permute-start(f32[32,64,128]{2,1,0:T(8,128)} %param.4), channel_id=1, source_target_pairs={{0,16},{1,17},{2,18},{3,19},{4,20},{5,21},{6,22},{7,23},{8,24},{9,... | collective-permute-start | bytes 3145736 | tf_op jit(solution)/shard_map/ppermute | solution.py:14
  4.1 25.8 %collective-permute-start.1 = (f32[32,64,128]{2,1,0:T(8,128)}, f32[32,64,128]{2,1,0:T(8,128)S(1)}, u32[]{:S(2)}, u32[]{:S(2)}) collective-permute-start(f32[32,64,128]{2,1,0:T(8,128)} %param.4), channel_id=1, source_target_pairs={{16,0},{17,1},{18,2},{19,3},{20,4},{21,5},{22,6},{23,7},{24,8},{25... | collective-permute-start | bytes 3145736 | tf_op jit(solution)/shard_map/ppermute | solution.py:17
  30.0 1.0 copy-start.3
  81.8 6.9 copy-start.10
  81.9 13.4 %collective-permute-start.3 = (f32[32,32,128]{2,1,0:T(8,128)S(1)}, f32[32,32,128]{2,1,0:T(8,128)S(1)}, u32[]{:S(2)}, u32[]{:S(2)}) collective-permute-start(f32[32,32,128]{2,1,0:T(8,128)S(1)} %get-tuple-element.20), channel_id=1, source_target_pairs={{8,0},{9,1},{10,2},{11,3},{12,4},{13,5},{14,6},{15,7},{24,16},{25,... | collective-permute-start | bytes 1572872 | tf_op jit(solution)/shard_map/ppermute | solution.py:17
  83.2 13.1 %collective-permute-start.2 = (f32[32,32,128]{2,1,0:T(8,128)S(1)}, f32[32,32,128]{2,1,0:T(8,128)S(1)}, u32[]{:S(2)}, u32[]{:S(2)}) collective-permute-start(f32[32,32,128]{2,1,0:T(8,128)S(1)} %get-tuple-element.19), channel_id=1, source_target_pairs={{0,8},{1,9},{2,10},{3,11},{4,12},{5,13},{6,14},{7,15},{16,24},{17,... | collective-permute-start | bytes 1572872 | tf_op jit(solution)/shard_map/ppermute | solution.py:14
  95.4 0.9 copy-start.8
  162.2 13.3 %collective-permute-start.5 = (f32[32,64,32]{1,2,0:T(8,128)}, f32[32,64,32]{1,2,0:T(8,128)}, u32[]{:S(2)}, u32[]{:S(2)}) collective-permute-start(f32[32,64,32]{1,2,0:T(8,128)} %copy.16), channel_id=1, source_target_pairs={{1,0},{2,1},{3,2},{4,3},{5,4},{6,5},{7,6},{9,8},{10,9},{11,10},{12... | collective-permute-start | bytes 786440 | tf_op jit(solution)/shard_map/ppermute | solution.py:17
  168.2 9.5 collective-permute-start.4
  262.9 24.6 %collective-permute-start.7 = (f32[32,64,128]{2,1,0:T(8,128)S(1)}, f32[32,64,128]{2,1,0:T(8,128)S(1)}, u32[]{:S(2)}, u32[]{:S(2)}) collective-permute-start(f32[32,64,128]{2,1,0:T(8,128)S(1)} %fusion.1875), channel_id=1, source_target_pairs={{16,0},{17,1},{18,2},{19,3},{20,4},{21,5},{22,6},{23,7},{24,8},{25... | collective-permute-start | bytes 3145736 | tf_op jit(solution)/shard_map/ppermute | solution.py:17
  264.2 25.2 %collective-permute-start.6 = (f32[32,64,128]{2,1,0:T(8,128)S(1)}, f32[32,64,128]{2,1,0:T(8,128)S(1)}, u32[]{:S(2)}, u32[]{:S(2)}) collective-permute-start(f32[32,64,128]{2,1,0:T(8,128)S(1)} %fusion.1875), channel_id=1, source_target_pairs={{0,16},{1,17},{2,18},{3,19},{4,20},{5,21},{6,22},{7,23},{8,24},{9,... | collective-permute-start | bytes 3145736 | tf_op jit(solution)/shard_map/ppermute | solution.py:14
  289.4 1.0 copy-start.4
  346.9 14.5 %collective-permute-start.9 = (f32[32,32,128]{2,1,0:T(8,128)S(1)}, f32[32,32,128]{2,1,0:T(8,128)S(1)}, u32[]{:S(2)}, u32[]{:S(2)}) collective-permute-start(f32[32,32,128]{2,1,0:T(8,128)S(1)} %get-tuple-element.16), channel_id=1, source_target_pairs={{8,0},{9,1},{10,2},{11,3},{12,4},{13,5},{14,6},{15,7},{24,16},{25,... | collective-permute-start | bytes 1572872 | tf_op jit(solution)/shard_map/ppermute | solution.py:17
  348.2 15.0 %collective-permute-start.8 = (f32[32,32,128]{2,1,0:T(8,128)S(1)}, f32[32,32,128]{2,1,0:T(8,128)S(1)}, u32[]{:S(2)}, u32[]{:S(2)}) collective-permute-start(f32[32,32,128]{2,1,0:T(8,128)S(1)} %get-tuple-element.15), channel_id=1, source_target_pairs={{0,8},{1,9},{2,10},{3,11},{4,12},{5,13},{6,14},{7,15},{16,24},{17,... | collective-permute-start | bytes 1572872 | tf_op jit(solution)/shard_map/ppermute | solution.py:14
  361.4 1.8 copy-start.5
  429.0 11.3 %collective-permute-start.11 = (f32[32,64,32]{1,2,0:T(8,128)}, f32[32,64,32]{1,2,0:T(8,128)}, u32[]{:S(2)}, u32[]{:S(2)}) collective-permute-start(f32[32,64,32]{1,2,0:T(8,128)} %copy.20), channel_id=1, source_target_pairs={{1,0},{2,1},{3,2},{4,3},{5,4},{6,5},{7,6},{9,8},{10,9},{11,10},{12... | collective-permute-start | bytes 786440 | tf_op jit(solution)/shard_map/ppermute | solution.py:17
  432.0 10.6 %collective-permute-start.10 = (f32[32,64,32]{1,2,0:T(8,128)}, f32[32,64,32]{1,2,0:T(8,128)}, u32[]{:S(2)}, u32[]{:S(2)}) collective-permute-start(f32[32,64,32]{1,2,0:T(8,128)} %copy.18), channel_id=1, source_target_pairs={{0,1},{1,2},{2,3},{3,4},{4,5},{5,6},{6,7},{8,9},{9,10},{10,11},{11... | collective-permute-start | bytes 786440 | tf_op jit(solution)/shard_map/ppermute | solution.py:14
  527.3 82.6 %copy-start.1 = (f32[32,64,128]{2,1,0:T(8,128)}, f32[32,64,128]{2,1,0:T(8,128)S(1)}, u32[]{:S(2)}) copy-start(f32[32,64,128]{2,1,0:T(8,128)S(1)} %fusion.1686) | copy-start | bytes 3145732
  527.4 23.5 %collective-permute-start.13 = (f32[32,64,128]{2,1,0:T(8,128)S(1)}, f32[32,64,128]{2,1,0:T(8,128)S(1)}, u32[]{:S(2)}, u32[]{:S(2)}) collective-permute-start(f32[32,64,128]{2,1,0:T(8,128)S(1)} %fusion.1686), channel_id=1, source_target_pairs={{16,0},{17,1},{18,2},{19,3},{20,4},{21,5},{22,6},{23,7},{24,8},{25... | collective-permute-start | bytes 3145736 | tf_op jit(solution)/shard_map/ppermute | solution.py:17
  528.7 24.0 %collective-permute-start.12 = (f32[32,64,128]{2,1,0:T(8,128)S(1)}, f32[32,64,128]{2,1,0:T(8,128)}, u32[]{:S(2)}, u32[]{:S(2)}) collective-permute-start(f32[32,64,128]{2,1,0:T(8,128)S(1)} %fusion.1686), channel_id=1, source_target_pairs={{0,16},{1,17},{2,18},{3,19},{4,20},{5,21},{6,22},{7,23},{8,24},{9,... | collective-permute-start | bytes 3145736 | tf_op jit(solution)/shard_map/ppermute | solution.py:14
  610.0 13.2 %collective-permute-start.15 = (f32[32,32,128]{2,1,0:T(8,128)S(1)}, f32[32,32,128]{2,1,0:T(8,128)S(1)}, u32[]{:S(2)}, u32[]{:S(2)}) collective-permute-start(f32[32,32,128]{2,1,0:T(8,128)S(1)} %get-tuple-element.12), channel_id=1, source_target_pairs={{8,0},{9,1},{10,2},{11,3},{12,4},{13,5},{14,6},{15,7},{24,16},{25,... | collective-permute-start | bytes 1572872 | tf_op jit(solution)/shard_map/ppermute | solution.py:17
  611.3 13.7 %collective-permute-start.14 = (f32[32,32,128]{2,1,0:T(8,128)S(1)}, f32[32,32,128]{2,1,0:T(8,128)}, u32[]{:S(2)}, u32[]{:S(2)}) collective-permute-start(f32[32,32,128]{2,1,0:T(8,128)S(1)} %get-tuple-element.11), channel_id=1, source_target_pairs={{0,8},{1,9},{2,10},{3,11},{4,12},{5,13},{6,14},{7,15},{16,24},{17,... | collective-permute-start | bytes 1572872 | tf_op jit(solution)/shard_map/ppermute | solution.py:14
  690.2 14.0 %collective-permute-start.17 = (f32[32,64,32]{1,2,0:T(8,128)}, f32[32,64,32]{1,2,0:T(8,128)}, u32[]{:S(2)}, u32[]{:S(2)}) collective-permute-start(f32[32,64,32]{1,2,0:T(8,128)} %copy.24), channel_id=1, source_target_pairs={{1,0},{2,1},{3,2},{4,3},{5,4},{6,5},{7,6},{9,8},{10,9},{11,10},{12... | collective-permute-start | bytes 786440 | tf_op jit(solution)/shard_map/ppermute | solution.py:17
  693.2 13.3 %collective-permute-start.16 = (f32[32,64,32]{1,2,0:T(8,128)}, f32[32,64,32]{1,2,0:T(8,128)}, u32[]{:S(2)}, u32[]{:S(2)}) collective-permute-start(f32[32,64,32]{1,2,0:T(8,128)} %copy.22), channel_id=1, source_target_pairs={{0,1},{1,2},{2,3},{3,4},{4,5},{5,6},{6,7},{8,9},{9,10},{10,11},{11... | collective-permute-start | bytes 786440 | tf_op jit(solution)/shard_map/ppermute | solution.py:14
  792.1 18.6 %collective-permute-start.19 = (f32[32,64,128]{2,1,0:T(8,128)S(1)}, f32[32,64,128]{2,1,0:T(8,128)S(1)}, u32[]{:S(2)}, u32[]{:S(2)}) collective-permute-start(f32[32,64,128]{2,1,0:T(8,128)S(1)} %fusion.1497), channel_id=1, source_target_pairs={{16,0},{17,1},{18,2},{19,3},{20,4},{21,5},{22,6},{23,7},{24,8},{25... | collective-permute-start | bytes 3145736 | tf_op jit(solution)/shard_map/ppermute | solution.py:17
  793.4 19.1 %collective-permute-start.18 = (f32[32,64,128]{2,1,0:T(8,128)S(1)}, f32[32,64,128]{2,1,0:T(8,128)S(1)}, u32[]{:S(2)}, u32[]{:S(2)}) collective-permute-start(f32[32,64,128]{2,1,0:T(8,128)S(1)} %fusion.1497), channel_id=1, source_target_pairs={{0,16},{1,17},{2,18},{3,19},{4,20},{5,21},{6,22},{7,23},{8,24},{9,... | collective-permute-start | bytes 3145736 | tf_op jit(solution)/shard_map/ppermute | solution.py:14
  863.5 9.9 collective-permute-start.21
  864.8 10.1 collective-permute-start.20
  927.5 20.4 %collective-permute-start.23 = (f32[32,64,32]{1,2,0:T(8,128)}, f32[32,64,32]{1,2,0:T(8,128)}, u32[]{:S(2)}, u32[]{:S(2)}) collective-permute-start(f32[32,64,32]{1,2,0:T(8,128)} %copy.28), channel_id=1, source_target_pairs={{1,0},{2,1},{3,2},{4,3},{5,4},{6,5},{7,6},{9,8},{10,9},{11,10},{12... | collective-permute-start | bytes 786440 | tf_op jit(solution)/shard_map/ppermute | solution.py:17
  929.4 23.2 %copy-start.2 = (f32[32,64,128]{2,1,0:T(8,128)S(1)}, f32[32,64,128]{2,1,0:T(8,128)}, u32[]{:S(2)}) copy-start(f32[32,64,128]{2,1,0:T(8,128)} %copy-done.1) | copy-start | bytes 3145732
  930.6 19.6 %collective-permute-start.22 = (f32[32,64,32]{1,2,0:T(8,128)}, f32[32,64,32]{1,2,0:T(8,128)}, u32[]{:S(2)}, u32[]{:S(2)}) collective-permute-start(f32[32,64,32]{1,2,0:T(8,128)} %copy.26), channel_id=1, source_target_pairs={{0,1},{1,2},{2,3},{3,4},{4,5},{5,6},{6,7},{8,9},{9,10},{10,11},{11... | collective-permute-start | bytes 786440 | tf_op jit(solution)/shard_map/ppermute | solution.py:14
  (3 other events, 2.4 us)
where the time goes:
time: 1050 us; the launch traced here: 1040 us
  other arithmetic  790 us (75%)
  waiting for transfers between devices  105 us (10%)
  starting transfers between devices  84.2 us (8%)
  local copies, waits for them, and re-layouts  56.7 us (5%)
    add x8, other arithmetic, pass_axis(): result + kernel[offset] * lax.slice_in_dim(extended, offset, offset + len...  451 us
    div x2, other arithmetic, per_device(): quotient = observed / blurred  166 us
    mul x2, other arithmetic, per_device(): estimate * blur(quotient, kernel_z[::-1], kernel_x[::-1], kernel_y[::-1])  166 us
    ppermute x12, waiting for transfers between devices, extended_2(): lax.ppermute(lax.slice_in_dim(block, 0, width, axis=dim), axis, backward)  83.1 us
    ppermute x12, starting transfers between devices, extended_2(): lax.ppermute(lax.slice_in_dim(block, block.shape[dim] - width, None, axis...  63.1 us
    ppermute x12, waiting for transfers between devices, extended_2(): lax.ppermute(lax.slice_in_dim(block, block.shape[dim] - width, None, axis...  21.9 us
    ppermute x12, starting transfers between devices, extended_2(): lax.ppermute(lax.slice_in_dim(block, 0, width, axis=dim), axis, backward)  21 us
  transfers between devices with their start and end apart: 24, of which 24 were waited for; matrix products, arithmetic and copies ran while one was open for 4% of the time, Pallas kernels for 0%

commit v1 on v0

v1 whole, which is shorter than its diff:
```python
import functools
import jax
import jax.numpy as jnp
from jax import lax
from jax.experimental import pallas as pl
from jax.experimental.pallas import tpu as pltpu
from jax.sharding import PartitionSpec as P

ITERS = 2
LANES = 128
F32 = jnp.float32
BF16 = jnp.bfloat16
VMEM = pl.BlockSpec(memory_space=pltpu.VMEM)
SMEM = pl.BlockSpec(memory_space=pltpu.SMEM)
PARAMS = pltpu.CompilerParams(vmem_limit_bytes=40 * 1024 * 1024)


def shaped(*shape):
    return jax.ShapeDtypeStruct(shape, F32)


def split(value):
    high = value.astype(BF16)
    return high, (value - high.astype(F32)).astype(BF16)


def dot(left, right):
    return lax.dot_general(left, right, (((1,), (0,)), ((), ())), preferred_element_type=F32)


def banded(taps, rows, width, start):
    room = (width + 2 * LANES - 1) // LANES * LANES
    base = jnp.concatenate([taps, jnp.zeros((1, room - LANES), F32)], axis=1)
    base = jnp.broadcast_to(base, (rows, room))
    return pltpu.roll(base, start % room, 1, stride=1, stride_axis=0)[:, :width]


def taps_kernel(psf_ref, out_ref):
    count = psf_ref.shape[1]
    row = lax.broadcasted_iota(jnp.int32, (LANES, LANES), 0)
    lane = lax.broadcasted_iota(jnp.int32, (LANES, LANES), 1)
    out_ref[...] = jnp.zeros_like(out_ref)
    for d in range(3):
        raw = psf_ref[d : d + 1, :]
        taps = raw / jnp.sum(raw, axis=1, keepdims=True)
        taps = jnp.concatenate([taps, jnp.zeros((1, LANES - count), F32)], axis=1)
        column = jnp.transpose(jnp.broadcast_to(taps, (LANES, LANES)))
        turned = jnp.sum(jnp.where(row + lane == count - 1, column, 0.0), axis=0, keepdims=True)
        out_ref[2 * d : 2 * d + 1, :] = taps
        out_ref[2 * d + 1 : 2 * d + 2, :] = turned


def turn_kernel(radius, chunk, where_ref, block_ref, own_ref, first_ref, last_ref, *part_refs):
    length, columns = block_ref.shape
    for at in range(0, length, LANES):
        own_ref[:, at : at + LANES] = jnp.transpose(block_ref[at : at + LANES, :])
    first_ref[...] = own_ref[:radius, :]
    last_ref[...] = own_ref[columns - radius :, :]
    for slot, part_ref in enumerate(part_refs):
        place = pl.multiple_of(where_ref[slot] * chunk, chunk)
        part_ref[...] = own_ref[pl.ds(place, chunk), :]


def ordered_rows(matrix, where_ref, order_ref, chunk):
    order_ref[1] = matrix
    for slot in range(matrix.shape[0] // chunk):
        place = pl.multiple_of(where_ref[slot] * chunk, chunk)
        order_ref[0, pl.ds(slot * chunk, chunk), :] = order_ref[1, pl.ds(place, chunk), :]
    return order_ref[0]


def left_product(stacked, high_rows, value):
    high, low = split(value)
    both = dot(stacked, high)
    return both[:high_rows] + (both[high_rows:] + dot(stacked[:high_rows], low))


def stack(matrix):
    return jnp.concatenate(split(matrix), axis=0)


def first_y_kernel(chunk, where_ref, taps_ref, own_ref, low_ref, high_ref, *refs):
    part_refs, order_ref = refs[:-1], refs[-1]
    columns, length = own_ref.shape
    radius = low_ref.shape[0]
    matrix = banded(taps_ref[4:5, :], columns, columns + 2 * radius, 0)
    matrix = stack(ordered_rows(matrix, where_ref, order_ref, chunk))
    step = 2 * LANES
    for at in range(0, length, step):
        here = slice(at, at + step)
        field = jnp.concatenate([low_ref[:, here], own_ref[:, here], high_ref[:, here]], axis=0)
        result = left_product(matrix, columns, field)
        for slot, part_ref in enumerate(part_refs):
            part_ref[:, here] = result[slot * chunk : (slot + 1) * chunk]


def gather_kernel(span, chunk, where_ref, *refs):
    count = where_ref.shape[0] // 2
    part_refs, (own_ref, first_ref, last_ref) = refs[:count], refs[count:]
    columns = own_ref.shape[0]
    for slot, part_ref in enumerate(part_refs):
        place = pl.multiple_of(where_ref[count + slot] * chunk, chunk)
        own_ref[pl.ds(place, chunk), :] = part_ref[...]
    first_ref[...] = own_ref[:span, :]
    last_ref[...] = own_ref[columns - span :, :]


def middle_y_kernel(chunk, where_ref, taps_ref, own_ref, low_ref, high_ref, seen_ref, seen_low_ref, seen_high_ref,
                    estimate_ref, *refs):
    part_refs, order_ref = refs[:-1], refs[-1]
    columns, length = own_ref.shape
    radius = seen_low_ref.shape[0]
    wide = columns + 2 * radius
    back = stack(banded(taps_ref[5:6, :], wide, wide + 2 * radius, 0))
    matrix = banded(taps_ref[4:5, :], columns, wide, 0)
    matrix = stack(ordered_rows(matrix, where_ref, order_ref, chunk))
    step = 2 * LANES
    for at in range(0, length, step):
        here = slice(at, at + step)
        field = jnp.concatenate([low_ref[:, here], own_ref[:, here], high_ref[:, here]], axis=0)
        seen = jnp.concatenate([seen_low_ref[:, here], seen_ref[:, here], seen_high_ref[:, here]], axis=0)
        estimate = seen * left_product(back, wide, field)
        estimate_ref[:, here] = estimate[radius : radius + columns]
        result = left_product(matrix, columns, estimate)
        for slot, part_ref in enumerate(part_refs):
            part_ref[:, here] = result[slot * chunk : (slot + 1) * chunk]


def last_y_kernel(taps_ref, own_ref, low_ref, high_ref, estimate_ref, out_ref):
    columns, length = own_ref.shape
    radius = low_ref.shape[0]
    back = stack(banded(taps_ref[5:6, :], columns, columns + 2 * radius, 0))
    step = 2 * LANES
    for at in range(0, length, step):
        here = slice(at, at + step)
        field = jnp.concatenate([low_ref[:, here], own_ref[:, here], high_ref[:, here]], axis=0)
        estimate = estimate_ref[:, here] * left_product(back, columns, field)
        for tile in range(0, step, LANES):
            out_ref[at + tile : at + tile + LANES, :] = jnp.transpose(estimate[:, tile : tile + LANES])


def put_rows(ref, lines, value):
    for tile in range(ref.shape[0]):
        ref[tile, lines, :] = value[:, tile * LANES : (tile + 1) * LANES]


def get_rows(ref, lines):
    return jnp.concatenate([ref[tile, lines, :] for tile in range(ref.shape[0])], axis=1)


def seen_kernel(sizes, where_ref, *refs):
    groups, beside, rows = sizes
    part_refs, out_ref, held_ref = refs[:-2], refs[-2], refs[-1]
    chunk, length = part_refs[0].shape
    tiles = length // LANES
    per = LANES // rows
    fill(sizes, where_ref, part_refs, held_ref)
    for at in range(groups * tiles):
        for k in range(per):
            pieces = [held_ref[b, at * chunk : (at + 1) * chunk, k * rows : (k + 1) * rows] for b in range(beside)]
            place = (at * per + k) * chunk
            put_rows(out_ref, slice(place, place + chunk), jnp.concatenate(pieces, axis=1))


def fill(sizes, where_ref, part_refs, held_ref):
    groups, beside, rows = sizes
    chunk, length = part_refs[0].shape
    tiles = length // LANES
    for slot, part_ref in enumerate(part_refs):
        dz, dx = slot // beside, slot % beside
        source_z = lax.rem(where_ref[0] + groups - dz, groups)
        source_x = lax.rem(where_ref[1] + beside - dx, beside)
        for t in range(tiles):
            place = pl.multiple_of((source_z * tiles + t) * chunk, chunk)
            held_ref[source_x, pl.ds(place, chunk), :] = part_ref[:, t * LANES : (t + 1) * LANES]


def planes_kernel(sizes, radius, where_ref, taps_ref, seen_ref, *refs):
    groups, beside, rows = sizes
    count = groups * beside
    part_refs, out_refs = refs[:count], refs[count : 2 * count]
    held_ref, field_ref, other_ref, weight_ref = refs[2 * count :]
    chunk, length = part_refs[0].shape
    tiles = length // LANES
    per = LANES // rows
    width = beside * rows
    planes = groups * tiles * per
    fill(sizes, where_ref, part_refs, held_ref)

    forward = banded(taps_ref[3:4, :], width, width, -radius)
    blocks = []
    for b in range(beside):
        for k in range(per):
            line = [jnp.zeros((rows, width), F32)] * per
            line[k] = forward[b * rows : (b + 1) * rows]
            blocks.append(jnp.concatenate(line, axis=1))
    high, low = split(jnp.concatenate(blocks, axis=0))
    both = jnp.concatenate([high, low], axis=1)
    group = min(tiles, max(1, 256 // chunk))
    for at in range(0, groups * tiles, group):
        here = slice(at * chunk, (at + group) * chunk)
        left = jnp.concatenate([held_ref[b, here, :] for b in range(beside)], axis=1)
        left_high, left_low = split(left)
        result = dot(left_high, both)
        result = result[:, : per * width] + (result[:, per * width :] + dot(left_low, high))
        for g in range(group):
            for k in range(per):
                place = ((at + g) * per + k) * chunk
                part = result[g * chunk : (g + 1) * chunk, k * width : (k + 1) * width]
                put_rows(field_ref, slice(place, place + chunk), part)

    def doubled(matrix):
        high, low = split(matrix)
        return jnp.concatenate(
            [jnp.concatenate([high, high], axis=1), jnp.concatenate([low, jnp.zeros_like(low)], axis=1)], axis=0
        )

    ahead = doubled(banded(taps_ref[0:1, :], planes, planes, -radius))
    back = doubled(banded(taps_ref[1:2, :], planes, planes, -radius))

    def over_planes(matrix, value):
        result = dot(matrix, jnp.concatenate(split(value), axis=0))
        return result[:planes] + result[planes:]

    for y in range(0, chunk, 2):
        lines = [pl.ds(y + k, planes, stride=chunk) for k in range(2)]
        value = jnp.concatenate([get_rows(field_ref, line) for line in lines], axis=1)
        seen = jnp.concatenate([get_rows(seen_ref, line) for line in lines], axis=1)
        value = over_planes(back, seen / over_planes(ahead, value))
        for k, line in enumerate(lines):
            put_rows(other_ref, line, value[:, k * width : (k + 1) * width])

    turned = banded(taps_ref[2:3, :], width, width, -radius)
    for b in range(beside):
        blocks = []
        for k in range(per):
            line = [jnp.zeros((width, rows), F32)] * per
            line[k] = turned[:, b * rows : (b + 1) * rows]
            blocks.append(jnp.concatenate(line, axis=1))
        high, low = split(jnp.concatenate(blocks, axis=0))
        weight_ref[b] = jnp.concatenate([high, low], axis=1)
    for dz in range(groups):
        target_z = lax.rem(where_ref[0] + dz, groups)
        for at in range(0, tiles, group):
            pieces = []
            for g in range(group):
                line = []
                for k in range(per):
                    place = pl.multiple_of(((target_z * tiles + at + g) * per + k) * chunk, chunk)
                    line.append(get_rows(other_ref, pl.ds(place, chunk)))
                pieces.append(jnp.concatenate(line, axis=1))
            left_high, left_low = split(jnp.concatenate(pieces, axis=0))
            for dx in range(beside):
                target_x = lax.rem(where_ref[1] + dx, beside)
                result = dot(left_high, weight_ref[target_x])
                result = result[:, :LANES] + (result[:, LANES:] + dot(left_low, weight_ref[target_x][:, :LANES]))
                for g in range(group):
                    out_refs[dz * beside + dx][:, (at + g) * LANES : (at + g + 1) * LANES] = result[
                        g * chunk : (g + 1) * chunk
                    ]


def per_device(observed, psf_z, psf_x, psf_y):
    groups, beside = lax.axis_size("gz"), lax.axis_size("bx")
    along = lax.axis_size("by")
    count = groups * beside
    planes, rows, columns = observed.shape
    length = planes * rows
    chunk = columns // count
    radius = psf_z.shape[0] // 2
    sizes = (groups, beside, rows)
    me_z, me_x = lax.axis_index("gz"), lax.axis_index("bx")
    offsets = [(dz, dx) for dz in range(groups) for dx in range(beside)]
    place = jnp.stack([me_z, me_x]).astype(jnp.int32)
    ahead = [lax.rem(me_z + dz, groups) * beside + lax.rem(me_x + dx, beside) for dz, dx in offsets]
    behind = [
        lax.rem(me_z + groups - dz, groups) * beside + lax.rem(me_x + beside - dx, beside) for dz, dx in offsets
    ]
    where = jnp.stack(ahead + behind).astype(jnp.int32)

    def exchanged(parts):
        result = [parts[0]]
        for (dz, dx), part in list(zip(offsets, parts))[1:]:
            pairs = [
                (z * beside + x, ((z + dz) % groups) * beside + (x + dx) % beside)
                for z in range(groups)
                for x in range(beside)
            ]
            result.append(lax.ppermute(part, ("gz", "bx"), pairs))
        return result

    def from_sides(first, last):
        up = [(i, i + 1) for i in range(along - 1)]
        down = [(i + 1, i) for i in range(along - 1)]
        return lax.ppermute(last, "by", up), lax.ppermute(first, "by", down)

    part = shaped(chunk, length)
    whole = shaped(columns, length)

    def call(kernel, outs, specs, scratch=()):
        return pl.pallas_call(
            kernel,
            out_shape=outs,
            in_specs=specs,
            out_specs=jax.tree.map(lambda _: VMEM, outs),
            scratch_shapes=list(scratch),
            compiler_params=PARAMS,
        )

    seen, first, last, *parts = call(
        functools.partial(turn_kernel, radius, chunk),
        [whole, shaped(radius, length), shaped(radius, length)] + [part] * count,
        [SMEM, VMEM],
    )(where, observed.reshape(length, columns))
    seen_low, seen_high = from_sides(first, last)
    seen_parts = exchanged(parts)
    taps = call(taps_kernel, shaped(8, LANES), [VMEM])(jnp.stack([psf_z, psf_x, psf_y]))

    order = pltpu.VMEM((2, columns, columns + 2 * radius), F32)
    parts = call(
        functools.partial(first_y_kernel, chunk), [part] * count, [SMEM] + [VMEM] * 4, [order]
    )(where, taps, seen, seen_low, seen_high)
    parts = exchanged(parts)

    lines = groups * planes * chunk
    across = (beside * rows // LANES, lines, LANES)
    held = pltpu.VMEM((beside, groups * (length // LANES) * chunk, LANES), F32)
    seen_across = call(
        functools.partial(seen_kernel, sizes), shaped(*across), [SMEM] + [VMEM] * count, [held]
    )(place, *seen_parts)

    def through_planes(parts):
        return call(
            functools.partial(planes_kernel, sizes, radius),
            [part] * count,
            [SMEM] + [VMEM] * (2 + count),
            [
                held,
                pltpu.VMEM(across, F32),
                pltpu.VMEM(across, F32),
                pltpu.VMEM((beside, beside * LANES, 2 * LANES), BF16),
            ],
        )(place, taps, seen_across, *parts)

    def gathered(parts, span):
        own, first, last = call(
            functools.partial(gather_kernel, span, chunk),
            [whole, shaped(span, length), shaped(span, length)],
            [SMEM] + [VMEM] * count,
        )(where, *parts)
        return own, *from_sides(first, last)

    estimate = seen
    estimate_low, estimate_high = seen_low, seen_high
    for sweep in range(ITERS):
        parts = exchanged(through_planes(parts))
        if sweep < ITERS - 1:
            own, low, high = gathered(parts, 2 * radius)
            estimate, *parts = call(
                functools.partial(middle_y_kernel, chunk), [whole] + [part] * count, [SMEM] + [VMEM] * 7, [order]
            )(where, taps, own, low, high, estimate, estimate_low, estimate_high)
            parts = exchanged(parts)
        else:
            own, low, high = gathered(parts, radius)
            out = call(last_y_kernel, shaped(length, columns), [VMEM] * 5)(taps, own, low, high, estimate)
    return out.reshape(planes, rows, columns)


def solution(mesh):
    placed = (P("gz", "bx", "by"), P(), P(), P())
    return jax.shard_map(
        per_device, mesh=mesh, in_specs=placed, out_specs=P("gz", "bx", "by"), check_vma=False
    )
```

time: 1050 us -> 118 us (0.11); the launches traced: 1040 us -> 118 us
  other arithmetic: 790 us -> 0.08 us
  local copies, waits for them, and re-layouts: 56.7 us -> 2 us
  waiting for transfers between devices: 105 us -> 56.8 us
  starting transfers between devices: 84.2 us -> 41.5 us
  Pallas kernels: 0 us -> 17.5 us
    add x8 -> x0, other arithmetic: 451 us -> none  [pass_axis(): result + kernel[offset] * lax.slice_in_dim(extended, offset, offset + len...]
    div x5 -> x0, other arithmetic: 169 us -> none  [the longest x2 166 us: per_device(): quotient = observed / blurred]
    mul x2 -> x0, other arithmetic: 166 us -> none  [per_device(): estimate * blur(quotient, kernel_z[::-1], kernel_x[::-1], kernel_y[::-1])]
    ppermute x24 -> x21, waiting for transfers between devices: 105 us -> 56.8 us  [the longest x15 39.7 us: exchanged(): result.append(lax.ppermute(part, ('gz', 'bx'), pairs))]
    ppermute x24 -> x21, starting transfers between devices: 84.2 us -> 41.5 us  [the longest x6 27.6 us: from_sides(): return (lax.ppermute(last, 'by', up), lax.ppermute(first, 'by', down))]
    slice x40 -> x0, local copies, waits for them, and re-layouts: 34.6 us -> none  [the longest x18 12.8 us: pass_axis(): kernel[offset]]
    pallas_call x0 -> x10, Pallas kernels: none -> 17.5 us  [the longest x2 7.61 us: through_planes(): call(functools.partial(planes_kernel, sizes, radius), [part] * count, [SM...]
    ppermute x8 -> x0, local copies, waits for them, and re-layouts: 15.2 us -> none  [the longest x4 9.61 us: extended_2(): lax.ppermute(lax.slice_in_dim(block, block.shape[dim] - width, None, axis...]
  transfers between devices with their start and end apart: 24 -> 21, of which waited for: 24 -> 18; matrix products, arithmetic and copies ran while one was open for 4% -> 0% of each run, Pallas kernels for 0% -> 2%
where the time goes in v1:
time: 118 us
  waiting for transfers between devices  56.8 us (48%)
  starting transfers between devices  41.5 us (35%)
  Pallas kernels  17.5 us (15%)
  local copies, waits for them, and re-layouts  2 us (2%)
    ppermute x15, waiting for transfers between devices, exchanged(): result.append(lax.ppermute(part, ('gz', 'bx'), pairs))  39.7 us
    ppermute x6, starting transfers between devices, from_sides(): return (lax.ppermute(last, 'by', up), lax.ppermute(first, 'by', down))  27.6 us
    ppermute x6, waiting for transfers between devices, from_sides(): return (lax.ppermute(last, 'by', up), lax.ppermute(first, 'by', down))  17.1 us
    ppermute x15, starting transfers between devices, exchanged(): result.append(lax.ppermute(part, ('gz', 'bx'), pairs))  13.8 us
    pallas_call x2, Pallas kernels, through_planes(): call(functools.partial(planes_kernel, sizes, radius), [part] * count, [SM...  7.61 us
    pallas_call x1, Pallas kernels, per_device(): call(functools.partial(middle_y_kernel, chunk), [whole] + [part] * count,...  3.49 us
  transfers between devices with their start and end apart: 21, of which 18 were waited for; matrix products, arithmetic and copies ran while one was open for 0% of the time, Pallas kernels for 2%

profile of v1, /device:TPU:1, one launch (start us, length us, event | category | flops | bytes accessed | tf_op | source)
XLA Modules:
  0.0 118.0 jit_solution(6449789557713989240)
XLA Ops:
  0.1 1.2 %copy-done = f32[32,64,128]{2,1,0:T(8,128)S(1)} copy-done((f32[32,64,128]{2,1,0:T(8,128)S(1)}, f32[32,64,128]{2,1,0:T(8,128)}, u32[]{:S(2)}) %copy-start) | copy-done | bytes 1048600
  2.3 4.6 %collective-permute-start.3 = (f32[32,2048]{1,0:T(8,128)S(1)}, f32[32,2048]{1,0:T(8,128)S(1)}, u32[]{:S(2)}, u32[]{:S(2)}) collective-permute-start(f32[32,2048]{1,0:T(8,128)S(1)} %get-tuple-element.40), channel_id=1, source_target_pairs={{0,1},{1,2},{2,3},{3,4},{4,5},{5,6},{6,7},{8,9},{9,10},{10,11},{11... | collective-permute-start | bytes 786440 | tf_op jit(solution)/shard_map/ppermute | solution.py:295
  6.9 1.9 %collective-permute-start.4 = (f32[32,2048]{1,0:T(8,128)S(1)}, f32[32,2048]{1,0:T(8,128)S(1)}, u32[]{:S(2)}, u32[]{:S(2)}) collective-permute-start(f32[32,2048]{1,0:T(8,128)S(1)} %get-tuple-element.41), channel_id=1, source_target_pairs={{1,0},{2,1},{3,2},{4,3},{5,4},{6,5},{7,6},{9,8},{10,9},{11,10},{12... | collective-permute-start | bytes 786440 | tf_op jit(solution)/shard_map/ppermute | solution.py:295
  8.8 1.3 %collective-permute-start = (f32[32,2048]{1,0:T(8,128)S(1)}, f32[32,2048]{1,0:T(8,128)S(1)}, u32[]{:S(2)}, u32[]{:S(2)}) collective-permute-start(f32[32,2048]{1,0:T(8,128)S(1)} %get-tuple-element.36), channel_id=1, source_target_pairs={{0,8},{8,0},{16,24},{24,16},{1,9},{9,1},{17,25},{25,17},{2,10},{10... | collective-permute-start | bytes 786440 | tf_op jit(solution)/shard_map/ppermute | solution.py:289
  12.4 2.4 %collective-permute-done.4.high_ref.seen_high_ref = f32[32,2048]{1,0:T(8,128)S(1)} collective-permute-done((f32[32,2048]{1,0:T(8,128)S(1)}, f32[32,2048]{1,0:T(8,128)S(1)}, u32[]{:S(2)}, u32[]{:S(2)}) %collective-permute-start.4) | collective-permute-done | bytes 262176 | tf_op jit(solution)/shard_map/ppermute | solution.py:295
  17.1 1.5 %collective-permute-start.6 = (f32[32,2048]{1,0:T(8,128)S(1)}, f32[32,2048]{1,0:T(8,128)S(1)}, u32[]{:S(2)}, u32[]{:S(2)}) collective-permute-start(f32[32,2048]{1,0:T(8,128)S(1)} %get-tuple-element.44), channel_id=1, source_target_pairs={{0,16},{8,24},{16,0},{24,8},{1,17},{9,25},{17,1},{25,9},{2,18},{10... | collective-permute-start | bytes 786440 | tf_op jit(solution)/shard_map/ppermute | solution.py:289
  18.9 4.9 %collective-permute-done.2.refs_3_ = f32[32,2048]{1,0:T(8,128)S(1)} collective-permute-done((f32[32,2048]{1,0:T(8,128)S(1)}, f32[32,2048]{1,0:T(8,128)S(1)}, u32[]{:S(2)}, u32[]{:S(2)}) %collective-permute-start.2) | collective-permute-done | bytes 262176 | tf_op jit(solution)/shard_map/ppermute | solution.py:289
  24.8 1.8 %collective-permute-done.5.refs_1_ = f32[32,2048]{1,0:T(8,128)S(1)} collective-permute-done((f32[32,2048]{1,0:T(8,128)S(1)}, f32[32,2048]{1,0:T(8,128)S(1)}, u32[]{:S(2)}, u32[]{:S(2)}) %collective-permute-start.5) | collective-permute-done | bytes 262176 | tf_op jit(solution)/shard_map/ppermute | solution.py:289
  26.6 3.2 %collective-permute-done.6.refs_2_ = f32[32,2048]{1,0:T(8,128)S(1)} collective-permute-done((f32[32,2048]{1,0:T(8,128)S(1)}, f32[32,2048]{1,0:T(8,128)S(1)}, u32[]{:S(2)}, u32[]{:S(2)}) %collective-permute-start.6) | collective-permute-done | bytes 262176 | tf_op jit(solution)/shard_map/ppermute | solution.py:289
  29.7 3.6 %collective-permute-done.7.refs_3_ = f32[32,2048]{1,0:T(8,128)S(1)} collective-permute-done((f32[32,2048]{1,0:T(8,128)S(1)}, f32[32,2048]{1,0:T(8,128)S(1)}, u32[]{:S(2)}, u32[]{:S(2)}) %collective-permute-start.7) | collective-permute-done | bytes 262176 | tf_op jit(solution)/shard_map/ppermute | solution.py:289
  33.3 3.8 %shard_map.50 = (f32[32,2048]{1,0:T(8,128)S(1)}, f32[32,2048]{1,0:T(8,128)S(1)}, f32[32,2048]{1,0:T(8,128)S(1)}, f32[32,2048]{1,0:T(8,128)S(1)}) custom-call(s32[2]{0:T(128)S(1)} %pad_add_fusion.where_ref, f32[8,128]{1,0:T(8,128)S(1)} %shard_map.46.taps_ref, f32[1,2048,128]{2,1,0:T(8,128)S(1)} %shard_map.48.seen_ref, ...), custom_call_target="tpu_custom_call" | custom-call | tf_op jit(solution)/shard_map/pallas_call | solution.py:333
  37.1 1.7 %collective-permute-start.8 = (f32[32,2048]{1,0:T(8,128)S(1)}, f32[32,2048]{1,0:T(8,128)S(1)}, u32[]{:S(2)}, u32[]{:S(2)}) collective-permute-start(f32[32,2048]{1,0:T(8,128)S(1)} %get-tuple-element.47), channel_id=1, source_target_pairs={{0,8},{8,0},{16,24},{24,16},{1,9},{9,1},{17,25},{25,17},{2,10},{10... | collective-permute-start | bytes 786440 | tf_op jit(solution)/shard_map/ppermute | solution.py:289
  40.1 5.2 %collective-permute-done.8.refs_1_ = f32[32,2048]{1,0:T(8,128)S(1)} collective-permute-done((f32[32,2048]{1,0:T(8,128)S(1)}, f32[32,2048]{1,0:T(8,128)S(1)}, u32[]{:S(2)}, u32[]{:S(2)}) %collective-permute-start.8) | collective-permute-done | bytes 262176 | tf_op jit(solution)/shard_map/ppermute | solution.py:289
  45.3 1.7 %collective-permute-done.9.refs_2_ = f32[32,2048]{1,0:T(8,128)S(1)} collective-permute-done((f32[32,2048]{1,0:T(8,128)S(1)}, f32[32,2048]{1,0:T(8,128)S(1)}, u32[]{:S(2)}, u32[]{:S(2)}) %collective-permute-start.9) | collective-permute-done | bytes 262176 | tf_op jit(solution)/shard_map/ppermute | solution.py:289
  47.0 5.4 %collective-permute-done.10.refs_3_ = f32[32,2048]{1,0:T(8,128)S(1)} collective-permute-done((f32[32,2048]{1,0:T(8,128)S(1)}, f32[32,2048]{1,0:T(8,128)S(1)}, u32[]{:S(2)}, u32[]{:S(2)}) %collective-permute-start.10) | collective-permute-done | bytes 262176 | tf_op jit(solution)/shard_map/ppermute | solution.py:289
  53.1 4.0 %collective-permute-start.11 = (f32[64,2048]{1,0:T(8,128)S(1)}, f32[64,2048]{1,0:T(8,128)S(1)}, u32[]{:S(2)}, u32[]{:S(2)}) collective-permute-start(f32[64,2048]{1,0:T(8,128)S(1)} %get-tuple-element.51), channel_id=1, source_target_pairs={{0,1},{1,2},{2,3},{3,4},{4,5},{5,6},{6,7},{8,9},{9,10},{10,11},{11... | collective-permute-start | bytes 1572872 | tf_op jit(solution)/shard_map/ppermute | solution.py:295
  57.1 1.9 %collective-permute-start.12 = (f32[64,2048]{1,0:T(8,128)S(1)}, f32[64,2048]{1,0:T(8,128)S(1)}, u32[]{:S(2)}, u32[]{:S(2)}) collective-permute-start(f32[64,2048]{1,0:T(8,128)S(1)} %get-tuple-element.52), channel_id=1, source_target_pairs={{1,0},{2,1},{3,2},{4,3},{5,4},{6,5},{7,6},{9,8},{10,9},{11,10},{12... | collective-permute-start | bytes 1572872 | tf_op jit(solution)/shard_map/ppermute | solution.py:295
  59.0 4.2 %collective-permute-done.11.low_ref = f32[64,2048]{1,0:T(8,128)S(1)} collective-permute-done((f32[64,2048]{1,0:T(8,128)S(1)}, f32[64,2048]{1,0:T(8,128)S(1)}, u32[]{:S(2)}, u32[]{:S(2)}) %collective-permute-start.11) | collective-permute-done | bytes 524320 | tf_op jit(solution)/shard_map/ppermute | solution.py:295
  63.2 4.7 %collective-permute-done.12.high_ref = f32[64,2048]{1,0:T(8,128)S(1)} collective-permute-done((f32[64,2048]{1,0:T(8,128)S(1)}, f32[64,2048]{1,0:T(8,128)S(1)}, u32[]{:S(2)}, u32[]{:S(2)}) %collective-permute-start.12) | collective-permute-done | bytes 524320 | tf_op jit(solution)/shard_map/ppermute | solution.py:295
  67.9 3.5 %shard_map.52 = (f32[128,2048]{1,0:T(8,128)S(1)}, f32[32,2048]{1,0:T(8,128)S(1)}, f32[32,2048]{1,0:T(8,128)S(1)}, f32[32,2048]{1,0:T(8,128)S(1)}, f32[32,2048]{1,0:T(8,128)S(1)}) custom-call(s32[8]{0:T(128)S(1)} %stack.57.where_ref, f32[8,128]{1,0:T(8,128)S(1)} %shard_map.46.taps_ref, f32[128,2048]{1,0:T(8,128)S(1)} %get-tuple-element.50.own_ref, ...), custom_call_target="tpu_custom_call" | custom-call | tf_op jit(solution)/shard_map/pallas_call | solution.py:359
  71.4 1.3 %collective-permute-start.13 = (f32[32,2048]{1,0:T(8,128)S(1)}, f32[32,2048]{1,0:T(8,128)S(1)}, u32[]{:S(2)}, u32[]{:S(2)}) collective-permute-start(f32[32,2048]{1,0:T(8,128)S(1)} %get-tuple-element.54), channel_id=1, source_target_pairs={{0,8},{8,0},{16,24},{24,16},{1,9},{9,1},{17,25},{25,17},{2,10},{10... | collective-permute-start | bytes 786440 | tf_op jit(solution)/shard_map/ppermute | solution.py:289
  74.1 3.1 %collective-permute-done.13.refs_1_ = f32[32,2048]{1,0:T(8,128)S(1)} collective-permute-done((f32[32,2048]{1,0:T(8,128)S(1)}, f32[32,2048]{1,0:T(8,128)S(1)}, u32[]{:S(2)}, u32[]{:S(2)}) %collective-permute-start.13) | collective-permute-done | bytes 262176 | tf_op jit(solution)/shard_map/ppermute | solution.py:289
  77.9 2.8 %collective-permute-done.15.refs_3_ = f32[32,2048]{1,0:T(8,128)S(1)} collective-permute-done((f32[32,2048]{1,0:T(8,128)S(1)}, f32[32,2048]{1,0:T(8,128)S(1)}, u32[]{:S(2)}, u32[]{:S(2)}) %collective-permute-start.15) | collective-permute-done | bytes 262176 | tf_op jit(solution)/shard_map/ppermute | solution.py:289
  80.7 3.8 %shard_map.53 = (f32[32,2048]{1,0:T(8,128)S(1)}, f32[32,2048]{1,0:T(8,128)S(1)}, f32[32,2048]{1,0:T(8,128)S(1)}, f32[32,2048]{1,0:T(8,128)S(1)}) custom-call(s32[2]{0:T(128)S(1)} %pad_add_fusion.where_ref, f32[8,128]{1,0:T(8,128)S(1)} %shard_map.46.taps_ref, f32[1,2048,128]{2,1,0:T(8,128)S(1)} %shard_map.48.seen_ref, ...), custom_call_target="tpu_custom_call" | custom-call | tf_op jit(solution)/shard_map/pallas_call | solution.py:333
  84.5 1.3 %collective-permute-start.16 = (f32[32,2048]{1,0:T(8,128)S(1)}, f32[32,2048]{1,0:T(8,128)S(1)}, u32[]{:S(2)}, u32[]{:S(2)}) collective-permute-start(f32[32,2048]{1,0:T(8,128)S(1)} %get-tuple-element.58), channel_id=1, source_target_pairs={{0,8},{8,0},{16,24},{24,16},{1,9},{9,1},{17,25},{25,17},{2,10},{10... | collective-permute-start | bytes 786440 | tf_op jit(solution)/shard_map/ppermute | solution.py:289
  87.2 4.6 %collective-permute-done.16.refs_1_ = f32[32,2048]{1,0:T(8,128)S(1)} collective-permute-done((f32[32,2048]{1,0:T(8,128)S(1)}, f32[32,2048]{1,0:T(8,128)S(1)}, u32[]{:S(2)}, u32[]{:S(2)}) %collective-permute-start.16) | collective-permute-done | bytes 262176 | tf_op jit(solution)/shard_map/ppermute | solution.py:289
  91.9 2.8 %collective-permute-done.18.refs_3_ = f32[32,2048]{1,0:T(8,128)S(1)} collective-permute-done((f32[32,2048]{1,0:T(8,128)S(1)}, f32[32,2048]{1,0:T(8,128)S(1)}, u32[]{:S(2)}, u32[]{:S(2)}) %collective-permute-start.18) | collective-permute-done | bytes 262176 | tf_op jit(solution)/shard_map/ppermute | solution.py:289
  95.3 13.2 %collective-permute-start.19 = (f32[32,2048]{1,0:T(8,128)S(1)}, f32[32,2048]{1,0:T(8,128)S(1)}, u32[]{:S(2)}, u32[]{:S(2)}) collective-permute-start(f32[32,2048]{1,0:T(8,128)S(1)} %get-tuple-element.62), channel_id=1, source_target_pairs={{0,1},{1,2},{2,3},{3,4},{4,5},{5,6},{6,7},{8,9},{9,10},{10,11},{11... | collective-permute-start | bytes 786440 | tf_op jit(solution)/shard_map/ppermute | solution.py:295
  108.6 1.9 %collective-permute-start.20 = (f32[32,2048]{1,0:T(8,128)S(1)}, f32[32,2048]{1,0:T(8,128)S(1)}, u32[]{:S(2)}, u32[]{:S(2)}) collective-permute-start(f32[32,2048]{1,0:T(8,128)S(1)} %get-tuple-element.63), channel_id=1, source_target_pairs={{1,0},{2,1},{3,2},{4,3},{5,4},{6,5},{7,6},{9,8},{10,9},{11,10},{12... | collective-permute-start | bytes 786440 | tf_op jit(solution)/shard_map/ppermute | solution.py:295
  110.5 1.4 %collective-permute-done.19.low_ref = f32[32,2048]{1,0:T(8,128)S(1)} collective-permute-done((f32[32,2048]{1,0:T(8,128)S(1)}, f32[32,2048]{1,0:T(8,128)S(1)}, u32[]{:S(2)}, u32[]{:S(2)}) %collective-permute-start.19) | collective-permute-done | bytes 262176 | tf_op jit(solution)/shard_map/ppermute | solution.py:295
  111.9 4.4 %collective-permute-done.20.high_ref = f32[32,2048]{1,0:T(8,128)S(1)} collective-permute-done((f32[32,2048]{1,0:T(8,128)S(1)}, f32[32,2048]{1,0:T(8,128)S(1)}, u32[]{:S(2)}, u32[]{:S(2)}) %collective-permute-start.20) | collective-permute-done | bytes 262176 | tf_op jit(solution)/shard_map/ppermute | solution.py:295
  116.3 1.8 %shard_map.55 = f32[2048,128]{1,0:T(8,128)} custom-call(f32[8,128]{1,0:T(8,128)S(1)} %shard_map.46.taps_ref, f32[128,2048]{1,0:T(8,128)S(1)} %get-tuple-element.61.own_ref, f32[32,2048]{1,0:T(8,128)S(1)} %collective-permute-done.19.low_ref, f32[32,2048]{1,0:T(8,128)S(1)} %collective-permute-done.20.high_ref, f32[128,2048]{1,0:T(8,128)S(1)} %get-tuple-element.64.estimate_ref), custom_call_target="tpu_custom_call" | custom-call | tf_op jit(solution)/shard_map/pallas_call | solution.py:365
  (31 shorter events, 12.9 us)
Async XLA Ops:
  0.1 1.2 %copy-start = (f32[32,64,128]{2,1,0:T(8,128)S(1)}, f32[32,64,128]{2,1,0:T(8,128)}, u32[]{:S(2)}) copy-start(f32[32,64,128]{2,1,0:T(8,128)} %param.4) | copy-start | bytes 3145732
  2.3 10.2 %collective-permute-start.3 = (f32[32,2048]{1,0:T(8,128)S(1)}, f32[32,2048]{1,0:T(8,128)S(1)}, u32[]{:S(2)}, u32[]{:S(2)}) collective-permute-start(f32[32,2048]{1,0:T(8,128)S(1)} %get-tuple-element.40), channel_id=1, source_target_pairs={{0,1},{1,2},{2,3},{3,4},{4,5},{5,6},{6,7},{8,9},{9,10},{10,11},{11... | collective-permute-start | bytes 786440 | tf_op jit(solution)/shard_map/ppermute | solution.py:295
  6.9 8.0 %collective-permute-start.4 = (f32[32,2048]{1,0:T(8,128)S(1)}, f32[32,2048]{1,0:T(8,128)S(1)}, u32[]{:S(2)}, u32[]{:S(2)}) collective-permute-start(f32[32,2048]{1,0:T(8,128)S(1)} %get-tuple-element.41), channel_id=1, source_target_pairs={{1,0},{2,1},{3,2},{4,3},{5,4},{6,5},{7,6},{9,8},{10,9},{11,10},{12... | collective-permute-start | bytes 786440 | tf_op jit(solution)/shard_map/ppermute | solution.py:295
  8.8 9.8 %collective-permute-start = (f32[32,2048]{1,0:T(8,128)S(1)}, f32[32,2048]{1,0:T(8,128)S(1)}, u32[]{:S(2)}, u32[]{:S(2)}) collective-permute-start(f32[32,2048]{1,0:T(8,128)S(1)} %get-tuple-element.36), channel_id=1, source_target_pairs={{0,8},{8,0},{16,24},{24,16},{1,9},{9,1},{17,25},{25,17},{2,10},{10... | collective-permute-start | bytes 786440 | tf_op jit(solution)/shard_map/ppermute | solution.py:289
  10.1 8.8 %collective-permute-start.1 = (f32[32,2048]{1,0:T(8,128)S(1)}, f32[32,2048]{1,0:T(8,128)S(1)}, u32[]{:S(2)}, u32[]{:S(2)}) collective-permute-start(f32[32,2048]{1,0:T(8,128)S(1)} %get-tuple-element.37), channel_id=1, source_target_pairs={{0,16},{8,24},{16,0},{24,8},{1,17},{9,25},{17,1},{25,9},{2,18},{10... | collective-permute-start | bytes 786440 | tf_op jit(solution)/shard_map/ppermute | solution.py:289
  11.3 12.5 %collective-permute-start.2 = (f32[32,2048]{1,0:T(8,128)S(1)}, f32[32,2048]{1,0:T(8,128)S(1)}, u32[]{:S(2)}, u32[]{:S(2)}) collective-permute-start(f32[32,2048]{1,0:T(8,128)S(1)} %get-tuple-element.38), channel_id=1, source_target_pairs={{0,24},{8,16},{16,8},{24,0},{1,25},{9,17},{17,9},{25,1},{2,26},{10... | collective-permute-start | bytes 786440 | tf_op jit(solution)/shard_map/ppermute | solution.py:289
  11.5 0.7 copy-start.1
  11.5 0.7 copy-start.2
  11.5 0.7 copy-start.3
  16.1 10.5 %collective-permute-start.5 = (f32[32,2048]{1,0:T(8,128)S(1)}, f32[32,2048]{1,0:T(8,128)S(1)}, u32[]{:S(2)}, u32[]{:S(2)}) collective-permute-start(f32[32,2048]{1,0:T(8,128)S(1)} %get-tuple-element.43), channel_id=1, source_target_pairs={{0,8},{8,0},{16,24},{24,16},{1,9},{9,1},{17,25},{25,17},{2,10},{10... | collective-permute-start | bytes 786440 | tf_op jit(solution)/shard_map/ppermute | solution.py:289
  17.1 12.7 %collective-permute-start.6 = (f32[32,2048]{1,0:T(8,128)S(1)}, f32[32,2048]{1,0:T(8,128)S(1)}, u32[]{:S(2)}, u32[]{:S(2)}) collective-permute-start(f32[32,2048]{1,0:T(8,128)S(1)} %get-tuple-element.44), channel_id=1, source_target_pairs={{0,16},{8,24},{16,0},{24,8},{1,17},{9,25},{17,1},{25,9},{2,18},{10... | collective-permute-start | bytes 786440 | tf_op jit(solution)/shard_map/ppermute | solution.py:289
  18.6 14.7 %collective-permute-start.7 = (f32[32,2048]{1,0:T(8,128)S(1)}, f32[32,2048]{1,0:T(8,128)S(1)}, u32[]{:S(2)}, u32[]{:S(2)}) collective-permute-start(f32[32,2048]{1,0:T(8,128)S(1)} %get-tuple-element.45), channel_id=1, source_target_pairs={{0,24},{8,16},{16,8},{24,0},{1,25},{9,17},{17,9},{25,1},{2,26},{10... | collective-permute-start | bytes 786440 | tf_op jit(solution)/shard_map/ppermute | solution.py:289
  37.1 8.2 %collective-permute-start.8 = (f32[32,2048]{1,0:T(8,128)S(1)}, f32[32,2048]{1,0:T(8,128)S(1)}, u32[]{:S(2)}, u32[]{:S(2)}) collective-permute-start(f32[32,2048]{1,0:T(8,128)S(1)} %get-tuple-element.47), channel_id=1, source_target_pairs={{0,8},{8,0},{16,24},{24,16},{1,9},{9,1},{17,25},{25,17},{2,10},{10... | collective-permute-start | bytes 786440 | tf_op jit(solution)/shard_map/ppermute | solution.py:289
  38.9 8.2 %collective-permute-start.9 = (f32[32,2048]{1,0:T(8,128)S(1)}, f32[32,2048]{1,0:T(8,128)S(1)}, u32[]{:S(2)}, u32[]{:S(2)}) collective-permute-start(f32[32,2048]{1,0:T(8,128)S(1)} %get-tuple-element.48), channel_id=1, source_target_pairs={{0,16},{8,24},{16,0},{24,8},{1,17},{9,25},{17,1},{25,9},{2,18},{10... | collective-permute-start | bytes 786440 | tf_op jit(solution)/shard_map/ppermute | solution.py:289
  40.1 12.3 %collective-permute-start.10 = (f32[32,2048]{1,0:T(8,128)S(1)}, f32[32,2048]{1,0:T(8,128)S(1)}, u32[]{:S(2)}, u32[]{:S(2)}) collective-permute-start(f32[32,2048]{1,0:T(8,128)S(1)} %get-tuple-element.49), channel_id=1, source_target_pairs={{0,24},{8,16},{16,8},{24,0},{1,25},{9,17},{17,9},{25,1},{2,26},{10... | collective-permute-start | bytes 786440 | tf_op jit(solution)/shard_map/ppermute | solution.py:289
  53.1 10.1 %collective-permute-start.11 = (f32[64,2048]{1,0:T(8,128)S(1)}, f32[64,2048]{1,0:T(8,128)S(1)}, u32[]{:S(2)}, u32[]{:S(2)}) collective-permute-start(f32[64,2048]{1,0:T(8,128)S(1)} %get-tuple-element.51), channel_id=1, source_target_pairs={{0,1},{1,2},{2,3},{3,4},{4,5},{5,6},{6,7},{8,9},{9,10},{10,11},{11... | collective-permute-start | bytes 1572872 | tf_op jit(solution)/shard_map/ppermute | solution.py:295
  57.1 10.8 %collective-permute-start.12 = (f32[64,2048]{1,0:T(8,128)S(1)}, f32[64,2048]{1,0:T(8,128)S(1)}, u32[]{:S(2)}, u32[]{:S(2)}) collective-permute-start(f32[64,2048]{1,0:T(8,128)S(1)} %get-tuple-element.52), channel_id=1, source_target_pairs={{1,0},{2,1},{3,2},{4,3},{5,4},{6,5},{7,6},{9,8},{10,9},{11,10},{12... | collective-permute-start | bytes 1572872 | tf_op jit(solution)/shard_map/ppermute | solution.py:295
  71.4 5.8 %collective-permute-start.13 = (f32[32,2048]{1,0:T(8,128)S(1)}, f32[32,2048]{1,0:T(8,128)S(1)}, u32[]{:S(2)}, u32[]{:S(2)}) collective-permute-start(f32[32,2048]{1,0:T(8,128)S(1)} %get-tuple-element.54), channel_id=1, source_target_pairs={{0,8},{8,0},{16,24},{24,16},{1,9},{9,1},{17,25},{25,17},{2,10},{10... | collective-permute-start | bytes 786440 | tf_op jit(solution)/shard_map/ppermute | solution.py:289
  72.7 5.2 %collective-permute-start.14 = (f32[32,2048]{1,0:T(8,128)S(1)}, f32[32,2048]{1,0:T(8,128)S(1)}, u32[]{:S(2)}, u32[]{:S(2)}) collective-permute-start(f32[32,2048]{1,0:T(8,128)S(1)} %get-tuple-element.55), channel_id=1, source_target_pairs={{0,16},{8,24},{16,0},{24,8},{1,17},{9,25},{17,1},{25,9},{2,18},{10... | collective-permute-start | bytes 786440 | tf_op jit(solution)/shard_map/ppermute | solution.py:289
  73.9 6.8 %collective-permute-start.15 = (f32[32,2048]{1,0:T(8,128)S(1)}, f32[32,2048]{1,0:T(8,128)S(1)}, u32[]{:S(2)}, u32[]{:S(2)}) collective-permute-start(f32[32,2048]{1,0:T(8,128)S(1)} %get-tuple-element.56), channel_id=1, source_target_pairs={{0,24},{8,16},{16,8},{24,0},{1,25},{9,17},{17,9},{25,1},{2,26},{10... | collective-permute-start | bytes 786440 | tf_op jit(solution)/shard_map/ppermute | solution.py:289
  84.5 7.3 %collective-permute-start.16 = (f32[32,2048]{1,0:T(8,128)S(1)}, f32[32,2048]{1,0:T(8,128)S(1)}, u32[]{:S(2)}, u32[]{:S(2)}) collective-permute-start(f32[32,2048]{1,0:T(8,128)S(1)} %get-tuple-element.58), channel_id=1, source_target_pairs={{0,8},{8,0},{16,24},{24,16},{1,9},{9,1},{17,25},{25,17},{2,10},{10... | collective-permute-start | bytes 786440 | tf_op jit(solution)/shard_map/ppermute | solution.py:289
  85.8 6.1 %collective-permute-start.17 = (f32[32,2048]{1,0:T(8,128)S(1)}, f32[32,2048]{1,0:T(8,128)S(1)}, u32[]{:S(2)}, u32[]{:S(2)}) collective-permute-start(f32[32,2048]{1,0:T(8,128)S(1)} %get-tuple-element.59), channel_id=1, source_target_pairs={{0,16},{8,24},{16,0},{24,8},{1,17},{9,25},{17,1},{25,9},{2,18},{10... | collective-permute-start | bytes 786440 | tf_op jit(solution)/shard_map/ppermute | solution.py:289
  87.0 7.6 %collective-permute-start.18 = (f32[32,2048]{1,0:T(8,128)S(1)}, f32[32,2048]{1,0:T(8,128)S(1)}, u32[]{:S(2)}, u32[]{:S(2)}) collective-permute-start(f32[32,2048]{1,0:T(8,128)S(1)} %get-tuple-element.60), channel_id=1, source_target_pairs={{0,24},{8,16},{16,8},{24,0},{1,25},{9,17},{17,9},{25,1},{2,26},{10... | collective-permute-start | bytes 786440 | tf_op jit(solution)/shard_map/ppermute | solution.py:289
  95.3 16.5 %collective-permute-start.19 = (f32[32,2048]{1,0:T(8,128)S(1)}, f32[32,2048]{1,0:T(8,128)S(1)}, u32[]{:S(2)}, u32[]{:S(2)}) collective-permute-start(f32[32,2048]{1,0:T(8,128)S(1)} %get-tuple-element.62), channel_id=1, source_target_pairs={{0,1},{1,2},{2,3},{3,4},{4,5},{5,6},{6,7},{8,9},{9,10},{10,11},{11... | collective-permute-start | bytes 786440 | tf_op jit(solution)/shard_map/ppermute | solution.py:295
  108.6 7.7 %collective-permute-start.20 = (f32[32,2048]{1,0:T(8,128)S(1)}, f32[32,2048]{1,0:T(8,128)S(1)}, u32[]{:S(2)}, u32[]{:S(2)}) collective-permute-start(f32[32,2048]{1,0:T(8,128)S(1)} %get-tuple-element.63), channel_id=1, source_target_pairs={{1,0},{2,1},{3,2},{4,3},{5,4},{6,5},{7,6},{9,8},{10,9},{11,10},{12... | collective-permute-start | bytes 786440 | tf_op jit(solution)/shard_map/ppermute | solution.py:295

commit v2 on v0

v2 whole, which is shorter than its diff:
```python
import functools
import jax
import jax.numpy as jnp
from jax import lax
from jax.experimental import pallas as pl
from jax.experimental.pallas import tpu as pltpu
from jax.sharding import PartitionSpec as P

LANES = 128
RATE = 1150 * 1000 * 1000
STEP = 2 * LANES
F32 = jnp.float32
BF16 = jnp.bfloat16
VMEM = pl.BlockSpec(memory_space=pltpu.VMEM)
SMEM = pl.BlockSpec(memory_space=pltpu.SMEM)


def shaped(*shape):
    return jax.ShapeDtypeStruct(shape, F32)


def call(cost, kernel, outs, specs, scratch=()):
    return pl.pallas_call(
        kernel,
        out_shape=outs,
        in_specs=specs,
        out_specs=jax.tree.map(lambda _: VMEM, outs),
        scratch_shapes=list(scratch),
        compiler_params=pltpu.CompilerParams(vmem_limit_bytes=40 * 1024 * 1024),
        cost_estimate=pl.CostEstimate(flops=int(cost * RATE), bytes_accessed=0, transcendentals=0),
    )


def parts_of(columns, radius, count):
    outer = [(0, radius), (columns - radius, radius)]
    inner = [(radius, columns - 2 * radius)]
    fits = columns >= 3 * radius and count % 2 == 0
    for runs in (outer, inner):
        fits = fits and sum(size for _, size in runs) % (8 * count) == 0
    return [outer, inner] if fits else [[(0, columns)]]


def size_of(runs):
    return sum(size for _, size in runs)


def rows_of(value, runs):
    return jnp.concatenate([value[start : start + size] for start, size in runs], axis=0)


def place_of(runs, offset):
    place, before = runs[0][0] + offset, 0
    for (start, size), (after, _) in zip(runs, runs[1:]):
        before += size
        place = jnp.where(offset >= before, after - before + offset, place)
    return place


def split(value):
    high = value.astype(BF16)
    return high, (value - high.astype(F32)).astype(BF16)


def dot(left, right):
    return lax.dot_general(left, right, (((1,), (0,)), ((), ())), preferred_element_type=F32)


def banded(taps, rows, width, start):
    room = (width + 2 * LANES - 1) // LANES * LANES
    base = jnp.concatenate([taps, jnp.zeros((1, room - LANES), F32)], axis=1)
    base = jnp.broadcast_to(base, (rows, room))
    return pltpu.roll(base, start % room, 1, stride=1, stride_axis=0)[:, :width]


def stack(matrix):
    return jnp.concatenate(split(matrix), axis=0)


def left_product(stacked, value):
    rows = stacked.shape[0] // 2
    high, low = split(value)
    both = dot(stacked, high)
    return both[:rows] + (both[rows:] + dot(stacked[:rows], low))


def ordered_rows(matrix, where_ref, order_ref, runs, count):
    size = size_of(runs)
    chunk = size // count
    width = matrix.shape[1]
    order_ref[0, :size, :width] = rows_of(matrix, runs)
    for slot in range(count):
        place = pl.multiple_of(where_ref[slot] * chunk, chunk)
        order_ref[1, slot * chunk : (slot + 1) * chunk, :width] = order_ref[0, pl.ds(place, chunk), :width]
    return order_ref[1, :size, :width]


def taps_of(psf_ref):
    count = psf_ref.shape[1]
    row = lax.broadcasted_iota(jnp.int32, (LANES, LANES), 0)
    lane = lax.broadcasted_iota(jnp.int32, (LANES, LANES), 1)
    taps = psf_ref[...] / jnp.sum(psf_ref[...], axis=1, keepdims=True)
    taps = jnp.concatenate([taps, jnp.zeros((1, LANES - count), F32)], axis=1)
    column = jnp.transpose(jnp.broadcast_to(taps, (LANES, LANES)))
    return taps, jnp.sum(jnp.where(row + lane == count - 1, column, 0.0), axis=0, keepdims=True)


def weights_kernel(sizes, psf_z_ref, psf_x_ref, rows_ahead_ref, rows_back_ref, planes_ahead_ref, planes_back_ref):
    groups, beside, radius, depth, rows = sizes
    per = LANES // rows
    width = beside * rows
    taps, turned = taps_of(psf_x_ref)
    ahead = banded(turned, width, width, -radius)
    back = banded(taps, width, width, -radius)
    blocks = []
    for b in range(beside):
        for k in range(per):
            line = [jnp.zeros((rows, width), F32)] * per
            line[k] = ahead[b * rows : (b + 1) * rows]
            blocks.append(jnp.concatenate(line, axis=1))
    rows_ahead_ref[...] = jnp.concatenate(split(jnp.concatenate(blocks, axis=0)), axis=1)
    for b in range(beside):
        blocks = []
        for k in range(per):
            line = [jnp.zeros((width, rows), F32)] * per
            line[k] = back[:, b * rows : (b + 1) * rows]
            blocks.append(jnp.concatenate(line, axis=1))
        rows_back_ref[b] = jnp.concatenate(split(jnp.concatenate(blocks, axis=0)), axis=1)
    planes = groups * depth
    for ref, line in zip((planes_ahead_ref, planes_back_ref), taps_of(psf_z_ref)):
        high, low = split(banded(line, planes, planes, -radius))
        ref[...] = jnp.concatenate(
            [jnp.concatenate([high, high], axis=1), jnp.concatenate([low, jnp.zeros_like(low)], axis=1)], axis=0
        )


def send_sides(where_ref, count, value_ref, span, sibling_ref, other_ref):
    odd = where_ref[2 * count]
    room = value_ref.shape[0] - span
    sibling_ref[...] = value_ref[pl.ds(pl.multiple_of((1 - odd) * room, 8), span), :]
    other_ref[...] = value_ref[pl.ds(pl.multiple_of(odd * room, 8), span), :]


def start_kernel(parts, radius, count, where_ref, psf_ref, block_ref, *refs):
    own_ref, sibling_ref, other_ref, taps_ref = refs[:4]
    part_refs, order_ref = refs[4:-1], refs[-1]
    length, columns = block_ref.shape
    for at in range(0, length, LANES):
        own_ref[:, at : at + LANES] = jnp.transpose(block_ref[at : at + LANES, :])
    send_sides(where_ref, count, own_ref, radius, sibling_ref, other_ref)
    taps, turned = taps_of(psf_ref)
    taps_ref[...] = jnp.concatenate([taps, turned, jnp.zeros((6, LANES), F32)], axis=0)
    before = 0
    for k, runs in reversed(list(enumerate(parts))):
        chunk = size_of(runs) // count
        for slot, part_ref in enumerate(part_refs):
            place = pl.multiple_of(place_of(runs, where_ref[slot] * chunk), 8)
            part_ref[before : before + chunk, :] = own_ref[pl.ds(place, chunk), :]
        before += chunk
        if k:
            matrix = banded(taps, columns, columns, -radius)
            matrix = stack(ordered_rows(matrix, where_ref, order_ref, runs, count))
            for at in range(0, length, STEP):
                here = slice(at, at + STEP)
                result = left_product(matrix, own_ref[:, here])
                for slot, part_ref in enumerate(part_refs):
                    part_ref[before : before + chunk, here] = result[slot * chunk : (slot + 1) * chunk]
            before += chunk


def first_y_kernel(runs, radius, where_ref, taps_ref, own_ref, sibling_ref, other_ref, *refs):
    part_refs, order_ref = refs[:-1], refs[-1]
    columns, length = own_ref.shape
    count = len(part_refs)
    chunk = size_of(runs) // count
    matrix = banded(taps_ref[0:1, :], columns, columns + 2 * radius, 0)
    matrix = stack(ordered_rows(matrix, where_ref, order_ref, runs, count))
    odd = where_ref[2 * count] == 1
    for at in range(0, length, STEP):
        here = slice(at, at + STEP)
        field = assembled([[(0, columns)]], odd, [own_ref], [(sibling_ref, other_ref)], here)
        result = left_product(matrix, field)
        for slot, part_ref in enumerate(part_refs):
            part_ref[:, here] = result[slot * chunk : (slot + 1) * chunk]


def put_chunks(where_ref, count, part_refs, own_ref):
    chunk = part_refs[0].shape[0]
    for slot, part_ref in enumerate(part_refs):
        place = pl.multiple_of(where_ref[count + slot] * chunk, chunk)
        own_ref[pl.ds(place, chunk), :] = part_ref[...]


def gather_kernel(span, where_ref, *refs):
    sides = 2 if span else 0
    count = len(refs) - 2 - sides
    part_refs, own_ref = refs[:count], refs[count + 1]
    put_chunks(where_ref, count, part_refs, own_ref)
    if span:
        send_sides(where_ref, count, own_ref, span, *refs[count + 2 :])


def assembled(parts, odd, own_refs, side_refs, here):
    total = max(start + size for runs in parts for start, size in runs)
    pieces = {}
    for runs, ref in zip(parts, own_refs):
        at = 0
        for start, size in runs:
            pieces[start] = ref[at : at + size] if isinstance(ref, jax.Array) else ref[at : at + size, here]
            at += size
    own = [pieces[start] for start in sorted(pieces)]
    low, high = [], []
    for sibling_ref, other_ref in side_refs:
        sibling, other = sibling_ref[:, here], other_ref[:, here]
        low.insert(0, jnp.where(odd, sibling, other))
        high.append(jnp.where(odd, other, sibling))
    return jnp.concatenate(low + own + high, axis=0)


def middle_y_kernel(parts, radius, count, where_ref, taps_ref, *refs):
    kinds = len(parts)
    own_refs, refs = refs[:kinds], refs[kinds:]
    side_refs, refs = [refs[2 * k : 2 * k + 2] for k in range(kinds)], refs[2 * kinds :]
    seen_ref, seen_sibling_ref, seen_other_ref, estimate_ref = refs[:4]
    part_refs, order_ref = refs[4:-1], refs[-1]
    columns, length = seen_ref.shape
    wide = columns + 2 * radius
    odd = where_ref[2 * count] == 1
    back = stack(banded(taps_ref[1:2, :], wide, wide + 2 * radius, 0))
    matrix = banded(taps_ref[0:1, :], columns, wide, 0)
    rows = [ordered_rows(matrix, where_ref, order_ref, runs, count) for runs in parts]
    matrix = stack(jnp.concatenate(rows, axis=0))
    for at in range(0, length, STEP):
        here = slice(at, at + STEP)
        seen = assembled([[(0, columns)]], odd, [seen_ref], [(seen_sibling_ref, seen_other_ref)], here)
        estimate = seen * left_product(back, assembled(parts, odd, own_refs, side_refs, here))
        estimate_ref[:, here] = estimate[radius : radius + columns]
        result = left_product(matrix, estimate)
        place = 0
        for part_ref in part_refs:
            chunk = part_ref.shape[0]
            part_ref[:, here] = result[place : place + chunk]
            place += chunk


def inner_y_kernel(parts, radius, count, where_ref, taps_ref, outer_ref, estimate_ref, *refs):
    part_refs, (own_ref, out_ref) = refs[:count], refs[count:]
    put_chunks(where_ref, count, part_refs, own_ref)
    columns, length = estimate_ref.shape
    ((start, size),) = parts[1]
    back = stack(banded(taps_ref[1:2, :], size, columns, start - radius))
    for at in range(0, length, STEP):
        here = slice(at, at + STEP)
        field = assembled(parts, None, [outer_ref, own_ref], [], here)
        out_ref[:, here] = estimate_ref[start : start + size, here] * left_product(back, field)


def last_y_kernel(parts, radius, count, where_ref, taps_ref, *refs):
    kinds = len(parts)
    sibling_ref, other_ref, estimate_ref, *refs, out_ref = refs
    own_refs, ready_refs = refs[:kinds], refs[kinds:]
    columns, length = estimate_ref.shape
    odd = where_ref[2 * count] == 1
    back = stack(rows_of(banded(taps_ref[1:2, :], columns, columns + 2 * radius, 0), parts[0]))
    for at in range(0, length, STEP):
        here = slice(at, at + STEP)
        field = assembled(parts, odd, own_refs, [(sibling_ref, other_ref)], here)
        outer = rows_of(estimate_ref[:, here], parts[0]) * left_product(back, field)
        estimate = assembled(parts, None, [outer, *ready_refs], [], here)
        for tile in range(0, STEP, LANES):
            out_ref[at + tile : at + tile + LANES, :] = jnp.transpose(estimate[:, tile : tile + LANES])


def put_lines(ref, lines, value):
    for tile in range(ref.shape[0]):
        ref[tile, lines, :] = value[:, tile * LANES : (tile + 1) * LANES]


def get_lines(ref, lines):
    return jnp.concatenate([ref[tile, lines, :] for tile in range(ref.shape[0])], axis=1)


def fill(sizes, where_ref, part_refs, first, chunk, held_ref):
    groups, beside = sizes[:2]
    count = groups * beside
    tiles = part_refs[0].shape[1] // LANES
    for slot, part_ref in enumerate(part_refs):
        dz, dx = slot // beside, slot % beside
        source_z = lax.rem(where_ref[2 * count + 1] + groups - dz, groups)
        source_x = lax.rem(where_ref[2 * count + 2] + beside - dx, beside)
        for t in range(tiles):
            place = pl.multiple_of((source_z * tiles + t) * chunk, chunk)
            held_ref[source_x, pl.ds(place, chunk), :] = part_ref[first : first + chunk, t * LANES : (t + 1) * LANES]


def planes_kernel(
    sizes, first, seen_first, where_ref, rows_ahead_ref, rows_back_ref, planes_ahead_ref, planes_back_ref, *refs
):
    groups, beside, _, _, rows = sizes
    count = groups * beside
    part_refs, refs = refs[:count], refs[count:]
    begins = seen_first is not None
    if begins:
        seen_refs, refs = refs[:count], refs[count:]
        out_refs, (mark_ref, seen_ref, held_ref, field_ref, other_ref) = refs[:count], refs[count:]
    else:
        seen_ref, out_refs, (mark_ref, held_ref, field_ref, other_ref) = refs[0], refs[1 : count + 1], refs[count + 1 :]
    mark_ref[...] = jnp.zeros_like(mark_ref)
    chunk, length = out_refs[0].shape
    tiles = length // LANES
    per = LANES // rows
    width = beside * rows
    planes = groups * tiles * per
    if begins:
        fill(sizes, where_ref, seen_refs, seen_first, chunk, held_ref)
        for at in range(groups * tiles):
            for k in range(per):
                lines = slice(at * chunk, (at + 1) * chunk)
                pieces = [held_ref[b, lines, k * rows : (k + 1) * rows] for b in range(beside)]
                place = (at * per + k) * chunk
                put_lines(seen_ref, slice(place, place + chunk), jnp.concatenate(pieces, axis=1))
    fill(sizes, where_ref, part_refs, first, chunk, held_ref)

    across = per * width
    group = min(tiles, max(1, STEP // chunk))
    for at in range(0, groups * tiles, group):
        here = slice(at * chunk, (at + group) * chunk)
        high, low = split(jnp.concatenate([held_ref[b, here, :] for b in range(beside)], axis=1))
        result = dot(high, rows_ahead_ref[...])
        result = result[:, :across] + (result[:, across:] + dot(low, rows_ahead_ref[:, :across]))
        for g in range(group):
            for k in range(per):
                place = ((at + g) * per + k) * chunk
                part = result[g * chunk : (g + 1) * chunk, k * width : (k + 1) * width]
                put_lines(field_ref, slice(place, place + chunk), part)

    def over_planes(matrix_ref, value):
        result = dot(matrix_ref[...], jnp.concatenate(split(value), axis=0))
        return result[:planes] + result[planes:]

    for y in range(0, chunk, 2):
        lines = [pl.ds(y + k, planes, stride=chunk) for k in range(2)]
        value = jnp.concatenate([get_lines(field_ref, line) for line in lines], axis=1)
        seen = jnp.concatenate([get_lines(seen_ref, line) for line in lines], axis=1)
        value = over_planes(planes_back_ref, seen / over_planes(planes_ahead_ref, value))
        for k, line in enumerate(lines):
            put_lines(other_ref, line, value[:, k * width : (k + 1) * width])

    for dz in range(groups):
        target_z = lax.rem(where_ref[2 * count + 1] + dz, groups)
        for at in range(0, tiles, group):
            pieces = []
            for g in range(group):
                line = []
                for k in range(per):
                    place = pl.multiple_of(((target_z * tiles + at + g) * per + k) * chunk, chunk)
                    line.append(get_lines(other_ref, pl.ds(place, chunk)))
                pieces.append(jnp.concatenate(line, axis=1))
            high, low = split(jnp.concatenate(pieces, axis=0))
            for dx in range(beside):
                target_x = lax.rem(where_ref[2 * count + 2] + dx, beside)
                result = dot(high, rows_back_ref[target_x])
                result = result[:, :LANES] + (result[:, LANES:] + dot(low, rows_back_ref[target_x][:, :LANES]))
                for g in range(group):
                    out_refs[dz * beside + dx][:, (at + g) * LANES : (at + g + 1) * LANES] = result[
                        g * chunk : (g + 1) * chunk
                    ]


def per_device(observed, psf_z, psf_x, psf_y):
    groups, beside, along = (lax.axis_size(axis) for axis in ("gz", "bx", "by"))
    count = groups * beside
    planes, rows, columns = observed.shape
    length = planes * rows
    radius = psf_z.shape[0] // 2
    sizes = (groups, beside, radius, planes, rows)
    width = beside * rows
    parts = parts_of(columns, radius, count)
    chunks = [size_of(runs) // count for runs in parts]

    me_z, me_x = lax.axis_index("gz"), lax.axis_index("bx")
    offsets = [(dz, dx) for dz in range(groups) for dx in range(beside)]
    ahead = [lax.rem(me_z + dz, groups) * beside + lax.rem(me_x + dx, beside) for dz, dx in offsets]
    behind = [
        lax.rem(me_z + groups - dz, groups) * beside + lax.rem(me_x + beside - dx, beside) for dz, dx in offsets
    ]
    where = jnp.stack(ahead + behind + [lax.rem(lax.axis_index("by"), 2), me_z, me_x]).astype(jnp.int32)

    def exchanged(values):
        result = [values[0]]
        for (dz, dx), value in list(zip(offsets, values))[1:]:
            pairs = [
                (z * beside + x, ((z + dz) % groups) * beside + (x + dx) % beside)
                for z in range(groups)
                for x in range(beside)
            ]
            result.append(lax.ppermute(value, ("gz", "bx"), pairs))
        return result

    def from_sides(sibling, other):
        result = []
        for value, first in ((other, 1), (sibling, 0)):
            pairs = [(i, i + 1) for i in range(first, along - 1, 2)]
            result.append(lax.ppermute(value, "by", pairs + [(j, i) for i, j in pairs]))
        return result[1], result[0]

    line = (1, psf_z.shape[0])
    matrix = jax.ShapeDtypeStruct((2 * groups * planes,) * 2, BF16)
    order = pltpu.VMEM((2, columns, columns + 2 * radius), F32)
    block = sum(chunks)
    seen, sibling, other, taps, *parcels = call(
            1.3,
        functools.partial(start_kernel, parts, radius, count),
        [shaped(columns, length), shaped(radius, length), shaped(radius, length), shaped(8, LANES)]
        + [shaped(block + sum(chunks[1:]), length)] * count,
        [SMEM, VMEM, VMEM],
        [order],
    )(where, psf_y.reshape(line), observed.reshape(length, columns))
    seen_sides = from_sides(sibling, other)
    parcels = exchanged(parcels)
    weights = call(
            0.4,
        functools.partial(weights_kernel, sizes),
        [
            jax.ShapeDtypeStruct((beside * LANES, 2 * LANES // rows * width), BF16),
            jax.ShapeDtypeStruct((beside, LANES // rows * width, 2 * LANES), BF16),
            matrix,
            matrix,
        ],
        [VMEM] * 2,
    )(psf_z.reshape(line), psf_x.reshape(line))
    outer = exchanged(
        call(
            1.1,
            functools.partial(first_y_kernel, parts[0], radius),
            [shaped(chunks[0], length)] * count,
            [SMEM] + [VMEM] * 4,
            [order],
        )(where, taps, seen, *seen_sides)
    )

    def through_planes(values, first, chunk, seen_values, seen_first=None):
        lines = groups * planes * chunk
        across = (width // LANES, lines, LANES)
        begins = seen_first is not None
        result = call(
            50,
            functools.partial(planes_kernel, sizes, first, seen_first),
            [shaped(chunk, length)] * count + [shaped(8, LANES)] + [shaped(*across)] * begins,
            [SMEM] + [VMEM] * (4 + len(values) + len(seen_values)),
            [
                pltpu.VMEM((beside, groups * (length // LANES) * chunk, LANES), F32),
                pltpu.VMEM(across, F32),
                pltpu.VMEM(across, F32),
            ],
        )(where, *weights, *values, *seen_values)
        return result[:count], result[count], result[count + 1 :] if begins else seen_values

    def gathered(values, chunk, span, mark):
        own, *sides = call(
            0.6,
            functools.partial(gather_kernel, span),
            [shaped(chunk * count, length)] + [shaped(span, length)] * (2 if span else 0),
            [SMEM] + [VMEM] * count + [pl.BlockSpec(memory_space=pl.ANY)],
        )(where, *values, mark)
        return own, from_sides(*sides) if span else []

    fields, across, owns, sides = ([None] * len(parts) for _ in range(4))
    before = 0
    for k in reversed(range(len(parts))):
        values, first = (parcels, before + chunks[k]) if k else (outer, 0)
        fields[k], mark, across[k] = through_planes(values, first, chunks[k], parcels, before)
        fields[k] = exchanged(fields[k])
        before += chunks[k] * (2 if k else 1)
    for k in reversed(range(len(parts))):
        owns[k], sides[k] = gathered(fields[k], chunks[k], 2 * radius // len(parts), mark)
    estimate, *parcels = call(
            3.5,
        functools.partial(middle_y_kernel, parts, radius, count),
        [shaped(columns, length)] + [shaped(chunk, length) for chunk in chunks for _ in range(count)],
        [SMEM] + [VMEM] * (4 + 3 * len(parts)),
        [order],
    )(where, taps, *owns, *[side for pair in sides for side in pair], seen, *seen_sides)
    for k in range(len(parts)):
        fields[k] = exchanged(parcels[k * count : (k + 1) * count])
    for k in range(len(parts)):
        values, mark, _ = through_planes(fields[k], 0, chunks[k], across[k])
        fields[k] = exchanged(values)
    own, sides = gathered(fields[0], chunks[0], radius, mark)
    owns, ready = [own], []
    if len(parts) > 1:
        inner = shaped(size_of(parts[1]), length)
        inner, result = call(
            50,
            functools.partial(inner_y_kernel, parts, radius, count), [inner, inner], [SMEM] + [VMEM] * (3 + count)
        )(where, taps, own, estimate, *fields[1])
        owns, ready = [own, inner], [result]
    out = call(
            2.2,
        functools.partial(last_y_kernel, parts, radius, count),
        shaped(length, columns),
        [SMEM] + [VMEM] * (3 + 2 * len(parts)),
    )(where, taps, *sides, estimate, *owns, *ready)
    return out.reshape(planes, rows, columns)


def solution(mesh):
    placed = (P("gz", "bx", "by"), P(), P(), P())
    return jax.shard_map(
        per_device, mesh=mesh, in_specs=placed, out_specs=P("gz", "bx", "by"), check_vma=False
    )
```

time: 1050 us -> 89.4 us (0.09); the launches traced: 1040 us -> 89.1 us
  other arithmetic: 790 us -> 0 us
  waiting for transfers between devices: 105 us -> 17.6 us
  local copies, waits for them, and re-layouts: 56.7 us -> 2.62 us
  starting transfers between devices: 84.2 us -> 48.2 us
  Pallas kernels: 0 us -> 20.5 us
    add x8 -> x0, other arithmetic: 451 us -> none  [pass_axis(): result + kernel[offset] * lax.slice_in_dim(extended, offset, offset + len...]
    div x5 -> x0, other arithmetic: 169 us -> none  [the longest x2 166 us: per_device(): quotient = observed / blurred]
    mul x2 -> x0, other arithmetic: 166 us -> none  [per_device(): estimate * blur(quotient, kernel_z[::-1], kernel_x[::-1], kernel_y[::-1])]
    ppermute x24 -> x32, waiting for transfers between devices: 105 us -> 17.6 us  [the longest x8 10.5 us: from_sides(): result.append(lax.ppermute(value, 'by', pairs + [(j, i) for i, j in pairs]))]
    ppermute x24 -> x32, starting transfers between devices: 84.2 us -> 48.2 us  [the longest x8 25 us: from_sides(): result.append(lax.ppermute(value, 'by', pairs + [(j, i) for i, j in pairs]))]
    slice x40 -> x0, local copies, waits for them, and re-layouts: 34.6 us -> none  [the longest x18 12.8 us: pass_axis(): kernel[offset]]
    pallas_call x0 -> x13, Pallas kernels: none -> 20.5 us  [the longest x4 9.21 us: through_planes(): call(50, functools.partial(planes_kernel, sizes, first, seen_first), [sha...]
    ppermute x8 -> x0, local copies, waits for them, and re-layouts: 15.2 us -> none  [the longest x4 9.61 us: extended_2(): lax.ppermute(lax.slice_in_dim(block, block.shape[dim] - width, None, axis...]
  transfers between devices with their start and end apart: 24 -> 32, of which waited for: 24 -> 8; matrix products, arithmetic and copies ran while one was open for 4% -> 0% of each run, Pallas kernels for 0% -> 15%
where the time goes in v2:
time: 89.4 us; the launch traced here: 89.1 us
  starting transfers between devices  48.2 us (54%)
  Pallas kernels  20.5 us (23%)
  waiting for transfers between devices  17.6 us (20%)
  local copies, waits for them, and re-layouts  2.62 us (3%)
    ppermute x8, starting transfers between devices, from_sides(): result.append(lax.ppermute(value, 'by', pairs + [(j, i) for i, j in pairs]))  25 us
    ppermute x24, starting transfers between devices, exchanged(): result.append(lax.ppermute(value, ('gz', 'bx'), pairs))  23.2 us
    ppermute x8, waiting for transfers between devices, from_sides(): result.append(lax.ppermute(value, 'by', pairs + [(j, i) for i, j in pairs]))  10.5 us
    pallas_call x4, Pallas kernels, through_planes(): call(50, functools.partial(planes_kernel, sizes, first, seen_first), [sha...  9.21 us
    ppermute x24, waiting for transfers between devices, exchanged(): result.append(lax.ppermute(value, ('gz', 'bx'), pairs))  7.08 us
    pallas_call x1, Pallas kernels, per_device(): call(3.5, functools.partial(middle_y_kernel, parts, radius, count), [shap...  3.5 us
    unnamed x8, local copies, waits for them, and re-layouts  2.54 us
    pallas_call x1, Pallas kernels, per_device(): call(2.2, functools.partial(last_y_kernel, parts, radius, count), shaped(...  2.17 us
  transfers between devices with their start and end apart: 32, of which 8 were waited for; matrix products, arithmetic and copies ran while one was open for 0% of the time, Pallas kernels for 15%

profile of v2, /device:TPU:1, one launch (start us, length us, event | category | flops | bytes accessed | tf_op | source)
XLA Modules:
  0.0 89.1 jit_solution(15623378217917549)
XLA Ops:
  0.7 1.2 %copy-done = f32[32,64,128]{2,1,0:T(8,128)S(1)} copy-done((f32[32,64,128]{2,1,0:T(8,128)S(1)}, f32[32,64,128]{2,1,0:T(8,128)}, u32[]{:S(2)}) %copy-start) | copy-done | bytes 1048600
  2.0 1.3 %shard_map.46 = (f32[128,2048]{1,0:T(8,128)S(1)}, f32[32,2048]{1,0:T(8,128)S(1)}, f32[32,2048]{1,0:T(8,128)S(1)}, f32[8,128]{1,0:T(8,128)S(1)}, f32[48,2048]{1,0...) custom-call(s32[11]{0:T(128)S(1)} %stack.44.where_ref, ...), custom_call_target="tpu_custom_call" | custom-call | flops 1495000064 | tf_op jit(solution)/shard_map/pallas_call | solution.py:410
  3.3 2.1 %collective-permute-start.5 = (f32[48,2048]{1,0:T(8,128)S(1)}, f32[48,2048]{1,0:T(8,128)S(1)}, u32[]{:S(2)}, u32[]{:S(2)}) collective-permute-start(f32[48,2048]{1,0:T(8,128)S(1)} %get-tuple-element.74), channel_id=1, source_target_pairs={{0,8},{8,0},{16,24},{24,16},{1,9},{9,1},{17,25},{25,17},{2,10},{10... | collective-permute-start | bytes 1179656 | tf_op jit(solution)/shard_map/ppermute | solution.py:396
  5.4 1.2 %collective-permute-start.6 = (f32[48,2048]{1,0:T(8,128)S(1)}, f32[48,2048]{1,0:T(8,128)S(1)}, u32[]{:S(2)}, u32[]{:S(2)}) collective-permute-start(f32[48,2048]{1,0:T(8,128)S(1)} %get-tuple-element.75), channel_id=1, source_target_pairs={{0,16},{8,24},{16,0},{24,8},{1,17},{9,25},{17,1},{25,9},{2,18},{10... | collective-permute-start | bytes 1179656 | tf_op jit(solution)/shard_map/ppermute | solution.py:396
  6.7 1.2 %collective-permute-start = (f32[32,2048]{1,0:T(8,128)S(1)}, f32[32,2048]{1,0:T(8,128)S(1)}, u32[]{:S(2)}, u32[]{:S(2)}) collective-permute-start(f32[32,2048]{1,0:T(8,128)S(1)} %get-tuple-element.67), channel_id=1, source_target_pairs={{0,1},{2,3},{4,5},{6,7},{1,0},{3,2},{5,4},{7,6},{8,9},{10,11},{12,... | collective-permute-start | bytes 786440 | tf_op jit(solution)/shard_map/ppermute | solution.py:403
  7.9 3.5 %collective-permute-start.1 = (f32[32,2048]{1,0:T(8,128)S(1)}, f32[32,2048]{1,0:T(8,128)S(1)}, u32[]{:S(2)}, u32[]{:S(2)}) collective-permute-start(f32[32,2048]{1,0:T(8,128)S(1)} %get-tuple-element.68), channel_id=1, source_target_pairs={{1,2},{3,4},{5,6},{2,1},{4,3},{6,5},{9,10},{11,12},{13,14},{10,9},... | collective-permute-start | bytes 786440 | tf_op jit(solution)/shard_map/ppermute | solution.py:403
  12.5 3.4 %collective-permute-done.1.other_ref.refs_8_ = f32[32,2048]{1,0:T(8,128)S(1)} collective-permute-done((f32[32,2048]{1,0:T(8,128)S(1)}, f32[32,2048]{1,0:T(8,128)S(1)}, u32[]{:S(2)}, u32[]{:S(2)}) %collective-permute-start.1) | collective-permute-done | bytes 262176 | tf_op jit(solution)/shard_map/ppermute | solution.py:403
  17.0 1.7 %collective-permute-start.2 = (f32[16,2048]{1,0:T(8,128)S(1)}, f32[16,2048]{1,0:T(8,128)S(1)}, u32[]{:S(2)}, u32[]{:S(2)}) collective-permute-start(f32[16,2048]{1,0:T(8,128)S(1)} %get-tuple-element.70), channel_id=1, source_target_pairs={{0,8},{8,0},{16,24},{24,16},{1,9},{9,1},{17,25},{25,17},{2,10},{10... | collective-permute-start | bytes 393224 | tf_op jit(solution)/shard_map/ppermute | solution.py:396
  18.7 1.2 %collective-permute-start.3 = (f32[16,2048]{1,0:T(8,128)S(1)}, f32[16,2048]{1,0:T(8,128)S(1)}, u32[]{:S(2)}, u32[]{:S(2)}) collective-permute-start(f32[16,2048]{1,0:T(8,128)S(1)} %get-tuple-element.71), channel_id=1, source_target_pairs={{0,16},{8,24},{16,0},{24,8},{1,17},{9,25},{17,1},{25,9},{2,18},{10... | collective-permute-start | bytes 393224 | tf_op jit(solution)/shard_map/ppermute | solution.py:396
  20.0 3.7 %collective-permute-done.7.refs_7_.refs_3_ = f32[48,2048]{1,0:T(8,128)S(1)} collective-permute-done((f32[48,2048]{1,0:T(8,128)S(1)}, f32[48,2048]{1,0:T(8,128)S(1)}, u32[]{:S(2)}, u32[]{:S(2)}) %collective-permute-start.7) | collective-permute-done | bytes 393248 | tf_op jit(solution)/shard_map/ppermute | solution.py:396
  23.7 2.6 %shard_map.51 = (f32[16,2048]{1,0:T(8,128)S(1)}, f32[16,2048]{1,0:T(8,128)S(1)}, f32[16,2048]{1,0:T(8,128)S(1)}, f32[16,2048]{1,0:T(8,128)S(1)}, f32[8,128]{1,0:T(8,128)}, /*index=5*/f32[1,1024,128]{2,1,0:T(8,128)S(1)}) custom-call(s32[11]{0:T(128)S(1)} %stack.44.where_ref, bf16[256,512]{1,0:T(8,128)(2,1)S(1)} %get-tuple-element.62.rows_ahead_ref, ...), custom_call_target="tpu_custom_call" | custom-call | flops 57500000256 | tf_op jit(solution)/shard_map/pallas_call | solution.py:445
  27.4 1.2 %collective-permute-start.12 = (f32[16,2048]{1,0:T(8,128)S(1)}, f32[16,2048]{1,0:T(8,128)S(1)}, u32[]{:S(2)}, u32[]{:S(2)}) collective-permute-start(f32[16,2048]{1,0:T(8,128)S(1)} %get-tuple-element.85), channel_id=1, source_target_pairs={{0,16},{8,24},{16,0},{24,8},{1,17},{9,25},{17,1},{25,9},{2,18},{10... | collective-permute-start | bytes 393224 | tf_op jit(solution)/shard_map/ppermute | solution.py:396
  29.3 2.1 %shard_map.49 = (f32[16,2048]{1,0:T(8,128)S(1)}, f32[16,2048]{1,0:T(8,128)S(1)}, f32[16,2048]{1,0:T(8,128)S(1)}, f32[16,2048]{1,0:T(8,128)S(1)}, f32[8,128]{1,0:T(8,128)S(1)}, /*index=5*/f32[1,1024,128]{2,1,0:T(8,128)S(1)}) custom-call(s32[11]{0:T(128)S(1)} %stack.44.where_ref, bf16[256,512]{1,0:T(8,128)(2,1)S(1)} %get-tuple-element.62.rows_ahead_ref, ...), custom_call_target="tpu_custom_call" | custom-call | flops 57500000256 | tf_op jit(solution)/shard_map/pallas_call | solution.py:445
  32.3 1.2 %collective-permute-start.9 = (f32[16,2048]{1,0:T(8,128)S(1)}, f32[16,2048]{1,0:T(8,128)S(1)}, u32[]{:S(2)}, u32[]{:S(2)}) collective-permute-start(f32[16,2048]{1,0:T(8,128)S(1)} %get-tuple-element.79), channel_id=1, source_target_pairs={{0,16},{8,24},{16,0},{24,8},{1,17},{9,25},{17,1},{25,9},{2,18},{10... | collective-permute-start | bytes 393224 | tf_op jit(solution)/shard_map/ppermute | solution.py:396
  34.8 5.7 %collective-permute-start.16 = (f32[32,2048]{1,0:T(8,128)S(1)}, f32[32,2048]{1,0:T(8,128)S(1)}, u32[]{:S(2)}, u32[]{:S(2)}) collective-permute-start(f32[32,2048]{1,0:T(8,128)S(1)} %get-tuple-element.90), channel_id=1, source_target_pairs={{0,1},{2,3},{4,5},{6,7},{1,0},{3,2},{5,4},{7,6},{8,9},{10,11},{12,... | collective-permute-start | bytes 786440 | tf_op jit(solution)/shard_map/ppermute | solution.py:403
  40.5 3.9 %collective-permute-start.17 = (f32[32,2048]{1,0:T(8,128)S(1)}, f32[32,2048]{1,0:T(8,128)S(1)}, u32[]{:S(2)}, u32[]{:S(2)}) collective-permute-start(f32[32,2048]{1,0:T(8,128)S(1)} %get-tuple-element.91), channel_id=1, source_target_pairs={{1,2},{3,4},{5,6},{2,1},{4,3},{6,5},{9,10},{11,12},{13,14},{10,9},... | collective-permute-start | bytes 786440 | tf_op jit(solution)/shard_map/ppermute | solution.py:403
  45.1 3.6 %collective-permute-start.15 = (f32[32,2048]{1,0:T(8,128)S(1)}, f32[32,2048]{1,0:T(8,128)S(1)}, u32[]{:S(2)}, u32[]{:S(2)}) collective-permute-start(f32[32,2048]{1,0:T(8,128)S(1)} %get-tuple-element.89), channel_id=1, source_target_pairs={{1,2},{3,4},{5,6},{2,1},{4,3},{6,5},{9,10},{11,12},{13,14},{10,9},... | collective-permute-start | bytes 786440 | tf_op jit(solution)/shard_map/ppermute | solution.py:403
  48.7 4.1 %collective-permute-done.15.refs_3_ = f32[32,2048]{1,0:T(8,128)S(1)} collective-permute-done((f32[32,2048]{1,0:T(8,128)S(1)}, f32[32,2048]{1,0:T(8,128)S(1)}, u32[]{:S(2)}, u32[]{:S(2)}) %collective-permute-start.15) | collective-permute-done | bytes 262176 | tf_op jit(solution)/shard_map/ppermute | solution.py:403
  52.8 3.5 %shard_map.53 = (f32[128,2048]{1,0:T(8,128)S(1)}, f32[16,2048]{1,0:T(8,128)S(1)}, f32[16,2048]{1,0:T(8,128)S(1)}, f32[16,2048]{1,0:T(8,128)S(1)}, f32[16,2048]{1...) custom-call(s32[11]{0:T(128)S(1)} %stack.44.where_ref, ...), custom_call_target="tpu_custom_call" | custom-call | flops 4024999936 | tf_op jit(solution)/shard_map/pallas_call | solution.py:476
  56.3 1.8 %collective-permute-start.19 = (f32[16,2048]{1,0:T(8,128)S(1)}, f32[16,2048]{1,0:T(8,128)S(1)}, u32[]{:S(2)}, u32[]{:S(2)}) collective-permute-start(f32[16,2048]{1,0:T(8,128)S(1)} %get-tuple-element.94), channel_id=1, source_target_pairs={{0,16},{8,24},{16,0},{24,8},{1,17},{9,25},{17,1},{25,9},{2,18},{10... | collective-permute-start | bytes 393224 | tf_op jit(solution)/shard_map/ppermute | solution.py:396
  59.3 1.5 %collective-permute-start.25 = (f32[16,2048]{1,0:T(8,128)S(1)}, f32[16,2048]{1,0:T(8,128)S(1)}, u32[]{:S(2)}, u32[]{:S(2)}) collective-permute-start(f32[16,2048]{1,0:T(8,128)S(1)} %get-tuple-element.103), channel_id=1, source_target_pairs={{0,16},{8,24},{16,0},{24,8},{1,17},{9,25},{17,1},{25,9},{2,18},{10... | collective-permute-start | bytes 393224 | tf_op jit(solution)/shard_map/ppermute | solution.py:396
  61.7 1.6 %collective-permute-start.26 = (f32[16,2048]{1,0:T(8,128)S(1)}, f32[16,2048]{1,0:T(8,128)S(1)}, u32[]{:S(2)}, u32[]{:S(2)}) collective-permute-start(f32[16,2048]{1,0:T(8,128)S(1)} %get-tuple-element.104), channel_id=1, source_target_pairs={{0,24},{8,16},{16,8},{24,0},{1,25},{9,17},{17,9},{25,1},{2,26},{10... | collective-permute-start | bytes 393224 | tf_op jit(solution)/shard_map/ppermute | solution.py:396
  63.9 2.5 %shard_map.54 = (f32[16,2048]{1,0:T(8,128)S(1)}, f32[16,2048]{1,0:T(8,128)S(1)}, f32[16,2048]{1,0:T(8,128)S(1)}, f32[16,2048]{1,0:T(8,128)S(1)}, f32[8,128]{1,0:T(8,128)}) custom-call(s32[11]{0:T(128)S(1)} %stack.44.where_ref, bf16[256,512]{1,0:T(8,128)(2,1)S(1)} %get-tuple-element.62.rows_ahead_ref, ...), custom_call_target="tpu_custom_call" | custom-call | flops 57500000256 | tf_op jit(solution)/shard_map/pallas_call | solution.py:445
  66.3 1.5 %collective-permute-start.22 = (f32[16,2048]{1,0:T(8,128)S(1)}, f32[16,2048]{1,0:T(8,128)S(1)}, u32[]{:S(2)}, u32[]{:S(2)}) collective-permute-start(f32[16,2048]{1,0:T(8,128)S(1)} %get-tuple-element.99), channel_id=1, source_target_pairs={{0,16},{8,24},{16,0},{24,8},{1,17},{9,25},{17,1},{25,9},{2,18},{10... | collective-permute-start | bytes 393224 | tf_op jit(solution)/shard_map/ppermute | solution.py:396
  67.9 1.1 %collective-permute-start.23 = (f32[16,2048]{1,0:T(8,128)S(1)}, f32[16,2048]{1,0:T(8,128)S(1)}, u32[]{:S(2)}, u32[]{:S(2)}) collective-permute-start(f32[16,2048]{1,0:T(8,128)S(1)} %get-tuple-element.100), channel_id=1, source_target_pairs={{0,24},{8,16},{16,8},{24,0},{1,25},{9,17},{17,9},{25,1},{2,26},{10... | collective-permute-start | bytes 393224 | tf_op jit(solution)/shard_map/ppermute | solution.py:396
  69.0 2.0 %shard_map.55 = (f32[16,2048]{1,0:T(8,128)S(1)}, f32[16,2048]{1,0:T(8,128)S(1)}, f32[16,2048]{1,0:T(8,128)S(1)}, f32[16,2048]{1,0:T(8,128)S(1)}, f32[8,128]{1,0:T(8,128)S(1)}) custom-call(s32[11]{0:T(128)S(1)} %stack.44.where_ref, bf16[256,512]{1,0:T(8,128)(2,1)S(1)} %get-tuple-element.62.rows_ahead_ref, ...), custom_call_target="tpu_custom_call" | custom-call | flops 57500000256 | tf_op jit(solution)/shard_map/pallas_call | solution.py:445
  71.1 1.5 %collective-permute-start.30 = (f32[16,2048]{1,0:T(8,128)S(1)}, f32[16,2048]{1,0:T(8,128)S(1)}, u32[]{:S(2)}, u32[]{:S(2)}) collective-permute-start(f32[16,2048]{1,0:T(8,128)S(1)} %get-tuple-element.113), channel_id=1, source_target_pairs={{0,16},{8,24},{16,0},{24,8},{1,17},{9,25},{17,1},{25,9},{2,18},{10... | collective-permute-start | bytes 393224 | tf_op jit(solution)/shard_map/ppermute | solution.py:396
  72.6 1.2 %collective-permute-start.31 = (f32[16,2048]{1,0:T(8,128)S(1)}, f32[16,2048]{1,0:T(8,128)S(1)}, u32[]{:S(2)}, u32[]{:S(2)}) collective-permute-start(f32[16,2048]{1,0:T(8,128)S(1)} %get-tuple-element.114), channel_id=1, source_target_pairs={{0,24},{8,16},{16,8},{24,0},{1,25},{9,17},{17,9},{25,1},{2,26},{10... | collective-permute-start | bytes 393224 | tf_op jit(solution)/shard_map/ppermute | solution.py:396
  73.8 1.5 %collective-permute-done.23.refs_3_ = f32[16,2048]{1,0:T(8,128)S(1)} collective-permute-done((f32[16,2048]{1,0:T(8,128)S(1)}, f32[16,2048]{1,0:T(8,128)S(1)}, u32[]{:S(2)}, u32[]{:S(2)}) %collective-permute-start.23) | collective-permute-done | bytes 131104 | tf_op jit(solution)/shard_map/ppermute | solution.py:396
  75.9 7.0 %collective-permute-start.28 = (f32[32,2048]{1,0:T(8,128)S(1)}, f32[32,2048]{1,0:T(8,128)S(1)}, u32[]{:S(2)}, u32[]{:S(2)}) collective-permute-start(f32[32,2048]{1,0:T(8,128)S(1)} %get-tuple-element.108), channel_id=1, source_target_pairs={{1,2},{3,4},{5,6},{2,1},{4,3},{6,5},{9,10},{11,12},{13,14},{10,9},... | collective-permute-start | bytes 786440 | tf_op jit(solution)/shard_map/ppermute | solution.py:403
  84.0 3.0 %collective-permute-done.28.refs_1_ = f32[32,2048]{1,0:T(8,128)S(1)} collective-permute-done((f32[32,2048]{1,0:T(8,128)S(1)}, f32[32,2048]{1,0:T(8,128)S(1)}, u32[]{:S(2)}, u32[]{:S(2)}) %collective-permute-start.28) | collective-permute-done | bytes 262176 | tf_op jit(solution)/shard_map/ppermute | solution.py:403
  87.0 2.2 %shard_map.58 = f32[2048,128]{1,0:T(8,128)} custom-call(s32[11]{0:T(128)S(1)} %stack.44.where_ref, f32[8,128]{1,0:T(8,128)S(1)} %get-tuple-element.61.taps_ref, f32[32,2048]{1,0:T(8,128)S(1)} %collective-permute-done.27.refs_0_, f32[32,2048]{1,0:T(8,128)S(1)} %collective-permute-done.28.refs_1_, f32[128,2048]{1,0:T(8,128)S(1)} %get-tuple-element.109.estimate_ref.refs_2_, ...), custom_call_target="tpu_custom_call" | custom-call | flops 2529999872 | tf_op jit(solution)/shard_map/pallas_call | solution.py:497
  (54 shorter events, 12.1 us)
Async XLA Ops:
  3.3 16.6 %collective-permute-start.5 = (f32[48,2048]{1,0:T(8,128)S(1)}, f32[48,2048]{1,0:T(8,128)S(1)}, u32[]{:S(2)}, u32[]{:S(2)}) collective-permute-start(f32[48,2048]{1,0:T(8,128)S(1)} %get-tuple-element.74), channel_id=1, source_target_pairs={{0,8},{8,0},{16,24},{24,16},{1,9},{9,1},{17,25},{25,17},{2,10},{10... | collective-permute-start | bytes 1179656 | tf_op jit(solution)/shard_map/ppermute | solution.py:396
  5.4 14.5 %collective-permute-start.6 = (f32[48,2048]{1,0:T(8,128)S(1)}, f32[48,2048]{1,0:T(8,128)S(1)}, u32[]{:S(2)}, u32[]{:S(2)}) collective-permute-start(f32[48,2048]{1,0:T(8,128)S(1)} %get-tuple-element.75), channel_id=1, source_target_pairs={{0,16},{8,24},{16,0},{24,8},{1,17},{9,25},{17,1},{25,9},{2,18},{10... | collective-permute-start | bytes 1179656 | tf_op jit(solution)/shard_map/ppermute | solution.py:396
  6.7 17.0 %collective-permute-start.7 = (f32[48,2048]{1,0:T(8,128)S(1)}, f32[48,2048]{1,0:T(8,128)S(1)}, u32[]{:S(2)}, u32[]{:S(2)}) collective-permute-start(f32[48,2048]{1,0:T(8,128)S(1)} %get-tuple-element.76), channel_id=1, source_target_pairs={{0,24},{8,16},{16,8},{24,0},{1,25},{9,17},{17,9},{25,1},{2,26},{10... | collective-permute-start | bytes 1179656 | tf_op jit(solution)/shard_map/ppermute | solution.py:396
  6.7 5.8 %collective-permute-start = (f32[32,2048]{1,0:T(8,128)S(1)}, f32[32,2048]{1,0:T(8,128)S(1)}, u32[]{:S(2)}, u32[]{:S(2)}) collective-permute-start(f32[32,2048]{1,0:T(8,128)S(1)} %get-tuple-element.67), channel_id=1, source_target_pairs={{0,1},{2,3},{4,5},{6,7},{1,0},{3,2},{5,4},{7,6},{8,9},{10,11},{12,... | collective-permute-start | bytes 786440 | tf_op jit(solution)/shard_map/ppermute | solution.py:403
  7.9 8.0 %collective-permute-start.1 = (f32[32,2048]{1,0:T(8,128)S(1)}, f32[32,2048]{1,0:T(8,128)S(1)}, u32[]{:S(2)}, u32[]{:S(2)}) collective-permute-start(f32[32,2048]{1,0:T(8,128)S(1)} %get-tuple-element.68), channel_id=1, source_target_pairs={{1,2},{3,4},{5,6},{2,1},{4,3},{6,5},{9,10},{11,12},{13,14},{10,9},... | collective-permute-start | bytes 786440 | tf_op jit(solution)/shard_map/ppermute | solution.py:403
  17.0 11.6 %collective-permute-start.2 = (f32[16,2048]{1,0:T(8,128)S(1)}, f32[16,2048]{1,0:T(8,128)S(1)}, u32[]{:S(2)}, u32[]{:S(2)}) collective-permute-start(f32[16,2048]{1,0:T(8,128)S(1)} %get-tuple-element.70), channel_id=1, source_target_pairs={{0,8},{8,0},{16,24},{24,16},{1,9},{9,1},{17,25},{25,17},{2,10},{10... | collective-permute-start | bytes 393224 | tf_op jit(solution)/shard_map/ppermute | solution.py:396
  18.7 10.3 %collective-permute-start.3 = (f32[16,2048]{1,0:T(8,128)S(1)}, f32[16,2048]{1,0:T(8,128)S(1)}, u32[]{:S(2)}, u32[]{:S(2)}) collective-permute-start(f32[16,2048]{1,0:T(8,128)S(1)} %get-tuple-element.71), channel_id=1, source_target_pairs={{0,16},{8,24},{16,0},{24,8},{1,17},{9,25},{17,1},{25,9},{2,18},{10... | collective-permute-start | bytes 393224 | tf_op jit(solution)/shard_map/ppermute | solution.py:396
  19.9 9.4 %collective-permute-start.4 = (f32[16,2048]{1,0:T(8,128)S(1)}, f32[16,2048]{1,0:T(8,128)S(1)}, u32[]{:S(2)}, u32[]{:S(2)}) collective-permute-start(f32[16,2048]{1,0:T(8,128)S(1)} %get-tuple-element.72), channel_id=1, source_target_pairs={{0,24},{8,16},{16,8},{24,0},{1,25},{9,17},{17,9},{25,1},{2,26},{10... | collective-permute-start | bytes 393224 | tf_op jit(solution)/shard_map/ppermute | solution.py:396
  26.3 7.2 %collective-permute-start.11 = (f32[16,2048]{1,0:T(8,128)S(1)}, f32[16,2048]{1,0:T(8,128)S(1)}, u32[]{:S(2)}, u32[]{:S(2)}) collective-permute-start(f32[16,2048]{1,0:T(8,128)S(1)} %get-tuple-element.84), channel_id=1, source_target_pairs={{0,8},{8,0},{16,24},{24,16},{1,9},{9,1},{17,25},{25,17},{2,10},{10... | collective-permute-start | bytes 393224 | tf_op jit(solution)/shard_map/ppermute | solution.py:396
  27.4 6.8 %collective-permute-start.12 = (f32[16,2048]{1,0:T(8,128)S(1)}, f32[16,2048]{1,0:T(8,128)S(1)}, u32[]{:S(2)}, u32[]{:S(2)}) collective-permute-start(f32[16,2048]{1,0:T(8,128)S(1)} %get-tuple-element.85), channel_id=1, source_target_pairs={{0,16},{8,24},{16,0},{24,8},{1,17},{9,25},{17,1},{25,9},{2,18},{10... | collective-permute-start | bytes 393224 | tf_op jit(solution)/shard_map/ppermute | solution.py:396
  28.6 5.5 %collective-permute-start.13 = (f32[16,2048]{1,0:T(8,128)S(1)}, f32[16,2048]{1,0:T(8,128)S(1)}, u32[]{:S(2)}, u32[]{:S(2)}) collective-permute-start(f32[16,2048]{1,0:T(8,128)S(1)} %get-tuple-element.86), channel_id=1, source_target_pairs={{0,24},{8,16},{16,8},{24,0},{1,25},{9,17},{17,9},{25,1},{2,26},{10... | collective-permute-start | bytes 393224 | tf_op jit(solution)/shard_map/ppermute | solution.py:396
  31.4 12.9 %collective-permute-start.8 = (f32[16,2048]{1,0:T(8,128)S(1)}, f32[16,2048]{1,0:T(8,128)S(1)}, u32[]{:S(2)}, u32[]{:S(2)}) collective-permute-start(f32[16,2048]{1,0:T(8,128)S(1)} %get-tuple-element.78), channel_id=1, source_target_pairs={{0,8},{8,0},{16,24},{24,16},{1,9},{9,1},{17,25},{25,17},{2,10},{10... | collective-permute-start | bytes 393224 | tf_op jit(solution)/shard_map/ppermute | solution.py:396
  32.3 12.1 %collective-permute-start.9 = (f32[16,2048]{1,0:T(8,128)S(1)}, f32[16,2048]{1,0:T(8,128)S(1)}, u32[]{:S(2)}, u32[]{:S(2)}) collective-permute-start(f32[16,2048]{1,0:T(8,128)S(1)} %get-tuple-element.79), channel_id=1, source_target_pairs={{0,16},{8,24},{16,0},{24,8},{1,17},{9,25},{17,1},{25,9},{2,18},{10... | collective-permute-start | bytes 393224 | tf_op jit(solution)/shard_map/ppermute | solution.py:396
  33.5 10.8 %collective-permute-start.10 = (f32[16,2048]{1,0:T(8,128)S(1)}, f32[16,2048]{1,0:T(8,128)S(1)}, u32[]{:S(2)}, u32[]{:S(2)}) collective-permute-start(f32[16,2048]{1,0:T(8,128)S(1)} %get-tuple-element.80), channel_id=1, source_target_pairs={{0,24},{8,16},{16,8},{24,0},{1,25},{9,17},{17,9},{25,1},{2,26},{10... | collective-permute-start | bytes 393224 | tf_op jit(solution)/shard_map/ppermute | solution.py:396
  34.8 13.9 %collective-permute-start.16 = (f32[32,2048]{1,0:T(8,128)S(1)}, f32[32,2048]{1,0:T(8,128)S(1)}, u32[]{:S(2)}, u32[]{:S(2)}) collective-permute-start(f32[32,2048]{1,0:T(8,128)S(1)} %get-tuple-element.90), channel_id=1, source_target_pairs={{0,1},{2,3},{4,5},{6,7},{1,0},{3,2},{5,4},{7,6},{8,9},{10,11},{12,... | collective-permute-start | bytes 786440 | tf_op jit(solution)/shard_map/ppermute | solution.py:403
  40.5 8.2 %collective-permute-start.17 = (f32[32,2048]{1,0:T(8,128)S(1)}, f32[32,2048]{1,0:T(8,128)S(1)}, u32[]{:S(2)}, u32[]{:S(2)}) collective-permute-start(f32[32,2048]{1,0:T(8,128)S(1)} %get-tuple-element.91), channel_id=1, source_target_pairs={{1,2},{3,4},{5,6},{2,1},{4,3},{6,5},{9,10},{11,12},{13,14},{10,9},... | collective-permute-start | bytes 786440 | tf_op jit(solution)/shard_map/ppermute | solution.py:403
  45.0 3.7 %collective-permute-start.14 = (f32[32,2048]{1,0:T(8,128)S(1)}, f32[32,2048]{1,0:T(8,128)S(1)}, u32[]{:S(2)}, u32[]{:S(2)}) collective-permute-start(f32[32,2048]{1,0:T(8,128)S(1)} %get-tuple-element.88), channel_id=1, source_target_pairs={{0,1},{2,3},{4,5},{6,7},{1,0},{3,2},{5,4},{7,6},{8,9},{10,11},{12,... | collective-permute-start | bytes 786440 | tf_op jit(solution)/shard_map/ppermute | solution.py:403
  45.1 7.7 %collective-permute-start.15 = (f32[32,2048]{1,0:T(8,128)S(1)}, f32[32,2048]{1,0:T(8,128)S(1)}, u32[]{:S(2)}, u32[]{:S(2)}) collective-permute-start(f32[32,2048]{1,0:T(8,128)S(1)} %get-tuple-element.89), channel_id=1, source_target_pairs={{1,2},{3,4},{5,6},{2,1},{4,3},{6,5},{9,10},{11,12},{13,14},{10,9},... | collective-permute-start | bytes 786440 | tf_op jit(solution)/shard_map/ppermute | solution.py:403
  56.3 5.5 %collective-permute-start.18 = (f32[16,2048]{1,0:T(8,128)S(1)}, f32[16,2048]{1,0:T(8,128)S(1)}, u32[]{:S(2)}, u32[]{:S(2)}) collective-permute-start(f32[16,2048]{1,0:T(8,128)S(1)} %get-tuple-element.93), channel_id=1, source_target_pairs={{0,8},{8,0},{16,24},{24,16},{1,9},{9,1},{17,25},{25,17},{2,10},{10... | collective-permute-start | bytes 393224 | tf_op jit(solution)/shard_map/ppermute | solution.py:396
  56.3 6.9 %collective-permute-start.19 = (f32[16,2048]{1,0:T(8,128)S(1)}, f32[16,2048]{1,0:T(8,128)S(1)}, u32[]{:S(2)}, u32[]{:S(2)}) collective-permute-start(f32[16,2048]{1,0:T(8,128)S(1)} %get-tuple-element.94), channel_id=1, source_target_pairs={{0,16},{8,24},{16,0},{24,8},{1,17},{9,25},{17,1},{25,9},{2,18},{10... | collective-permute-start | bytes 393224 | tf_op jit(solution)/shard_map/ppermute | solution.py:396
  58.1 5.7 %collective-permute-start.20 = (f32[16,2048]{1,0:T(8,128)S(1)}, f32[16,2048]{1,0:T(8,128)S(1)}, u32[]{:S(2)}, u32[]{:S(2)}) collective-permute-start(f32[16,2048]{1,0:T(8,128)S(1)} %get-tuple-element.95), channel_id=1, source_target_pairs={{0,24},{8,16},{16,8},{24,0},{1,25},{9,17},{17,9},{25,1},{2,26},{10... | collective-permute-start | bytes 393224 | tf_op jit(solution)/shard_map/ppermute | solution.py:396
  59.0 8.9 %collective-permute-start.24 = (f32[16,2048]{1,0:T(8,128)S(1)}, f32[16,2048]{1,0:T(8,128)S(1)}, u32[]{:S(2)}, u32[]{:S(2)}) collective-permute-start(f32[16,2048]{1,0:T(8,128)S(1)} %get-tuple-element.102), channel_id=1, source_target_pairs={{0,8},{8,0},{16,24},{24,16},{1,9},{9,1},{17,25},{25,17},{2,10},{10... | collective-permute-start | bytes 393224 | tf_op jit(solution)/shard_map/ppermute | solution.py:396
  59.3 9.7 %collective-permute-start.25 = (f32[16,2048]{1,0:T(8,128)S(1)}, f32[16,2048]{1,0:T(8,128)S(1)}, u32[]{:S(2)}, u32[]{:S(2)}) collective-permute-start(f32[16,2048]{1,0:T(8,128)S(1)} %get-tuple-element.103), channel_id=1, source_target_pairs={{0,16},{8,24},{16,0},{24,8},{1,17},{9,25},{17,1},{25,9},{2,18},{10... | collective-permute-start | bytes 393224 | tf_op jit(solution)/shard_map/ppermute | solution.py:396
  61.7 7.3 %collective-permute-start.26 = (f32[16,2048]{1,0:T(8,128)S(1)}, f32[16,2048]{1,0:T(8,128)S(1)}, u32[]{:S(2)}, u32[]{:S(2)}) collective-permute-start(f32[16,2048]{1,0:T(8,128)S(1)} %get-tuple-element.104), channel_id=1, source_target_pairs={{0,24},{8,16},{16,8},{24,0},{1,25},{9,17},{17,9},{25,1},{2,26},{10... | collective-permute-start | bytes 393224 | tf_op jit(solution)/shard_map/ppermute | solution.py:396
  66.3 6.2 %collective-permute-start.21 = (f32[16,2048]{1,0:T(8,128)S(1)}, f32[16,2048]{1,0:T(8,128)S(1)}, u32[]{:S(2)}, u32[]{:S(2)}) collective-permute-start(f32[16,2048]{1,0:T(8,128)S(1)} %get-tuple-element.98), channel_id=1, source_target_pairs={{0,8},{8,0},{16,24},{24,16},{1,9},{9,1},{17,25},{25,17},{2,10},{10... | collective-permute-start | bytes 393224 | tf_op jit(solution)/shard_map/ppermute | solution.py:396
  66.3 7.4 %collective-permute-start.22 = (f32[16,2048]{1,0:T(8,128)S(1)}, f32[16,2048]{1,0:T(8,128)S(1)}, u32[]{:S(2)}, u32[]{:S(2)}) collective-permute-start(f32[16,2048]{1,0:T(8,128)S(1)} %get-tuple-element.99), channel_id=1, source_target_pairs={{0,16},{8,24},{16,0},{24,8},{1,17},{9,25},{17,1},{25,9},{2,18},{10... | collective-permute-start | bytes 393224 | tf_op jit(solution)/shard_map/ppermute | solution.py:396
  67.9 7.4 %collective-permute-start.23 = (f32[16,2048]{1,0:T(8,128)S(1)}, f32[16,2048]{1,0:T(8,128)S(1)}, u32[]{:S(2)}, u32[]{:S(2)}) collective-permute-start(f32[16,2048]{1,0:T(8,128)S(1)} %get-tuple-element.100), channel_id=1, source_target_pairs={{0,24},{8,16},{16,8},{24,0},{1,25},{9,17},{17,9},{25,1},{2,26},{10... | collective-permute-start | bytes 393224 | tf_op jit(solution)/shard_map/ppermute | solution.py:396
  71.0 12.0 %collective-permute-start.29 = (f32[16,2048]{1,0:T(8,128)S(1)}, f32[16,2048]{1,0:T(8,128)S(1)}, u32[]{:S(2)}, u32[]{:S(2)}) collective-permute-start(f32[16,2048]{1,0:T(8,128)S(1)} %get-tuple-element.112), channel_id=1, source_target_pairs={{0,8},{8,0},{16,24},{24,16},{1,9},{9,1},{17,25},{25,17},{2,10},{10... | collective-permute-start | bytes 393224 | tf_op jit(solution)/shard_map/ppermute | solution.py:396
  71.1 11.8 %collective-permute-start.30 = (f32[16,2048]{1,0:T(8,128)S(1)}, f32[16,2048]{1,0:T(8,128)S(1)}, u32[]{:S(2)}, u32[]{:S(2)}) collective-permute-start(f32[16,2048]{1,0:T(8,128)S(1)} %get-tuple-element.113), channel_id=1, source_target_pairs={{0,16},{8,24},{16,0},{24,8},{1,17},{9,25},{17,1},{25,9},{2,18},{10... | collective-permute-start | bytes 393224 | tf_op jit(solution)/shard_map/ppermute | solution.py:396
  72.6 10.4 %collective-permute-start.31 = (f32[16,2048]{1,0:T(8,128)S(1)}, f32[16,2048]{1,0:T(8,128)S(1)}, u32[]{:S(2)}, u32[]{:S(2)}) collective-permute-start(f32[16,2048]{1,0:T(8,128)S(1)} %get-tuple-element.114), channel_id=1, source_target_pairs={{0,24},{8,16},{16,8},{24,0},{1,25},{9,17},{17,9},{25,1},{2,26},{10... | collective-permute-start | bytes 393224 | tf_op jit(solution)/shard_map/ppermute | solution.py:396
  75.9 8.1 %collective-permute-start.27 = (f32[32,2048]{1,0:T(8,128)S(1)}, f32[32,2048]{1,0:T(8,128)S(1)}, u32[]{:S(2)}, u32[]{:S(2)}) collective-permute-start(f32[32,2048]{1,0:T(8,128)S(1)} %get-tuple-element.107), channel_id=1, source_target_pairs={{0,1},{2,3},{4,5},{6,7},{1,0},{3,2},{5,4},{7,6},{8,9},{10,11},{12,... | collective-permute-start | bytes 786440 | tf_op jit(solution)/shard_map/ppermute | solution.py:403
  75.9 11.0 %collective-permute-start.28 = (f32[32,2048]{1,0:T(8,128)S(1)}, f32[32,2048]{1,0:T(8,128)S(1)}, u32[]{:S(2)}, u32[]{:S(2)}) collective-permute-start(f32[32,2048]{1,0:T(8,128)S(1)} %get-tuple-element.108), channel_id=1, source_target_pairs={{1,2},{3,4},{5,6},{2,1},{4,3},{6,5},{9,10},{11,12},{13,14},{10,9},... | collective-permute-start | bytes 786440 | tf_op jit(solution)/shard_map/ppermute | solution.py:403
  (4 other events, 3.2 us)

commit v3 on v2

v3 whole, which is shorter than its diff:
```python
import functools
import jax
import jax.numpy as jnp
from jax import lax
from jax.experimental import pallas as pl
from jax.experimental.pallas import tpu as pltpu
from jax.sharding import PartitionSpec as P

LANES = 128
RATE = 1150 * 1000 * 1000
STEP = 4 * LANES
F32 = jnp.float32
BF16 = jnp.bfloat16
VMEM = pl.BlockSpec(memory_space=pltpu.VMEM)
SMEM = pl.BlockSpec(memory_space=pltpu.SMEM)
ANY = pl.BlockSpec(memory_space=pl.ANY)
HBM = pl.BlockSpec(memory_space=pltpu.HBM)


def shaped(*shape):
    return jax.ShapeDtypeStruct(shape, F32)


def stays(value):
    return pltpu.with_memory_space_constraint(value, pltpu.HBM)


def call(cost, kernel, outs, specs, scratch=(), place=VMEM):
    return pl.pallas_call(
        kernel,
        out_shape=outs,
        in_specs=specs,
        out_specs=jax.tree.map(lambda _: place, outs),
        scratch_shapes=list(scratch),
        compiler_params=pltpu.CompilerParams(vmem_limit_bytes=40 * 1024 * 1024),
        cost_estimate=pl.CostEstimate(flops=int(cost * RATE), bytes_accessed=0, transcendentals=0),
    )


def parts_of(columns, radius, count):
    outer = [(0, radius), (columns - radius, radius)]
    inner = [(radius, columns - 2 * radius)]
    fits = columns >= 3 * radius and count % 2 == 0
    for runs in (outer, inner):
        fits = fits and sum(size for _, size in runs) % (8 * count) == 0
    return [outer, inner] if fits else [[(0, columns)]]


def flat(lists):
    return [value for values in lists for value in values]


def size_of(runs):
    return sum(size for _, size in runs)


def rows_of(value, runs):
    return jnp.concatenate([value[start : start + size] for start, size in runs], axis=0)


def place_of(runs, offset):
    place, before = runs[0][0] + offset, 0
    for (start, size), (after, _) in zip(runs, runs[1:]):
        before += size
        place = jnp.where(offset >= before, after - before + offset, place)
    return place


def offsets_of(groups, beside):
    offsets = [(dz, dx) for dz in range(groups) for dx in range(beside)]
    return offsets[:1] + sorted(offsets[1:], key=lambda offset: offset.count(0))


def split(value):
    high = value.astype(BF16)
    return high, (value - high.astype(F32)).astype(BF16)


def dot(left, right):
    return lax.dot_general(left, right, (((1,), (0,)), ((), ())), preferred_element_type=F32)


def banded(taps, rows, width, start):
    room = (width + 2 * LANES - 1) // LANES * LANES
    base = jnp.concatenate([taps, jnp.zeros((1, room - LANES), F32)], axis=1)
    base = jnp.broadcast_to(base, (rows, room))
    return pltpu.roll(base, start % room, 1, stride=1, stride_axis=0)[:, :width]


def as_left(matrix):
    high, low = split(matrix)
    return jnp.concatenate([high, high, low], axis=1)


def left_product(matrix, value):
    high, low = split(value)
    return dot(matrix, jnp.concatenate([high, low, high], axis=0))


def as_right(matrix):
    high, low = split(matrix)
    return jnp.concatenate([high, high, low], axis=0)


def right_product(value, matrix):
    high, low = split(value)
    return dot(jnp.concatenate([high, low, high], axis=1), matrix)


def ordered_rows(matrix, where_ref, order_ref, runs, count):
    size = size_of(runs)
    chunk = size // count
    width = matrix.shape[1]
    order_ref[0, :size, :width] = rows_of(matrix, runs)
    for slot in range(count):
        place = pl.multiple_of(where_ref[slot] * chunk, chunk)
        order_ref[1, slot * chunk : (slot + 1) * chunk, :width] = order_ref[0, pl.ds(place, chunk), :width]
    return order_ref[1, :size, :width]


def columns_of(matrix, runs):
    return jnp.concatenate([matrix[:, start : start + size] for start, size in runs], axis=1)


def taps_of(psf_ref):
    count = psf_ref.shape[1]
    row = lax.broadcasted_iota(jnp.int32, (LANES, LANES), 0)
    lane = lax.broadcasted_iota(jnp.int32, (LANES, LANES), 1)
    taps = psf_ref[...] / jnp.sum(psf_ref[...], axis=1, keepdims=True)
    taps = jnp.concatenate([taps, jnp.zeros((1, LANES - count), F32)], axis=1)
    column = jnp.transpose(jnp.broadcast_to(taps, (LANES, LANES)))
    return taps, jnp.sum(jnp.where(row + lane == count - 1, column, 0.0), axis=0, keepdims=True)


def weights_kernel(
    sizes,
    parts,
    where_ref,
    psf_z_ref,
    psf_x_ref,
    psf_y_ref,
    first_ref,
    back_early_ref,
    back_late_ref,
    ahead_early_ref,
    ahead_late_ref,
    end_early_ref,
    end_late_ref,
    rows_ahead_ref,
    rows_back_ref,
    planes_ahead_ref,
    planes_back_ref,
    order_ref,
):
    groups, beside, radius, depth, rows, columns = sizes
    count = groups * beside
    taps, turned = taps_of(psf_y_ref)
    wide = columns + 2 * radius
    span = 2 * radius // len(parts)
    edges = [(0, 2 * radius), (wide - 2 * radius, 2 * radius)]

    ahead = banded(taps, columns, wide, 0)
    ahead = jnp.concatenate([ordered_rows(ahead, where_ref, order_ref, runs, count) for runs in parts], axis=0)
    first_ref[...] = as_left(ahead[: size_of(parts[0])])
    ahead_early_ref[...] = as_left(ahead[:, 2 * radius : columns])
    ahead_late_ref[...] = as_left(columns_of(ahead, edges))
    back = banded(turned, wide, wide + 2 * radius, 0)
    late = [(2 * radius - span, span), (columns + 2 * radius, span)]
    early = [(0, 2 * radius - span), (2 * radius, columns), (columns + 2 * radius + span, 2 * radius - span)]
    back_early_ref[...] = as_left(columns_of(back, [run for run in early if run[1]]))
    back_late_ref[...] = as_left(columns_of(rows_of(back, edges), late))
    back = banded(turned, columns, wide, 0)
    end_early_ref[...] = as_left(back[:, radius : radius + columns])
    edges = [(0, radius), (columns - radius, radius)]
    end_late_ref[...] = as_left(columns_of(rows_of(back, edges), [(0, radius), (columns + radius, radius)]))

    per = LANES // rows
    width = beside * rows
    taps, turned = taps_of(psf_x_ref)
    ahead = banded(turned, width, width, -radius)
    back = banded(taps, width, width, -radius)
    blocks = []
    for b in range(beside):
        for k in range(per):
            line = [jnp.zeros((rows, width), F32)] * per
            line[k] = ahead[b * rows : (b + 1) * rows]
            blocks.append(jnp.concatenate(line, axis=1))
    rows_ahead_ref[...] = as_right(jnp.concatenate(blocks, axis=0))
    for b in range(beside):
        blocks = []
        for k in range(per):
            line = [jnp.zeros((width, rows), F32)] * per
            line[k] = back[:, b * rows : (b + 1) * rows]
            blocks.append(jnp.concatenate(line, axis=1))
        slot = lax.rem(b + beside - where_ref[2 * count + 2], beside)
        rows_back_ref[:, pl.ds(pl.multiple_of(slot * LANES, LANES), LANES)] = as_right(jnp.concatenate(blocks, axis=0))
    planes = groups * depth
    for ref, line in zip((planes_ahead_ref, planes_back_ref), taps_of(psf_z_ref)):
        ref[...] = as_left(banded(line, planes, planes, -radius))


def send_sides(where_ref, count, value_ref, span, sibling_ref, other_ref):
    odd = where_ref[2 * count]
    room = value_ref.shape[0] - span
    sibling_ref[...] = value_ref[pl.ds(pl.multiple_of((1 - odd) * room, 8), span), :]
    other_ref[...] = value_ref[pl.ds(pl.multiple_of(odd * room, 8), span), :]


def start_kernel(parts, radius, count, where_ref, psf_hbm, block_hbm, *refs):
    own_ref, sibling_ref, other_ref = refs[:3]
    part_refs, (order_ref, psf_ref, block_ref, sems) = refs[3:-4], refs[-4:]
    length, columns = block_ref.shape
    pieces = sems.shape[0] - 1
    piece = length // pieces
    copies = [pltpu.make_async_copy(psf_hbm, psf_ref, sems.at[pieces])]
    for k in range(pieces):
        here = pl.ds(k * piece, piece)
        copies.append(pltpu.make_async_copy(block_hbm.at[here], block_ref.at[here], sems.at[k]))
    for copy in copies:
        copy.start()
    copies[0].wait()
    taps, _ = taps_of(psf_ref)
    matrices = [None]
    for runs in parts[1:]:
        matrix = banded(taps, columns, columns, -radius)
        matrices.append(as_left(ordered_rows(matrix, where_ref, order_ref, runs, count)))
    for k in range(pieces):
        copies[k + 1].wait()
        for at in range(k * piece, (k + 1) * piece, LANES):
            own_ref[:, at : at + LANES] = jnp.transpose(block_ref[at : at + LANES, :])
    send_sides(where_ref, count, own_ref, radius, sibling_ref, other_ref)
    before = 0
    for k, runs in reversed(list(enumerate(parts))):
        chunk = size_of(runs) // count
        for slot, part_ref in enumerate(part_refs):
            place = pl.multiple_of(place_of(runs, where_ref[slot] * chunk), 8)
            part_ref[before : before + chunk, :] = own_ref[pl.ds(place, chunk), :]
        before += chunk
        if k:
            for at in range(0, length, STEP):
                here = slice(at, at + STEP)
                result = left_product(matrices[k], own_ref[:, here])
                for slot, part_ref in enumerate(part_refs):
                    part_ref[before : before + chunk, here] = result[slot * chunk : (slot + 1) * chunk]
            before += chunk


def first_y_kernel(where_ref, matrix_ref, own_ref, other_ref, sibling_ref, *part_refs):
    columns, length = own_ref.shape
    count = len(part_refs)
    chunk = part_refs[0].shape[0]
    odd = where_ref[2 * count] == 1
    for at in range(0, length, STEP):
        here = slice(at, at + STEP)
        field = assembled([[(0, columns)]], odd, [own_ref], [(other_ref, sibling_ref)], here)
        result = left_product(matrix_ref[...], field)
        for slot, part_ref in enumerate(part_refs):
            part_ref[:, here] = result[slot * chunk : (slot + 1) * chunk]


def put_parts(where_ref, count, part_refs, own_refs):
    for k, own_ref in enumerate(own_refs):
        for slot, part_ref in enumerate(part_refs[k * count : (k + 1) * count]):
            chunk = part_ref.shape[0]
            place = pl.multiple_of(where_ref[count + slot] * chunk, chunk)
            own_ref[pl.ds(place, chunk), :] = part_ref[...]


def sides_kernel(count, where_ref, *refs):
    part_refs, (_, sibling_ref, other_ref) = refs[:count], refs[count:]
    span = sibling_ref.shape[0]
    chunk = part_refs[0].shape[0]
    odd = where_ref[2 * count]
    for slot, part_ref in enumerate(part_refs):
        start = where_ref[count + slot] * chunk
        for first, to_sibling in ((0, odd), (count * chunk - span, 1 - odd)):
            inside = (start >= first) & (start < first + span)

            def put(ref, start=start, first=first, part_ref=part_ref):
                ref[pl.ds(pl.multiple_of(start - first, 8), chunk), :] = part_ref[...]

            pl.when(inside & (to_sibling == 1))(functools.partial(put, sibling_ref))
            pl.when(inside & (to_sibling == 0))(functools.partial(put, other_ref))


def assembled(parts, odd, own_refs, side_refs, here):
    pieces = {}
    for runs, ref in zip(parts, own_refs):
        at = 0
        for start, size in runs:
            pieces[start] = ref[at : at + size] if isinstance(ref, jax.Array) else ref[at : at + size, here]
            at += size
    own = [pieces[start] for start in sorted(pieces)]
    low, high = [], []
    for other_ref, sibling_ref in side_refs:
        sibling, other = sibling_ref[:, here], other_ref[:, here]
        low.insert(0, jnp.where(odd, sibling, other))
        high.append(jnp.where(odd, other, sibling))
    return jnp.concatenate(low + own + high, axis=0)


def middle_early_kernel(parts, radius, count, where_ref, back_ref, ahead_ref, *refs):
    kinds = len(parts)
    own_refs, refs = refs[-kinds:], refs[:-kinds]
    put_parts(where_ref, count, refs, own_refs)
    refs = refs[kinds * count :]
    side_refs = [refs[2 * k : 2 * k + 2] for k in range(kinds - 1)]
    seen_ref, outer_ref, inner_ref, result_ref = refs[2 * kinds - 2 :]
    columns, length = seen_ref.shape
    wide = columns + 2 * radius
    edges = [(0, 2 * radius), (wide - 2 * radius, 2 * radius)]
    odd = where_ref[2 * count] == 1
    for at in range(0, length, STEP):
        here = slice(at, at + STEP)
        blurred = left_product(back_ref[...], assembled(parts, odd, own_refs, side_refs, here))
        outer_ref[:, here] = rows_of(blurred, edges)
        inner = seen_ref[radius : columns - radius, here] * blurred[2 * radius : columns]
        inner_ref[:, here] = inner
        result_ref[:, here] = left_product(ahead_ref[...], inner)


def middle_late_kernel(parts, radius, count, where_ref, back_ref, ahead_ref, *refs):
    (other_ref, sibling_ref, outer_ref, inner_ref, result_ref), refs = refs[:5], refs[5:]
    seen_ref, seen_other_ref, seen_sibling_ref, estimate_ref, *part_refs = refs
    columns, length = seen_ref.shape
    wide = columns + 2 * radius
    edges = [(0, 2 * radius), (wide - 2 * radius, 2 * radius)]
    odd = where_ref[2 * count] == 1
    for at in range(0, length, STEP):
        here = slice(at, at + STEP)
        sides = assembled([], odd, [], [(other_ref, sibling_ref)], here)
        seen = assembled([[(0, columns)]], odd, [seen_ref], [(seen_other_ref, seen_sibling_ref)], here)
        outer = rows_of(seen, edges) * (outer_ref[:, here] + left_product(back_ref[...], sides))
        estimate_ref[:, here] = jnp.concatenate(
            [outer[radius : 2 * radius], inner_ref[:, here], outer[2 * radius : 3 * radius]], axis=0
        )
        result = result_ref[:, here] + left_product(ahead_ref[...], outer)
        place = 0
        for part_ref in part_refs:
            chunk = part_ref.shape[0]
            part_ref[:, here] = result[place : place + chunk]
            place += chunk


def last_early_kernel(parts, radius, count, where_ref, back_ref, estimate_ref, *refs):
    outer_ref, inner_ref, *own_refs = refs[len(parts) * count :]
    put_parts(where_ref, count, refs, own_refs)
    columns, length = estimate_ref.shape
    edges = [(0, radius), (columns - radius, radius)]
    for at in range(0, length, STEP):
        here = slice(at, at + STEP)
        blurred = left_product(back_ref[...], assembled(parts, None, own_refs, [], here))
        outer_ref[:, here] = rows_of(blurred, edges)
        inner_ref[:, here] = estimate_ref[radius : columns - radius, here] * blurred[radius : columns - radius]


def last_late_kernel(
    radius, count, where_ref, back_ref, other_ref, sibling_ref, outer_ref, inner_ref, estimate_ref, out_hbm, out_ref, sems
):
    columns, length = estimate_ref.shape
    odd = where_ref[2 * count] == 1
    edges = [(0, radius), (columns - radius, radius)]
    pieces = sems.shape[0]
    piece = length // pieces
    copies = []
    for at in range(0, length, STEP):
        here = slice(at, at + STEP)
        sides = assembled([], odd, [], [(other_ref, sibling_ref)], here)
        outer = rows_of(estimate_ref[:, here], edges) * (outer_ref[:, here] + left_product(back_ref[...], sides))
        estimate = jnp.concatenate([outer[:radius], inner_ref[:, here], outer[radius:]], axis=0)
        for tile in range(0, STEP, LANES):
            out_ref[at + tile : at + tile + LANES, :] = jnp.transpose(estimate[:, tile : tile + LANES])
        if (at + STEP) % piece == 0:
            k = at // piece
            lines = pl.ds(k * piece, piece)
            copies.append(pltpu.make_async_copy(out_ref.at[lines], out_hbm.at[lines], sems.at[k]))
            copies[-1].start()
    for copy in copies:
        copy.wait()


def put_lines(ref, lines, value):
    for tile in range(ref.shape[0]):
        ref[tile, lines, :] = value[:, tile * LANES : (tile + 1) * LANES]


def get_lines(ref, lines):
    return jnp.concatenate([ref[tile, lines, :] for tile in range(ref.shape[0])], axis=1)


def fill(sizes, where_ref, part_refs, first, chunk, held_ref):
    groups, beside = sizes[:2]
    count = groups * beside
    tiles = part_refs[0].shape[1] // LANES
    for (dz, dx), part_ref in zip(offsets_of(groups, beside), part_refs):
        source_z = lax.rem(where_ref[2 * count + 1] + groups - dz, groups)
        source_x = lax.rem(where_ref[2 * count + 2] + beside - dx, beside)
        for t in range(tiles):
            place = pl.multiple_of((source_z * tiles + t) * chunk, chunk)
            held_ref[source_x, pl.ds(place, chunk), :] = part_ref[first : first + chunk, t * LANES : (t + 1) * LANES]


def planes_kernel(
    sizes, first, seen_first, where_ref, rows_ahead_ref, rows_back_ref, planes_ahead_ref, planes_back_ref, *refs
):
    groups, beside, _, _, rows, _ = sizes
    count = groups * beside
    part_refs, refs = refs[:count], refs[count:]
    begins = seen_first is not None
    if begins:
        seen_refs, refs = refs[:count], refs[count:]
        out_refs, (mark_ref, seen_ref, held_ref, field_ref, other_ref) = refs[:count], refs[count:]
    else:
        seen_ref, out_refs, (mark_ref, held_ref, field_ref, other_ref) = refs[0], refs[1 : count + 1], refs[count + 1 :]
    mark_ref[...] = jnp.zeros_like(mark_ref)
    chunk, length = out_refs[0].shape
    tiles = length // LANES
    per = LANES // rows
    width = beside * rows
    planes = groups * tiles * per
    if begins:
        fill(sizes, where_ref, seen_refs, seen_first, chunk, held_ref)
        for at in range(groups * tiles):
            for k in range(per):
                lines = slice(at * chunk, (at + 1) * chunk)
                pieces = [held_ref[b, lines, k * rows : (k + 1) * rows] for b in range(beside)]
                place = (at * per + k) * chunk
                put_lines(seen_ref, slice(place, place + chunk), jnp.concatenate(pieces, axis=1))
    fill(sizes, where_ref, part_refs, first, chunk, held_ref)

    group = min(tiles, max(1, 4 * LANES // chunk))
    for at in range(0, groups * tiles, group):
        here = slice(at * chunk, (at + group) * chunk)
        left = jnp.concatenate([held_ref[b, here, :] for b in range(beside)], axis=1)
        result = right_product(left, rows_ahead_ref[...])
        for g in range(group):
            for k in range(per):
                place = ((at + g) * per + k) * chunk
                part = result[g * chunk : (g + 1) * chunk, k * width : (k + 1) * width]
                put_lines(field_ref, slice(place, place + chunk), part)

    for y in range(0, chunk, 2):
        lines = [pl.ds(y + k, planes, stride=chunk) for k in range(2)]
        value = jnp.concatenate([get_lines(field_ref, line) for line in lines], axis=1)
        seen = jnp.concatenate([get_lines(seen_ref, line) for line in lines], axis=1)
        value = left_product(planes_back_ref[...], seen / left_product(planes_ahead_ref[...], value))
        for k, line in enumerate(lines):
            put_lines(other_ref, line, value[:, k * width : (k + 1) * width])

    offsets = offsets_of(groups, beside)
    for dz in range(groups):
        target_z = lax.rem(where_ref[2 * count + 1] + dz, groups)
        for at in range(0, tiles, group):
            pieces = []
            for g in range(group):
                line = []
                for k in range(per):
                    place = pl.multiple_of(((target_z * tiles + at + g) * per + k) * chunk, chunk)
                    line.append(get_lines(other_ref, pl.ds(place, chunk)))
                pieces.append(jnp.concatenate(line, axis=1))
            left = jnp.concatenate(pieces, axis=0)
            result = right_product(left, rows_back_ref[...])
            for dx in range(beside):
                for g in range(group):
                    out_refs[offsets.index((dz, dx))][:, (at + g) * LANES : (at + g + 1) * LANES] = result[
                        g * chunk : (g + 1) * chunk, dx * LANES : (dx + 1) * LANES
                    ]


def per_device(observed, psf_z, psf_x, psf_y):
    groups, beside, along = (lax.axis_size(axis) for axis in ("gz", "bx", "by"))
    count = groups * beside
    planes, rows, columns = observed.shape
    length = planes * rows
    radius = psf_z.shape[0] // 2
    sizes = (groups, beside, radius, planes, rows, columns)
    width = beside * rows
    parts = parts_of(columns, radius, count)
    chunks = [size_of(runs) // count for runs in parts]

    me_z, me_x = lax.axis_index("gz"), lax.axis_index("bx")
    offsets = offsets_of(groups, beside)
    ahead = [lax.rem(me_z + dz, groups) * beside + lax.rem(me_x + dx, beside) for dz, dx in offsets]
    behind = [
        lax.rem(me_z + groups - dz, groups) * beside + lax.rem(me_x + beside - dx, beside) for dz, dx in offsets
    ]
    where = jnp.stack(ahead + behind + [lax.rem(lax.axis_index("by"), 2), me_z, me_x]).astype(jnp.int32)

    def exchanged(values):
        result = [values[0]]
        for (dz, dx), value in list(zip(offsets, values))[1:]:
            pairs = [
                (z * beside + x, ((z + dz) % groups) * beside + (x + dx) % beside)
                for z in range(groups)
                for x in range(beside)
            ]
            result.append(lax.ppermute(value, ("gz", "bx"), pairs))
        return result

    def from_sides(sibling, other):
        result = []
        for value, first in ((other, 1), (sibling, 0)):
            pairs = [(i, i + 1) for i in range(first, along - 1, 2)]
            result.append(lax.ppermute(value, "by", pairs + [(j, i) for i, j in pairs]))
        return result

    line = (1, psf_z.shape[0])
    psf_z, psf_x, psf_y = psf_z.reshape(line), psf_x.reshape(line), psf_y.reshape(line)
    order = pltpu.VMEM((2, columns, columns + 2 * radius), F32)
    block = sum(chunks)
    pieces = 4
    seen, sibling, other, *parcels = call(
        1.3,
        functools.partial(start_kernel, parts, radius, count),
        [shaped(columns, length), shaped(radius, length), shaped(radius, length)]
        + [shaped(block + sum(chunks[1:]), length)] * count,
        [SMEM, HBM, HBM],
        [order, pltpu.VMEM(line, F32), pltpu.VMEM((length, columns), F32), pltpu.SemaphoreType.DMA((pieces + 1,))],
    )(where, stays(psf_y), stays(observed.reshape(length, columns)))
    seen_sides = from_sides(sibling, other)
    parcels = exchanged(parcels)

    def left(rows, width):
        return jax.ShapeDtypeStruct((rows, 3 * width), BF16)

    def right(rows, width):
        return jax.ShapeDtypeStruct((3 * rows, width), BF16)

    span = 2 * radius // len(parts)
    across = LANES // rows * width
    first, back_early, back_late, ahead_early, ahead_late, end_early, end_late, *weights = call(
        0.8,
        functools.partial(weights_kernel, sizes, parts),
        [
            left(size_of(parts[0]), columns + 2 * radius),
            left(columns + 2 * radius, columns + 4 * radius - 2 * span),
            left(4 * radius, 2 * span),
            left(columns, columns - 2 * radius),
            left(columns, 4 * radius),
            left(columns, columns),
            left(2 * radius, 2 * radius),
            right(beside * LANES, across),
            right(across, beside * LANES),
            left(groups * planes, groups * planes),
            left(groups * planes, groups * planes),
        ],
        [SMEM] + [VMEM] * 3,
        [order],
    )(where, psf_z, psf_x, psf_y)
    outer = exchanged(
        call(
            0.8,
            first_y_kernel,
            [shaped(chunks[0], length)] * count,
            [SMEM] + [VMEM] * 4,
        )(where, first, seen, *seen_sides)
    )

    def through_planes(values, first, chunk, seen_values, seen_first=None):
        lines = groups * planes * chunk
        across = (width // LANES, lines, LANES)
        begins = seen_first is not None
        result = call(
            50,
            functools.partial(planes_kernel, sizes, first, seen_first),
            [shaped(chunk, length)] * count + [shaped(8, LANES)] + [shaped(*across)] * begins,
            [SMEM] + [VMEM] * (4 + len(values) + len(seen_values)),
            [
                pltpu.VMEM((beside, groups * (length // LANES) * chunk, LANES), F32),
                pltpu.VMEM(across, F32),
                pltpu.VMEM(across, F32),
            ],
        )(where, *weights, *values, *seen_values)
        return result[:count], result[count], result[count + 1 :] if begins else seen_values

    def sides_of(cost, values, span, mark):
        sides = call(
            cost,
            functools.partial(sides_kernel, count),
            [shaped(span, length)] * 2,
            [SMEM] + [VMEM] * count + [ANY],
        )(where, *values, mark)
        return from_sides(*sides)

    fields, across, sides = ([None] * len(parts) for _ in range(3))
    before = 0
    for k in reversed(range(len(parts))):
        values, first = (parcels, before + chunks[k]) if k else (outer, 0)
        fields[k], mark, across[k] = through_planes(values, first, chunks[k], parcels, before)
        fields[k] = exchanged(fields[k])
        before += chunks[k] * (2 if k else 1)
    for k in reversed(range(len(parts))):
        sides[k] = sides_of(50, fields[k], span, mark)
    partial = [shaped(4 * radius, length), shaped(columns - 2 * radius, length), shaped(columns, length)]
    partial = call(
        2.2,
        functools.partial(middle_early_kernel, parts, radius, count),
        partial,
        [SMEM] + [VMEM] * (1 + (count + 2) * len(parts)),
        [pltpu.VMEM((size_of(runs), length), F32) for runs in parts],
    )(where, back_early, ahead_early, *flat(fields), *flat(sides[1:]), seen)
    estimate, *parcels = call(
        1.3,
        functools.partial(middle_late_kernel, parts, radius, count),
        [shaped(columns, length)] + [shaped(chunk, length) for chunk in chunks for _ in range(count)],
        [SMEM] + [VMEM] * 10,
    )(where, back_late, ahead_late, *sides[0], *partial, seen, *seen_sides)
    for k in range(len(parts)):
        fields[k] = exchanged(parcels[k * count : (k + 1) * count])
    for k in range(len(parts)):
        values, mark, _ = through_planes(fields[k], 0, chunks[k], across[k])
        fields[k] = exchanged(values)
    sides = sides_of(0.6, fields[0], radius, mark)
    partial = call(
        50,
        functools.partial(last_early_kernel, parts, radius, count),
        [shaped(2 * radius, length), shaped(columns - 2 * radius, length)],
        [SMEM] + [VMEM] * (2 + count * len(parts)),
        [pltpu.VMEM((size_of(runs), length), F32) for runs in parts],
    )(where, end_early, estimate, *flat(fields))
    out = call(
        1.5,
        functools.partial(last_late_kernel, radius, count),
        shaped(length, columns),
        [SMEM] + [VMEM] * 6,
        [pltpu.VMEM((length, columns), F32), pltpu.SemaphoreType.DMA((pieces,))],
        HBM,
    )(where, end_late, *sides, *partial, estimate)
    return out.reshape(planes, rows, columns)


def solution(mesh):
    placed = (P("gz", "bx", "by"), P(), P(), P())
    return jax.shard_map(
        per_device, mesh=mesh, in_specs=placed, out_specs=P("gz", "bx", "by"), check_vma=False
    )
```

time: 89.4 us -> 86 us (0.962)
  starting transfers between devices: 48.2 us -> 43 us
  Pallas kernels: 20.5 us -> 22.7 us
  local copies, waits for them, and re-layouts: 2.62 us -> 0.78 us
  waiting for transfers between devices: 17.6 us -> 19 us
    ppermute x24, waiting for transfers between devices: 7.08 us -> 12.1 us  [exchanged(): result.append(lax.ppermute(value, ('gz', 'bx'), pairs))]
    ppermute x8, starting transfers between devices: 25 us -> 21.1 us  [from_sides(): result.append(lax.ppermute(value, 'by', pairs + [(j, i) for i, j in pairs]))]
    ppermute x8, waiting for transfers between devices: 10.5 us -> 6.86 us  [from_sides(): result.append(lax.ppermute(value, 'by', pairs + [(j, i) for i, j in pairs]))]
    unnamed x8 -> x18, local copies, waits for them, and re-layouts: 2.54 us -> 0.69 us
    pallas_call x8 -> x9, Pallas kernels: 9.94 us -> 11.4 us  [the longest x1 2.16 us: per_device(): call(2.2, functools.partial(middle_early_kernel, parts, radius, count), p...]
    ppermute x24, starting transfers between devices: 23.2 us -> 21.9 us  [exchanged(): result.append(lax.ppermute(value, ('gz', 'bx'), pairs))]
    pallas_call x1, Pallas kernels: 1.33 us -> 2.47 us  [per_device(): call(1.3, functools.partial(start_kernel, parts, radius, count), [shaped(...]
  transfers between devices with their start and end apart: 32 -> 32, of which waited for: 8 -> 8; matrix products, arithmetic and copies ran while one was open for 0% -> 0% of each run, Pallas kernels for 15% -> 19%
where the time goes in v3:
time: 86 us; the launch traced here: 85.8 us
  starting transfers between devices  43 us (50%)
  Pallas kernels  22.7 us (26%)
  waiting for transfers between devices  19 us (22%)
    ppermute x24, starting transfers between devices, exchanged(): result.append(lax.ppermute(value, ('gz', 'bx'), pairs))  21.9 us
    ppermute x8, starting transfers between devices, from_sides(): result.append(lax.ppermute(value, 'by', pairs + [(j, i) for i, j in pairs]))  21.1 us
    ppermute x24, waiting for transfers between devices, exchanged(): result.append(lax.ppermute(value, ('gz', 'bx'), pairs))  12.1 us
    pallas_call x4, Pallas kernels, through_planes(): call(50, functools.partial(planes_kernel, sizes, first, seen_first), [sha...  8.83 us
    ppermute x8, waiting for transfers between devices, from_sides(): result.append(lax.ppermute(value, 'by', pairs + [(j, i) for i, j in pairs]))  6.86 us
    pallas_call x1, Pallas kernels, per_device(): call(1.3, functools.partial(start_kernel, parts, radius, count), [shaped(...  2.47 us
    pallas_call x1, Pallas kernels, per_device(): call(2.2, functools.partial(middle_early_kernel, parts, radius, count), p...  2.16 us
    pallas_call x3, Pallas kernels, sides_of(): call(cost, functools.partial(sides_kernel, count), [shaped(span, length)]...  2.04 us
  transfers between devices with their start and end apart: 32, of which 8 were waited for; matrix products, arithmetic and copies ran while one was open for 0% of the time, Pallas kernels for 19%

profile of v3, /device:TPU:1, one launch (start us, length us, event | category | flops | bytes accessed | tf_op | source)
XLA Modules:
  0.0 85.8 jit_solution(1776936632324908138)
XLA Ops:
  0.1 2.5 %shard_map.47 = (f32[128,2048]{1,0:T(8,128)S(1)}, f32[32,2048]{1,0:T(8,128)S(1)}, f32[32,2048]{1,0:T(8,128)S(1)}, f32[48,2048]{1,0:T(8,128)S(1)}, f32[48,2048]{1...) custom-call(s32[11]{0:T(128)S(1)} %stack.44.where_ref, f32[1,65]{1,0:T(1,128)} %bitcast.17, ...), custom_call_target="tpu_custom_call" | custom-call | flops 1495000064 | tf_op jit(solution)/shard_map/pallas_call | solution.py:512
  2.6 3.1 %collective-permute-start.5 = (f32[48,2048]{1,0:T(8,128)S(1)}, f32[48,2048]{1,0:T(8,128)S(1)}, u32[]{:S(2)}, u32[]{:S(2)}) collective-permute-start(f32[48,2048]{1,0:T(8,128)S(1)} %get-tuple-element.83), channel_id=1, source_target_pairs={{0,24},{8,16},{16,8},{24,0},{1,25},{9,17},{17,9},{25,1},{2,26},{10... | collective-permute-start | bytes 1179656 | tf_op jit(solution)/shard_map/ppermute | solution.py:497
  6.0 4.7 %collective-permute-start = (f32[32,2048]{1,0:T(8,128)S(1)}, f32[32,2048]{1,0:T(8,128)S(1)}, u32[]{:S(2)}, u32[]{:S(2)}) collective-permute-start(f32[32,2048]{1,0:T(8,128)S(1)} %get-tuple-element.76), channel_id=1, source_target_pairs={{1,2},{3,4},{5,6},{2,1},{4,3},{6,5},{9,10},{11,12},{13,14},{10,9},... | collective-permute-start | bytes 786440 | tf_op jit(solution)/shard_map/ppermute | solution.py:504
  11.5 1.4 %shard_map.46 = (bf16[64,576]{1,0:T(8,128)(2,1)S(1)}, bf16[192,576]{1,0:T(8,128)(2,1)S(1)}, bf16[128,192]{1,0:T(8,128)(2,1)S(1)}, bf16[128,192]{1,0:T(8,128)(2,1...) custom-call(s32[11]{0:T(128)S(1)} %stack.44.where_ref, ...), custom_call_target="tpu_custom_call" | custom-call | flops 920000000 | tf_op jit(solution)/shard_map/pallas_call | solution.py:531
  12.9 2.2 %collective-permute-done.other_ref.refs_6_ = f32[32,2048]{1,0:T(8,128)S(1)} collective-permute-done((f32[32,2048]{1,0:T(8,128)S(1)}, f32[32,2048]{1,0:T(8,128)S(1)}, u32[]{:S(2)}, u32[]{:S(2)}) %collective-permute-start) | collective-permute-done | bytes 262176 | tf_op jit(solution)/shard_map/ppermute | solution.py:504
  15.1 1.1 %shard_map.48 = (f32[16,2048]{1,0:T(8,128)S(1)}, f32[16,2048]{1,0:T(8,128)S(1)}, f32[16,2048]{1,0:T(8,128)S(1)}, f32[16,2048]{1,0:T(8,128)S(1)}) custom-call(s32[11]{0:T(128)S(1)} %stack.44.where_ref, bf16[64,576]{1,0:T(8,128)(2,1)S(1)} %get-tuple-element.74.matrix_ref, f32[128,2048]{1,0:T(8,128)S(1)} %get-tuple-element.75.own_ref.refs_10_.refs_5_, ...), custom_call_target="tpu_custom_call" | custom-call | flops 920000000 | tf_op jit(solution)/shard_map/pallas_call | solution.py:551
  16.2 2.2 %collective-permute-start.2 = (f32[16,2048]{1,0:T(8,128)S(1)}, f32[16,2048]{1,0:T(8,128)S(1)}, u32[]{:S(2)}, u32[]{:S(2)}) collective-permute-start(f32[16,2048]{1,0:T(8,128)S(1)} %get-tuple-element.79), channel_id=1, source_target_pairs={{0,24},{8,16},{16,8},{24,0},{1,25},{9,17},{17,9},{25,1},{2,26},{10... | collective-permute-start | bytes 393224 | tf_op jit(solution)/shard_map/ppermute | solution.py:497
  19.0 5.4 %collective-permute-done.6.refs_6_.refs_2_ = f32[48,2048]{1,0:T(8,128)S(1)} collective-permute-done((f32[48,2048]{1,0:T(8,128)S(1)}, f32[48,2048]{1,0:T(8,128)S(1)}, u32[]{:S(2)}, u32[]{:S(2)}) %collective-permute-start.6) | collective-permute-done | bytes 393248 | tf_op jit(solution)/shard_map/ppermute | solution.py:497
  24.3 2.5 %shard_map.51 = (f32[16,2048]{1,0:T(8,128)S(1)}, f32[16,2048]{1,0:T(8,128)S(1)}, f32[16,2048]{1,0:T(8,128)S(1)}, f32[16,2048]{1,0:T(8,128)S(1)}, f32[8,128]{1,0:T(8,128)}, /*index=5*/f32[1,1024,128]{2,1,0:T(8,128)S(1)}) custom-call(s32[11]{0:T(128)S(1)} %stack.44.where_ref, bf16[768,256]{1,0:T(8,128)(2,1)S(1)} %get-tuple-element.68.rows_ahead_ref, ...), custom_call_target="tpu_custom_call" | custom-call | flops 57500000256 | tf_op jit(solution)/shard_map/pallas_call | solution.py:563
  27.1 2.7 %collective-permute-start.14 = (f32[16,2048]{1,0:T(8,128)S(1)}, f32[16,2048]{1,0:T(8,128)S(1)}, u32[]{:S(2)}, u32[]{:S(2)}) collective-permute-start(f32[16,2048]{1,0:T(8,128)S(1)} %get-tuple-element.97), channel_id=1, source_target_pairs={{0,8},{8,0},{16,24},{24,16},{1,9},{9,1},{17,25},{25,17},{2,10},{10... | collective-permute-start | bytes 393224 | tf_op jit(solution)/shard_map/ppermute | solution.py:497
  29.8 2.0 %shard_map.49 = (f32[16,2048]{1,0:T(8,128)S(1)}, f32[16,2048]{1,0:T(8,128)S(1)}, f32[16,2048]{1,0:T(8,128)S(1)}, f32[16,2048]{1,0:T(8,128)S(1)}, f32[8,128]{1,0:T(8,128)S(1)}, /*index=5*/f32[1,1024,128]{2,1,0:T(8,128)S(1)}) custom-call(s32[11]{0:T(128)S(1)} %stack.44.where_ref, bf16[768,256]{1,0:T(8,128)(2,1)S(1)} %get-tuple-element.68.rows_ahead_ref, ...), custom_call_target="tpu_custom_call" | custom-call | flops 57500000256 | tf_op jit(solution)/shard_map/pallas_call | solution.py:563
  31.8 1.3 %collective-permute-start.8 = (f32[16,2048]{1,0:T(8,128)S(1)}, f32[16,2048]{1,0:T(8,128)S(1)}, u32[]{:S(2)}, u32[]{:S(2)}) collective-permute-start(f32[16,2048]{1,0:T(8,128)S(1)} %get-tuple-element.87), channel_id=1, source_target_pairs={{0,24},{8,16},{16,8},{24,0},{1,25},{9,17},{17,9},{25,1},{2,26},{10... | collective-permute-start | bytes 393224 | tf_op jit(solution)/shard_map/ppermute | solution.py:497
  33.1 1.4 %collective-permute-start.9 = (f32[16,2048]{1,0:T(8,128)S(1)}, f32[16,2048]{1,0:T(8,128)S(1)}, u32[]{:S(2)}, u32[]{:S(2)}) collective-permute-start(f32[16,2048]{1,0:T(8,128)S(1)} %get-tuple-element.88), channel_id=1, source_target_pairs={{0,8},{8,0},{16,24},{24,16},{1,9},{9,1},{17,25},{25,17},{2,10},{10... | collective-permute-start | bytes 393224 | tf_op jit(solution)/shard_map/ppermute | solution.py:497
  34.6 1.1 %collective-permute-done.14.refs_2_.refs_6_ = f32[16,2048]{1,0:T(8,128)S(1)} collective-permute-done((f32[16,2048]{1,0:T(8,128)S(1)}, f32[16,2048]{1,0:T(8,128)S(1)}, u32[]{:S(2)}, u32[]{:S(2)}) %collective-permute-start.14) | collective-permute-done | bytes 131104 | tf_op jit(solution)/shard_map/ppermute | solution.py:497
  36.4 6.6 %collective-permute-start.16 = (f32[32,2048]{1,0:T(8,128)S(1)}, f32[32,2048]{1,0:T(8,128)S(1)}, u32[]{:S(2)}, u32[]{:S(2)}) collective-permute-start(f32[32,2048]{1,0:T(8,128)S(1)} %get-tuple-element.99), channel_id=1, source_target_pairs={{1,2},{3,4},{5,6},{2,1},{4,3},{6,5},{9,10},{11,12},{13,14},{10,9},... | collective-permute-start | bytes 786440 | tf_op jit(solution)/shard_map/ppermute | solution.py:504
  43.8 3.6 %collective-permute-start.11 = (f32[32,2048]{1,0:T(8,128)S(1)}, f32[32,2048]{1,0:T(8,128)S(1)}, u32[]{:S(2)}, u32[]{:S(2)}) collective-permute-start(f32[32,2048]{1,0:T(8,128)S(1)} %get-tuple-element.91), channel_id=1, source_target_pairs={{1,2},{3,4},{5,6},{2,1},{4,3},{6,5},{9,10},{11,12},{13,14},{10,9},... | collective-permute-start | bytes 786440 | tf_op jit(solution)/shard_map/ppermute | solution.py:504
  47.4 2.2 %shard_map.53 = (f32[128,2048]{1,0:T(8,128)S(1)}, f32[64,2048]{1,0:T(8,128)S(1)}, f32[128,2048]{1,0:T(8,128)S(1)}) custom-call(s32[11]{0:T(128)S(1)} %stack.44.where_ref, bf16[192,576]{1,0:T(8,128)(2,1)S(1)} %get-tuple-element.93.back_ref, bf16[128,192]{1,0:T(8,128)(2,1)S(1)} %get-tuple-element.94.ahead_ref, f32[16,2048]{1,0:T(8,128)S(1)} %get-tuple-element.86.refs_0_, ...), custom_call_target="tpu_custom_call" | custom-call | flops 2529999872 | tf_op jit(solution)/shard_map/pallas_call | solution.py:595
  49.6 1.8 %collective-permute-done.11.refs_0_ = f32[32,2048]{1,0:T(8,128)S(1)} collective-permute-done((f32[32,2048]{1,0:T(8,128)S(1)}, f32[32,2048]{1,0:T(8,128)S(1)}, u32[]{:S(2)}, u32[]{:S(2)}) %collective-permute-start.11) | collective-permute-done | bytes 262176 | tf_op jit(solution)/shard_map/ppermute | solution.py:504
  51.5 1.8 %shard_map.54 = (f32[128,2048]{1,0:T(8,128)S(1)}, f32[16,2048]{1,0:T(8,128)S(1)}, f32[16,2048]{1,0:T(8,128)S(1)}, f32[16,2048]{1,0:T(8,128)S(1)}, f32[16,2048]{1...) custom-call(s32[11]{0:T(128)S(1)} %stack.44.where_ref, ...), custom_call_target="tpu_custom_call" | custom-call | flops 1495000064 | tf_op jit(solution)/shard_map/pallas_call | solution.py:602
  57.7 1.7 %collective-permute-done.18.refs_1_ = f32[16,2048]{1,0:T(8,128)S(1)} collective-permute-done((f32[16,2048]{1,0:T(8,128)S(1)}, f32[16,2048]{1,0:T(8,128)S(1)}, u32[]{:S(2)}, u32[]{:S(2)}) %collective-permute-start.18) | collective-permute-done | bytes 131104 | tf_op jit(solution)/shard_map/ppermute | solution.py:497
  59.7 2.9 %collective-permute-done.19.refs_2_ = f32[16,2048]{1,0:T(8,128)S(1)} collective-permute-done((f32[16,2048]{1,0:T(8,128)S(1)}, f32[16,2048]{1,0:T(8,128)S(1)}, u32[]{:S(2)}, u32[]{:S(2)}) %collective-permute-start.19) | collective-permute-done | bytes 131104 | tf_op jit(solution)/shard_map/ppermute | solution.py:497
  62.6 2.4 %shard_map.55 = (f32[16,2048]{1,0:T(8,128)S(1)}, f32[16,2048]{1,0:T(8,128)S(1)}, f32[16,2048]{1,0:T(8,128)S(1)}, f32[16,2048]{1,0:T(8,128)S(1)}, f32[8,128]{1,0:T(8,128)}) custom-call(s32[11]{0:T(128)S(1)} %stack.44.where_ref, bf16[768,256]{1,0:T(8,128)(2,1)S(1)} %get-tuple-element.68.rows_ahead_ref, bf16[768,256]{1,0:T(8,128)(2,1)S(1)} %get-tuple-element.69.rows_back_ref, ...), custom_call_target="tpu_custom_call" | custom-call | flops 57500000256 | tf_op jit(solution)/shard_map/pallas_call | solution.py:563
  65.4 1.0 %collective-permute-start.22 = (f32[16,2048]{1,0:T(8,128)S(1)}, f32[16,2048]{1,0:T(8,128)S(1)}, u32[]{:S(2)}, u32[]{:S(2)}) collective-permute-start(f32[16,2048]{1,0:T(8,128)S(1)} %get-tuple-element.111), channel_id=1, source_target_pairs={{0,8},{8,0},{16,24},{24,16},{1,9},{9,1},{17,25},{25,17},{2,10},{10... | collective-permute-start | bytes 393224 | tf_op jit(solution)/shard_map/ppermute | solution.py:497
  66.4 1.2 %collective-permute-start.23 = (f32[16,2048]{1,0:T(8,128)S(1)}, f32[16,2048]{1,0:T(8,128)S(1)}, u32[]{:S(2)}, u32[]{:S(2)}) collective-permute-start(f32[16,2048]{1,0:T(8,128)S(1)} %get-tuple-element.112), channel_id=1, source_target_pairs={{0,16},{8,24},{16,0},{24,8},{1,17},{9,25},{17,1},{25,9},{2,18},{10... | collective-permute-start | bytes 393224 | tf_op jit(solution)/shard_map/ppermute | solution.py:497
  67.6 1.9 %shard_map.56 = (f32[16,2048]{1,0:T(8,128)S(1)}, f32[16,2048]{1,0:T(8,128)S(1)}, f32[16,2048]{1,0:T(8,128)S(1)}, f32[16,2048]{1,0:T(8,128)S(1)}, f32[8,128]{1,0:T(8,128)S(1)}) custom-call(s32[11]{0:T(128)S(1)} %stack.44.where_ref, bf16[768,256]{1,0:T(8,128)(2,1)S(1)} %get-tuple-element.68.rows_ahead_ref, ...), custom_call_target="tpu_custom_call" | custom-call | flops 57500000256 | tf_op jit(solution)/shard_map/pallas_call | solution.py:563
  70.1 1.0 %collective-permute-start.30 = (f32[16,2048]{1,0:T(8,128)S(1)}, f32[16,2048]{1,0:T(8,128)S(1)}, u32[]{:S(2)}, u32[]{:S(2)}) collective-permute-start(f32[16,2048]{1,0:T(8,128)S(1)} %get-tuple-element.125), channel_id=1, source_target_pairs={{0,8},{8,0},{16,24},{24,16},{1,9},{9,1},{17,25},{25,17},{2,10},{10... | collective-permute-start | bytes 393224 | tf_op jit(solution)/shard_map/ppermute | solution.py:497
  71.1 1.2 %collective-permute-start.31 = (f32[16,2048]{1,0:T(8,128)S(1)}, f32[16,2048]{1,0:T(8,128)S(1)}, u32[]{:S(2)}, u32[]{:S(2)}) collective-permute-start(f32[16,2048]{1,0:T(8,128)S(1)} %get-tuple-element.126), channel_id=1, source_target_pairs={{0,16},{8,24},{16,0},{24,8},{1,17},{9,25},{17,1},{25,9},{2,18},{10... | collective-permute-start | bytes 393224 | tf_op jit(solution)/shard_map/ppermute | solution.py:497
  72.2 1.0 %collective-permute-done.22.refs_2_ = f32[16,2048]{1,0:T(8,128)S(1)} collective-permute-done((f32[16,2048]{1,0:T(8,128)S(1)}, f32[16,2048]{1,0:T(8,128)S(1)}, u32[]{:S(2)}, u32[]{:S(2)}) %collective-permute-start.22) | collective-permute-done | bytes 131104 | tf_op jit(solution)/shard_map/ppermute | solution.py:497
  73.9 6.0 %collective-permute-start.27 = (f32[32,2048]{1,0:T(8,128)S(1)}, f32[32,2048]{1,0:T(8,128)S(1)}, u32[]{:S(2)}, u32[]{:S(2)}) collective-permute-start(f32[32,2048]{1,0:T(8,128)S(1)} %get-tuple-element.119), channel_id=1, source_target_pairs={{1,2},{3,4},{5,6},{2,1},{4,3},{6,5},{9,10},{11,12},{13,14},{10,9},... | collective-permute-start | bytes 786440 | tf_op jit(solution)/shard_map/ppermute | solution.py:504
  80.0 1.1 %shard_map.58 = (f32[64,2048]{1,0:T(8,128)S(1)}, f32[64,2048]{1,0:T(8,128)S(1)}) custom-call(s32[11]{0:T(128)S(1)} %stack.44.where_ref, bf16[128,384]{1,0:T(8,128)(2,1)S(1)} %get-tuple-element.121.back_ref, f32[128,2048]{1,0:T(8,128)S(1)} %get-tuple-element.122.estimate_ref, f32[16,2048]{1,0:T(8,128)S(1)} %get-tuple-element.109.refs_0_, ...), custom_call_target="tpu_custom_call" | custom-call | flops 57500000256 | tf_op jit(solution)/shard_map/pallas_call | solution.py:614
  81.1 2.9 %collective-permute-done.27.other_ref = f32[32,2048]{1,0:T(8,128)S(1)} collective-permute-done((f32[32,2048]{1,0:T(8,128)S(1)}, f32[32,2048]{1,0:T(8,128)S(1)}, u32[]{:S(2)}, u32[]{:S(2)}) %collective-permute-start.27) | collective-permute-done | bytes 262176 | tf_op jit(solution)/shard_map/ppermute | solution.py:504
  83.9 1.8 %shard_map.59 = f32[2048,128]{1,0:T(8,128)} custom-call(s32[11]{0:T(128)S(1)} %stack.44.where_ref, bf16[64,192]{1,0:T(8,128)(2,1)S(1)} %get-tuple-element.67.back_ref, f32[32,2048]{1,0:T(8,128)S(1)} %collective-permute-done.27.other_ref, f32[32,2048]{1,0:T(8,128)S(1)} %collective-permute-done.28.sibling_ref, f32[64,2048]{1,0:T(8,128)S(1)} %get-tuple-element.127.outer_ref, ...), custom_call_target="tpu_custom_call" | custom-call | flops 1724999936 | tf_op jit(solution)/shard_map/pallas_call | solution.py:621
  (65 shorter events, 10.1 us)
Async XLA Ops:
  2.6 16.1 %collective-permute-start.5 = (f32[48,2048]{1,0:T(8,128)S(1)}, f32[48,2048]{1,0:T(8,128)S(1)}, u32[]{:S(2)}, u32[]{:S(2)}) collective-permute-start(f32[48,2048]{1,0:T(8,128)S(1)} %get-tuple-element.83), channel_id=1, source_target_pairs={{0,24},{8,16},{16,8},{24,0},{1,25},{9,17},{17,9},{25,1},{2,26},{10... | collective-permute-start | bytes 1179656 | tf_op jit(solution)/shard_map/ppermute | solution.py:497
  5.6 18.7 %collective-permute-start.6 = (f32[48,2048]{1,0:T(8,128)S(1)}, f32[48,2048]{1,0:T(8,128)S(1)}, u32[]{:S(2)}, u32[]{:S(2)}) collective-permute-start(f32[48,2048]{1,0:T(8,128)S(1)} %get-tuple-element.84), channel_id=1, source_target_pairs={{0,8},{8,0},{16,24},{24,16},{1,9},{9,1},{17,25},{25,17},{2,10},{10... | collective-permute-start | bytes 1179656 | tf_op jit(solution)/shard_map/ppermute | solution.py:497
  5.9 18.5 %collective-permute-start.7 = (f32[48,2048]{1,0:T(8,128)S(1)}, f32[48,2048]{1,0:T(8,128)S(1)}, u32[]{:S(2)}, u32[]{:S(2)}) collective-permute-start(f32[48,2048]{1,0:T(8,128)S(1)} %get-tuple-element.85), channel_id=1, source_target_pairs={{0,16},{8,24},{16,0},{24,8},{1,17},{9,25},{17,1},{25,9},{2,18},{10... | collective-permute-start | bytes 1179656 | tf_op jit(solution)/shard_map/ppermute | solution.py:497
  6.0 9.1 %collective-permute-start = (f32[32,2048]{1,0:T(8,128)S(1)}, f32[32,2048]{1,0:T(8,128)S(1)}, u32[]{:S(2)}, u32[]{:S(2)}) collective-permute-start(f32[32,2048]{1,0:T(8,128)S(1)} %get-tuple-element.76), channel_id=1, source_target_pairs={{1,2},{3,4},{5,6},{2,1},{4,3},{6,5},{9,10},{11,12},{13,14},{10,9},... | collective-permute-start | bytes 786440 | tf_op jit(solution)/shard_map/ppermute | solution.py:504
  10.7 4.3 %collective-permute-start.1 = (f32[32,2048]{1,0:T(8,128)S(1)}, f32[32,2048]{1,0:T(8,128)S(1)}, u32[]{:S(2)}, u32[]{:S(2)}) collective-permute-start(f32[32,2048]{1,0:T(8,128)S(1)} %get-tuple-element.77), channel_id=1, source_target_pairs={{0,1},{2,3},{4,5},{6,7},{1,0},{3,2},{5,4},{7,6},{8,9},{10,11},{12,... | collective-permute-start | bytes 786440 | tf_op jit(solution)/shard_map/ppermute | solution.py:504
  16.2 13.5 %collective-permute-start.2 = (f32[16,2048]{1,0:T(8,128)S(1)}, f32[16,2048]{1,0:T(8,128)S(1)}, u32[]{:S(2)}, u32[]{:S(2)}) collective-permute-start(f32[16,2048]{1,0:T(8,128)S(1)} %get-tuple-element.79), channel_id=1, source_target_pairs={{0,24},{8,16},{16,8},{24,0},{1,25},{9,17},{17,9},{25,1},{2,26},{10... | collective-permute-start | bytes 393224 | tf_op jit(solution)/shard_map/ppermute | solution.py:497
  18.5 11.3 %collective-permute-start.3 = (f32[16,2048]{1,0:T(8,128)S(1)}, f32[16,2048]{1,0:T(8,128)S(1)}, u32[]{:S(2)}, u32[]{:S(2)}) collective-permute-start(f32[16,2048]{1,0:T(8,128)S(1)} %get-tuple-element.80), channel_id=1, source_target_pairs={{0,8},{8,0},{16,24},{24,16},{1,9},{9,1},{17,25},{25,17},{2,10},{10... | collective-permute-start | bytes 393224 | tf_op jit(solution)/shard_map/ppermute | solution.py:497
  18.7 11.1 %collective-permute-start.4 = (f32[16,2048]{1,0:T(8,128)S(1)}, f32[16,2048]{1,0:T(8,128)S(1)}, u32[]{:S(2)}, u32[]{:S(2)}) collective-permute-start(f32[16,2048]{1,0:T(8,128)S(1)} %get-tuple-element.81), channel_id=1, source_target_pairs={{0,16},{8,24},{16,0},{24,8},{1,17},{9,25},{17,1},{25,9},{2,18},{10... | collective-permute-start | bytes 393224 | tf_op jit(solution)/shard_map/ppermute | solution.py:497
  26.8 7.7 %collective-permute-start.13 = (f32[16,2048]{1,0:T(8,128)S(1)}, f32[16,2048]{1,0:T(8,128)S(1)}, u32[]{:S(2)}, u32[]{:S(2)}) collective-permute-start(f32[16,2048]{1,0:T(8,128)S(1)} %get-tuple-element.96), channel_id=1, source_target_pairs={{0,24},{8,16},{16,8},{24,0},{1,25},{9,17},{17,9},{25,1},{2,26},{10... | collective-permute-start | bytes 393224 | tf_op jit(solution)/shard_map/ppermute | solution.py:497
  27.1 8.6 %collective-permute-start.14 = (f32[16,2048]{1,0:T(8,128)S(1)}, f32[16,2048]{1,0:T(8,128)S(1)}, u32[]{:S(2)}, u32[]{:S(2)}) collective-permute-start(f32[16,2048]{1,0:T(8,128)S(1)} %get-tuple-element.97), channel_id=1, source_target_pairs={{0,8},{8,0},{16,24},{24,16},{1,9},{9,1},{17,25},{25,17},{2,10},{10... | collective-permute-start | bytes 393224 | tf_op jit(solution)/shard_map/ppermute | solution.py:497
  29.8 5.9 %collective-permute-start.15 = (f32[16,2048]{1,0:T(8,128)S(1)}, f32[16,2048]{1,0:T(8,128)S(1)}, u32[]{:S(2)}, u32[]{:S(2)}) collective-permute-start(f32[16,2048]{1,0:T(8,128)S(1)} %get-tuple-element.98), channel_id=1, source_target_pairs={{0,16},{8,24},{16,0},{24,8},{1,17},{9,25},{17,1},{25,9},{2,18},{10... | collective-permute-start | bytes 393224 | tf_op jit(solution)/shard_map/ppermute | solution.py:497
  31.8 11.2 %collective-permute-start.8 = (f32[16,2048]{1,0:T(8,128)S(1)}, f32[16,2048]{1,0:T(8,128)S(1)}, u32[]{:S(2)}, u32[]{:S(2)}) collective-permute-start(f32[16,2048]{1,0:T(8,128)S(1)} %get-tuple-element.87), channel_id=1, source_target_pairs={{0,24},{8,16},{16,8},{24,0},{1,25},{9,17},{17,9},{25,1},{2,26},{10... | collective-permute-start | bytes 393224 | tf_op jit(solution)/shard_map/ppermute | solution.py:497
  33.1 9.9 %collective-permute-start.9 = (f32[16,2048]{1,0:T(8,128)S(1)}, f32[16,2048]{1,0:T(8,128)S(1)}, u32[]{:S(2)}, u32[]{:S(2)}) collective-permute-start(f32[16,2048]{1,0:T(8,128)S(1)} %get-tuple-element.88), channel_id=1, source_target_pairs={{0,8},{8,0},{16,24},{24,16},{1,9},{9,1},{17,25},{25,17},{2,10},{10... | collective-permute-start | bytes 393224 | tf_op jit(solution)/shard_map/ppermute | solution.py:497
  34.5 8.5 %collective-permute-start.10 = (f32[16,2048]{1,0:T(8,128)S(1)}, f32[16,2048]{1,0:T(8,128)S(1)}, u32[]{:S(2)}, u32[]{:S(2)}) collective-permute-start(f32[16,2048]{1,0:T(8,128)S(1)} %get-tuple-element.89), channel_id=1, source_target_pairs={{0,16},{8,24},{16,0},{24,8},{1,17},{9,25},{17,1},{25,9},{2,18},{10... | collective-permute-start | bytes 393224 | tf_op jit(solution)/shard_map/ppermute | solution.py:497
  36.4 11.0 %collective-permute-start.16 = (f32[32,2048]{1,0:T(8,128)S(1)}, f32[32,2048]{1,0:T(8,128)S(1)}, u32[]{:S(2)}, u32[]{:S(2)}) collective-permute-start(f32[32,2048]{1,0:T(8,128)S(1)} %get-tuple-element.99), channel_id=1, source_target_pairs={{1,2},{3,4},{5,6},{2,1},{4,3},{6,5},{9,10},{11,12},{13,14},{10,9},... | collective-permute-start | bytes 786440 | tf_op jit(solution)/shard_map/ppermute | solution.py:504
  42.9 4.5 %collective-permute-start.17 = (f32[32,2048]{1,0:T(8,128)S(1)}, f32[32,2048]{1,0:T(8,128)S(1)}, u32[]{:S(2)}, u32[]{:S(2)}) collective-permute-start(f32[32,2048]{1,0:T(8,128)S(1)} %get-tuple-element.100), channel_id=1, source_target_pairs={{0,1},{2,3},{4,5},{6,7},{1,0},{3,2},{5,4},{7,6},{8,9},{10,11},{12,... | collective-permute-start | bytes 786440 | tf_op jit(solution)/shard_map/ppermute | solution.py:504
  43.8 7.7 %collective-permute-start.11 = (f32[32,2048]{1,0:T(8,128)S(1)}, f32[32,2048]{1,0:T(8,128)S(1)}, u32[]{:S(2)}, u32[]{:S(2)}) collective-permute-start(f32[32,2048]{1,0:T(8,128)S(1)} %get-tuple-element.91), channel_id=1, source_target_pairs={{1,2},{3,4},{5,6},{2,1},{4,3},{6,5},{9,10},{11,12},{13,14},{10,9},... | collective-permute-start | bytes 786440 | tf_op jit(solution)/shard_map/ppermute | solution.py:504
  47.3 4.1 %collective-permute-start.12 = (f32[32,2048]{1,0:T(8,128)S(1)}, f32[32,2048]{1,0:T(8,128)S(1)}, u32[]{:S(2)}, u32[]{:S(2)}) collective-permute-start(f32[32,2048]{1,0:T(8,128)S(1)} %get-tuple-element.92), channel_id=1, source_target_pairs={{0,1},{2,3},{4,5},{6,7},{1,0},{3,2},{5,4},{7,6},{8,9},{10,11},{12,... | collective-permute-start | bytes 786440 | tf_op jit(solution)/shard_map/ppermute | solution.py:504
  53.3 6.2 %collective-permute-start.18 = (f32[16,2048]{1,0:T(8,128)S(1)}, f32[16,2048]{1,0:T(8,128)S(1)}, u32[]{:S(2)}, u32[]{:S(2)}) collective-permute-start(f32[16,2048]{1,0:T(8,128)S(1)} %get-tuple-element.105), channel_id=1, source_target_pairs={{0,24},{8,16},{16,8},{24,0},{1,25},{9,17},{17,9},{25,1},{2,26},{10... | collective-permute-start | bytes 393224 | tf_op jit(solution)/shard_map/ppermute | solution.py:497
  54.2 8.4 %collective-permute-start.19 = (f32[16,2048]{1,0:T(8,128)S(1)}, f32[16,2048]{1,0:T(8,128)S(1)}, u32[]{:S(2)}, u32[]{:S(2)}) collective-permute-start(f32[16,2048]{1,0:T(8,128)S(1)} %get-tuple-element.106), channel_id=1, source_target_pairs={{0,8},{8,0},{16,24},{24,16},{1,9},{9,1},{17,25},{25,17},{2,10},{10... | collective-permute-start | bytes 393224 | tf_op jit(solution)/shard_map/ppermute | solution.py:497
  55.1 7.5 %collective-permute-start.20 = (f32[16,2048]{1,0:T(8,128)S(1)}, f32[16,2048]{1,0:T(8,128)S(1)}, u32[]{:S(2)}, u32[]{:S(2)}) collective-permute-start(f32[16,2048]{1,0:T(8,128)S(1)} %get-tuple-element.107), channel_id=1, source_target_pairs={{0,16},{8,24},{16,0},{24,8},{1,17},{9,25},{17,1},{25,9},{2,18},{10... | collective-permute-start | bytes 393224 | tf_op jit(solution)/shard_map/ppermute | solution.py:497
  56.0 10.5 %collective-permute-start.24 = (f32[16,2048]{1,0:T(8,128)S(1)}, f32[16,2048]{1,0:T(8,128)S(1)}, u32[]{:S(2)}, u32[]{:S(2)}) collective-permute-start(f32[16,2048]{1,0:T(8,128)S(1)} %get-tuple-element.114), channel_id=1, source_target_pairs={{0,24},{8,16},{16,8},{24,0},{1,25},{9,17},{17,9},{25,1},{2,26},{10... | collective-permute-start | bytes 393224 | tf_op jit(solution)/shard_map/ppermute | solution.py:497
  56.8 10.8 %collective-permute-start.25 = (f32[16,2048]{1,0:T(8,128)S(1)}, f32[16,2048]{1,0:T(8,128)S(1)}, u32[]{:S(2)}, u32[]{:S(2)}) collective-permute-start(f32[16,2048]{1,0:T(8,128)S(1)} %get-tuple-element.115), channel_id=1, source_target_pairs={{0,8},{8,0},{16,24},{24,16},{1,9},{9,1},{17,25},{25,17},{2,10},{10... | collective-permute-start | bytes 393224 | tf_op jit(solution)/shard_map/ppermute | solution.py:497
  59.4 8.2 %collective-permute-start.26 = (f32[16,2048]{1,0:T(8,128)S(1)}, f32[16,2048]{1,0:T(8,128)S(1)}, u32[]{:S(2)}, u32[]{:S(2)}) collective-permute-start(f32[16,2048]{1,0:T(8,128)S(1)} %get-tuple-element.116), channel_id=1, source_target_pairs={{0,16},{8,24},{16,0},{24,8},{1,17},{9,25},{17,1},{25,9},{2,18},{10... | collective-permute-start | bytes 393224 | tf_op jit(solution)/shard_map/ppermute | solution.py:497
  65.0 6.1 %collective-permute-start.21 = (f32[16,2048]{1,0:T(8,128)S(1)}, f32[16,2048]{1,0:T(8,128)S(1)}, u32[]{:S(2)}, u32[]{:S(2)}) collective-permute-start(f32[16,2048]{1,0:T(8,128)S(1)} %get-tuple-element.110), channel_id=1, source_target_pairs={{0,24},{8,16},{16,8},{24,0},{1,25},{9,17},{17,9},{25,1},{2,26},{10... | collective-permute-start | bytes 393224 | tf_op jit(solution)/shard_map/ppermute | solution.py:497
  65.4 7.8 %collective-permute-start.22 = (f32[16,2048]{1,0:T(8,128)S(1)}, f32[16,2048]{1,0:T(8,128)S(1)}, u32[]{:S(2)}, u32[]{:S(2)}) collective-permute-start(f32[16,2048]{1,0:T(8,128)S(1)} %get-tuple-element.111), channel_id=1, source_target_pairs={{0,8},{8,0},{16,24},{24,16},{1,9},{9,1},{17,25},{25,17},{2,10},{10... | collective-permute-start | bytes 393224 | tf_op jit(solution)/shard_map/ppermute | solution.py:497
  66.4 6.8 %collective-permute-start.23 = (f32[16,2048]{1,0:T(8,128)S(1)}, f32[16,2048]{1,0:T(8,128)S(1)}, u32[]{:S(2)}, u32[]{:S(2)}) collective-permute-start(f32[16,2048]{1,0:T(8,128)S(1)} %get-tuple-element.112), channel_id=1, source_target_pairs={{0,16},{8,24},{16,0},{24,8},{1,17},{9,25},{17,1},{25,9},{2,18},{10... | collective-permute-start | bytes 393224 | tf_op jit(solution)/shard_map/ppermute | solution.py:497
  69.5 10.5 %collective-permute-start.29 = (f32[16,2048]{1,0:T(8,128)S(1)}, f32[16,2048]{1,0:T(8,128)S(1)}, u32[]{:S(2)}, u32[]{:S(2)}) collective-permute-start(f32[16,2048]{1,0:T(8,128)S(1)} %get-tuple-element.124), channel_id=1, source_target_pairs={{0,24},{8,16},{16,8},{24,0},{1,25},{9,17},{17,9},{25,1},{2,26},{10... | collective-permute-start | bytes 393224 | tf_op jit(solution)/shard_map/ppermute | solution.py:497
  70.1 9.9 %collective-permute-start.30 = (f32[16,2048]{1,0:T(8,128)S(1)}, f32[16,2048]{1,0:T(8,128)S(1)}, u32[]{:S(2)}, u32[]{:S(2)}) collective-permute-start(f32[16,2048]{1,0:T(8,128)S(1)} %get-tuple-element.125), channel_id=1, source_target_pairs={{0,8},{8,0},{16,24},{24,16},{1,9},{9,1},{17,25},{25,17},{2,10},{10... | collective-permute-start | bytes 393224 | tf_op jit(solution)/shard_map/ppermute | solution.py:497
  71.1 8.9 %collective-permute-start.31 = (f32[16,2048]{1,0:T(8,128)S(1)}, f32[16,2048]{1,0:T(8,128)S(1)}, u32[]{:S(2)}, u32[]{:S(2)}) collective-permute-start(f32[16,2048]{1,0:T(8,128)S(1)} %get-tuple-element.126), channel_id=1, source_target_pairs={{0,16},{8,24},{16,0},{24,8},{1,17},{9,25},{17,1},{25,9},{2,18},{10... | collective-permute-start | bytes 393224 | tf_op jit(solution)/shard_map/ppermute | solution.py:497
  73.9 10.0 %collective-permute-start.27 = (f32[32,2048]{1,0:T(8,128)S(1)}, f32[32,2048]{1,0:T(8,128)S(1)}, u32[]{:S(2)}, u32[]{:S(2)}) collective-permute-start(f32[32,2048]{1,0:T(8,128)S(1)} %get-tuple-element.119), channel_id=1, source_target_pairs={{1,2},{3,4},{5,6},{2,1},{4,3},{6,5},{9,10},{11,12},{13,14},{10,9},... | collective-permute-start | bytes 786440 | tf_op jit(solution)/shard_map/ppermute | solution.py:504
  79.9 4.0 %collective-permute-start.28 = (f32[32,2048]{1,0:T(8,128)S(1)}, f32[32,2048]{1,0:T(8,128)S(1)}, u32[]{:S(2)}, u32[]{:S(2)}) collective-permute-start(f32[32,2048]{1,0:T(8,128)S(1)} %get-tuple-element.120), channel_id=1, source_target_pairs={{0,1},{2,3},{4,5},{6,7},{1,0},{3,2},{5,4},{7,6},{8,9},{10,11},{12,... | collective-permute-start | bytes 786440 | tf_op jit(solution)/shard_map/ppermute | solution.py:504
  (9 other events, 29.2 us)

commit v4 on v3

--- a/solution.py
+++ b/solution.py
@@ -12,8 +12,6 @@
 F32 = jnp.float32
 BF16 = jnp.bfloat16
 VMEM = pl.BlockSpec(memory_space=pltpu.VMEM)
-SMEM = pl.BlockSpec(memory_space=pltpu.SMEM)
-ANY = pl.BlockSpec(memory_space=pl.ANY)
 HBM = pl.BlockSpec(memory_space=pltpu.HBM)
 
 
@@ -27,7 +25,7 @@
 
 def call(cost, kernel, outs, specs, scratch=(), place=VMEM):
     return pl.pallas_call(
-        kernel,
+        lambda *refs: kernel(place_of_device(), *refs),
         out_shape=outs,
         in_specs=specs,
         out_specs=jax.tree.map(lambda _: place, outs),
@@ -71,6 +69,17 @@
     return offsets[:1] + sorted(offsets[1:], key=lambda offset: offset.count(0))
 
 
+def place_of_device():
+    groups, beside = lax.axis_size("gz"), lax.axis_size("bx")
+    me_z, me_x = lax.axis_index("gz"), lax.axis_index("bx")
+    offsets = offsets_of(groups, beside)
+    ahead = [lax.rem(me_z + dz, groups) * beside + lax.rem(me_x + dx, beside) for dz, dx in offsets]
+    behind = [
+        lax.rem(me_z + groups - dz, groups) * beside + lax.rem(me_x + beside - dx, beside) for dz, dx in offsets
+    ]
+    return ahead + behind + [lax.rem(lax.axis_index("by"), 2), me_z, me_x]
+
+
 def split(value):
     high = value.astype(BF16)
     return high, (value - high.astype(F32)).astype(BF16)
@@ -107,13 +116,13 @@
     return dot(jnp.concatenate([high, low, high], axis=1), matrix)
 
 
-def ordered_rows(matrix, where_ref, order_ref, runs, count):
+def ordered_rows(matrix, where, order_ref, runs, count):
     size = size_of(runs)
     chunk = size // count
     width = matrix.shape[1]
     order_ref[0, :size, :width] = rows_of(matrix, runs)
     for slot in range(count):
-        place = pl.multiple_of(where_ref[slot] * chunk, chunk)
+        place = pl.multiple_of(where[slot] * chunk, chunk)
         order_ref[1, slot * chunk : (slot + 1) * chunk, :width] = order_ref[0, pl.ds(place, chunk), :width]
     return order_ref[1, :size, :width]
 
@@ -135,7 +144,7 @@
 def weights_kernel(
     sizes,
     parts,
-    where_ref,
+    where,
     psf_z_ref,
     psf_x_ref,
     psf_y_ref,
@@ -160,7 +169,7 @@
     edges = [(0, 2 * radius), (wide - 2 * radius, 2 * radius)]
 
     ahead = banded(taps, columns, wide, 0)
-    ahead = jnp.concatenate([ordered_rows(ahead, where_ref, order_ref, runs, count) for runs in parts], axis=0)
+    ahead = jnp.concatenate([ordered_rows(ahead, where, order_ref, runs, count) for runs in parts], axis=0)
     first_ref[...] = as_left(ahead[: size_of(parts[0])])
     ahead_early_ref[...] = as_left(ahead[:, 2 * radius : columns])
     ahead_late_ref[...] = as_left(columns_of(ahead, edges))
@@ -192,21 +201,21 @@
             line = [jnp.zeros((width, rows), F32)] * per
             line[k] = back[:, b * rows : (b + 1) * rows]
             blocks.append(jnp.concatenate(line, axis=1))
-        slot = lax.rem(b + beside - where_ref[2 * count + 2], beside)
+        slot = lax.rem(b + beside - where[2 * count + 2], beside)
         rows_back_ref[:, pl.ds(pl.multiple_of(slot * LANES, LANES), LANES)] = as_right(jnp.concatenate(blocks, axis=0))
     planes = groups * depth
     for ref, line in zip((planes_ahead_ref, planes_back_ref), taps_of(psf_z_ref)):
         ref[...] = as_left(banded(line, planes, planes, -radius))
 
 
-def send_sides(where_ref, count, value_ref, span, sibling_ref, other_ref):
-    odd = where_ref[2 * count]
+def send_sides(where, count, value_ref, span, sibling_ref, other_ref):
+    odd = where[2 * count]
     room = value_ref.shape[0] - span
     sibling_ref[...] = value_ref[pl.ds(pl.multiple_of((1 - odd) * room, 8), span), :]
     other_ref[...] = value_ref[pl.ds(pl.multiple_of(odd * room, 8), span), :]
 
 
-def start_kernel(parts, radius, count, where_ref, psf_hbm, block_hbm, *refs):
+def start_kernel(parts, radius, count, where, psf_hbm, block_hbm, *refs):
     own_ref, sibling_ref, other_ref = refs[:3]
     part_refs, (order_ref, psf_ref, block_ref, sems) = refs[3:-4], refs[-4:]
     length, columns = block_ref.shape
@@ -223,17 +232,17 @@
     matrices = [None]
     for runs in parts[1:]:
         matrix = banded(taps, columns, columns, -radius)
-        matrices.append(as_left(ordered_rows(matrix, where_ref, order_ref, runs, count)))
+        matrices.append(as_left(ordered_rows(matrix, where, order_ref, runs, count)))
     for k in range(pieces):
         copies[k + 1].wait()
         for at in range(k * piece, (k + 1) * piece, LANES):
             own_ref[:, at : at + LANES] = jnp.transpose(block_ref[at : at + LANES, :])
-    send_sides(where_ref, count, own_ref, radius, sibling_ref, other_ref)
+    send_sides(where, count, own_ref, radius, sibling_ref, other_ref)
     before = 0
     for k, runs in reversed(list(enumerate(parts))):
         chunk = size_of(runs) // count
         for slot, part_ref in enumerate(part_refs):
-            place = pl.multiple_of(place_of(runs, where_ref[slot] * chunk), 8)
+            place = pl.multiple_of(place_of(runs, where[slot] * chunk), 8)
             part_ref[before : before + chunk, :] = own_ref[pl.ds(place, chunk), :]
         before += chunk
         if k:
@@ -245,11 +254,11 @@
             before += chunk
 
 
-def first_y_kernel(where_ref, matrix_ref, own_ref, other_ref, sibling_ref, *part_refs):
+def first_y_kernel(where, matrix_ref, own_ref, other_ref, sibling_ref, *part_refs):
     columns, length = own_ref.shape
     count = len(part_refs)
     chunk = part_refs[0].shape[0]
-    odd = where_ref[2 * count] == 1
+    odd = where[2 * count] == 1
     for at in range(0, length, STEP):
         here = slice(at, at + STEP)
         field = assembled([[(0, columns)]], odd, [own_ref], [(other_ref, sibling_ref)], here)
@@ -258,21 +267,21 @@
             part_ref[:, here] = result[slot * chunk : (slot + 1) * chunk]
 
 
-def put_parts(where_ref, count, part_refs, own_refs):
+def put_parts(where, count, part_refs, own_refs):
     for k, own_ref in enumerate(own_refs):
         for slot, part_ref in enumerate(part_refs[k * count : (k + 1) * count]):
             chunk = part_ref.shape[0]
-            place = pl.multiple_of(where_ref[count + slot] * chunk, chunk)
+            place = pl.multiple_of(where[count + slot] * chunk, chunk)
             own_ref[pl.ds(place, chunk), :] = part_ref[...]
 
 
-def sides_kernel(count, where_ref, *refs):
+def sides_kernel(count, where, *refs):
     part_refs, (_, sibling_ref, other_ref) = refs[:count], refs[count:]
     span = sibling_ref.shape[0]
     chunk = part_refs[0].shape[0]
-    odd = where_ref[2 * count]
+    odd = where[2 * count]
     for slot, part_ref in enumerate(part_refs):
-        start = where_ref[count + slot] * chunk
+        start = where[count + slot] * chunk
         for first, to_sibling in ((0, odd), (count * chunk - span, 1 - odd)):
             inside = (start >= first) & (start < first + span)
 
@@ -299,17 +308,17 @@
     return jnp.concatenate(low + own + high, axis=0)
 
 
-def middle_early_kernel(parts, radius, count, where_ref, back_ref, ahead_ref, *refs):
+def middle_early_kernel(parts, radius, count, where, back_ref, ahead_ref, *refs):
     kinds = len(parts)
     own_refs, refs = refs[-kinds:], refs[:-kinds]
-    put_parts(where_ref, count, refs, own_refs)
+    put_parts(where, count, refs, own_refs)
     refs = refs[kinds * count :]
     side_refs = [refs[2 * k : 2 * k + 2] for k in range(kinds - 1)]
     seen_ref, outer_ref, inner_ref, result_ref = refs[2 * kinds - 2 :]
     columns, length = seen_ref.shape
     wide = columns + 2 * radius
     edges = [(0, 2 * radius), (wide - 2 * radius, 2 * radius)]
-    odd = where_ref[2 * count] == 1
+    odd = where[2 * count] == 1
     for at in range(0, length, STEP):
         here = slice(at, at + STEP)
         blurred = left_product(back_ref[...], assembled(parts, odd, own_refs, side_refs, here))
@@ -319,13 +328,13 @@
         result_ref[:, here] = left_product(ahead_ref[...], inner)
 
 
-def middle_late_kernel(parts, radius, count, where_ref, back_ref, ahead_ref, *refs):
+def middle_late_kernel(parts, radius, count, where, back_ref, ahead_ref, *refs):
     (other_ref, sibling_ref, outer_ref, inner_ref, result_ref), refs = refs[:5], refs[5:]
     seen_ref, seen_other_ref, seen_sibling_ref, estimate_ref, *part_refs = refs
     columns, length = seen_ref.shape
     wide = columns + 2 * radius
     edges = [(0, 2 * radius), (wide - 2 * radius, 2 * radius)]
-    odd = where_ref[2 * count] == 1
+    odd = where[2 * count] == 1
     for at in range(0, length, STEP):
         here = slice(at, at + STEP)
         sides = assembled([], odd, [], [(other_ref, sibling_ref)], here)
@@ -342,9 +351,9 @@
             place += chunk
 
 
-def last_early_kernel(parts, radius, count, where_ref, back_ref, estimate_ref, *refs):
+def last_early_kernel(parts, radius, count, where, back_ref, estimate_ref, *refs):
     outer_ref, inner_ref, *own_refs = refs[len(parts) * count :]
-    put_parts(where_ref, count, refs, own_refs)
+    put_parts(where, count, refs, own_refs)
     columns, length = estimate_ref.shape
     edges = [(0, radius), (columns - radius, radius)]
     for at in range(0, length, STEP):
@@ -355,10 +364,10 @@
 
 
 def last_late_kernel(
-    radius, count, where_ref, back_ref, other_ref, sibling_ref, outer_ref, inner_ref, estimate_ref, out_hbm, out_ref, sems
+    radius, count, where, back_ref, other_ref, sibling_ref, outer_ref, inner_ref, estimate_ref, out_hbm, out_ref, sems
 ):
     columns, length = estimate_ref.shape
-    odd = where_ref[2 * count] == 1
+    odd = where[2 * count] == 1
     edges = [(0, radius), (columns - radius, radius)]
     pieces = sems.shape[0]
     piece = length // pieces
@@ -370,11 +379,11 @@
         estimate = jnp.concatenate([outer[:radius], inner_ref[:, here], outer[radius:]], axis=0)
         for tile in range(0, STEP, LANES):
             out_ref[at + tile : at + tile + LANES, :] = jnp.transpose(estimate[:, tile : tile + LANES])
-        if (at + STEP) % piece == 0:
-            k = at // piece
-            lines = pl.ds(k * piece, piece)
-            copies.append(pltpu.make_async_copy(out_ref.at[lines], out_hbm.at[lines], sems.at[k]))
-            copies[-1].start()
+            if (at + tile + LANES) % piece == 0:
+                k = (at + tile) // piece
+                lines = pl.ds(k * piece, piece)
+                copies.append(pltpu.make_async_copy(out_ref.at[lines], out_hbm.at[lines], sems.at[k]))
+                copies[-1].start()
     for copy in copies:
         copy.wait()
 
@@ -388,20 +397,20 @@
     return jnp.concatenate([ref[tile, lines, :] for tile in range(ref.shape[0])], axis=1)
 
 
-def fill(sizes, where_ref, part_refs, first, chunk, held_ref):
+def fill(sizes, where, part_refs, first, chunk, held_ref):
     groups, beside = sizes[:2]
     count = groups * beside
     tiles = part_refs[0].shape[1] // LANES
     for (dz, dx), part_ref in zip(offsets_of(groups, beside), part_refs):
-        source_z = lax.rem(where_ref[2 * count + 1] + groups - dz, groups)
-        source_x = lax.rem(where_ref[2 * count + 2] + beside - dx, beside)
+        source_z = lax.rem(where[2 * count + 1] + groups - dz, groups)
+        source_x = lax.rem(where[2 * count + 2] + beside - dx, beside)
         for t in range(tiles):
             place = pl.multiple_of((source_z * tiles + t) * chunk, chunk)
             held_ref[source_x, pl.ds(place, chunk), :] = part_ref[first : first + chunk, t * LANES : (t + 1) * LANES]
 
 
 def planes_kernel(
-    sizes, first, seen_first, where_ref, rows_ahead_ref, rows_back_ref, planes_ahead_ref, planes_back_ref, *refs
+    sizes, first, seen_first, where, rows_ahead_ref, rows_back_ref, planes_ahead_ref, planes_back_ref, *refs
 ):
     groups, beside, _, _, rows, _ = sizes
     count = groups * beside
@@ -409,24 +418,23 @@
     begins = seen_first is not None
     if begins:
         seen_refs, refs = refs[:count], refs[count:]
-        out_refs, (mark_ref, seen_ref, held_ref, field_ref, other_ref) = refs[:count], refs[count:]
+        out_refs, (seen_ref, held_ref, field_ref, other_ref) = refs[:count], refs[count:]
     else:
-        seen_ref, out_refs, (mark_ref, held_ref, field_ref, other_ref) = refs[0], refs[1 : count + 1], refs[count + 1 :]
-    mark_ref[...] = jnp.zeros_like(mark_ref)
+        seen_ref, out_refs, (held_ref, field_ref, other_ref) = refs[0], refs[1 : count + 1], refs[count + 1 :]
     chunk, length = out_refs[0].shape
     tiles = length // LANES
     per = LANES // rows
     width = beside * rows
     planes = groups * tiles * per
     if begins:
-        fill(sizes, where_ref, seen_refs, seen_first, chunk, held_ref)
+        fill(sizes, where, seen_refs, seen_first, chunk, held_ref)
         for at in range(groups * tiles):
             for k in range(per):
                 lines = slice(at * chunk, (at + 1) * chunk)
                 pieces = [held_ref[b, lines, k * rows : (k + 1) * rows] for b in range(beside)]
                 place = (at * per + k) * chunk
                 put_lines(seen_ref, slice(place, place + chunk), jnp.concatenate(pieces, axis=1))
-    fill(sizes, where_ref, part_refs, first, chunk, held_ref)
+    fill(sizes, where, part_refs, first, chunk, held_ref)
 
     group = min(tiles, max(1, 4 * LANES // chunk))
     for at in range(0, groups * tiles, group):
@@ -449,7 +457,7 @@
 
     offsets = offsets_of(groups, beside)
     for dz in range(groups):
-        target_z = lax.rem(where_ref[2 * count + 1] + dz, groups)
+        target_z = lax.rem(where[2 * count + 1] + dz, groups)
         for at in range(0, tiles, group):
             pieces = []
             for g in range(group):
@@ -478,13 +486,7 @@
     parts = parts_of(columns, radius, count)
     chunks = [size_of(runs) // count for runs in parts]
 
-    me_z, me_x = lax.axis_index("gz"), lax.axis_index("bx")
     offsets = offsets_of(groups, beside)
-    ahead = [lax.rem(me_z + dz, groups) * beside + lax.rem(me_x + dx, beside) for dz, dx in offsets]
-    behind = [
-        lax.rem(me_z + groups - dz, groups) * beside + lax.rem(me_x + beside - dx, beside) for dz, dx in offsets
-    ]
-    where = jnp.stack(ahead + behind + [lax.rem(lax.axis_index("by"), 2), me_z, me_x]).astype(jnp.int32)
 
     def exchanged(values):
         result = [values[0]]
@@ -514,9 +516,9 @@
         functools.partial(start_kernel, parts, radius, count),
         [shaped(columns, length), shaped(radius, length), shaped(radius, length)]
         + [shaped(block + sum(chunks[1:]), length)] * count,
-        [SMEM, HBM, HBM],
+        [HBM, HBM],
         [order, pltpu.VMEM(line, F32), pltpu.VMEM((length, columns), F32), pltpu.SemaphoreType.DMA((pieces + 1,))],
-    )(where, stays(psf_y), stays(observed.reshape(length, columns)))
+    )(stays(psf_y), stays(observed.reshape(length, columns)))
     seen_sides = from_sides(sibling, other)
     parcels = exchanged(parcels)
 
@@ -544,16 +546,16 @@
             left(groups * planes, groups * planes),
             left(groups * planes, groups * planes),
         ],
-        [SMEM] + [VMEM] * 3,
+        [VMEM] * 3,
         [order],
-    )(where, psf_z, psf_x, psf_y)
+    )(psf_z, psf_x, psf_y)
     outer = exchanged(
         call(
             0.8,
             first_y_kernel,
             [shaped(chunks[0], length)] * count,
-            [SMEM] + [VMEM] * 4,
-        )(where, first, seen, *seen_sides)
+            [VMEM] * 4,
+        )(first, seen, *seen_sides)
     )
 
     def through_planes(values, first, chunk, seen_values, seen_first=None):
@@ -563,69 +565,69 @@
         result = call(
             50,
             functools.partial(planes_kernel, sizes, first, seen_first),
-            [shaped(chunk, length)] * count + [shaped(8, LANES)] + [shaped(*across)] * begins,
-            [SMEM] + [VMEM] * (4 + len(values) + len(seen_values)),
+            [shaped(chunk, length)] * count + [shaped(*across)] * begins,
+            [VMEM] * (4 + len(values) + len(seen_values)),
             [
                 pltpu.VMEM((beside, groups * (length // LANES) * chunk, LANES), F32),
                 pltpu.VMEM(across, F32),
                 pltpu.VMEM(across, F32),
             ],
-        )(where, *weights, *values, *seen_values)
-        return result[:count], result[count], result[count + 1 :] if begins else seen_values
-
-    def sides_of(cost, values, span, mark):
+        )(*weights, *values, *seen_values)
+        return result[:count], result[count:] if begins else seen_values
+
+    def sides_of(cost, values, span, after):
         sides = call(
             cost,
             functools.partial(sides_kernel, count),
             [shaped(span, length)] * 2,
-            [SMEM] + [VMEM] * count + [ANY],
-        )(where, *values, mark)
+            [VMEM] * (count + 1),
+        )(*values, after)
         return from_sides(*sides)
 
     fields, across, sides = ([None] * len(parts) for _ in range(3))
     before = 0
     for k in reversed(range(len(parts))):
         values, first = (parcels, before + chunks[k]) if k else (outer, 0)
-        fields[k], mark, across[k] = through_planes(values, first, chunks[k], parcels, before)
+        fields[k], across[k] = through_planes(values, first, chunks[k], parcels, before)
         fields[k] = exchanged(fields[k])
         before += chunks[k] * (2 if k else 1)
     for k in reversed(range(len(parts))):
-        sides[k] = sides_of(50, fields[k], span, mark)
+        sides[k] = sides_of(50, fields[k], span, fields[0][0])
     partial = [shaped(4 * radius, length), shaped(columns - 2 * radius, length), shaped(columns, length)]
     partial = call(
         2.2,
         functools.partial(middle_early_kernel, parts, radius, count),
         partial,
-        [SMEM] + [VMEM] * (1 + (count + 2) * len(parts)),
+        [VMEM] * (1 + (count + 2) * len(parts)),
         [pltpu.VMEM((size_of(runs), length), F32) for runs in parts],
-    )(where, back_early, ahead_early, *flat(fields), *flat(sides[1:]), seen)
+    )(back_early, ahead_early, *flat(fields), *flat(sides[1:]), seen)
     estimate, *parcels = call(
         1.3,
         functools.partial(middle_late_kernel, parts, radius, count),
         [shaped(columns, length)] + [shaped(chunk, length) for chunk in chunks for _ in range(count)],
-        [SMEM] + [VMEM] * 10,
-    )(where, back_late, ahead_late, *sides[0], *partial, seen, *seen_sides)
+        [VMEM] * 10,
+    )(back_late, ahead_late, *sides[0], *partial, seen, *seen_sides)
     for k in range(len(parts)):
         fields[k] = exchanged(parcels[k * count : (k + 1) * count])
     for k in range(len(parts)):
-        values, mark, _ = through_planes(fields[k], 0, chunks[k], across[k])
+        values, _ = through_planes(fields[k], 0, chunks[k], across[k])
         fields[k] = exchanged(values)
-    sides = sides_of(0.6, fields[0], radius, mark)
+    sides = sides_of(0.6, fields[0], radius, fields[-1][0])
     partial = call(
         50,
         functools.partial(last_early_kernel, parts, radius, count),
         [shaped(2 * radius, length), shaped(columns - 2 * radius, length)],
-        [SMEM] + [VMEM] * (2 + count * len(parts)),
+        [VMEM] * (2 + count * len(parts)),
         [pltpu.VMEM((size_of(runs), length), F32) for runs in parts],
-    )(where, end_early, estimate, *flat(fields))
+    )(end_early, estimate, *flat(fields))
     out = call(
         1.5,
         functools.partial(last_late_kernel, radius, count),
         shaped(length, columns),
-        [SMEM] + [VMEM] * 6,
+        [VMEM] * 6,
         [pltpu.VMEM((length, columns), F32), pltpu.SemaphoreType.DMA((pieces,))],
         HBM,
-    )(where, end_late, *sides, *partial, estimate)
+    )(end_late, *sides, *partial, estimate)
     return out.reshape(planes, rows, columns)
 
 

time: 86 us -> 81.5 us (0.948)
  Pallas kernels: 22.7 us -> 14.1 us
  waiting for transfers between devices: 19 us -> 24.3 us
  starting transfers between devices: 43 us -> 41.8 us
    ppermute x24, waiting for transfers between devices: 12.1 us -> 15.6 us  [exchanged(): result.append(lax.ppermute(value, ('gz', 'bx'), pairs))]
    pallas_call x4, Pallas kernels: 8.83 us -> 5.69 us  [through_planes(): call(50, functools.partial(planes_kernel, sizes, first, seen_first), [sha...]
    ppermute x8, waiting for transfers between devices: 6.86 us -> 8.67 us  [from_sides(): result.append(lax.ppermute(value, 'by', pairs + [(j, i) for i, j in pairs]))]
    pallas_call x3, Pallas kernels: 2.04 us -> 0.37 us  [sides_of(): call(cost, functools.partial(sides_kernel, count), [shaped(span, length)]...]
    ppermute x24, starting transfers between devices: 21.9 us -> 20.3 us  [exchanged(): result.append(lax.ppermute(value, ('gz', 'bx'), pairs))]
  transfers between devices with their start and end apart: 32 -> 32, of which waited for: 8 -> 12; matrix products, arithmetic and copies ran while one was open for 0% -> 0% of each run, Pallas kernels for 19% -> 12%
where the time goes in v4:
time: 81.5 us; the launch traced here: 81.3 us
  starting transfers between devices  41.8 us (51%)
  waiting for transfers between devices  24.3 us (30%)
  Pallas kernels  14.1 us (17%)
  local copies, waits for them, and re-layouts  0.86 us (1%)
    ppermute x8, starting transfers between devices, from_sides(): result.append(lax.ppermute(value, 'by', pairs + [(j, i) for i, j in pairs]))  21.5 us
    ppermute x24, starting transfers between devices, exchanged(): result.append(lax.ppermute(value, ('gz', 'bx'), pairs))  20.3 us
    ppermute x24, waiting for transfers between devices, exchanged(): result.append(lax.ppermute(value, ('gz', 'bx'), pairs))  15.6 us
    ppermute x8, waiting for transfers between devices, from_sides(): result.append(lax.ppermute(value, 'by', pairs + [(j, i) for i, j in pairs]))  8.67 us
    pallas_call x4, Pallas kernels, through_planes(): call(50, functools.partial(planes_kernel, sizes, first, seen_first), [sha...  5.69 us
    pallas_call x1, Pallas kernels, per_device(): call(1.3, functools.partial(start_kernel, parts, radius, count), [shaped(...  1.92 us
  transfers between devices with their start and end apart: 32, of which 12 were waited for; matrix products, arithmetic and copies ran while one was open for 0% of the time, Pallas kernels for 12%

profile of v4, /device:TPU:1, one launch (start us, length us, event | category | flops | bytes accessed | tf_op | source)
XLA Modules:
  0.0 81.3 jit_solution(10688658299911530123)
XLA Ops:
  0.0 1.9 %shard_map.47 = (f32[128,2048]{1,0:T(8,128)S(1)}, f32[32,2048]{1,0:T(8,128)S(1)}, f32[32,2048]{1,0:T(8,128)S(1)}, f32[48,2048]{1,0:T(8,128)S(1)}, f32[48,2048]{1...) custom-call(f32[1,65]{1,0:T(1,128)} %bitcast.7, f32[2048,128]{1,0:T(8,128)} %bitcast.9), custom_call_target="tpu_custom_call" | custom-call | flops 1495000064 | tf_op jit(solution)/shard_map/pallas_call | solution.py:514
  1.9 3.1 %collective-permute-start.5 = (f32[48,2048]{1,0:T(8,128)S(1)}, f32[48,2048]{1,0:T(8,128)S(1)}, u32[]{:S(2)}, u32[]{:S(2)}) collective-permute-start(f32[48,2048]{1,0:T(8,128)S(1)} %get-tuple-element.81), channel_id=1, source_target_pairs={{0,24},{8,16},{16,8},{24,0},{1,25},{9,17},{17,9},{25,1},{2,26},{10... | collective-permute-start | bytes 1179656 | tf_op jit(solution)/shard_map/ppermute | solution.py:499
  5.4 4.7 %collective-permute-start = (f32[32,2048]{1,0:T(8,128)S(1)}, f32[32,2048]{1,0:T(8,128)S(1)}, u32[]{:S(2)}, u32[]{:S(2)}) collective-permute-start(f32[32,2048]{1,0:T(8,128)S(1)} %get-tuple-element.74), channel_id=1, source_target_pairs={{1,2},{3,4},{5,6},{2,1},{4,3},{6,5},{9,10},{11,12},{13,14},{10,9},... | collective-permute-start | bytes 786440 | tf_op jit(solution)/shard_map/ppermute | solution.py:506
  10.9 0.9 %shard_map.46 = (bf16[64,576]{1,0:T(8,128)(2,1)S(1)}, bf16[192,576]{1,0:T(8,128)(2,1)S(1)}, bf16[128,192]{1,0:T(8,128)(2,1)S(1)}, bf16[128,192]{1,0:T(8,128)(2,1...) custom-call(f32[1,65]{1,0:T(1,128)S(1)} %bitcast.5, ...), custom_call_target="tpu_custom_call" | custom-call | flops 920000000 | tf_op jit(solution)/shard_map/pallas_call | solution.py:533
  11.8 2.7 %collective-permute-done.refs_2_.refs_8_ = f32[32,2048]{1,0:T(8,128)S(1)} collective-permute-done((f32[32,2048]{1,0:T(8,128)S(1)}, f32[32,2048]{1,0:T(8,128)S(1)}, u32[]{:S(2)}, u32[]{:S(2)}) %collective-permute-start) | collective-permute-done | bytes 262176 | tf_op jit(solution)/shard_map/ppermute | solution.py:506
  15.2 2.2 %collective-permute-start.2 = (f32[16,2048]{1,0:T(8,128)S(1)}, f32[16,2048]{1,0:T(8,128)S(1)}, u32[]{:S(2)}, u32[]{:S(2)}) collective-permute-start(f32[16,2048]{1,0:T(8,128)S(1)} %get-tuple-element.77), channel_id=1, source_target_pairs={{0,24},{8,16},{16,8},{24,0},{1,25},{9,17},{17,9},{25,1},{2,26},{10... | collective-permute-start | bytes 393224 | tf_op jit(solution)/shard_map/ppermute | solution.py:499
  17.9 5.8 %collective-permute-done.6.refs_10_.refs_6_ = f32[48,2048]{1,0:T(8,128)S(1)} collective-permute-done((f32[48,2048]{1,0:T(8,128)S(1)}, f32[48,2048]{1,0:T(8,128)S(1)}, u32[]{:S(2)}, u32[]{:S(2)}) %collective-permute-start.6) | collective-permute-done | bytes 393248 | tf_op jit(solution)/shard_map/ppermute | solution.py:499
  23.7 1.5 %shard_map.51 = (f32[16,2048]{1,0:T(8,128)S(1)}, f32[16,2048]{1,0:T(8,128)S(1)}, f32[16,2048]{1,0:T(8,128)S(1)}, f32[16,2048]{1,0:T(8,128)S(1)}, f32[1,1024,128]{2,1,0:T(8,128)S(1)}) custom-call(bf16[768,256]{1,0:T(8,128)(2,1)S(1)} %get-tuple-element.66.refs_0_, bf16[768,256]{1,0:T(8,128)(2,1)S(1)} %get-tuple-element.67.refs_1_, ...), custom_call_target="tpu_custom_call" | custom-call | flops 57500000256 | tf_op jit(solution)/shard_map/pallas_call | solution.py:565
  25.5 2.7 %collective-permute-start.14 = (f32[16,2048]{1,0:T(8,128)S(1)}, f32[16,2048]{1,0:T(8,128)S(1)}, u32[]{:S(2)}, u32[]{:S(2)}) collective-permute-start(f32[16,2048]{1,0:T(8,128)S(1)} %get-tuple-element.94), channel_id=1, source_target_pairs={{0,8},{8,0},{16,24},{24,16},{1,9},{9,1},{17,25},{25,17},{2,10},{10... | collective-permute-start | bytes 393224 | tf_op jit(solution)/shard_map/ppermute | solution.py:499
  28.6 1.5 %shard_map.49 = (f32[16,2048]{1,0:T(8,128)S(1)}, f32[16,2048]{1,0:T(8,128)S(1)}, f32[16,2048]{1,0:T(8,128)S(1)}, f32[16,2048]{1,0:T(8,128)S(1)}, f32[1,1024,128]{2,1,0:T(8,128)S(1)}) custom-call(bf16[768,256]{1,0:T(8,128)(2,1)S(1)} %get-tuple-element.66.refs_0_, bf16[768,256]{1,0:T(8,128)(2,1)S(1)} %get-tuple-element.67.refs_1_, ...), custom_call_target="tpu_custom_call" | custom-call | flops 57500000256 | tf_op jit(solution)/shard_map/pallas_call | solution.py:565
  30.1 0.8 %collective-permute-start.8 = (f32[16,2048]{1,0:T(8,128)S(1)}, f32[16,2048]{1,0:T(8,128)S(1)}, u32[]{:S(2)}, u32[]{:S(2)}) collective-permute-start(f32[16,2048]{1,0:T(8,128)S(1)} %get-tuple-element.85), channel_id=1, source_target_pairs={{0,24},{8,16},{16,8},{24,0},{1,25},{9,17},{17,9},{25,1},{2,26},{10... | collective-permute-start | bytes 393224 | tf_op jit(solution)/shard_map/ppermute | solution.py:499
  31.0 1.8 %collective-permute-start.9 = (f32[16,2048]{1,0:T(8,128)S(1)}, f32[16,2048]{1,0:T(8,128)S(1)}, u32[]{:S(2)}, u32[]{:S(2)}) collective-permute-start(f32[16,2048]{1,0:T(8,128)S(1)} %get-tuple-element.86), channel_id=1, source_target_pairs={{0,8},{8,0},{16,24},{24,16},{1,9},{9,1},{17,25},{25,17},{2,10},{10... | collective-permute-start | bytes 393224 | tf_op jit(solution)/shard_map/ppermute | solution.py:499
  32.8 1.4 %collective-permute-done.14.refs_2_.refs_8_ = f32[16,2048]{1,0:T(8,128)S(1)} collective-permute-done((f32[16,2048]{1,0:T(8,128)S(1)}, f32[16,2048]{1,0:T(8,128)S(1)}, u32[]{:S(2)}, u32[]{:S(2)}) %collective-permute-start.14) | collective-permute-done | bytes 131104 | tf_op jit(solution)/shard_map/ppermute | solution.py:499
  34.4 6.9 %collective-permute-start.16 = (f32[32,2048]{1,0:T(8,128)S(1)}, f32[32,2048]{1,0:T(8,128)S(1)}, u32[]{:S(2)}, u32[]{:S(2)}) collective-permute-start(f32[32,2048]{1,0:T(8,128)S(1)} %get-tuple-element.96), channel_id=1, source_target_pairs={{1,2},{3,4},{5,6},{2,1},{4,3},{6,5},{9,10},{11,12},{13,14},{10,9},... | collective-permute-start | bytes 786440 | tf_op jit(solution)/shard_map/ppermute | solution.py:506
  41.6 3.5 %collective-permute-start.11 = (f32[32,2048]{1,0:T(8,128)S(1)}, f32[32,2048]{1,0:T(8,128)S(1)}, u32[]{:S(2)}, u32[]{:S(2)}) collective-permute-start(f32[32,2048]{1,0:T(8,128)S(1)} %get-tuple-element.88), channel_id=1, source_target_pairs={{1,2},{3,4},{5,6},{2,1},{4,3},{6,5},{9,10},{11,12},{13,14},{10,9},... | collective-permute-start | bytes 786440 | tf_op jit(solution)/shard_map/ppermute | solution.py:506
  45.4 1.5 %shard_map.53 = (f32[128,2048]{1,0:T(8,128)S(1)}, f32[64,2048]{1,0:T(8,128)S(1)}, f32[128,2048]{1,0:T(8,128)S(1)}) custom-call(bf16[192,576]{1,0:T(8,128)(2,1)S(1)} %get-tuple-element.90.refs_0_, bf16[128,192]{1,0:T(8,128)(2,1)S(1)} %get-tuple-element.91.refs_1_, f32[16,2048]{1,0:T(8,128)S(1)} %get-tuple-element.84.refs_0_.refs_4_.refs_2_, ...), custom_call_target="tpu_custom_call" | custom-call | flops 2529999872 | tf_op jit(solution)/shard_map/pallas_call | solution.py:597
  46.9 2.5 %collective-permute-done.11.refs_2_ = f32[32,2048]{1,0:T(8,128)S(1)} collective-permute-done((f32[32,2048]{1,0:T(8,128)S(1)}, f32[32,2048]{1,0:T(8,128)S(1)}, u32[]{:S(2)}, u32[]{:S(2)}) %collective-permute-start.11) | collective-permute-done | bytes 262176 | tf_op jit(solution)/shard_map/ppermute | solution.py:506
  49.4 1.2 %shard_map.54 = (f32[128,2048]{1,0:T(8,128)S(1)}, f32[16,2048]{1,0:T(8,128)S(1)}, f32[16,2048]{1,0:T(8,128)S(1)}, f32[16,2048]{1,0:T(8,128)S(1)}, f32[16,2048]{1...) custom-call(bf16[128,192]{1,0:T(8,128)(2,1)S(1)} %get-tuple-element., ...), custom_call_target="tpu_custom_call" | custom-call | flops 1495000064 | tf_op jit(solution)/shard_map/pallas_call | solution.py:604
  51.0 1.1 %collective-permute-start.19 = (f32[16,2048]{1,0:T(8,128)S(1)}, f32[16,2048]{1,0:T(8,128)S(1)}, u32[]{:S(2)}, u32[]{:S(2)}) collective-permute-start(f32[16,2048]{1,0:T(8,128)S(1)} %get-tuple-element.103), channel_id=1, source_target_pairs={{0,8},{8,0},{16,24},{24,16},{1,9},{9,1},{17,25},{25,17},{2,10},{10... | collective-permute-start | bytes 393224 | tf_op jit(solution)/shard_map/ppermute | solution.py:499
  52.1 1.2 %collective-permute-start.20 = (f32[16,2048]{1,0:T(8,128)S(1)}, f32[16,2048]{1,0:T(8,128)S(1)}, u32[]{:S(2)}, u32[]{:S(2)}) collective-permute-start(f32[16,2048]{1,0:T(8,128)S(1)} %get-tuple-element.104), channel_id=1, source_target_pairs={{0,16},{8,24},{16,0},{24,8},{1,17},{9,25},{17,1},{25,9},{2,18},{10... | collective-permute-start | bytes 393224 | tf_op jit(solution)/shard_map/ppermute | solution.py:499
  53.8 1.0 %collective-permute-start.25 = (f32[16,2048]{1,0:T(8,128)S(1)}, f32[16,2048]{1,0:T(8,128)S(1)}, u32[]{:S(2)}, u32[]{:S(2)}) collective-permute-start(f32[16,2048]{1,0:T(8,128)S(1)} %get-tuple-element.112), channel_id=1, source_target_pairs={{0,8},{8,0},{16,24},{24,16},{1,9},{9,1},{17,25},{25,17},{2,10},{10... | collective-permute-start | bytes 393224 | tf_op jit(solution)/shard_map/ppermute | solution.py:499
  54.8 2.4 %collective-permute-done.18.refs_5_ = f32[16,2048]{1,0:T(8,128)S(1)} collective-permute-done((f32[16,2048]{1,0:T(8,128)S(1)}, f32[16,2048]{1,0:T(8,128)S(1)}, u32[]{:S(2)}, u32[]{:S(2)}) %collective-permute-start.18) | collective-permute-done | bytes 131104 | tf_op jit(solution)/shard_map/ppermute | solution.py:499
  57.2 2.7 %collective-permute-done.19.refs_6_ = f32[16,2048]{1,0:T(8,128)S(1)} collective-permute-done((f32[16,2048]{1,0:T(8,128)S(1)}, f32[16,2048]{1,0:T(8,128)S(1)}, u32[]{:S(2)}, u32[]{:S(2)}) %collective-permute-start.19) | collective-permute-done | bytes 131104 | tf_op jit(solution)/shard_map/ppermute | solution.py:499
  59.8 1.4 %shard_map.55 = (f32[16,2048]{1,0:T(8,128)S(1)}, f32[16,2048]{1,0:T(8,128)S(1)}, f32[16,2048]{1,0:T(8,128)S(1)}, f32[16,2048]{1,0:T(8,128)S(1)}) custom-call(bf16[768,256]{1,0:T(8,128)(2,1)S(1)} %get-tuple-element.66.refs_0_, bf16[768,256]{1,0:T(8,128)(2,1)S(1)} %get-tuple-element.67.refs_1_, bf16[64,192]{1,0:T(8,128)(2,1)S(1)} %get-tuple-element.68.refs_2_, ...), custom_call_target="tpu_custom_call" | custom-call | flops 57500000256 | tf_op jit(solution)/shard_map/pallas_call | solution.py:565
  62.4 1.6 %collective-permute-start.23 = (f32[16,2048]{1,0:T(8,128)S(1)}, f32[16,2048]{1,0:T(8,128)S(1)}, u32[]{:S(2)}, u32[]{:S(2)}) collective-permute-start(f32[16,2048]{1,0:T(8,128)S(1)} %get-tuple-element.109), channel_id=1, source_target_pairs={{0,16},{8,24},{16,0},{24,8},{1,17},{9,25},{17,1},{25,9},{2,18},{10... | collective-permute-start | bytes 393224 | tf_op jit(solution)/shard_map/ppermute | solution.py:499
  63.9 1.4 %shard_map.56 = (f32[16,2048]{1,0:T(8,128)S(1)}, f32[16,2048]{1,0:T(8,128)S(1)}, f32[16,2048]{1,0:T(8,128)S(1)}, f32[16,2048]{1,0:T(8,128)S(1)}) custom-call(bf16[768,256]{1,0:T(8,128)(2,1)S(1)} %get-tuple-element.66.refs_0_, bf16[768,256]{1,0:T(8,128)(2,1)S(1)} %get-tuple-element.67.refs_1_, bf16[64,192]{1,0:T(8,128)(2,1)S(1)} %get-tuple-element.68.refs_2_, ...), custom_call_target="tpu_custom_call" | custom-call | flops 57500000256 | tf_op jit(solution)/shard_map/pallas_call | solution.py:565
  65.8 0.8 %collective-permute-start.30 = (f32[16,2048]{1,0:T(8,128)S(1)}, f32[16,2048]{1,0:T(8,128)S(1)}, u32[]{:S(2)}, u32[]{:S(2)}) collective-permute-start(f32[16,2048]{1,0:T(8,128)S(1)} %get-tuple-element.121), channel_id=1, source_target_pairs={{0,8},{8,0},{16,24},{24,16},{1,9},{9,1},{17,25},{25,17},{2,10},{10... | collective-permute-start | bytes 393224 | tf_op jit(solution)/shard_map/ppermute | solution.py:499
  66.6 0.8 collective-permute-done.21.refs_1_.refs_3_
  68.0 1.7 %collective-permute-done.22.refs_2_.refs_4_ = f32[16,2048]{1,0:T(8,128)S(1)} collective-permute-done((f32[16,2048]{1,0:T(8,128)S(1)}, f32[16,2048]{1,0:T(8,128)S(1)}, u32[]{:S(2)}, u32[]{:S(2)}) %collective-permute-start.22) | collective-permute-done | bytes 131104 | tf_op jit(solution)/shard_map/ppermute | solution.py:499
  69.9 6.1 %collective-permute-start.27 = (f32[32,2048]{1,0:T(8,128)S(1)}, f32[32,2048]{1,0:T(8,128)S(1)}, u32[]{:S(2)}, u32[]{:S(2)}) collective-permute-start(f32[32,2048]{1,0:T(8,128)S(1)} %get-tuple-element.116), channel_id=1, source_target_pairs={{1,2},{3,4},{5,6},{2,1},{4,3},{6,5},{9,10},{11,12},{13,14},{10,9},... | collective-permute-start | bytes 786440 | tf_op jit(solution)/shard_map/ppermute | solution.py:506
  76.6 3.4 %collective-permute-done.27.refs_1_ = f32[32,2048]{1,0:T(8,128)S(1)} collective-permute-done((f32[32,2048]{1,0:T(8,128)S(1)}, f32[32,2048]{1,0:T(8,128)S(1)}, u32[]{:S(2)}, u32[]{:S(2)}) %collective-permute-start.27) | collective-permute-done | bytes 262176 | tf_op jit(solution)/shard_map/ppermute | solution.py:506
  80.0 1.3 %shard_map.59 = f32[2048,128]{1,0:T(8,128)} custom-call(bf16[64,192]{1,0:T(8,128)(2,1)S(1)} %get-tuple-element.65.refs_0_, f32[32,2048]{1,0:T(8,128)S(1)} %collective-permute-done.27.refs_1_, f32[32,2048]{1,0:T(8,128)S(1)} %collective-permute-done.28.refs_2_, f32[64,2048]{1,0:T(8,128)S(1)} %get-tuple-element.123.refs_3_, ...), custom_call_target="tpu_custom_call" | custom-call | flops 1724999936 | tf_op jit(solution)/shard_map/pallas_call | solution.py:623
  (64 shorter events, 7.6 us)
Async XLA Ops:
  1.9 15.7 %collective-permute-start.5 = (f32[48,2048]{1,0:T(8,128)S(1)}, f32[48,2048]{1,0:T(8,128)S(1)}, u32[]{:S(2)}, u32[]{:S(2)}) collective-permute-start(f32[48,2048]{1,0:T(8,128)S(1)} %get-tuple-element.81), channel_id=1, source_target_pairs={{0,24},{8,16},{16,8},{24,0},{1,25},{9,17},{17,9},{25,1},{2,26},{10... | collective-permute-start | bytes 1179656 | tf_op jit(solution)/shard_map/ppermute | solution.py:499
  5.0 18.7 %collective-permute-start.6 = (f32[48,2048]{1,0:T(8,128)S(1)}, f32[48,2048]{1,0:T(8,128)S(1)}, u32[]{:S(2)}, u32[]{:S(2)}) collective-permute-start(f32[48,2048]{1,0:T(8,128)S(1)} %get-tuple-element.82), channel_id=1, source_target_pairs={{0,8},{8,0},{16,24},{24,16},{1,9},{9,1},{17,25},{25,17},{2,10},{10... | collective-permute-start | bytes 1179656 | tf_op jit(solution)/shard_map/ppermute | solution.py:499
  5.2 18.5 %collective-permute-start.7 = (f32[48,2048]{1,0:T(8,128)S(1)}, f32[48,2048]{1,0:T(8,128)S(1)}, u32[]{:S(2)}, u32[]{:S(2)}) collective-permute-start(f32[48,2048]{1,0:T(8,128)S(1)} %get-tuple-element.83), channel_id=1, source_target_pairs={{0,16},{8,24},{16,0},{24,8},{1,17},{9,25},{17,1},{25,9},{2,18},{10... | collective-permute-start | bytes 1179656 | tf_op jit(solution)/shard_map/ppermute | solution.py:499
  5.4 9.1 %collective-permute-start = (f32[32,2048]{1,0:T(8,128)S(1)}, f32[32,2048]{1,0:T(8,128)S(1)}, u32[]{:S(2)}, u32[]{:S(2)}) collective-permute-start(f32[32,2048]{1,0:T(8,128)S(1)} %get-tuple-element.74), channel_id=1, source_target_pairs={{1,2},{3,4},{5,6},{2,1},{4,3},{6,5},{9,10},{11,12},{13,14},{10,9},... | collective-permute-start | bytes 786440 | tf_op jit(solution)/shard_map/ppermute | solution.py:506
  10.1 4.3 %collective-permute-start.1 = (f32[32,2048]{1,0:T(8,128)S(1)}, f32[32,2048]{1,0:T(8,128)S(1)}, u32[]{:S(2)}, u32[]{:S(2)}) collective-permute-start(f32[32,2048]{1,0:T(8,128)S(1)} %get-tuple-element.75), channel_id=1, source_target_pairs={{0,1},{2,3},{4,5},{6,7},{1,0},{3,2},{5,4},{7,6},{8,9},{10,11},{12,... | collective-permute-start | bytes 786440 | tf_op jit(solution)/shard_map/ppermute | solution.py:506
  15.2 13.0 %collective-permute-start.2 = (f32[16,2048]{1,0:T(8,128)S(1)}, f32[16,2048]{1,0:T(8,128)S(1)}, u32[]{:S(2)}, u32[]{:S(2)}) collective-permute-start(f32[16,2048]{1,0:T(8,128)S(1)} %get-tuple-element.77), channel_id=1, source_target_pairs={{0,24},{8,16},{16,8},{24,0},{1,25},{9,17},{17,9},{25,1},{2,26},{10... | collective-permute-start | bytes 393224 | tf_op jit(solution)/shard_map/ppermute | solution.py:499
  17.4 11.2 %collective-permute-start.3 = (f32[16,2048]{1,0:T(8,128)S(1)}, f32[16,2048]{1,0:T(8,128)S(1)}, u32[]{:S(2)}, u32[]{:S(2)}) collective-permute-start(f32[16,2048]{1,0:T(8,128)S(1)} %get-tuple-element.78), channel_id=1, source_target_pairs={{0,8},{8,0},{16,24},{24,16},{1,9},{9,1},{17,25},{25,17},{2,10},{10... | collective-permute-start | bytes 393224 | tf_op jit(solution)/shard_map/ppermute | solution.py:499
  17.6 11.0 %collective-permute-start.4 = (f32[16,2048]{1,0:T(8,128)S(1)}, f32[16,2048]{1,0:T(8,128)S(1)}, u32[]{:S(2)}, u32[]{:S(2)}) collective-permute-start(f32[16,2048]{1,0:T(8,128)S(1)} %get-tuple-element.79), channel_id=1, source_target_pairs={{0,16},{8,24},{16,0},{24,8},{1,17},{9,25},{17,1},{25,9},{2,18},{10... | collective-permute-start | bytes 393224 | tf_op jit(solution)/shard_map/ppermute | solution.py:499
  25.2 7.6 %collective-permute-start.13 = (f32[16,2048]{1,0:T(8,128)S(1)}, f32[16,2048]{1,0:T(8,128)S(1)}, u32[]{:S(2)}, u32[]{:S(2)}) collective-permute-start(f32[16,2048]{1,0:T(8,128)S(1)} %get-tuple-element.93), channel_id=1, source_target_pairs={{0,24},{8,16},{16,8},{24,0},{1,25},{9,17},{17,9},{25,1},{2,26},{10... | collective-permute-start | bytes 393224 | tf_op jit(solution)/shard_map/ppermute | solution.py:499
  25.5 8.8 %collective-permute-start.14 = (f32[16,2048]{1,0:T(8,128)S(1)}, f32[16,2048]{1,0:T(8,128)S(1)}, u32[]{:S(2)}, u32[]{:S(2)}) collective-permute-start(f32[16,2048]{1,0:T(8,128)S(1)} %get-tuple-element.94), channel_id=1, source_target_pairs={{0,8},{8,0},{16,24},{24,16},{1,9},{9,1},{17,25},{25,17},{2,10},{10... | collective-permute-start | bytes 393224 | tf_op jit(solution)/shard_map/ppermute | solution.py:499
  28.2 6.1 %collective-permute-start.15 = (f32[16,2048]{1,0:T(8,128)S(1)}, f32[16,2048]{1,0:T(8,128)S(1)}, u32[]{:S(2)}, u32[]{:S(2)}) collective-permute-start(f32[16,2048]{1,0:T(8,128)S(1)} %get-tuple-element.95), channel_id=1, source_target_pairs={{0,16},{8,24},{16,0},{24,8},{1,17},{9,25},{17,1},{25,9},{2,18},{10... | collective-permute-start | bytes 393224 | tf_op jit(solution)/shard_map/ppermute | solution.py:499
  30.1 11.3 %collective-permute-start.8 = (f32[16,2048]{1,0:T(8,128)S(1)}, f32[16,2048]{1,0:T(8,128)S(1)}, u32[]{:S(2)}, u32[]{:S(2)}) collective-permute-start(f32[16,2048]{1,0:T(8,128)S(1)} %get-tuple-element.85), channel_id=1, source_target_pairs={{0,24},{8,16},{16,8},{24,0},{1,25},{9,17},{17,9},{25,1},{2,26},{10... | collective-permute-start | bytes 393224 | tf_op jit(solution)/shard_map/ppermute | solution.py:499
  31.0 10.4 %collective-permute-start.9 = (f32[16,2048]{1,0:T(8,128)S(1)}, f32[16,2048]{1,0:T(8,128)S(1)}, u32[]{:S(2)}, u32[]{:S(2)}) collective-permute-start(f32[16,2048]{1,0:T(8,128)S(1)} %get-tuple-element.86), channel_id=1, source_target_pairs={{0,8},{8,0},{16,24},{24,16},{1,9},{9,1},{17,25},{25,17},{2,10},{10... | collective-permute-start | bytes 393224 | tf_op jit(solution)/shard_map/ppermute | solution.py:499
  32.8 8.6 %collective-permute-start.10 = (f32[16,2048]{1,0:T(8,128)S(1)}, f32[16,2048]{1,0:T(8,128)S(1)}, u32[]{:S(2)}, u32[]{:S(2)}) collective-permute-start(f32[16,2048]{1,0:T(8,128)S(1)} %get-tuple-element.87), channel_id=1, source_target_pairs={{0,16},{8,24},{16,0},{24,8},{1,17},{9,25},{17,1},{25,9},{2,18},{10... | collective-permute-start | bytes 393224 | tf_op jit(solution)/shard_map/ppermute | solution.py:499
  34.4 11.0 %collective-permute-start.16 = (f32[32,2048]{1,0:T(8,128)S(1)}, f32[32,2048]{1,0:T(8,128)S(1)}, u32[]{:S(2)}, u32[]{:S(2)}) collective-permute-start(f32[32,2048]{1,0:T(8,128)S(1)} %get-tuple-element.96), channel_id=1, source_target_pairs={{1,2},{3,4},{5,6},{2,1},{4,3},{6,5},{9,10},{11,12},{13,14},{10,9},... | collective-permute-start | bytes 786440 | tf_op jit(solution)/shard_map/ppermute | solution.py:506
  41.3 4.0 %collective-permute-start.17 = (f32[32,2048]{1,0:T(8,128)S(1)}, f32[32,2048]{1,0:T(8,128)S(1)}, u32[]{:S(2)}, u32[]{:S(2)}) collective-permute-start(f32[32,2048]{1,0:T(8,128)S(1)} %get-tuple-element.97), channel_id=1, source_target_pairs={{0,1},{2,3},{4,5},{6,7},{1,0},{3,2},{5,4},{7,6},{8,9},{10,11},{12,... | collective-permute-start | bytes 786440 | tf_op jit(solution)/shard_map/ppermute | solution.py:506
  41.6 7.8 %collective-permute-start.11 = (f32[32,2048]{1,0:T(8,128)S(1)}, f32[32,2048]{1,0:T(8,128)S(1)}, u32[]{:S(2)}, u32[]{:S(2)}) collective-permute-start(f32[32,2048]{1,0:T(8,128)S(1)} %get-tuple-element.88), channel_id=1, source_target_pairs={{1,2},{3,4},{5,6},{2,1},{4,3},{6,5},{9,10},{11,12},{13,14},{10,9},... | collective-permute-start | bytes 786440 | tf_op jit(solution)/shard_map/ppermute | solution.py:506
  45.1 4.3 %collective-permute-start.12 = (f32[32,2048]{1,0:T(8,128)S(1)}, f32[32,2048]{1,0:T(8,128)S(1)}, u32[]{:S(2)}, u32[]{:S(2)}) collective-permute-start(f32[32,2048]{1,0:T(8,128)S(1)} %get-tuple-element.89), channel_id=1, source_target_pairs={{0,1},{2,3},{4,5},{6,7},{1,0},{3,2},{5,4},{7,6},{8,9},{10,11},{12,... | collective-permute-start | bytes 786440 | tf_op jit(solution)/shard_map/ppermute | solution.py:506
  50.6 6.5 %collective-permute-start.18 = (f32[16,2048]{1,0:T(8,128)S(1)}, f32[16,2048]{1,0:T(8,128)S(1)}, u32[]{:S(2)}, u32[]{:S(2)}) collective-permute-start(f32[16,2048]{1,0:T(8,128)S(1)} %get-tuple-element.102), channel_id=1, source_target_pairs={{0,24},{8,16},{16,8},{24,0},{1,25},{9,17},{17,9},{25,1},{2,26},{10... | collective-permute-start | bytes 393224 | tf_op jit(solution)/shard_map/ppermute | solution.py:499
  51.0 8.8 %collective-permute-start.19 = (f32[16,2048]{1,0:T(8,128)S(1)}, f32[16,2048]{1,0:T(8,128)S(1)}, u32[]{:S(2)}, u32[]{:S(2)}) collective-permute-start(f32[16,2048]{1,0:T(8,128)S(1)} %get-tuple-element.103), channel_id=1, source_target_pairs={{0,8},{8,0},{16,24},{24,16},{1,9},{9,1},{17,25},{25,17},{2,10},{10... | collective-permute-start | bytes 393224 | tf_op jit(solution)/shard_map/ppermute | solution.py:499
  52.1 7.7 %collective-permute-start.20 = (f32[16,2048]{1,0:T(8,128)S(1)}, f32[16,2048]{1,0:T(8,128)S(1)}, u32[]{:S(2)}, u32[]{:S(2)}) collective-permute-start(f32[16,2048]{1,0:T(8,128)S(1)} %get-tuple-element.104), channel_id=1, source_target_pairs={{0,16},{8,24},{16,0},{24,8},{1,17},{9,25},{17,1},{25,9},{2,18},{10... | collective-permute-start | bytes 393224 | tf_op jit(solution)/shard_map/ppermute | solution.py:499
  53.3 9.0 %collective-permute-start.24 = (f32[16,2048]{1,0:T(8,128)S(1)}, f32[16,2048]{1,0:T(8,128)S(1)}, u32[]{:S(2)}, u32[]{:S(2)}) collective-permute-start(f32[16,2048]{1,0:T(8,128)S(1)} %get-tuple-element.111), channel_id=1, source_target_pairs={{0,24},{8,16},{16,8},{24,0},{1,25},{9,17},{17,9},{25,1},{2,26},{10... | collective-permute-start | bytes 393224 | tf_op jit(solution)/shard_map/ppermute | solution.py:499
  53.8 10.2 %collective-permute-start.25 = (f32[16,2048]{1,0:T(8,128)S(1)}, f32[16,2048]{1,0:T(8,128)S(1)}, u32[]{:S(2)}, u32[]{:S(2)}) collective-permute-start(f32[16,2048]{1,0:T(8,128)S(1)} %get-tuple-element.112), channel_id=1, source_target_pairs={{0,8},{8,0},{16,24},{24,16},{1,9},{9,1},{17,25},{25,17},{2,10},{10... | collective-permute-start | bytes 393224 | tf_op jit(solution)/shard_map/ppermute | solution.py:499
  57.2 6.7 %collective-permute-start.26 = (f32[16,2048]{1,0:T(8,128)S(1)}, f32[16,2048]{1,0:T(8,128)S(1)}, u32[]{:S(2)}, u32[]{:S(2)}) collective-permute-start(f32[16,2048]{1,0:T(8,128)S(1)} %get-tuple-element.113), channel_id=1, source_target_pairs={{0,16},{8,24},{16,0},{24,8},{1,17},{9,25},{17,1},{25,9},{2,18},{10... | collective-permute-start | bytes 393224 | tf_op jit(solution)/shard_map/ppermute | solution.py:499
  61.2 6.2 %collective-permute-start.21 = (f32[16,2048]{1,0:T(8,128)S(1)}, f32[16,2048]{1,0:T(8,128)S(1)}, u32[]{:S(2)}, u32[]{:S(2)}) collective-permute-start(f32[16,2048]{1,0:T(8,128)S(1)} %get-tuple-element.107), channel_id=1, source_target_pairs={{0,24},{8,16},{16,8},{24,0},{1,25},{9,17},{17,9},{25,1},{2,26},{10... | collective-permute-start | bytes 393224 | tf_op jit(solution)/shard_map/ppermute | solution.py:499
  61.3 8.5 %collective-permute-start.22 = (f32[16,2048]{1,0:T(8,128)S(1)}, f32[16,2048]{1,0:T(8,128)S(1)}, u32[]{:S(2)}, u32[]{:S(2)}) collective-permute-start(f32[16,2048]{1,0:T(8,128)S(1)} %get-tuple-element.108), channel_id=1, source_target_pairs={{0,8},{8,0},{16,24},{24,16},{1,9},{9,1},{17,25},{25,17},{2,10},{10... | collective-permute-start | bytes 393224 | tf_op jit(solution)/shard_map/ppermute | solution.py:499
  62.4 7.4 %collective-permute-start.23 = (f32[16,2048]{1,0:T(8,128)S(1)}, f32[16,2048]{1,0:T(8,128)S(1)}, u32[]{:S(2)}, u32[]{:S(2)}) collective-permute-start(f32[16,2048]{1,0:T(8,128)S(1)} %get-tuple-element.109), channel_id=1, source_target_pairs={{0,16},{8,24},{16,0},{24,8},{1,17},{9,25},{17,1},{25,9},{2,18},{10... | collective-permute-start | bytes 393224 | tf_op jit(solution)/shard_map/ppermute | solution.py:499
  65.3 10.8 %collective-permute-start.29 = (f32[16,2048]{1,0:T(8,128)S(1)}, f32[16,2048]{1,0:T(8,128)S(1)}, u32[]{:S(2)}, u32[]{:S(2)}) collective-permute-start(f32[16,2048]{1,0:T(8,128)S(1)} %get-tuple-element.120), channel_id=1, source_target_pairs={{0,24},{8,16},{16,8},{24,0},{1,25},{9,17},{17,9},{25,1},{2,26},{10... | collective-permute-start | bytes 393224 | tf_op jit(solution)/shard_map/ppermute | solution.py:499
  65.8 10.3 %collective-permute-start.30 = (f32[16,2048]{1,0:T(8,128)S(1)}, f32[16,2048]{1,0:T(8,128)S(1)}, u32[]{:S(2)}, u32[]{:S(2)}) collective-permute-start(f32[16,2048]{1,0:T(8,128)S(1)} %get-tuple-element.121), channel_id=1, source_target_pairs={{0,8},{8,0},{16,24},{24,16},{1,9},{9,1},{17,25},{25,17},{2,10},{10... | collective-permute-start | bytes 393224 | tf_op jit(solution)/shard_map/ppermute | solution.py:499
  67.4 8.7 %collective-permute-start.31 = (f32[16,2048]{1,0:T(8,128)S(1)}, f32[16,2048]{1,0:T(8,128)S(1)}, u32[]{:S(2)}, u32[]{:S(2)}) collective-permute-start(f32[16,2048]{1,0:T(8,128)S(1)} %get-tuple-element.122), channel_id=1, source_target_pairs={{0,16},{8,24},{16,0},{24,8},{1,17},{9,25},{17,1},{25,9},{2,18},{10... | collective-permute-start | bytes 393224 | tf_op jit(solution)/shard_map/ppermute | solution.py:499
  69.9 10.1 %collective-permute-start.27 = (f32[32,2048]{1,0:T(8,128)S(1)}, f32[32,2048]{1,0:T(8,128)S(1)}, u32[]{:S(2)}, u32[]{:S(2)}) collective-permute-start(f32[32,2048]{1,0:T(8,128)S(1)} %get-tuple-element.116), channel_id=1, source_target_pairs={{1,2},{3,4},{5,6},{2,1},{4,3},{6,5},{9,10},{11,12},{13,14},{10,9},... | collective-permute-start | bytes 786440 | tf_op jit(solution)/shard_map/ppermute | solution.py:506
  76.0 4.0 %collective-permute-start.28 = (f32[32,2048]{1,0:T(8,128)S(1)}, f32[32,2048]{1,0:T(8,128)S(1)}, u32[]{:S(2)}, u32[]{:S(2)}) collective-permute-start(f32[32,2048]{1,0:T(8,128)S(1)} %get-tuple-element.117), channel_id=1, source_target_pairs={{0,1},{2,3},{4,5},{6,7},{1,0},{3,2},{5,4},{7,6},{8,9},{10,11},{12,... | collective-permute-start | bytes 786440 | tf_op jit(solution)/shard_map/ppermute | solution.py:506
  (9 other events, 28.1 us)

commit v5 on v4

--- a/solution.py
+++ b/solution.py
@@ -30,7 +30,7 @@
         in_specs=specs,
         out_specs=jax.tree.map(lambda _: place, outs),
         scratch_shapes=list(scratch),
-        compiler_params=pltpu.CompilerParams(vmem_limit_bytes=40 * 1024 * 1024),
+        compiler_params=pltpu.CompilerParams(vmem_limit_bytes=16 * 1024 * 1024),
         cost_estimate=pl.CostEstimate(flops=int(cost * RATE), bytes_accessed=0, transcendentals=0),
     )
 
@@ -153,6 +153,7 @@
     back_late_ref,
     ahead_early_ref,
     ahead_late_ref,
+    ahead_rest_ref,
     end_early_ref,
     end_late_ref,
     rows_ahead_ref,
@@ -167,12 +168,15 @@
     wide = columns + 2 * radius
     span = 2 * radius // len(parts)
     edges = [(0, 2 * radius), (wide - 2 * radius, 2 * radius)]
+    rest_rows = ahead_rest_ref.shape[0]
 
     ahead = banded(taps, columns, wide, 0)
     ahead = jnp.concatenate([ordered_rows(ahead, where, order_ref, runs, count) for runs in parts], axis=0)
     first_ref[...] = as_left(ahead[: size_of(parts[0])])
     ahead_early_ref[...] = as_left(ahead[:, 2 * radius : columns])
-    ahead_late_ref[...] = as_left(columns_of(ahead, edges))
+    ahead = columns_of(ahead, edges)
+    ahead_late_ref[...] = as_left(ahead[: size_of(parts[0])])
+    ahead_rest_ref[...] = as_left(ahead[-rest_rows:])
     back = banded(turned, wide, wide + 2 * radius, 0)
     late = [(2 * radius - span, span), (columns + 2 * radius, span)]
     early = [(0, 2 * radius - span), (2 * radius, columns), (columns + 2 * radius + span, 2 * radius - span)]
@@ -329,21 +333,38 @@
 
 
 def middle_late_kernel(parts, radius, count, where, back_ref, ahead_ref, *refs):
-    (other_ref, sibling_ref, outer_ref, inner_ref, result_ref), refs = refs[:5], refs[5:]
+    (other_ref, sibling_ref, outer_ref, result_ref), refs = refs[:4], refs[4:]
     seen_ref, seen_other_ref, seen_sibling_ref, estimate_ref, *part_refs = refs
     columns, length = seen_ref.shape
     wide = columns + 2 * radius
     edges = [(0, 2 * radius), (wide - 2 * radius, 2 * radius)]
     odd = where[2 * count] == 1
+    rows = size_of(parts[0])
     for at in range(0, length, STEP):
         here = slice(at, at + STEP)
         sides = assembled([], odd, [], [(other_ref, sibling_ref)], here)
         seen = assembled([[(0, columns)]], odd, [seen_ref], [(seen_other_ref, seen_sibling_ref)], here)
         outer = rows_of(seen, edges) * (outer_ref[:, here] + left_product(back_ref[...], sides))
+        estimate_ref[:, here] = outer
+        result = result_ref[:rows, here] + left_product(ahead_ref[...], outer)
+        place = 0
+        for part_ref in part_refs:
+            chunk = part_ref.shape[0]
+            part_ref[:, here] = result[place : place + chunk]
+            place += chunk
+
+
+def middle_rest_kernel(parts, radius, where, ahead_ref, outer_ref, inner_ref, result_ref, _, estimate_ref, *part_refs):
+    length = outer_ref.shape[1]
+    rows = size_of(parts[0])
+    for at in range(0, length, STEP):
+        here = slice(at, at + STEP)
+        outer = outer_ref[:, here]
         estimate_ref[:, here] = jnp.concatenate(
             [outer[radius : 2 * radius], inner_ref[:, here], outer[2 * radius : 3 * radius]], axis=0
         )
-        result = result_ref[:, here] + left_product(ahead_ref[...], outer)
+        if part_refs:
+            result = result_ref[rows:, here] + left_product(ahead_ref[...], outer)
         place = 0
         for part_ref in part_refs:
             chunk = part_ref.shape[0]
@@ -530,7 +551,7 @@
 
     span = 2 * radius // len(parts)
     across = LANES // rows * width
-    first, back_early, back_late, ahead_early, ahead_late, end_early, end_late, *weights = call(
+    first, back_early, back_late, ahead_early, ahead_late, ahead_rest, end_early, end_late, *weights = call(
         0.8,
         functools.partial(weights_kernel, sizes, parts),
         [
@@ -538,7 +559,8 @@
             left(columns + 2 * radius, columns + 4 * radius - 2 * span),
             left(4 * radius, 2 * span),
             left(columns, columns - 2 * radius),
-            left(columns, 4 * radius),
+            left(size_of(parts[0]), 4 * radius),
+            left(size_of(parts[-1]), 4 * radius),
             left(columns, columns),
             left(2 * radius, 2 * radius),
             right(beside * LANES, across),
@@ -601,14 +623,21 @@
         [VMEM] * (1 + (count + 2) * len(parts)),
         [pltpu.VMEM((size_of(runs), length), F32) for runs in parts],
     )(back_early, ahead_early, *flat(fields), *flat(sides[1:]), seen)
-    estimate, *parcels = call(
-        1.3,
+    estimate, *values = call(
+        0.8,
         functools.partial(middle_late_kernel, parts, radius, count),
-        [shaped(columns, length)] + [shaped(chunk, length) for chunk in chunks for _ in range(count)],
-        [VMEM] * 10,
-    )(back_late, ahead_late, *sides[0], *partial, seen, *seen_sides)
-    for k in range(len(parts)):
-        fields[k] = exchanged(parcels[k * count : (k + 1) * count])
+        [shaped(4 * radius, length)] + [shaped(chunks[0], length)] * count,
+        [VMEM] * 9,
+    )(back_late, ahead_late, *sides[0], partial[0], partial[2], seen, *seen_sides)
+    fields[0] = exchanged(values)
+    estimate, *values = call(
+        50,
+        functools.partial(middle_rest_kernel, parts, radius),
+        [shaped(columns, length)] + [shaped(chunk, length) for chunk in chunks[1:] for _ in range(count)],
+        [VMEM] * 5,
+    )(ahead_rest, estimate, *partial[1:], fields[0][0])
+    if len(parts) > 1:
+        fields[1] = exchanged(values)
     for k in range(len(parts)):
         values, _ = through_planes(fields[k], 0, chunks[k], across[k])
         fields[k] = exchanged(values)

time: 81.5 us -> 80.5 us (0.988)
  waiting for transfers between devices: 24.3 us -> 17.7 us
  starting transfers between devices: 41.8 us -> 46.1 us
    ppermute x24, waiting for transfers between devices: 15.6 us -> 9.37 us  [exchanged(): result.append(lax.ppermute(value, ('gz', 'bx'), pairs))]
    ppermute x24, starting transfers between devices: 20.3 us -> 25 us  [exchanged(): result.append(lax.ppermute(value, ('gz', 'bx'), pairs))]
    unnamed x18 -> x30, local copies, waits for them, and re-layouts: 0.86 us -> 1.66 us
  transfers between devices with their start and end apart: 32 -> 32, of which waited for: 12 -> 8; matrix products, arithmetic and copies ran while one was open for 0% -> 0% of each run, Pallas kernels for 12% -> 13%
where the time goes in v5:
time: 80.5 us; the launch traced here: 80.3 us
  starting transfers between devices  46.1 us (57%)
  waiting for transfers between devices  17.7 us (22%)
  Pallas kernels  14.4 us (18%)
  local copies, waits for them, and re-layouts  1.66 us (2%)
    ppermute x24, starting transfers between devices, exchanged(): result.append(lax.ppermute(value, ('gz', 'bx'), pairs))  25 us
    ppermute x8, starting transfers between devices, from_sides(): result.append(lax.ppermute(value, 'by', pairs + [(j, i) for i, j in pairs]))  21.1 us
    ppermute x24, waiting for transfers between devices, exchanged(): result.append(lax.ppermute(value, ('gz', 'bx'), pairs))  9.37 us
    ppermute x8, waiting for transfers between devices, from_sides(): result.append(lax.ppermute(value, 'by', pairs + [(j, i) for i, j in pairs]))  8.38 us
    pallas_call x4, Pallas kernels, through_planes(): call(50, functools.partial(planes_kernel, sizes, first, seen_first), [sha...  5.69 us
    pallas_call x1, Pallas kernels, per_device(): call(1.3, functools.partial(start_kernel, parts, radius, count), [shaped(...  1.92 us
    unnamed x30, local copies, waits for them, and re-layouts  1.66 us
  transfers between devices with their start and end apart: 32, of which 8 were waited for; matrix products, arithmetic and copies ran while one was open for 0% of the time, Pallas kernels for 13%

profile of v5, /device:TPU:1, one launch (start us, length us, event | category | flops | bytes accessed | tf_op | source)
XLA Modules:
  0.0 80.3 jit_solution(8663195752250704413)
XLA Ops:
  0.0 1.9 %shard_map.47 = (f32[128,2048]{1,0:T(8,128)S(1)}, f32[32,2048]{1,0:T(8,128)S(1)}, f32[32,2048]{1,0:T(8,128)S(1)}, f32[48,2048]{1,0:T(8,128)S(1)}, f32[48,2048]{1...) custom-call(f32[1,65]{1,0:T(1,128)} %bitcast.7, f32[2048,128]{1,0:T(8,128)} %bitcast.9), custom_call_target="tpu_custom_call" | custom-call | flops 1495000064 | tf_op jit(solution)/shard_map/pallas_call | solution.py:535
  1.9 3.1 %collective-permute-start.5 = (f32[48,2048]{1,0:T(8,128)S(1)}, f32[48,2048]{1,0:T(8,128)S(1)}, u32[]{:S(2)}, u32[]{:S(2)}) collective-permute-start(f32[48,2048]{1,0:T(8,128)S(1)} %get-tuple-element.83), channel_id=1, source_target_pairs={{0,24},{8,16},{16,8},{24,0},{1,25},{9,17},{17,9},{25,1},{2,26},{10... | collective-permute-start | bytes 1179656 | tf_op jit(solution)/shard_map/ppermute | solution.py:520
  5.4 4.7 %collective-permute-start = (f32[32,2048]{1,0:T(8,128)S(1)}, f32[32,2048]{1,0:T(8,128)S(1)}, u32[]{:S(2)}, u32[]{:S(2)}) collective-permute-start(f32[32,2048]{1,0:T(8,128)S(1)} %get-tuple-element.76), channel_id=1, source_target_pairs={{1,2},{3,4},{5,6},{2,1},{4,3},{6,5},{9,10},{11,12},{13,14},{10,9},... | collective-permute-start | bytes 786440 | tf_op jit(solution)/shard_map/ppermute | solution.py:527
  11.8 2.6 %collective-permute-done.refs_2_.refs_7_ = f32[32,2048]{1,0:T(8,128)S(1)} collective-permute-done((f32[32,2048]{1,0:T(8,128)S(1)}, f32[32,2048]{1,0:T(8,128)S(1)}, u32[]{:S(2)}, u32[]{:S(2)}) %collective-permute-start) | collective-permute-done | bytes 262176 | tf_op jit(solution)/shard_map/ppermute | solution.py:527
  15.2 2.2 %collective-permute-start.2 = (f32[16,2048]{1,0:T(8,128)S(1)}, f32[16,2048]{1,0:T(8,128)S(1)}, u32[]{:S(2)}, u32[]{:S(2)}) collective-permute-start(f32[16,2048]{1,0:T(8,128)S(1)} %get-tuple-element.79), channel_id=1, source_target_pairs={{0,24},{8,16},{16,8},{24,0},{1,25},{9,17},{17,9},{25,1},{2,26},{10... | collective-permute-start | bytes 393224 | tf_op jit(solution)/shard_map/ppermute | solution.py:520
  17.9 5.8 %collective-permute-done.6.refs_10_.refs_6_ = f32[48,2048]{1,0:T(8,128)S(1)} collective-permute-done((f32[48,2048]{1,0:T(8,128)S(1)}, f32[48,2048]{1,0:T(8,128)S(1)}, u32[]{:S(2)}, u32[]{:S(2)}) %collective-permute-start.6) | collective-permute-done | bytes 393248 | tf_op jit(solution)/shard_map/ppermute | solution.py:520
  23.7 1.5 %shard_map.51 = (f32[16,2048]{1,0:T(8,128)S(1)}, f32[16,2048]{1,0:T(8,128)S(1)}, f32[16,2048]{1,0:T(8,128)S(1)}, f32[16,2048]{1,0:T(8,128)S(1)}, f32[1,1024,128]{2,1,0:T(8,128)S(1)}) custom-call(bf16[768,256]{1,0:T(8,128)(2,1)S(1)} %get-tuple-element.68.refs_0_, bf16[768,256]{1,0:T(8,128)(2,1)S(1)} %get-tuple-element.69.refs_1_, ...), custom_call_target="tpu_custom_call" | custom-call | flops 57500000256 | tf_op jit(solution)/shard_map/pallas_call | solution.py:587
  25.5 2.7 %collective-permute-start.14 = (f32[16,2048]{1,0:T(8,128)S(1)}, f32[16,2048]{1,0:T(8,128)S(1)}, u32[]{:S(2)}, u32[]{:S(2)}) collective-permute-start(f32[16,2048]{1,0:T(8,128)S(1)} %get-tuple-element.96), channel_id=1, source_target_pairs={{0,8},{8,0},{16,24},{24,16},{1,9},{9,1},{17,25},{25,17},{2,10},{10... | collective-permute-start | bytes 393224 | tf_op jit(solution)/shard_map/ppermute | solution.py:520
  28.6 1.5 %shard_map.49 = (f32[16,2048]{1,0:T(8,128)S(1)}, f32[16,2048]{1,0:T(8,128)S(1)}, f32[16,2048]{1,0:T(8,128)S(1)}, f32[16,2048]{1,0:T(8,128)S(1)}, f32[1,1024,128]{2,1,0:T(8,128)S(1)}) custom-call(bf16[768,256]{1,0:T(8,128)(2,1)S(1)} %get-tuple-element.68.refs_0_, bf16[768,256]{1,0:T(8,128)(2,1)S(1)} %get-tuple-element.69.refs_1_, ...), custom_call_target="tpu_custom_call" | custom-call | flops 57500000256 | tf_op jit(solution)/shard_map/pallas_call | solution.py:587
  30.1 1.5 %collective-permute-start.10 = (f32[16,2048]{1,0:T(8,128)S(1)}, f32[16,2048]{1,0:T(8,128)S(1)}, u32[]{:S(2)}, u32[]{:S(2)}) collective-permute-start(f32[16,2048]{1,0:T(8,128)S(1)} %get-tuple-element.89), channel_id=1, source_target_pairs={{0,16},{8,24},{16,0},{24,8},{1,17},{9,25},{17,1},{25,9},{2,18},{10... | collective-permute-start | bytes 393224 | tf_op jit(solution)/shard_map/ppermute | solution.py:520
  31.6 1.2 %collective-permute-start.8 = (f32[16,2048]{1,0:T(8,128)S(1)}, f32[16,2048]{1,0:T(8,128)S(1)}, u32[]{:S(2)}, u32[]{:S(2)}) collective-permute-start(f32[16,2048]{1,0:T(8,128)S(1)} %get-tuple-element.87), channel_id=1, source_target_pairs={{0,24},{8,16},{16,8},{24,0},{1,25},{9,17},{17,9},{25,1},{2,26},{10... | collective-permute-start | bytes 393224 | tf_op jit(solution)/shard_map/ppermute | solution.py:520
  32.9 1.1 %collective-permute-done.14.refs_2_.refs_8_ = f32[16,2048]{1,0:T(8,128)S(1)} collective-permute-done((f32[16,2048]{1,0:T(8,128)S(1)}, f32[16,2048]{1,0:T(8,128)S(1)}, u32[]{:S(2)}, u32[]{:S(2)}) %collective-permute-start.14) | collective-permute-done | bytes 131104 | tf_op jit(solution)/shard_map/ppermute | solution.py:520
  34.1 5.8 %collective-permute-start.16 = (f32[32,2048]{1,0:T(8,128)S(1)}, f32[32,2048]{1,0:T(8,128)S(1)}, u32[]{:S(2)}, u32[]{:S(2)}) collective-permute-start(f32[32,2048]{1,0:T(8,128)S(1)} %get-tuple-element.98), channel_id=1, source_target_pairs={{1,2},{3,4},{5,6},{2,1},{4,3},{6,5},{9,10},{11,12},{13,14},{10,9},... | collective-permute-start | bytes 786440 | tf_op jit(solution)/shard_map/ppermute | solution.py:527
  40.2 5.0 %collective-permute-start.11 = (f32[32,2048]{1,0:T(8,128)S(1)}, f32[32,2048]{1,0:T(8,128)S(1)}, u32[]{:S(2)}, u32[]{:S(2)}) collective-permute-start(f32[32,2048]{1,0:T(8,128)S(1)} %get-tuple-element.90), channel_id=1, source_target_pairs={{1,2},{3,4},{5,6},{2,1},{4,3},{6,5},{9,10},{11,12},{13,14},{10,9},... | collective-permute-start | bytes 786440 | tf_op jit(solution)/shard_map/ppermute | solution.py:527
  45.3 1.5 %shard_map.53 = (f32[128,2048]{1,0:T(8,128)S(1)}, f32[64,2048]{1,0:T(8,128)S(1)}, f32[128,2048]{1,0:T(8,128)S(1)}) custom-call(bf16[192,576]{1,0:T(8,128)(2,1)S(1)} %get-tuple-element.92.refs_0_, bf16[128,192]{1,0:T(8,128)(2,1)S(1)} %get-tuple-element.93.refs_1_, f32[16,2048]{1,0:T(8,128)S(1)} %get-tuple-element.86.refs_0_.refs_4_.refs_2_, ...), custom_call_target="tpu_custom_call" | custom-call | flops 2529999872 | tf_op jit(solution)/shard_map/pallas_call | solution.py:619
  46.8 2.4 %collective-permute-done.11.refs_2_ = f32[32,2048]{1,0:T(8,128)S(1)} collective-permute-done((f32[32,2048]{1,0:T(8,128)S(1)}, f32[32,2048]{1,0:T(8,128)S(1)}, u32[]{:S(2)}, u32[]{:S(2)}) %collective-permute-start.11) | collective-permute-done | bytes 262176 | tf_op jit(solution)/shard_map/ppermute | solution.py:527
  49.2 1.1 %shard_map.54 = (f32[128,2048]{1,0:T(8,128)S(1)}, f32[16,2048]{1,0:T(8,128)S(1)}, f32[16,2048]{1,0:T(8,128)S(1)}, f32[16,2048]{1,0:T(8,128)S(1)}, f32[16,2048]{1,0:T(8,128)S(1)}) custom-call(bf16[128,192]{1,0:T(8,128)(2,1)S(1)} %get-tuple-element.72.refs_0_, bf16[64,384]{1,0:T(8,128)(2,1)S(1)} %get-tuple-element.73.refs_1_, ...), custom_call_target="tpu_custom_call" | custom-call | flops 920000000 | tf_op jit(solution)/shard_map/pallas_call | solution.py:626
  50.3 1.5 %collective-permute-start.18 = (f32[16,2048]{1,0:T(8,128)S(1)}, f32[16,2048]{1,0:T(8,128)S(1)}, u32[]{:S(2)}, u32[]{:S(2)}) collective-permute-start(f32[16,2048]{1,0:T(8,128)S(1)} %get-tuple-element.103), channel_id=1, source_target_pairs={{0,24},{8,16},{16,8},{24,0},{1,25},{9,17},{17,9},{25,1},{2,26},{10... | collective-permute-start | bytes 393224 | tf_op jit(solution)/shard_map/ppermute | solution.py:520
  51.8 1.0 %collective-permute-start.19 = (f32[16,2048]{1,0:T(8,128)S(1)}, f32[16,2048]{1,0:T(8,128)S(1)}, u32[]{:S(2)}, u32[]{:S(2)}) collective-permute-start(f32[16,2048]{1,0:T(8,128)S(1)} %get-tuple-element.104), channel_id=1, source_target_pairs={{0,8},{8,0},{16,24},{24,16},{1,9},{9,1},{17,25},{25,17},{2,10},{10... | collective-permute-start | bytes 393224 | tf_op jit(solution)/shard_map/ppermute | solution.py:520
  53.5 1.5 %collective-permute-start.24 = (f32[16,2048]{1,0:T(8,128)S(1)}, f32[16,2048]{1,0:T(8,128)S(1)}, u32[]{:S(2)}, u32[]{:S(2)}) collective-permute-start(f32[16,2048]{1,0:T(8,128)S(1)} %get-tuple-element.115), channel_id=1, source_target_pairs={{0,24},{8,16},{16,8},{24,0},{1,25},{9,17},{17,9},{25,1},{2,26},{10... | collective-permute-start | bytes 393224 | tf_op jit(solution)/shard_map/ppermute | solution.py:520
  55.0 1.0 %collective-permute-start.25 = (f32[16,2048]{1,0:T(8,128)S(1)}, f32[16,2048]{1,0:T(8,128)S(1)}, u32[]{:S(2)}, u32[]{:S(2)}) collective-permute-start(f32[16,2048]{1,0:T(8,128)S(1)} %get-tuple-element.116), channel_id=1, source_target_pairs={{0,8},{8,0},{16,24},{24,16},{1,9},{9,1},{17,25},{25,17},{2,10},{10... | collective-permute-start | bytes 393224 | tf_op jit(solution)/shard_map/ppermute | solution.py:520
  56.0 1.8 %collective-permute-start.26 = (f32[16,2048]{1,0:T(8,128)S(1)}, f32[16,2048]{1,0:T(8,128)S(1)}, u32[]{:S(2)}, u32[]{:S(2)}) collective-permute-start(f32[16,2048]{1,0:T(8,128)S(1)} %get-tuple-element.117), channel_id=1, source_target_pairs={{0,16},{8,24},{16,0},{24,8},{1,17},{9,25},{17,1},{25,9},{2,18},{10... | collective-permute-start | bytes 393224 | tf_op jit(solution)/shard_map/ppermute | solution.py:520
  57.8 1.1 %collective-permute-done.19.refs_6_ = f32[16,2048]{1,0:T(8,128)S(1)} collective-permute-done((f32[16,2048]{1,0:T(8,128)S(1)}, f32[16,2048]{1,0:T(8,128)S(1)}, u32[]{:S(2)}, u32[]{:S(2)}) %collective-permute-start.19) | collective-permute-done | bytes 131104 | tf_op jit(solution)/shard_map/ppermute | solution.py:520
  58.9 1.4 %shard_map.55 = (f32[16,2048]{1,0:T(8,128)S(1)}, f32[16,2048]{1,0:T(8,128)S(1)}, f32[16,2048]{1,0:T(8,128)S(1)}, f32[16,2048]{1,0:T(8,128)S(1)}) custom-call(bf16[768,256]{1,0:T(8,128)(2,1)S(1)} %copy-done.10, bf16[768,256]{1,0:T(8,128)(2,1)S(1)} %copy-done.12, bf16[64,192]{1,0:T(8,128)(2,1)S(1)} %get-tuple-element.70.refs_2_, ...), custom_call_target="tpu_custom_call" | custom-call | flops 57500000256 | tf_op jit(solution)/shard_map/pallas_call | solution.py:587
  60.2 2.1 %collective-permute-start.21 = (f32[16,2048]{1,0:T(8,128)S(1)}, f32[16,2048]{1,0:T(8,128)S(1)}, u32[]{:S(2)}, u32[]{:S(2)}) collective-permute-start(f32[16,2048]{1,0:T(8,128)S(1)} %get-tuple-element.108), channel_id=1, source_target_pairs={{0,24},{8,16},{16,8},{24,0},{1,25},{9,17},{17,9},{25,1},{2,26},{10... | collective-permute-start | bytes 393224 | tf_op jit(solution)/shard_map/ppermute | solution.py:520
  62.3 1.3 %collective-permute-start.22 = (f32[16,2048]{1,0:T(8,128)S(1)}, f32[16,2048]{1,0:T(8,128)S(1)}, u32[]{:S(2)}, u32[]{:S(2)}) collective-permute-start(f32[16,2048]{1,0:T(8,128)S(1)} %get-tuple-element.109), channel_id=1, source_target_pairs={{0,8},{8,0},{16,24},{24,16},{1,9},{9,1},{17,25},{25,17},{2,10},{10... | collective-permute-start | bytes 393224 | tf_op jit(solution)/shard_map/ppermute | solution.py:520
  64.5 1.4 %shard_map.57 = (f32[16,2048]{1,0:T(8,128)S(1)}, f32[16,2048]{1,0:T(8,128)S(1)}, f32[16,2048]{1,0:T(8,128)S(1)}, f32[16,2048]{1,0:T(8,128)S(1)}) custom-call(bf16[768,256]{1,0:T(8,128)(2,1)S(1)} %copy-done.10, bf16[768,256]{1,0:T(8,128)(2,1)S(1)} %copy-done.12, bf16[64,192]{1,0:T(8,128)(2,1)S(1)} %get-tuple-element.70.refs_2_, ...), custom_call_target="tpu_custom_call" | custom-call | flops 57500000256 | tf_op jit(solution)/shard_map/pallas_call | solution.py:587
  65.8 1.5 %collective-permute-start.29 = (f32[16,2048]{1,0:T(8,128)S(1)}, f32[16,2048]{1,0:T(8,128)S(1)}, u32[]{:S(2)}, u32[]{:S(2)}) collective-permute-start(f32[16,2048]{1,0:T(8,128)S(1)} %get-tuple-element.124), channel_id=1, source_target_pairs={{0,24},{8,16},{16,8},{24,0},{1,25},{9,17},{17,9},{25,1},{2,26},{10... | collective-permute-start | bytes 393224 | tf_op jit(solution)/shard_map/ppermute | solution.py:520
  67.3 1.2 %collective-permute-start.30 = (f32[16,2048]{1,0:T(8,128)S(1)}, f32[16,2048]{1,0:T(8,128)S(1)}, u32[]{:S(2)}, u32[]{:S(2)}) collective-permute-start(f32[16,2048]{1,0:T(8,128)S(1)} %get-tuple-element.125), channel_id=1, source_target_pairs={{0,8},{8,0},{16,24},{24,16},{1,9},{9,1},{17,25},{25,17},{2,10},{10... | collective-permute-start | bytes 393224 | tf_op jit(solution)/shard_map/ppermute | solution.py:520
  69.6 5.3 %collective-permute-start.27 = (f32[32,2048]{1,0:T(8,128)S(1)}, f32[32,2048]{1,0:T(8,128)S(1)}, u32[]{:S(2)}, u32[]{:S(2)}) collective-permute-start(f32[32,2048]{1,0:T(8,128)S(1)} %get-tuple-element.120), channel_id=1, source_target_pairs={{1,2},{3,4},{5,6},{2,1},{4,3},{6,5},{9,10},{11,12},{13,14},{10,9},... | collective-permute-start | bytes 786440 | tf_op jit(solution)/shard_map/ppermute | solution.py:527
  75.6 3.3 %collective-permute-done.27.refs_1_ = f32[32,2048]{1,0:T(8,128)S(1)} collective-permute-done((f32[32,2048]{1,0:T(8,128)S(1)}, f32[32,2048]{1,0:T(8,128)S(1)}, u32[]{:S(2)}, u32[]{:S(2)}) %collective-permute-start.27) | collective-permute-done | bytes 262176 | tf_op jit(solution)/shard_map/ppermute | solution.py:527
  79.0 1.3 %shard_map.60 = f32[2048,128]{1,0:T(8,128)} custom-call(bf16[64,192]{1,0:T(8,128)(2,1)S(1)} %get-tuple-element.67.refs_0_, f32[32,2048]{1,0:T(8,128)S(1)} %collective-permute-done.27.refs_1_, f32[32,2048]{1,0:T(8,128)S(1)} %collective-permute-done.28.refs_2_, f32[64,2048]{1,0:T(8,128)S(1)} %get-tuple-element.127.refs_3_, ...), custom_call_target="tpu_custom_call" | custom-call | flops 1724999936 | tf_op jit(solution)/shard_map/pallas_call | solution.py:652
  (77 shorter events, 7.7 us)
Async XLA Ops:
  1.9 15.7 %collective-permute-start.5 = (f32[48,2048]{1,0:T(8,128)S(1)}, f32[48,2048]{1,0:T(8,128)S(1)}, u32[]{:S(2)}, u32[]{:S(2)}) collective-permute-start(f32[48,2048]{1,0:T(8,128)S(1)} %get-tuple-element.83), channel_id=1, source_target_pairs={{0,24},{8,16},{16,8},{24,0},{1,25},{9,17},{17,9},{25,1},{2,26},{10... | collective-permute-start | bytes 1179656 | tf_op jit(solution)/shard_map/ppermute | solution.py:520
  5.0 18.7 %collective-permute-start.6 = (f32[48,2048]{1,0:T(8,128)S(1)}, f32[48,2048]{1,0:T(8,128)S(1)}, u32[]{:S(2)}, u32[]{:S(2)}) collective-permute-start(f32[48,2048]{1,0:T(8,128)S(1)} %get-tuple-element.84), channel_id=1, source_target_pairs={{0,8},{8,0},{16,24},{24,16},{1,9},{9,1},{17,25},{25,17},{2,10},{10... | collective-permute-start | bytes 1179656 | tf_op jit(solution)/shard_map/ppermute | solution.py:520
  5.2 18.5 %collective-permute-start.7 = (f32[48,2048]{1,0:T(8,128)S(1)}, f32[48,2048]{1,0:T(8,128)S(1)}, u32[]{:S(2)}, u32[]{:S(2)}) collective-permute-start(f32[48,2048]{1,0:T(8,128)S(1)} %get-tuple-element.85), channel_id=1, source_target_pairs={{0,16},{8,24},{16,0},{24,8},{1,17},{9,25},{17,1},{25,9},{2,18},{10... | collective-permute-start | bytes 1179656 | tf_op jit(solution)/shard_map/ppermute | solution.py:520
  5.4 9.1 %collective-permute-start = (f32[32,2048]{1,0:T(8,128)S(1)}, f32[32,2048]{1,0:T(8,128)S(1)}, u32[]{:S(2)}, u32[]{:S(2)}) collective-permute-start(f32[32,2048]{1,0:T(8,128)S(1)} %get-tuple-element.76), channel_id=1, source_target_pairs={{1,2},{3,4},{5,6},{2,1},{4,3},{6,5},{9,10},{11,12},{13,14},{10,9},... | collective-permute-start | bytes 786440 | tf_op jit(solution)/shard_map/ppermute | solution.py:527
  10.1 4.3 %collective-permute-start.1 = (f32[32,2048]{1,0:T(8,128)S(1)}, f32[32,2048]{1,0:T(8,128)S(1)}, u32[]{:S(2)}, u32[]{:S(2)}) collective-permute-start(f32[32,2048]{1,0:T(8,128)S(1)} %get-tuple-element.77), channel_id=1, source_target_pairs={{0,1},{2,3},{4,5},{6,7},{1,0},{3,2},{5,4},{7,6},{8,9},{10,11},{12,... | collective-permute-start | bytes 786440 | tf_op jit(solution)/shard_map/ppermute | solution.py:527
  15.2 12.9 %collective-permute-start.2 = (f32[16,2048]{1,0:T(8,128)S(1)}, f32[16,2048]{1,0:T(8,128)S(1)}, u32[]{:S(2)}, u32[]{:S(2)}) collective-permute-start(f32[16,2048]{1,0:T(8,128)S(1)} %get-tuple-element.79), channel_id=1, source_target_pairs={{0,24},{8,16},{16,8},{24,0},{1,25},{9,17},{17,9},{25,1},{2,26},{10... | collective-permute-start | bytes 393224 | tf_op jit(solution)/shard_map/ppermute | solution.py:520
  17.4 11.2 %collective-permute-start.3 = (f32[16,2048]{1,0:T(8,128)S(1)}, f32[16,2048]{1,0:T(8,128)S(1)}, u32[]{:S(2)}, u32[]{:S(2)}) collective-permute-start(f32[16,2048]{1,0:T(8,128)S(1)} %get-tuple-element.80), channel_id=1, source_target_pairs={{0,8},{8,0},{16,24},{24,16},{1,9},{9,1},{17,25},{25,17},{2,10},{10... | collective-permute-start | bytes 393224 | tf_op jit(solution)/shard_map/ppermute | solution.py:520
  17.6 11.0 %collective-permute-start.4 = (f32[16,2048]{1,0:T(8,128)S(1)}, f32[16,2048]{1,0:T(8,128)S(1)}, u32[]{:S(2)}, u32[]{:S(2)}) collective-permute-start(f32[16,2048]{1,0:T(8,128)S(1)} %get-tuple-element.81), channel_id=1, source_target_pairs={{0,16},{8,24},{16,0},{24,8},{1,17},{9,25},{17,1},{25,9},{2,18},{10... | collective-permute-start | bytes 393224 | tf_op jit(solution)/shard_map/ppermute | solution.py:520
  25.2 7.6 %collective-permute-start.13 = (f32[16,2048]{1,0:T(8,128)S(1)}, f32[16,2048]{1,0:T(8,128)S(1)}, u32[]{:S(2)}, u32[]{:S(2)}) collective-permute-start(f32[16,2048]{1,0:T(8,128)S(1)} %get-tuple-element.95), channel_id=1, source_target_pairs={{0,24},{8,16},{16,8},{24,0},{1,25},{9,17},{17,9},{25,1},{2,26},{10... | collective-permute-start | bytes 393224 | tf_op jit(solution)/shard_map/ppermute | solution.py:520
  25.5 8.4 %collective-permute-start.14 = (f32[16,2048]{1,0:T(8,128)S(1)}, f32[16,2048]{1,0:T(8,128)S(1)}, u32[]{:S(2)}, u32[]{:S(2)}) collective-permute-start(f32[16,2048]{1,0:T(8,128)S(1)} %get-tuple-element.96), channel_id=1, source_target_pairs={{0,8},{8,0},{16,24},{24,16},{1,9},{9,1},{17,25},{25,17},{2,10},{10... | collective-permute-start | bytes 393224 | tf_op jit(solution)/shard_map/ppermute | solution.py:520
  28.2 5.8 %collective-permute-start.15 = (f32[16,2048]{1,0:T(8,128)S(1)}, f32[16,2048]{1,0:T(8,128)S(1)}, u32[]{:S(2)}, u32[]{:S(2)}) collective-permute-start(f32[16,2048]{1,0:T(8,128)S(1)} %get-tuple-element.97), channel_id=1, source_target_pairs={{0,16},{8,24},{16,0},{24,8},{1,17},{9,25},{17,1},{25,9},{2,18},{10... | collective-permute-start | bytes 393224 | tf_op jit(solution)/shard_map/ppermute | solution.py:520
  30.1 9.8 %collective-permute-start.10 = (f32[16,2048]{1,0:T(8,128)S(1)}, f32[16,2048]{1,0:T(8,128)S(1)}, u32[]{:S(2)}, u32[]{:S(2)}) collective-permute-start(f32[16,2048]{1,0:T(8,128)S(1)} %get-tuple-element.89), channel_id=1, source_target_pairs={{0,16},{8,24},{16,0},{24,8},{1,17},{9,25},{17,1},{25,9},{2,18},{10... | collective-permute-start | bytes 393224 | tf_op jit(solution)/shard_map/ppermute | solution.py:520
  31.6 8.4 %collective-permute-start.8 = (f32[16,2048]{1,0:T(8,128)S(1)}, f32[16,2048]{1,0:T(8,128)S(1)}, u32[]{:S(2)}, u32[]{:S(2)}) collective-permute-start(f32[16,2048]{1,0:T(8,128)S(1)} %get-tuple-element.87), channel_id=1, source_target_pairs={{0,24},{8,16},{16,8},{24,0},{1,25},{9,17},{17,9},{25,1},{2,26},{10... | collective-permute-start | bytes 393224 | tf_op jit(solution)/shard_map/ppermute | solution.py:520
  32.8 7.2 %collective-permute-start.9 = (f32[16,2048]{1,0:T(8,128)S(1)}, f32[16,2048]{1,0:T(8,128)S(1)}, u32[]{:S(2)}, u32[]{:S(2)}) collective-permute-start(f32[16,2048]{1,0:T(8,128)S(1)} %get-tuple-element.88), channel_id=1, source_target_pairs={{0,8},{8,0},{16,24},{24,16},{1,9},{9,1},{17,25},{25,17},{2,10},{10... | collective-permute-start | bytes 393224 | tf_op jit(solution)/shard_map/ppermute | solution.py:520
  34.1 11.2 %collective-permute-start.16 = (f32[32,2048]{1,0:T(8,128)S(1)}, f32[32,2048]{1,0:T(8,128)S(1)}, u32[]{:S(2)}, u32[]{:S(2)}) collective-permute-start(f32[32,2048]{1,0:T(8,128)S(1)} %get-tuple-element.98), channel_id=1, source_target_pairs={{1,2},{3,4},{5,6},{2,1},{4,3},{6,5},{9,10},{11,12},{13,14},{10,9},... | collective-permute-start | bytes 786440 | tf_op jit(solution)/shard_map/ppermute | solution.py:527
  39.9 5.3 %collective-permute-start.17 = (f32[32,2048]{1,0:T(8,128)S(1)}, f32[32,2048]{1,0:T(8,128)S(1)}, u32[]{:S(2)}, u32[]{:S(2)}) collective-permute-start(f32[32,2048]{1,0:T(8,128)S(1)} %get-tuple-element.99), channel_id=1, source_target_pairs={{0,1},{2,3},{4,5},{6,7},{1,0},{3,2},{5,4},{7,6},{8,9},{10,11},{12,... | collective-permute-start | bytes 786440 | tf_op jit(solution)/shard_map/ppermute | solution.py:527
  40.2 9.0 %collective-permute-start.11 = (f32[32,2048]{1,0:T(8,128)S(1)}, f32[32,2048]{1,0:T(8,128)S(1)}, u32[]{:S(2)}, u32[]{:S(2)}) collective-permute-start(f32[32,2048]{1,0:T(8,128)S(1)} %get-tuple-element.90), channel_id=1, source_target_pairs={{1,2},{3,4},{5,6},{2,1},{4,3},{6,5},{9,10},{11,12},{13,14},{10,9},... | collective-permute-start | bytes 786440 | tf_op jit(solution)/shard_map/ppermute | solution.py:527
  45.1 4.0 %collective-permute-start.12 = (f32[32,2048]{1,0:T(8,128)S(1)}, f32[32,2048]{1,0:T(8,128)S(1)}, u32[]{:S(2)}, u32[]{:S(2)}) collective-permute-start(f32[32,2048]{1,0:T(8,128)S(1)} %get-tuple-element.91), channel_id=1, source_target_pairs={{0,1},{2,3},{4,5},{6,7},{1,0},{3,2},{5,4},{7,6},{8,9},{10,11},{12,... | collective-permute-start | bytes 786440 | tf_op jit(solution)/shard_map/ppermute | solution.py:527
  50.3 5.7 %collective-permute-start.18 = (f32[16,2048]{1,0:T(8,128)S(1)}, f32[16,2048]{1,0:T(8,128)S(1)}, u32[]{:S(2)}, u32[]{:S(2)}) collective-permute-start(f32[16,2048]{1,0:T(8,128)S(1)} %get-tuple-element.103), channel_id=1, source_target_pairs={{0,24},{8,16},{16,8},{24,0},{1,25},{9,17},{17,9},{25,1},{2,26},{10... | collective-permute-start | bytes 393224 | tf_op jit(solution)/shard_map/ppermute | solution.py:520
  51.8 7.1 %collective-permute-start.19 = (f32[16,2048]{1,0:T(8,128)S(1)}, f32[16,2048]{1,0:T(8,128)S(1)}, u32[]{:S(2)}, u32[]{:S(2)}) collective-permute-start(f32[16,2048]{1,0:T(8,128)S(1)} %get-tuple-element.104), channel_id=1, source_target_pairs={{0,8},{8,0},{16,24},{24,16},{1,9},{9,1},{17,25},{25,17},{2,10},{10... | collective-permute-start | bytes 393224 | tf_op jit(solution)/shard_map/ppermute | solution.py:520
  52.8 6.0 %collective-permute-start.20 = (f32[16,2048]{1,0:T(8,128)S(1)}, f32[16,2048]{1,0:T(8,128)S(1)}, u32[]{:S(2)}, u32[]{:S(2)}) collective-permute-start(f32[16,2048]{1,0:T(8,128)S(1)} %get-tuple-element.105), channel_id=1, source_target_pairs={{0,16},{8,24},{16,0},{24,8},{1,17},{9,25},{17,1},{25,9},{2,18},{10... | collective-permute-start | bytes 393224 | tf_op jit(solution)/shard_map/ppermute | solution.py:520
  53.5 10.2 %collective-permute-start.24 = (f32[16,2048]{1,0:T(8,128)S(1)}, f32[16,2048]{1,0:T(8,128)S(1)}, u32[]{:S(2)}, u32[]{:S(2)}) collective-permute-start(f32[16,2048]{1,0:T(8,128)S(1)} %get-tuple-element.115), channel_id=1, source_target_pairs={{0,24},{8,16},{16,8},{24,0},{1,25},{9,17},{17,9},{25,1},{2,26},{10... | collective-permute-start | bytes 393224 | tf_op jit(solution)/shard_map/ppermute | solution.py:520
  55.0 8.7 %collective-permute-start.25 = (f32[16,2048]{1,0:T(8,128)S(1)}, f32[16,2048]{1,0:T(8,128)S(1)}, u32[]{:S(2)}, u32[]{:S(2)}) collective-permute-start(f32[16,2048]{1,0:T(8,128)S(1)} %get-tuple-element.116), channel_id=1, source_target_pairs={{0,8},{8,0},{16,24},{24,16},{1,9},{9,1},{17,25},{25,17},{2,10},{10... | collective-permute-start | bytes 393224 | tf_op jit(solution)/shard_map/ppermute | solution.py:520
  56.0 7.7 %collective-permute-start.26 = (f32[16,2048]{1,0:T(8,128)S(1)}, f32[16,2048]{1,0:T(8,128)S(1)}, u32[]{:S(2)}, u32[]{:S(2)}) collective-permute-start(f32[16,2048]{1,0:T(8,128)S(1)} %get-tuple-element.117), channel_id=1, source_target_pairs={{0,16},{8,24},{16,0},{24,8},{1,17},{9,25},{17,1},{25,9},{2,18},{10... | collective-permute-start | bytes 393224 | tf_op jit(solution)/shard_map/ppermute | solution.py:520
  60.2 8.3 %collective-permute-start.21 = (f32[16,2048]{1,0:T(8,128)S(1)}, f32[16,2048]{1,0:T(8,128)S(1)}, u32[]{:S(2)}, u32[]{:S(2)}) collective-permute-start(f32[16,2048]{1,0:T(8,128)S(1)} %get-tuple-element.108), channel_id=1, source_target_pairs={{0,24},{8,16},{16,8},{24,0},{1,25},{9,17},{17,9},{25,1},{2,26},{10... | collective-permute-start | bytes 393224 | tf_op jit(solution)/shard_map/ppermute | solution.py:520
  62.3 7.1 %collective-permute-start.22 = (f32[16,2048]{1,0:T(8,128)S(1)}, f32[16,2048]{1,0:T(8,128)S(1)}, u32[]{:S(2)}, u32[]{:S(2)}) collective-permute-start(f32[16,2048]{1,0:T(8,128)S(1)} %get-tuple-element.109), channel_id=1, source_target_pairs={{0,8},{8,0},{16,24},{24,16},{1,9},{9,1},{17,25},{25,17},{2,10},{10... | collective-permute-start | bytes 393224 | tf_op jit(solution)/shard_map/ppermute | solution.py:520
  63.6 5.8 %collective-permute-start.23 = (f32[16,2048]{1,0:T(8,128)S(1)}, f32[16,2048]{1,0:T(8,128)S(1)}, u32[]{:S(2)}, u32[]{:S(2)}) collective-permute-start(f32[16,2048]{1,0:T(8,128)S(1)} %get-tuple-element.110), channel_id=1, source_target_pairs={{0,16},{8,24},{16,0},{24,8},{1,17},{9,25},{17,1},{25,9},{2,18},{10... | collective-permute-start | bytes 393224 | tf_op jit(solution)/shard_map/ppermute | solution.py:520
  65.8 9.2 %collective-permute-start.29 = (f32[16,2048]{1,0:T(8,128)S(1)}, f32[16,2048]{1,0:T(8,128)S(1)}, u32[]{:S(2)}, u32[]{:S(2)}) collective-permute-start(f32[16,2048]{1,0:T(8,128)S(1)} %get-tuple-element.124), channel_id=1, source_target_pairs={{0,24},{8,16},{16,8},{24,0},{1,25},{9,17},{17,9},{25,1},{2,26},{10... | collective-permute-start | bytes 393224 | tf_op jit(solution)/shard_map/ppermute | solution.py:520
  67.3 7.7 %collective-permute-start.30 = (f32[16,2048]{1,0:T(8,128)S(1)}, f32[16,2048]{1,0:T(8,128)S(1)}, u32[]{:S(2)}, u32[]{:S(2)}) collective-permute-start(f32[16,2048]{1,0:T(8,128)S(1)} %get-tuple-element.125), channel_id=1, source_target_pairs={{0,8},{8,0},{16,24},{24,16},{1,9},{9,1},{17,25},{25,17},{2,10},{10... | collective-permute-start | bytes 393224 | tf_op jit(solution)/shard_map/ppermute | solution.py:520
  68.5 6.6 %collective-permute-start.31 = (f32[16,2048]{1,0:T(8,128)S(1)}, f32[16,2048]{1,0:T(8,128)S(1)}, u32[]{:S(2)}, u32[]{:S(2)}) collective-permute-start(f32[16,2048]{1,0:T(8,128)S(1)} %get-tuple-element.126), channel_id=1, source_target_pairs={{0,16},{8,24},{16,0},{24,8},{1,17},{9,25},{17,1},{25,9},{2,18},{10... | collective-permute-start | bytes 393224 | tf_op jit(solution)/shard_map/ppermute | solution.py:520
  69.6 9.4 %collective-permute-start.27 = (f32[32,2048]{1,0:T(8,128)S(1)}, f32[32,2048]{1,0:T(8,128)S(1)}, u32[]{:S(2)}, u32[]{:S(2)}) collective-permute-start(f32[32,2048]{1,0:T(8,128)S(1)} %get-tuple-element.120), channel_id=1, source_target_pairs={{1,2},{3,4},{5,6},{2,1},{4,3},{6,5},{9,10},{11,12},{13,14},{10,9},... | collective-permute-start | bytes 786440 | tf_op jit(solution)/shard_map/ppermute | solution.py:527
  74.9 4.0 %collective-permute-start.28 = (f32[32,2048]{1,0:T(8,128)S(1)}, f32[32,2048]{1,0:T(8,128)S(1)}, u32[]{:S(2)}, u32[]{:S(2)}) collective-permute-start(f32[32,2048]{1,0:T(8,128)S(1)} %get-tuple-element.121), channel_id=1, source_target_pairs={{0,1},{2,3},{4,5},{6,7},{1,0},{3,2},{5,4},{7,6},{8,9},{10,11},{12,... | collective-permute-start | bytes 786440 | tf_op jit(solution)/shard_map/ppermute | solution.py:527
  (15 other events, 122.5 us)

commit v6 on v5

--- a/solution.py
+++ b/solution.py
@@ -77,7 +77,10 @@
     behind = [
         lax.rem(me_z + groups - dz, groups) * beside + lax.rem(me_x + beside - dx, beside) for dz, dx in offsets
     ]
-    return ahead + behind + [lax.rem(lax.axis_index("by"), 2), me_z, me_x]
+    me_y, odd = lax.axis_index("by"), lax.rem(lax.axis_index("by"), 2)
+    other = me_y + 2 * odd - 1
+    alone = jnp.where((other < 0) | (other >= lax.axis_size("by")), 1, 0)
+    return ahead + behind + [odd, me_z, me_x, alone]
 
 
 def split(value):
@@ -262,7 +265,7 @@
     columns, length = own_ref.shape
     count = len(part_refs)
     chunk = part_refs[0].shape[0]
-    odd = where[2 * count] == 1
+    odd = where[2 * count] == 1, where[2 * count + 3] == 1
     for at in range(0, length, STEP):
         here = slice(at, at + STEP)
         field = assembled([[(0, columns)]], odd, [own_ref], [(other_ref, sibling_ref)], here)
@@ -305,8 +308,9 @@
             at += size
     own = [pieces[start] for start in sorted(pieces)]
     low, high = [], []
+    odd, alone = odd or (None, None)
     for other_ref, sibling_ref in side_refs:
-        sibling, other = sibling_ref[:, here], other_ref[:, here]
+        sibling, other = sibling_ref[:, here], jnp.where(alone, 0.0, other_ref[:, here])
         low.insert(0, jnp.where(odd, sibling, other))
         high.append(jnp.where(odd, other, sibling))
     return jnp.concatenate(low + own + high, axis=0)
@@ -322,7 +326,7 @@
     columns, length = seen_ref.shape
     wide = columns + 2 * radius
     edges = [(0, 2 * radius), (wide - 2 * radius, 2 * radius)]
-    odd = where[2 * count] == 1
+    odd = where[2 * count] == 1, where[2 * count + 3] == 1
     for at in range(0, length, STEP):
         here = slice(at, at + STEP)
         blurred = left_product(back_ref[...], assembled(parts, odd, own_refs, side_refs, here))
@@ -338,7 +342,7 @@
     columns, length = seen_ref.shape
     wide = columns + 2 * radius
     edges = [(0, 2 * radius), (wide - 2 * radius, 2 * radius)]
-    odd = where[2 * count] == 1
+    odd = where[2 * count] == 1, where[2 * count + 3] == 1
     rows = size_of(parts[0])
     for at in range(0, length, STEP):
         here = slice(at, at + STEP)
@@ -388,7 +392,7 @@
     radius, count, where, back_ref, other_ref, sibling_ref, outer_ref, inner_ref, estimate_ref, out_hbm, out_ref, sems
 ):
     columns, length = estimate_ref.shape
-    odd = where[2 * count] == 1
+    odd = where[2 * count] == 1, where[2 * count + 3] == 1
     edges = [(0, radius), (columns - radius, radius)]
     pieces = sems.shape[0]
     piece = length // pieces
@@ -520,11 +524,17 @@
             result.append(lax.ppermute(value, ("gz", "bx"), pairs))
         return result
 
-    def from_sides(sibling, other):
+    def from_sides(sibling, other, paced=False):
         result = []
         for value, first in ((other, 1), (sibling, 0)):
-            pairs = [(i, i + 1) for i in range(first, along - 1, 2)]
-            result.append(lax.ppermute(value, "by", pairs + [(j, i) for i, j in pairs]))
+            pairs = []
+            for place in range(count):
+                line = [place * along + i for i in range(along)]
+                pairs += [(line[i], line[i + 1]) for i in range(first, along - 1, 2)]
+                if paced and first and place + beside < count and place // beside % 2 == 0:
+                    ends = [0] + [along - 1] * (along % 2 == 0)
+                    pairs += [(line[i], line[i] + beside * along) for i in ends]
+            result.append(lax.ppermute(value, ("gz", "bx", "by"), pairs + [(j, i) for i, j in pairs]))
         return result
 
     line = (1, psf_z.shape[0])
@@ -597,14 +607,14 @@
         )(*weights, *values, *seen_values)
         return result[:count], result[count:] if begins else seen_values
 
-    def sides_of(cost, values, span, after):
+    def sides_of(cost, values, span, after, paced=False):
         sides = call(
             cost,
             functools.partial(sides_kernel, count),
             [shaped(span, length)] * 2,
             [VMEM] * (count + 1),
         )(*values, after)
-        return from_sides(*sides)
+        return from_sides(*sides, paced)
 
     fields, across, sides = ([None] * len(parts) for _ in range(3))
     before = 0
@@ -614,7 +624,7 @@
         fields[k] = exchanged(fields[k])
         before += chunks[k] * (2 if k else 1)
     for k in reversed(range(len(parts))):
-        sides[k] = sides_of(50, fields[k], span, fields[0][0])
+        sides[k] = sides_of(50, fields[k], span, fields[0][0], k == 0)
     partial = [shaped(4 * radius, length), shaped(columns - 2 * radius, length), shaped(columns, length)]
     partial = call(
         2.2,

time: 80.5 us -> 78.7 us (0.978)
  starting transfers between devices: 46.1 us -> 42.2 us
  waiting for transfers between devices: 17.7 us -> 19.8 us
    ppermute x8, starting transfers between devices: 21.1 us -> 18.7 us  [from_sides(): lax.ppermute(value, ('gz', 'bx', 'by'), pairs + [(j, i) for i, j in pairs])]
    ppermute x24, waiting for transfers between devices: 9.37 us -> 11.8 us  [exchanged(): result.append(lax.ppermute(value, ('gz', 'bx'), pairs))]
    ppermute x24, starting transfers between devices: 25 us -> 23.5 us  [exchanged(): result.append(lax.ppermute(value, ('gz', 'bx'), pairs))]
  transfers between devices with their start and end apart: 32 -> 32, of which waited for: 8 -> 10; matrix products, arithmetic and copies ran while one was open for 0% -> 0% of each run, Pallas kernels for 13% -> 13%
where the time goes in v6:
time: 78.7 us; the launch traced here: 78.5 us
  starting transfers between devices  42.2 us (54%)
  waiting for transfers between devices  19.8 us (25%)
  Pallas kernels  14.4 us (18%)
  local copies, waits for them, and re-layouts  1.64 us (2%)
    ppermute x24, starting transfers between devices, exchanged(): result.append(lax.ppermute(value, ('gz', 'bx'), pairs))  23.5 us
    ppermute x8, starting transfers between devices, from_sides(): lax.ppermute(value, ('gz', 'bx', 'by'), pairs + [(j, i) for i, j in pairs])  18.7 us
    ppermute x24, waiting for transfers between devices, exchanged(): result.append(lax.ppermute(value, ('gz', 'bx'), pairs))  11.8 us
    ppermute x8, waiting for transfers between devices, from_sides(): lax.ppermute(value, ('gz', 'bx', 'by'), pairs + [(j, i) for i, j in pairs])  8.06 us
    pallas_call x4, Pallas kernels, through_planes(): call(50, functools.partial(planes_kernel, sizes, first, seen_first), [sha...  5.69 us
    pallas_call x1, Pallas kernels, per_device(): call(1.3, functools.partial(start_kernel, parts, radius, count), [shaped(...  1.92 us
    unnamed x30, local copies, waits for them, and re-layouts  1.64 us
  transfers between devices with their start and end apart: 32, of which 10 were waited for; matrix products, arithmetic and copies ran while one was open for 0% of the time, Pallas kernels for 13%

profile of v6, /device:TPU:1, one launch (start us, length us, event | category | flops | bytes accessed | tf_op | source)
XLA Modules:
  0.0 78.5 jit_solution(15486560183180775463)
XLA Ops:
  0.0 1.9 %shard_map.47 = (f32[128,2048]{1,0:T(8,128)S(1)}, f32[32,2048]{1,0:T(8,128)S(1)}, f32[32,2048]{1,0:T(8,128)S(1)}, f32[48,2048]{1,0:T(8,128)S(1)}, f32[48,2048]{1...) custom-call(f32[1,65]{1,0:T(1,128)} %bitcast.7, f32[2048,128]{1,0:T(8,128)} %bitcast.9), custom_call_target="tpu_custom_call" | custom-call | flops 1495000064 | tf_op jit(solution)/shard_map/pallas_call | solution.py:545
  1.9 3.1 %collective-permute-start.5 = (f32[48,2048]{1,0:T(8,128)S(1)}, f32[48,2048]{1,0:T(8,128)S(1)}, u32[]{:S(2)}, u32[]{:S(2)}) collective-permute-start(f32[48,2048]{1,0:T(8,128)S(1)} %get-tuple-element.83), channel_id=1, source_target_pairs={{0,24},{8,16},{16,8},{24,0},{1,25},{9,17},{17,9},{25,1},{2,26},{10... | collective-permute-start | bytes 1179656 | tf_op jit(solution)/shard_map/ppermute | solution.py:524
  5.4 4.7 %collective-permute-start = (f32[32,2048]{1,0:T(8,128)S(1)}, f32[32,2048]{1,0:T(8,128)S(1)}, u32[]{:S(2)}, u32[]{:S(2)}) collective-permute-start(f32[32,2048]{1,0:T(8,128)S(1)} %get-tuple-element.76), channel_id=1, source_target_pairs={{1,2},{3,4},{5,6},{9,10},{11,12},{13,14},{17,18},{19,20},{21,22},{... | collective-permute-start | bytes 786440 | tf_op jit(solution)/shard_map/ppermute | solution.py:537
  10.9 0.9 %shard_map.46 = (bf16[64,576]{1,0:T(8,128)(2,1)S(1)}, bf16[192,576]{1,0:T(8,128)(2,1)S(1)}, bf16[128,192]{1,0:T(8,128)(2,1)S(1)}, bf16[128,192]{1,0:T(8,128)(2,1...) custom-call(f32[1,65]{1,0:T(1,128)S(1)} %bitcast.5, ...), custom_call_target="tpu_custom_call" | custom-call | flops 920000000 | tf_op jit(solution)/shard_map/pallas_call | solution.py:564
  11.8 2.6 %collective-permute-done.refs_2_.refs_7_ = f32[32,2048]{1,0:T(8,128)S(1)} collective-permute-done((f32[32,2048]{1,0:T(8,128)S(1)}, f32[32,2048]{1,0:T(8,128)S(1)}, u32[]{:S(2)}, u32[]{:S(2)}) %collective-permute-start) | collective-permute-done | bytes 262176 | tf_op jit(solution)/shard_map/ppermute | solution.py:537
  15.2 2.2 %collective-permute-start.2 = (f32[16,2048]{1,0:T(8,128)S(1)}, f32[16,2048]{1,0:T(8,128)S(1)}, u32[]{:S(2)}, u32[]{:S(2)}) collective-permute-start(f32[16,2048]{1,0:T(8,128)S(1)} %get-tuple-element.79), channel_id=1, source_target_pairs={{0,24},{8,16},{16,8},{24,0},{1,25},{9,17},{17,9},{25,1},{2,26},{10... | collective-permute-start | bytes 393224 | tf_op jit(solution)/shard_map/ppermute | solution.py:524
  17.9 5.8 %collective-permute-done.6.refs_10_.refs_6_ = f32[48,2048]{1,0:T(8,128)S(1)} collective-permute-done((f32[48,2048]{1,0:T(8,128)S(1)}, f32[48,2048]{1,0:T(8,128)S(1)}, u32[]{:S(2)}, u32[]{:S(2)}) %collective-permute-start.6) | collective-permute-done | bytes 393248 | tf_op jit(solution)/shard_map/ppermute | solution.py:524
  23.7 1.5 %shard_map.51 = (f32[16,2048]{1,0:T(8,128)S(1)}, f32[16,2048]{1,0:T(8,128)S(1)}, f32[16,2048]{1,0:T(8,128)S(1)}, f32[16,2048]{1,0:T(8,128)S(1)}, f32[1,1024,128]{2,1,0:T(8,128)S(1)}) custom-call(bf16[768,256]{1,0:T(8,128)(2,1)S(1)} %get-tuple-element.68.refs_0_, bf16[768,256]{1,0:T(8,128)(2,1)S(1)} %get-tuple-element.69.refs_1_, ...), custom_call_target="tpu_custom_call" | custom-call | flops 57500000256 | tf_op jit(solution)/shard_map/pallas_call | solution.py:597
  25.5 2.7 %collective-permute-start.14 = (f32[16,2048]{1,0:T(8,128)S(1)}, f32[16,2048]{1,0:T(8,128)S(1)}, u32[]{:S(2)}, u32[]{:S(2)}) collective-permute-start(f32[16,2048]{1,0:T(8,128)S(1)} %get-tuple-element.96), channel_id=1, source_target_pairs={{0,8},{8,0},{16,24},{24,16},{1,9},{9,1},{17,25},{25,17},{2,10},{10... | collective-permute-start | bytes 393224 | tf_op jit(solution)/shard_map/ppermute | solution.py:524
  28.6 1.5 %shard_map.49 = (f32[16,2048]{1,0:T(8,128)S(1)}, f32[16,2048]{1,0:T(8,128)S(1)}, f32[16,2048]{1,0:T(8,128)S(1)}, f32[16,2048]{1,0:T(8,128)S(1)}, f32[1,1024,128]{2,1,0:T(8,128)S(1)}) custom-call(bf16[768,256]{1,0:T(8,128)(2,1)S(1)} %get-tuple-element.68.refs_0_, bf16[768,256]{1,0:T(8,128)(2,1)S(1)} %get-tuple-element.69.refs_1_, ...), custom_call_target="tpu_custom_call" | custom-call | flops 57500000256 | tf_op jit(solution)/shard_map/pallas_call | solution.py:597
  30.1 1.5 %collective-permute-start.10 = (f32[16,2048]{1,0:T(8,128)S(1)}, f32[16,2048]{1,0:T(8,128)S(1)}, u32[]{:S(2)}, u32[]{:S(2)}) collective-permute-start(f32[16,2048]{1,0:T(8,128)S(1)} %get-tuple-element.89), channel_id=1, source_target_pairs={{0,16},{8,24},{16,0},{24,8},{1,17},{9,25},{17,1},{25,9},{2,18},{10... | collective-permute-start | bytes 393224 | tf_op jit(solution)/shard_map/ppermute | solution.py:524
  31.6 1.2 %collective-permute-start.8 = (f32[16,2048]{1,0:T(8,128)S(1)}, f32[16,2048]{1,0:T(8,128)S(1)}, u32[]{:S(2)}, u32[]{:S(2)}) collective-permute-start(f32[16,2048]{1,0:T(8,128)S(1)} %get-tuple-element.87), channel_id=1, source_target_pairs={{0,24},{8,16},{16,8},{24,0},{1,25},{9,17},{17,9},{25,1},{2,26},{10... | collective-permute-start | bytes 393224 | tf_op jit(solution)/shard_map/ppermute | solution.py:524
  32.9 1.1 %collective-permute-done.14.refs_2_.refs_8_ = f32[16,2048]{1,0:T(8,128)S(1)} collective-permute-done((f32[16,2048]{1,0:T(8,128)S(1)}, f32[16,2048]{1,0:T(8,128)S(1)}, u32[]{:S(2)}, u32[]{:S(2)}) %collective-permute-start.14) | collective-permute-done | bytes 131104 | tf_op jit(solution)/shard_map/ppermute | solution.py:524
  34.1 5.8 %collective-permute-start.16 = (f32[32,2048]{1,0:T(8,128)S(1)}, f32[32,2048]{1,0:T(8,128)S(1)}, u32[]{:S(2)}, u32[]{:S(2)}) collective-permute-start(f32[32,2048]{1,0:T(8,128)S(1)} %get-tuple-element.98), channel_id=1, source_target_pairs={{1,2},{3,4},{5,6},{9,10},{11,12},{13,14},{17,18},{19,20},{21,22},{... | collective-permute-start | bytes 786440 | tf_op jit(solution)/shard_map/ppermute | solution.py:537
  40.2 3.1 %collective-permute-start.11 = (f32[32,2048]{1,0:T(8,128)S(1)}, f32[32,2048]{1,0:T(8,128)S(1)}, u32[]{:S(2)}, u32[]{:S(2)}) collective-permute-start(f32[32,2048]{1,0:T(8,128)S(1)} %get-tuple-element.90), channel_id=1, source_target_pairs={{1,2},{3,4},{5,6},{0,16},{7,23},{9,10},{11,12},{13,14},{8,24},{15,... | collective-permute-start | bytes 786440 | tf_op jit(solution)/shard_map/ppermute | solution.py:537
  43.9 1.5 %shard_map.53 = (f32[128,2048]{1,0:T(8,128)S(1)}, f32[64,2048]{1,0:T(8,128)S(1)}, f32[128,2048]{1,0:T(8,128)S(1)}) custom-call(bf16[192,576]{1,0:T(8,128)(2,1)S(1)} %get-tuple-element.92.refs_0_, bf16[128,192]{1,0:T(8,128)(2,1)S(1)} %get-tuple-element.93.refs_1_, f32[16,2048]{1,0:T(8,128)S(1)} %get-tuple-element.86.refs_0_.refs_4_.refs_2_, ...), custom_call_target="tpu_custom_call" | custom-call | flops 2529999872 | tf_op jit(solution)/shard_map/pallas_call | solution.py:629
  45.5 2.1 %collective-permute-done.11.refs_2_ = f32[32,2048]{1,0:T(8,128)S(1)} collective-permute-done((f32[32,2048]{1,0:T(8,128)S(1)}, f32[32,2048]{1,0:T(8,128)S(1)}, u32[]{:S(2)}, u32[]{:S(2)}) %collective-permute-start.11) | collective-permute-done | bytes 262176 | tf_op jit(solution)/shard_map/ppermute | solution.py:537
  47.6 1.1 %shard_map.54 = (f32[128,2048]{1,0:T(8,128)S(1)}, f32[16,2048]{1,0:T(8,128)S(1)}, f32[16,2048]{1,0:T(8,128)S(1)}, f32[16,2048]{1,0:T(8,128)S(1)}, f32[16,2048]{1,0:T(8,128)S(1)}) custom-call(bf16[128,192]{1,0:T(8,128)(2,1)S(1)} %get-tuple-element.72.refs_0_, bf16[64,384]{1,0:T(8,128)(2,1)S(1)} %get-tuple-element.73.refs_1_, ...), custom_call_target="tpu_custom_call" | custom-call | flops 920000000 | tf_op jit(solution)/shard_map/pallas_call | solution.py:636
  48.8 1.5 %collective-permute-start.18 = (f32[16,2048]{1,0:T(8,128)S(1)}, f32[16,2048]{1,0:T(8,128)S(1)}, u32[]{:S(2)}, u32[]{:S(2)}) collective-permute-start(f32[16,2048]{1,0:T(8,128)S(1)} %get-tuple-element.103), channel_id=1, source_target_pairs={{0,24},{8,16},{16,8},{24,0},{1,25},{9,17},{17,9},{25,1},{2,26},{10... | collective-permute-start | bytes 393224 | tf_op jit(solution)/shard_map/ppermute | solution.py:524
  50.3 1.0 %collective-permute-start.19 = (f32[16,2048]{1,0:T(8,128)S(1)}, f32[16,2048]{1,0:T(8,128)S(1)}, u32[]{:S(2)}, u32[]{:S(2)}) collective-permute-start(f32[16,2048]{1,0:T(8,128)S(1)} %get-tuple-element.104), channel_id=1, source_target_pairs={{0,8},{8,0},{16,24},{24,16},{1,9},{9,1},{17,25},{25,17},{2,10},{10... | collective-permute-start | bytes 393224 | tf_op jit(solution)/shard_map/ppermute | solution.py:524
  51.9 1.5 %collective-permute-start.24 = (f32[16,2048]{1,0:T(8,128)S(1)}, f32[16,2048]{1,0:T(8,128)S(1)}, u32[]{:S(2)}, u32[]{:S(2)}) collective-permute-start(f32[16,2048]{1,0:T(8,128)S(1)} %get-tuple-element.115), channel_id=1, source_target_pairs={{0,24},{8,16},{16,8},{24,0},{1,25},{9,17},{17,9},{25,1},{2,26},{10... | collective-permute-start | bytes 393224 | tf_op jit(solution)/shard_map/ppermute | solution.py:524
  53.4 1.0 %collective-permute-start.25 = (f32[16,2048]{1,0:T(8,128)S(1)}, f32[16,2048]{1,0:T(8,128)S(1)}, u32[]{:S(2)}, u32[]{:S(2)}) collective-permute-start(f32[16,2048]{1,0:T(8,128)S(1)} %get-tuple-element.116), channel_id=1, source_target_pairs={{0,8},{8,0},{16,24},{24,16},{1,9},{9,1},{17,25},{25,17},{2,10},{10... | collective-permute-start | bytes 393224 | tf_op jit(solution)/shard_map/ppermute | solution.py:524
  54.5 1.1 %collective-permute-start.26 = (f32[16,2048]{1,0:T(8,128)S(1)}, f32[16,2048]{1,0:T(8,128)S(1)}, u32[]{:S(2)}, u32[]{:S(2)}) collective-permute-start(f32[16,2048]{1,0:T(8,128)S(1)} %get-tuple-element.117), channel_id=1, source_target_pairs={{0,16},{8,24},{16,0},{24,8},{1,17},{9,25},{17,1},{25,9},{2,18},{10... | collective-permute-start | bytes 393224 | tf_op jit(solution)/shard_map/ppermute | solution.py:524
  55.6 3.2 %collective-permute-done.19.refs_6_ = f32[16,2048]{1,0:T(8,128)S(1)} collective-permute-done((f32[16,2048]{1,0:T(8,128)S(1)}, f32[16,2048]{1,0:T(8,128)S(1)}, u32[]{:S(2)}, u32[]{:S(2)}) %collective-permute-start.19) | collective-permute-done | bytes 131104 | tf_op jit(solution)/shard_map/ppermute | solution.py:524
  58.8 1.4 %shard_map.55 = (f32[16,2048]{1,0:T(8,128)S(1)}, f32[16,2048]{1,0:T(8,128)S(1)}, f32[16,2048]{1,0:T(8,128)S(1)}, f32[16,2048]{1,0:T(8,128)S(1)}) custom-call(bf16[768,256]{1,0:T(8,128)(2,1)S(1)} %copy-done.10, bf16[768,256]{1,0:T(8,128)(2,1)S(1)} %copy-done.12, bf16[64,192]{1,0:T(8,128)(2,1)S(1)} %get-tuple-element.70.refs_2_, ...), custom_call_target="tpu_custom_call" | custom-call | flops 57500000256 | tf_op jit(solution)/shard_map/pallas_call | solution.py:597
  60.1 1.9 %collective-permute-start.21 = (f32[16,2048]{1,0:T(8,128)S(1)}, f32[16,2048]{1,0:T(8,128)S(1)}, u32[]{:S(2)}, u32[]{:S(2)}) collective-permute-start(f32[16,2048]{1,0:T(8,128)S(1)} %get-tuple-element.108), channel_id=1, source_target_pairs={{0,24},{8,16},{16,8},{24,0},{1,25},{9,17},{17,9},{25,1},{2,26},{10... | collective-permute-start | bytes 393224 | tf_op jit(solution)/shard_map/ppermute | solution.py:524
  62.1 0.8 collective-permute-start.23
  64.3 1.4 %shard_map.57 = (f32[16,2048]{1,0:T(8,128)S(1)}, f32[16,2048]{1,0:T(8,128)S(1)}, f32[16,2048]{1,0:T(8,128)S(1)}, f32[16,2048]{1,0:T(8,128)S(1)}) custom-call(bf16[768,256]{1,0:T(8,128)(2,1)S(1)} %copy-done.10, bf16[768,256]{1,0:T(8,128)(2,1)S(1)} %copy-done.12, bf16[64,192]{1,0:T(8,128)(2,1)S(1)} %get-tuple-element.70.refs_2_, ...), custom_call_target="tpu_custom_call" | custom-call | flops 57500000256 | tf_op jit(solution)/shard_map/pallas_call | solution.py:597
  65.6 1.6 %collective-permute-start.29 = (f32[16,2048]{1,0:T(8,128)S(1)}, f32[16,2048]{1,0:T(8,128)S(1)}, u32[]{:S(2)}, u32[]{:S(2)}) collective-permute-start(f32[16,2048]{1,0:T(8,128)S(1)} %get-tuple-element.124), channel_id=1, source_target_pairs={{0,24},{8,16},{16,8},{24,0},{1,25},{9,17},{17,9},{25,1},{2,26},{10... | collective-permute-start | bytes 393224 | tf_op jit(solution)/shard_map/ppermute | solution.py:524
  68.5 4.7 %collective-permute-start.27 = (f32[32,2048]{1,0:T(8,128)S(1)}, f32[32,2048]{1,0:T(8,128)S(1)}, u32[]{:S(2)}, u32[]{:S(2)}) collective-permute-start(f32[32,2048]{1,0:T(8,128)S(1)} %get-tuple-element.120), channel_id=1, source_target_pairs={{1,2},{3,4},{5,6},{9,10},{11,12},{13,14},{17,18},{19,20},{21,22},{... | collective-permute-start | bytes 786440 | tf_op jit(solution)/shard_map/ppermute | solution.py:537
  74.4 2.8 %collective-permute-done.27.refs_1_ = f32[32,2048]{1,0:T(8,128)S(1)} collective-permute-done((f32[32,2048]{1,0:T(8,128)S(1)}, f32[32,2048]{1,0:T(8,128)S(1)}, u32[]{:S(2)}, u32[]{:S(2)}) %collective-permute-start.27) | collective-permute-done | bytes 262176 | tf_op jit(solution)/shard_map/ppermute | solution.py:537
  77.2 1.3 %shard_map.60 = f32[2048,128]{1,0:T(8,128)} custom-call(bf16[64,192]{1,0:T(8,128)(2,1)S(1)} %get-tuple-element.67.refs_0_, f32[32,2048]{1,0:T(8,128)S(1)} %collective-permute-done.27.refs_1_, f32[32,2048]{1,0:T(8,128)S(1)} %collective-permute-done.28.refs_2_, f32[64,2048]{1,0:T(8,128)S(1)} %get-tuple-element.127.refs_3_, ...), custom_call_target="tpu_custom_call" | custom-call | flops 1724999936 | tf_op jit(solution)/shard_map/pallas_call | solution.py:662
  (77 shorter events, 8.7 us)
Async XLA Ops:
  1.9 15.7 %collective-permute-start.5 = (f32[48,2048]{1,0:T(8,128)S(1)}, f32[48,2048]{1,0:T(8,128)S(1)}, u32[]{:S(2)}, u32[]{:S(2)}) collective-permute-start(f32[48,2048]{1,0:T(8,128)S(1)} %get-tuple-element.83), channel_id=1, source_target_pairs={{0,24},{8,16},{16,8},{24,0},{1,25},{9,17},{17,9},{25,1},{2,26},{10... | collective-permute-start | bytes 1179656 | tf_op jit(solution)/shard_map/ppermute | solution.py:524
  5.0 18.7 %collective-permute-start.6 = (f32[48,2048]{1,0:T(8,128)S(1)}, f32[48,2048]{1,0:T(8,128)S(1)}, u32[]{:S(2)}, u32[]{:S(2)}) collective-permute-start(f32[48,2048]{1,0:T(8,128)S(1)} %get-tuple-element.84), channel_id=1, source_target_pairs={{0,8},{8,0},{16,24},{24,16},{1,9},{9,1},{17,25},{25,17},{2,10},{10... | collective-permute-start | bytes 1179656 | tf_op jit(solution)/shard_map/ppermute | solution.py:524
  5.2 18.5 %collective-permute-start.7 = (f32[48,2048]{1,0:T(8,128)S(1)}, f32[48,2048]{1,0:T(8,128)S(1)}, u32[]{:S(2)}, u32[]{:S(2)}) collective-permute-start(f32[48,2048]{1,0:T(8,128)S(1)} %get-tuple-element.85), channel_id=1, source_target_pairs={{0,16},{8,24},{16,0},{24,8},{1,17},{9,25},{17,1},{25,9},{2,18},{10... | collective-permute-start | bytes 1179656 | tf_op jit(solution)/shard_map/ppermute | solution.py:524
  5.4 9.1 %collective-permute-start = (f32[32,2048]{1,0:T(8,128)S(1)}, f32[32,2048]{1,0:T(8,128)S(1)}, u32[]{:S(2)}, u32[]{:S(2)}) collective-permute-start(f32[32,2048]{1,0:T(8,128)S(1)} %get-tuple-element.76), channel_id=1, source_target_pairs={{1,2},{3,4},{5,6},{9,10},{11,12},{13,14},{17,18},{19,20},{21,22},{... | collective-permute-start | bytes 786440 | tf_op jit(solution)/shard_map/ppermute | solution.py:537
  10.1 4.3 %collective-permute-start.1 = (f32[32,2048]{1,0:T(8,128)S(1)}, f32[32,2048]{1,0:T(8,128)S(1)}, u32[]{:S(2)}, u32[]{:S(2)}) collective-permute-start(f32[32,2048]{1,0:T(8,128)S(1)} %get-tuple-element.77), channel_id=1, source_target_pairs={{0,1},{2,3},{4,5},{6,7},{8,9},{10,11},{12,13},{14,15},{16,17},{18,... | collective-permute-start | bytes 786440 | tf_op jit(solution)/shard_map/ppermute | solution.py:537
  15.2 12.9 %collective-permute-start.2 = (f32[16,2048]{1,0:T(8,128)S(1)}, f32[16,2048]{1,0:T(8,128)S(1)}, u32[]{:S(2)}, u32[]{:S(2)}) collective-permute-start(f32[16,2048]{1,0:T(8,128)S(1)} %get-tuple-element.79), channel_id=1, source_target_pairs={{0,24},{8,16},{16,8},{24,0},{1,25},{9,17},{17,9},{25,1},{2,26},{10... | collective-permute-start | bytes 393224 | tf_op jit(solution)/shard_map/ppermute | solution.py:524
  17.4 11.2 %collective-permute-start.3 = (f32[16,2048]{1,0:T(8,128)S(1)}, f32[16,2048]{1,0:T(8,128)S(1)}, u32[]{:S(2)}, u32[]{:S(2)}) collective-permute-start(f32[16,2048]{1,0:T(8,128)S(1)} %get-tuple-element.80), channel_id=1, source_target_pairs={{0,8},{8,0},{16,24},{24,16},{1,9},{9,1},{17,25},{25,17},{2,10},{10... | collective-permute-start | bytes 393224 | tf_op jit(solution)/shard_map/ppermute | solution.py:524
  17.6 11.0 %collective-permute-start.4 = (f32[16,2048]{1,0:T(8,128)S(1)}, f32[16,2048]{1,0:T(8,128)S(1)}, u32[]{:S(2)}, u32[]{:S(2)}) collective-permute-start(f32[16,2048]{1,0:T(8,128)S(1)} %get-tuple-element.81), channel_id=1, source_target_pairs={{0,16},{8,24},{16,0},{24,8},{1,17},{9,25},{17,1},{25,9},{2,18},{10... | collective-permute-start | bytes 393224 | tf_op jit(solution)/shard_map/ppermute | solution.py:524
  25.2 7.6 %collective-permute-start.13 = (f32[16,2048]{1,0:T(8,128)S(1)}, f32[16,2048]{1,0:T(8,128)S(1)}, u32[]{:S(2)}, u32[]{:S(2)}) collective-permute-start(f32[16,2048]{1,0:T(8,128)S(1)} %get-tuple-element.95), channel_id=1, source_target_pairs={{0,24},{8,16},{16,8},{24,0},{1,25},{9,17},{17,9},{25,1},{2,26},{10... | collective-permute-start | bytes 393224 | tf_op jit(solution)/shard_map/ppermute | solution.py:524
  25.5 8.4 %collective-permute-start.14 = (f32[16,2048]{1,0:T(8,128)S(1)}, f32[16,2048]{1,0:T(8,128)S(1)}, u32[]{:S(2)}, u32[]{:S(2)}) collective-permute-start(f32[16,2048]{1,0:T(8,128)S(1)} %get-tuple-element.96), channel_id=1, source_target_pairs={{0,8},{8,0},{16,24},{24,16},{1,9},{9,1},{17,25},{25,17},{2,10},{10... | collective-permute-start | bytes 393224 | tf_op jit(solution)/shard_map/ppermute | solution.py:524
  28.2 5.8 %collective-permute-start.15 = (f32[16,2048]{1,0:T(8,128)S(1)}, f32[16,2048]{1,0:T(8,128)S(1)}, u32[]{:S(2)}, u32[]{:S(2)}) collective-permute-start(f32[16,2048]{1,0:T(8,128)S(1)} %get-tuple-element.97), channel_id=1, source_target_pairs={{0,16},{8,24},{16,0},{24,8},{1,17},{9,25},{17,1},{25,9},{2,18},{10... | collective-permute-start | bytes 393224 | tf_op jit(solution)/shard_map/ppermute | solution.py:524
  30.1 9.8 %collective-permute-start.10 = (f32[16,2048]{1,0:T(8,128)S(1)}, f32[16,2048]{1,0:T(8,128)S(1)}, u32[]{:S(2)}, u32[]{:S(2)}) collective-permute-start(f32[16,2048]{1,0:T(8,128)S(1)} %get-tuple-element.89), channel_id=1, source_target_pairs={{0,16},{8,24},{16,0},{24,8},{1,17},{9,25},{17,1},{25,9},{2,18},{10... | collective-permute-start | bytes 393224 | tf_op jit(solution)/shard_map/ppermute | solution.py:524
  31.6 8.4 %collective-permute-start.8 = (f32[16,2048]{1,0:T(8,128)S(1)}, f32[16,2048]{1,0:T(8,128)S(1)}, u32[]{:S(2)}, u32[]{:S(2)}) collective-permute-start(f32[16,2048]{1,0:T(8,128)S(1)} %get-tuple-element.87), channel_id=1, source_target_pairs={{0,24},{8,16},{16,8},{24,0},{1,25},{9,17},{17,9},{25,1},{2,26},{10... | collective-permute-start | bytes 393224 | tf_op jit(solution)/shard_map/ppermute | solution.py:524
  32.8 7.2 %collective-permute-start.9 = (f32[16,2048]{1,0:T(8,128)S(1)}, f32[16,2048]{1,0:T(8,128)S(1)}, u32[]{:S(2)}, u32[]{:S(2)}) collective-permute-start(f32[16,2048]{1,0:T(8,128)S(1)} %get-tuple-element.88), channel_id=1, source_target_pairs={{0,8},{8,0},{16,24},{24,16},{1,9},{9,1},{17,25},{25,17},{2,10},{10... | collective-permute-start | bytes 393224 | tf_op jit(solution)/shard_map/ppermute | solution.py:524
  34.1 9.9 %collective-permute-start.16 = (f32[32,2048]{1,0:T(8,128)S(1)}, f32[32,2048]{1,0:T(8,128)S(1)}, u32[]{:S(2)}, u32[]{:S(2)}) collective-permute-start(f32[32,2048]{1,0:T(8,128)S(1)} %get-tuple-element.98), channel_id=1, source_target_pairs={{1,2},{3,4},{5,6},{9,10},{11,12},{13,14},{17,18},{19,20},{21,22},{... | collective-permute-start | bytes 786440 | tf_op jit(solution)/shard_map/ppermute | solution.py:537
  39.9 4.0 %collective-permute-start.17 = (f32[32,2048]{1,0:T(8,128)S(1)}, f32[32,2048]{1,0:T(8,128)S(1)}, u32[]{:S(2)}, u32[]{:S(2)}) collective-permute-start(f32[32,2048]{1,0:T(8,128)S(1)} %get-tuple-element.99), channel_id=1, source_target_pairs={{0,1},{2,3},{4,5},{6,7},{8,9},{10,11},{12,13},{14,15},{16,17},{18,... | collective-permute-start | bytes 786440 | tf_op jit(solution)/shard_map/ppermute | solution.py:537
  40.2 7.5 %collective-permute-start.11 = (f32[32,2048]{1,0:T(8,128)S(1)}, f32[32,2048]{1,0:T(8,128)S(1)}, u32[]{:S(2)}, u32[]{:S(2)}) collective-permute-start(f32[32,2048]{1,0:T(8,128)S(1)} %get-tuple-element.90), channel_id=1, source_target_pairs={{1,2},{3,4},{5,6},{0,16},{7,23},{9,10},{11,12},{13,14},{8,24},{15,... | collective-permute-start | bytes 786440 | tf_op jit(solution)/shard_map/ppermute | solution.py:537
  43.3 4.4 %collective-permute-start.12 = (f32[32,2048]{1,0:T(8,128)S(1)}, f32[32,2048]{1,0:T(8,128)S(1)}, u32[]{:S(2)}, u32[]{:S(2)}) collective-permute-start(f32[32,2048]{1,0:T(8,128)S(1)} %get-tuple-element.91), channel_id=1, source_target_pairs={{0,1},{2,3},{4,5},{6,7},{8,9},{10,11},{12,13},{14,15},{16,17},{18,... | collective-permute-start | bytes 786440 | tf_op jit(solution)/shard_map/ppermute | solution.py:537
  48.8 5.7 %collective-permute-start.18 = (f32[16,2048]{1,0:T(8,128)S(1)}, f32[16,2048]{1,0:T(8,128)S(1)}, u32[]{:S(2)}, u32[]{:S(2)}) collective-permute-start(f32[16,2048]{1,0:T(8,128)S(1)} %get-tuple-element.103), channel_id=1, source_target_pairs={{0,24},{8,16},{16,8},{24,0},{1,25},{9,17},{17,9},{25,1},{2,26},{10... | collective-permute-start | bytes 393224 | tf_op jit(solution)/shard_map/ppermute | solution.py:524
  50.3 8.5 %collective-permute-start.19 = (f32[16,2048]{1,0:T(8,128)S(1)}, f32[16,2048]{1,0:T(8,128)S(1)}, u32[]{:S(2)}, u32[]{:S(2)}) collective-permute-start(f32[16,2048]{1,0:T(8,128)S(1)} %get-tuple-element.104), channel_id=1, source_target_pairs={{0,8},{8,0},{16,24},{24,16},{1,9},{9,1},{17,25},{25,17},{2,10},{10... | collective-permute-start | bytes 393224 | tf_op jit(solution)/shard_map/ppermute | solution.py:524
  51.3 7.5 %collective-permute-start.20 = (f32[16,2048]{1,0:T(8,128)S(1)}, f32[16,2048]{1,0:T(8,128)S(1)}, u32[]{:S(2)}, u32[]{:S(2)}) collective-permute-start(f32[16,2048]{1,0:T(8,128)S(1)} %get-tuple-element.105), channel_id=1, source_target_pairs={{0,16},{8,24},{16,0},{24,8},{1,17},{9,25},{17,1},{25,9},{2,18},{10... | collective-permute-start | bytes 393224 | tf_op jit(solution)/shard_map/ppermute | solution.py:524
  51.9 10.1 %collective-permute-start.24 = (f32[16,2048]{1,0:T(8,128)S(1)}, f32[16,2048]{1,0:T(8,128)S(1)}, u32[]{:S(2)}, u32[]{:S(2)}) collective-permute-start(f32[16,2048]{1,0:T(8,128)S(1)} %get-tuple-element.115), channel_id=1, source_target_pairs={{0,24},{8,16},{16,8},{24,0},{1,25},{9,17},{17,9},{25,1},{2,26},{10... | collective-permute-start | bytes 393224 | tf_op jit(solution)/shard_map/ppermute | solution.py:524
  53.4 10.0 %collective-permute-start.25 = (f32[16,2048]{1,0:T(8,128)S(1)}, f32[16,2048]{1,0:T(8,128)S(1)}, u32[]{:S(2)}, u32[]{:S(2)}) collective-permute-start(f32[16,2048]{1,0:T(8,128)S(1)} %get-tuple-element.116), channel_id=1, source_target_pairs={{0,8},{8,0},{16,24},{24,16},{1,9},{9,1},{17,25},{25,17},{2,10},{10... | collective-permute-start | bytes 393224 | tf_op jit(solution)/shard_map/ppermute | solution.py:524
  54.5 9.0 %collective-permute-start.26 = (f32[16,2048]{1,0:T(8,128)S(1)}, f32[16,2048]{1,0:T(8,128)S(1)}, u32[]{:S(2)}, u32[]{:S(2)}) collective-permute-start(f32[16,2048]{1,0:T(8,128)S(1)} %get-tuple-element.117), channel_id=1, source_target_pairs={{0,16},{8,24},{16,0},{24,8},{1,17},{9,25},{17,1},{25,9},{2,18},{10... | collective-permute-start | bytes 393224 | tf_op jit(solution)/shard_map/ppermute | solution.py:524
  60.1 7.7 %collective-permute-start.21 = (f32[16,2048]{1,0:T(8,128)S(1)}, f32[16,2048]{1,0:T(8,128)S(1)}, u32[]{:S(2)}, u32[]{:S(2)}) collective-permute-start(f32[16,2048]{1,0:T(8,128)S(1)} %get-tuple-element.108), channel_id=1, source_target_pairs={{0,24},{8,16},{16,8},{24,0},{1,25},{9,17},{17,9},{25,1},{2,26},{10... | collective-permute-start | bytes 393224 | tf_op jit(solution)/shard_map/ppermute | solution.py:524
  62.1 6.3 %collective-permute-start.22 = (f32[16,2048]{1,0:T(8,128)S(1)}, f32[16,2048]{1,0:T(8,128)S(1)}, u32[]{:S(2)}, u32[]{:S(2)}) collective-permute-start(f32[16,2048]{1,0:T(8,128)S(1)} %get-tuple-element.109), channel_id=1, source_target_pairs={{0,8},{8,0},{16,24},{24,16},{1,9},{9,1},{17,25},{25,17},{2,10},{10... | collective-permute-start | bytes 393224 | tf_op jit(solution)/shard_map/ppermute | solution.py:524
  62.1 6.3 %collective-permute-start.23 = (f32[16,2048]{1,0:T(8,128)S(1)}, f32[16,2048]{1,0:T(8,128)S(1)}, u32[]{:S(2)}, u32[]{:S(2)}) collective-permute-start(f32[16,2048]{1,0:T(8,128)S(1)} %get-tuple-element.110), channel_id=1, source_target_pairs={{0,16},{8,24},{16,0},{24,8},{1,17},{9,25},{17,1},{25,9},{2,18},{10... | collective-permute-start | bytes 393224 | tf_op jit(solution)/shard_map/ppermute | solution.py:524
  65.6 7.6 %collective-permute-start.29 = (f32[16,2048]{1,0:T(8,128)S(1)}, f32[16,2048]{1,0:T(8,128)S(1)}, u32[]{:S(2)}, u32[]{:S(2)}) collective-permute-start(f32[16,2048]{1,0:T(8,128)S(1)} %get-tuple-element.124), channel_id=1, source_target_pairs={{0,24},{8,16},{16,8},{24,0},{1,25},{9,17},{17,9},{25,1},{2,26},{10... | collective-permute-start | bytes 393224 | tf_op jit(solution)/shard_map/ppermute | solution.py:524
  67.2 6.6 %collective-permute-start.30 = (f32[16,2048]{1,0:T(8,128)S(1)}, f32[16,2048]{1,0:T(8,128)S(1)}, u32[]{:S(2)}, u32[]{:S(2)}) collective-permute-start(f32[16,2048]{1,0:T(8,128)S(1)} %get-tuple-element.125), channel_id=1, source_target_pairs={{0,8},{8,0},{16,24},{24,16},{1,9},{9,1},{17,25},{25,17},{2,10},{10... | collective-permute-start | bytes 393224 | tf_op jit(solution)/shard_map/ppermute | solution.py:524
  67.9 6.0 %collective-permute-start.31 = (f32[16,2048]{1,0:T(8,128)S(1)}, f32[16,2048]{1,0:T(8,128)S(1)}, u32[]{:S(2)}, u32[]{:S(2)}) collective-permute-start(f32[16,2048]{1,0:T(8,128)S(1)} %get-tuple-element.126), channel_id=1, source_target_pairs={{0,16},{8,24},{16,0},{24,8},{1,17},{9,25},{17,1},{25,9},{2,18},{10... | collective-permute-start | bytes 393224 | tf_op jit(solution)/shard_map/ppermute | solution.py:524
  68.5 8.7 %collective-permute-start.27 = (f32[32,2048]{1,0:T(8,128)S(1)}, f32[32,2048]{1,0:T(8,128)S(1)}, u32[]{:S(2)}, u32[]{:S(2)}) collective-permute-start(f32[32,2048]{1,0:T(8,128)S(1)} %get-tuple-element.120), channel_id=1, source_target_pairs={{1,2},{3,4},{5,6},{9,10},{11,12},{13,14},{17,18},{19,20},{21,22},{... | collective-permute-start | bytes 786440 | tf_op jit(solution)/shard_map/ppermute | solution.py:537
  73.1 4.0 %collective-permute-start.28 = (f32[32,2048]{1,0:T(8,128)S(1)}, f32[32,2048]{1,0:T(8,128)S(1)}, u32[]{:S(2)}, u32[]{:S(2)}) collective-permute-start(f32[32,2048]{1,0:T(8,128)S(1)} %get-tuple-element.121), channel_id=1, source_target_pairs={{0,1},{2,3},{4,5},{6,7},{8,9},{10,11},{12,13},{14,15},{16,17},{18,... | collective-permute-start | bytes 786440 | tf_op jit(solution)/shard_map/ppermute | solution.py:537
  (15 other events, 123.5 us)

commit v7 on v6

--- a/solution.py
+++ b/solution.py
@@ -293,7 +293,8 @@
             inside = (start >= first) & (start < first + span)
 
             def put(ref, start=start, first=first, part_ref=part_ref):
-                ref[pl.ds(pl.multiple_of(start - first, 8), chunk), :] = part_ref[...]
+                place = jnp.clip(start - first, 0, span - chunk)
+                ref[pl.ds(pl.multiple_of(place, 8), chunk), :] = part_ref[...]
 
             pl.when(inside & (to_sibling == 1))(functools.partial(put, sibling_ref))
             pl.when(inside & (to_sibling == 0))(functools.partial(put, other_ref))
@@ -592,7 +593,7 @@
 
     def through_planes(values, first, chunk, seen_values, seen_first=None):
         lines = groups * planes * chunk
-        across = (width // LANES, lines, LANES)
+        across = (width // LANES, lines + chunk, LANES)
         begins = seen_first is not None
         result = call(
             50,

time: 78.7 us -> 78.8 us (level)
  no operation moved by 1% of the time
where the time goes in v7:
time: 78.8 us; the launch traced here: 78.5 us
  starting transfers between devices  42.2 us (54%)
  waiting for transfers between devices  19.9 us (25%)
  Pallas kernels  14.6 us (19%)
  local copies, waits for them, and re-layouts  1.64 us (2%)
    ppermute x24, starting transfers between devices, exchanged(): result.append(lax.ppermute(value, ('gz', 'bx'), pairs))  23.5 us
    ppermute x8, starting transfers between devices, from_sides(): lax.ppermute(value, ('gz', 'bx', 'by'), pairs + [(j, i) for i, j in pairs])  18.7 us
    ppermute x24, waiting for transfers between devices, exchanged(): result.append(lax.ppermute(value, ('gz', 'bx'), pairs))  11.8 us
    ppermute x8, waiting for transfers between devices, from_sides(): lax.ppermute(value, ('gz', 'bx', 'by'), pairs + [(j, i) for i, j in pairs])  8.08 us
    pallas_call x4, Pallas kernels, through_planes(): call(50, functools.partial(planes_kernel, sizes, first, seen_first), [sha...  5.75 us
    pallas_call x1, Pallas kernels, per_device(): call(1.3, functools.partial(start_kernel, parts, radius, count), [shaped(...  1.92 us
    unnamed x30, local copies, waits for them, and re-layouts  1.64 us
  transfers between devices with their start and end apart: 32, of which 10 were waited for; matrix products, arithmetic and copies ran while one was open for 0% of the time, Pallas kernels for 13%

profile of v7, /device:TPU:1, one launch (start us, length us, event | category | flops | bytes accessed | tf_op | source)
XLA Modules:
  0.0 78.5 jit_solution(17068131342514361257)
XLA Ops:
  0.0 1.9 %shard_map.47 = (f32[128,2048]{1,0:T(8,128)S(1)}, f32[32,2048]{1,0:T(8,128)S(1)}, f32[32,2048]{1,0:T(8,128)S(1)}, f32[48,2048]{1,0:T(8,128)S(1)}, f32[48,2048]{1...) custom-call(f32[1,65]{1,0:T(1,128)} %bitcast.7, f32[2048,128]{1,0:T(8,128)} %bitcast.9), custom_call_target="tpu_custom_call" | custom-call | flops 1495000064 | tf_op jit(solution)/shard_map/pallas_call | solution.py:546
  1.9 3.1 %collective-permute-start.5 = (f32[48,2048]{1,0:T(8,128)S(1)}, f32[48,2048]{1,0:T(8,128)S(1)}, u32[]{:S(2)}, u32[]{:S(2)}) collective-permute-start(f32[48,2048]{1,0:T(8,128)S(1)} %get-tuple-element.83), channel_id=1, source_target_pairs={{0,24},{8,16},{16,8},{24,0},{1,25},{9,17},{17,9},{25,1},{2,26},{10... | collective-permute-start | bytes 1179656 | tf_op jit(solution)/shard_map/ppermute | solution.py:525
  5.4 4.7 %collective-permute-start = (f32[32,2048]{1,0:T(8,128)S(1)}, f32[32,2048]{1,0:T(8,128)S(1)}, u32[]{:S(2)}, u32[]{:S(2)}) collective-permute-start(f32[32,2048]{1,0:T(8,128)S(1)} %get-tuple-element.76), channel_id=1, source_target_pairs={{1,2},{3,4},{5,6},{9,10},{11,12},{13,14},{17,18},{19,20},{21,22},{... | collective-permute-start | bytes 786440 | tf_op jit(solution)/shard_map/ppermute | solution.py:538
  10.9 0.9 %shard_map.46 = (bf16[64,576]{1,0:T(8,128)(2,1)S(1)}, bf16[192,576]{1,0:T(8,128)(2,1)S(1)}, bf16[128,192]{1,0:T(8,128)(2,1)S(1)}, bf16[128,192]{1,0:T(8,128)(2,1...) custom-call(f32[1,65]{1,0:T(1,128)S(1)} %bitcast.5, ...), custom_call_target="tpu_custom_call" | custom-call | flops 920000000 | tf_op jit(solution)/shard_map/pallas_call | solution.py:565
  11.8 2.6 %collective-permute-done.refs_2_.refs_7_ = f32[32,2048]{1,0:T(8,128)S(1)} collective-permute-done((f32[32,2048]{1,0:T(8,128)S(1)}, f32[32,2048]{1,0:T(8,128)S(1)}, u32[]{:S(2)}, u32[]{:S(2)}) %collective-permute-start) | collective-permute-done | bytes 262176 | tf_op jit(solution)/shard_map/ppermute | solution.py:538
  15.2 2.2 %collective-permute-start.2 = (f32[16,2048]{1,0:T(8,128)S(1)}, f32[16,2048]{1,0:T(8,128)S(1)}, u32[]{:S(2)}, u32[]{:S(2)}) collective-permute-start(f32[16,2048]{1,0:T(8,128)S(1)} %get-tuple-element.79), channel_id=1, source_target_pairs={{0,24},{8,16},{16,8},{24,0},{1,25},{9,17},{17,9},{25,1},{2,26},{10... | collective-permute-start | bytes 393224 | tf_op jit(solution)/shard_map/ppermute | solution.py:525
  17.9 5.8 %collective-permute-done.6.refs_10_.refs_6_ = f32[48,2048]{1,0:T(8,128)S(1)} collective-permute-done((f32[48,2048]{1,0:T(8,128)S(1)}, f32[48,2048]{1,0:T(8,128)S(1)}, u32[]{:S(2)}, u32[]{:S(2)}) %collective-permute-start.6) | collective-permute-done | bytes 393248 | tf_op jit(solution)/shard_map/ppermute | solution.py:525
  23.7 1.5 %shard_map.51 = (f32[16,2048]{1,0:T(8,128)S(1)}, f32[16,2048]{1,0:T(8,128)S(1)}, f32[16,2048]{1,0:T(8,128)S(1)}, f32[16,2048]{1,0:T(8,128)S(1)}, f32[1,1040,128]{2,1,0:T(8,128)S(1)}) custom-call(bf16[768,256]{1,0:T(8,128)(2,1)S(1)} %get-tuple-element.68.refs_0_, bf16[768,256]{1,0:T(8,128)(2,1)S(1)} %get-tuple-element.69.refs_1_, ...), custom_call_target="tpu_custom_call" | custom-call | flops 57500000256 | tf_op jit(solution)/shard_map/pallas_call | solution.py:598
  25.5 2.7 %collective-permute-start.14 = (f32[16,2048]{1,0:T(8,128)S(1)}, f32[16,2048]{1,0:T(8,128)S(1)}, u32[]{:S(2)}, u32[]{:S(2)}) collective-permute-start(f32[16,2048]{1,0:T(8,128)S(1)} %get-tuple-element.96), channel_id=1, source_target_pairs={{0,8},{8,0},{16,24},{24,16},{1,9},{9,1},{17,25},{25,17},{2,10},{10... | collective-permute-start | bytes 393224 | tf_op jit(solution)/shard_map/ppermute | solution.py:525
  28.6 1.5 %shard_map.49 = (f32[16,2048]{1,0:T(8,128)S(1)}, f32[16,2048]{1,0:T(8,128)S(1)}, f32[16,2048]{1,0:T(8,128)S(1)}, f32[16,2048]{1,0:T(8,128)S(1)}, f32[1,1040,128]{2,1,0:T(8,128)S(1)}) custom-call(bf16[768,256]{1,0:T(8,128)(2,1)S(1)} %get-tuple-element.68.refs_0_, bf16[768,256]{1,0:T(8,128)(2,1)S(1)} %get-tuple-element.69.refs_1_, ...), custom_call_target="tpu_custom_call" | custom-call | flops 57500000256 | tf_op jit(solution)/shard_map/pallas_call | solution.py:598
  30.2 1.5 %collective-permute-start.10 = (f32[16,2048]{1,0:T(8,128)S(1)}, f32[16,2048]{1,0:T(8,128)S(1)}, u32[]{:S(2)}, u32[]{:S(2)}) collective-permute-start(f32[16,2048]{1,0:T(8,128)S(1)} %get-tuple-element.89), channel_id=1, source_target_pairs={{0,16},{8,24},{16,0},{24,8},{1,17},{9,25},{17,1},{25,9},{2,18},{10... | collective-permute-start | bytes 393224 | tf_op jit(solution)/shard_map/ppermute | solution.py:525
  31.6 1.2 %collective-permute-start.8 = (f32[16,2048]{1,0:T(8,128)S(1)}, f32[16,2048]{1,0:T(8,128)S(1)}, u32[]{:S(2)}, u32[]{:S(2)}) collective-permute-start(f32[16,2048]{1,0:T(8,128)S(1)} %get-tuple-element.87), channel_id=1, source_target_pairs={{0,24},{8,16},{16,8},{24,0},{1,25},{9,17},{17,9},{25,1},{2,26},{10... | collective-permute-start | bytes 393224 | tf_op jit(solution)/shard_map/ppermute | solution.py:525
  32.9 1.1 %collective-permute-done.14.refs_2_.refs_8_ = f32[16,2048]{1,0:T(8,128)S(1)} collective-permute-done((f32[16,2048]{1,0:T(8,128)S(1)}, f32[16,2048]{1,0:T(8,128)S(1)}, u32[]{:S(2)}, u32[]{:S(2)}) %collective-permute-start.14) | collective-permute-done | bytes 131104 | tf_op jit(solution)/shard_map/ppermute | solution.py:525
  34.1 5.8 %collective-permute-start.16 = (f32[32,2048]{1,0:T(8,128)S(1)}, f32[32,2048]{1,0:T(8,128)S(1)}, u32[]{:S(2)}, u32[]{:S(2)}) collective-permute-start(f32[32,2048]{1,0:T(8,128)S(1)} %get-tuple-element.98), channel_id=1, source_target_pairs={{1,2},{3,4},{5,6},{9,10},{11,12},{13,14},{17,18},{19,20},{21,22},{... | collective-permute-start | bytes 786440 | tf_op jit(solution)/shard_map/ppermute | solution.py:538
  40.2 3.1 %collective-permute-start.11 = (f32[32,2048]{1,0:T(8,128)S(1)}, f32[32,2048]{1,0:T(8,128)S(1)}, u32[]{:S(2)}, u32[]{:S(2)}) collective-permute-start(f32[32,2048]{1,0:T(8,128)S(1)} %get-tuple-element.90), channel_id=1, source_target_pairs={{1,2},{3,4},{5,6},{0,16},{7,23},{9,10},{11,12},{13,14},{8,24},{15,... | collective-permute-start | bytes 786440 | tf_op jit(solution)/shard_map/ppermute | solution.py:538
  44.0 1.5 %shard_map.53 = (f32[128,2048]{1,0:T(8,128)S(1)}, f32[64,2048]{1,0:T(8,128)S(1)}, f32[128,2048]{1,0:T(8,128)S(1)}) custom-call(bf16[192,576]{1,0:T(8,128)(2,1)S(1)} %get-tuple-element.92.refs_0_, bf16[128,192]{1,0:T(8,128)(2,1)S(1)} %get-tuple-element.93.refs_1_, f32[16,2048]{1,0:T(8,128)S(1)} %get-tuple-element.86.refs_0_.refs_4_.refs_2_, ...), custom_call_target="tpu_custom_call" | custom-call | flops 2529999872 | tf_op jit(solution)/shard_map/pallas_call | solution.py:630
  45.5 2.2 %collective-permute-done.11.refs_2_ = f32[32,2048]{1,0:T(8,128)S(1)} collective-permute-done((f32[32,2048]{1,0:T(8,128)S(1)}, f32[32,2048]{1,0:T(8,128)S(1)}, u32[]{:S(2)}, u32[]{:S(2)}) %collective-permute-start.11) | collective-permute-done | bytes 262176 | tf_op jit(solution)/shard_map/ppermute | solution.py:538
  47.7 1.1 %shard_map.54 = (f32[128,2048]{1,0:T(8,128)S(1)}, f32[16,2048]{1,0:T(8,128)S(1)}, f32[16,2048]{1,0:T(8,128)S(1)}, f32[16,2048]{1,0:T(8,128)S(1)}, f32[16,2048]{1,0:T(8,128)S(1)}) custom-call(bf16[128,192]{1,0:T(8,128)(2,1)S(1)} %get-tuple-element.72.refs_0_, bf16[64,384]{1,0:T(8,128)(2,1)S(1)} %get-tuple-element.73.refs_1_, ...), custom_call_target="tpu_custom_call" | custom-call | flops 920000000 | tf_op jit(solution)/shard_map/pallas_call | solution.py:637
  48.8 1.5 %collective-permute-start.18 = (f32[16,2048]{1,0:T(8,128)S(1)}, f32[16,2048]{1,0:T(8,128)S(1)}, u32[]{:S(2)}, u32[]{:S(2)}) collective-permute-start(f32[16,2048]{1,0:T(8,128)S(1)} %get-tuple-element.103), channel_id=1, source_target_pairs={{0,24},{8,16},{16,8},{24,0},{1,25},{9,17},{17,9},{25,1},{2,26},{10... | collective-permute-start | bytes 393224 | tf_op jit(solution)/shard_map/ppermute | solution.py:525
  50.3 1.0 %collective-permute-start.19 = (f32[16,2048]{1,0:T(8,128)S(1)}, f32[16,2048]{1,0:T(8,128)S(1)}, u32[]{:S(2)}, u32[]{:S(2)}) collective-permute-start(f32[16,2048]{1,0:T(8,128)S(1)} %get-tuple-element.104), channel_id=1, source_target_pairs={{0,8},{8,0},{16,24},{24,16},{1,9},{9,1},{17,25},{25,17},{2,10},{10... | collective-permute-start | bytes 393224 | tf_op jit(solution)/shard_map/ppermute | solution.py:525
  52.0 1.5 %collective-permute-start.24 = (f32[16,2048]{1,0:T(8,128)S(1)}, f32[16,2048]{1,0:T(8,128)S(1)}, u32[]{:S(2)}, u32[]{:S(2)}) collective-permute-start(f32[16,2048]{1,0:T(8,128)S(1)} %get-tuple-element.115), channel_id=1, source_target_pairs={{0,24},{8,16},{16,8},{24,0},{1,25},{9,17},{17,9},{25,1},{2,26},{10... | collective-permute-start | bytes 393224 | tf_op jit(solution)/shard_map/ppermute | solution.py:525
  53.5 1.0 %collective-permute-start.25 = (f32[16,2048]{1,0:T(8,128)S(1)}, f32[16,2048]{1,0:T(8,128)S(1)}, u32[]{:S(2)}, u32[]{:S(2)}) collective-permute-start(f32[16,2048]{1,0:T(8,128)S(1)} %get-tuple-element.116), channel_id=1, source_target_pairs={{0,8},{8,0},{16,24},{24,16},{1,9},{9,1},{17,25},{25,17},{2,10},{10... | collective-permute-start | bytes 393224 | tf_op jit(solution)/shard_map/ppermute | solution.py:525
  54.5 1.0 %collective-permute-start.26 = (f32[16,2048]{1,0:T(8,128)S(1)}, f32[16,2048]{1,0:T(8,128)S(1)}, u32[]{:S(2)}, u32[]{:S(2)}) collective-permute-start(f32[16,2048]{1,0:T(8,128)S(1)} %get-tuple-element.117), channel_id=1, source_target_pairs={{0,16},{8,24},{16,0},{24,8},{1,17},{9,25},{17,1},{25,9},{2,18},{10... | collective-permute-start | bytes 393224 | tf_op jit(solution)/shard_map/ppermute | solution.py:525
  55.6 3.3 %collective-permute-done.19.refs_6_ = f32[16,2048]{1,0:T(8,128)S(1)} collective-permute-done((f32[16,2048]{1,0:T(8,128)S(1)}, f32[16,2048]{1,0:T(8,128)S(1)}, u32[]{:S(2)}, u32[]{:S(2)}) %collective-permute-start.19) | collective-permute-done | bytes 131104 | tf_op jit(solution)/shard_map/ppermute | solution.py:525
  58.8 1.4 %shard_map.55 = (f32[16,2048]{1,0:T(8,128)S(1)}, f32[16,2048]{1,0:T(8,128)S(1)}, f32[16,2048]{1,0:T(8,128)S(1)}, f32[16,2048]{1,0:T(8,128)S(1)}) custom-call(bf16[768,256]{1,0:T(8,128)(2,1)S(1)} %copy-done.10, bf16[768,256]{1,0:T(8,128)(2,1)S(1)} %copy-done.12, bf16[64,192]{1,0:T(8,128)(2,1)S(1)} %get-tuple-element.70.refs_2_, ...), custom_call_target="tpu_custom_call" | custom-call | flops 57500000256 | tf_op jit(solution)/shard_map/pallas_call | solution.py:598
  60.2 1.9 %collective-permute-start.21 = (f32[16,2048]{1,0:T(8,128)S(1)}, f32[16,2048]{1,0:T(8,128)S(1)}, u32[]{:S(2)}, u32[]{:S(2)}) collective-permute-start(f32[16,2048]{1,0:T(8,128)S(1)} %get-tuple-element.108), channel_id=1, source_target_pairs={{0,24},{8,16},{16,8},{24,0},{1,25},{9,17},{17,9},{25,1},{2,26},{10... | collective-permute-start | bytes 393224 | tf_op jit(solution)/shard_map/ppermute | solution.py:525
  62.1 0.8 %collective-permute-start.23 = (f32[16,2048]{1,0:T(8,128)S(1)}, f32[16,2048]{1,0:T(8,128)S(1)}, u32[]{:S(2)}, u32[]{:S(2)}) collective-permute-start(f32[16,2048]{1,0:T(8,128)S(1)} %get-tuple-element.110), channel_id=1, source_target_pairs={{0,16},{8,24},{16,0},{24,8},{1,17},{9,25},{17,1},{25,9},{2,18},{10... | collective-permute-start | bytes 393224 | tf_op jit(solution)/shard_map/ppermute | solution.py:525
  64.3 1.4 %shard_map.57 = (f32[16,2048]{1,0:T(8,128)S(1)}, f32[16,2048]{1,0:T(8,128)S(1)}, f32[16,2048]{1,0:T(8,128)S(1)}, f32[16,2048]{1,0:T(8,128)S(1)}) custom-call(bf16[768,256]{1,0:T(8,128)(2,1)S(1)} %copy-done.10, bf16[768,256]{1,0:T(8,128)(2,1)S(1)} %copy-done.12, bf16[64,192]{1,0:T(8,128)(2,1)S(1)} %get-tuple-element.70.refs_2_, ...), custom_call_target="tpu_custom_call" | custom-call | flops 57500000256 | tf_op jit(solution)/shard_map/pallas_call | solution.py:598
  65.7 1.6 %collective-permute-start.29 = (f32[16,2048]{1,0:T(8,128)S(1)}, f32[16,2048]{1,0:T(8,128)S(1)}, u32[]{:S(2)}, u32[]{:S(2)}) collective-permute-start(f32[16,2048]{1,0:T(8,128)S(1)} %get-tuple-element.124), channel_id=1, source_target_pairs={{0,24},{8,16},{16,8},{24,0},{1,25},{9,17},{17,9},{25,1},{2,26},{10... | collective-permute-start | bytes 393224 | tf_op jit(solution)/shard_map/ppermute | solution.py:525
  68.5 4.7 %collective-permute-start.27 = (f32[32,2048]{1,0:T(8,128)S(1)}, f32[32,2048]{1,0:T(8,128)S(1)}, u32[]{:S(2)}, u32[]{:S(2)}) collective-permute-start(f32[32,2048]{1,0:T(8,128)S(1)} %get-tuple-element.120), channel_id=1, source_target_pairs={{1,2},{3,4},{5,6},{9,10},{11,12},{13,14},{17,18},{19,20},{21,22},{... | collective-permute-start | bytes 786440 | tf_op jit(solution)/shard_map/ppermute | solution.py:538
  74.5 2.8 %collective-permute-done.27.refs_1_ = f32[32,2048]{1,0:T(8,128)S(1)} collective-permute-done((f32[32,2048]{1,0:T(8,128)S(1)}, f32[32,2048]{1,0:T(8,128)S(1)}, u32[]{:S(2)}, u32[]{:S(2)}) %collective-permute-start.27) | collective-permute-done | bytes 262176 | tf_op jit(solution)/shard_map/ppermute | solution.py:538
  77.2 1.3 %shard_map.60 = f32[2048,128]{1,0:T(8,128)} custom-call(bf16[64,192]{1,0:T(8,128)(2,1)S(1)} %get-tuple-element.67.refs_0_, f32[32,2048]{1,0:T(8,128)S(1)} %collective-permute-done.27.refs_1_, f32[32,2048]{1,0:T(8,128)S(1)} %collective-permute-done.28.refs_2_, f32[64,2048]{1,0:T(8,128)S(1)} %get-tuple-element.127.refs_3_, ...), custom_call_target="tpu_custom_call" | custom-call | flops 1724999936 | tf_op jit(solution)/shard_map/pallas_call | solution.py:663
  (77 shorter events, 8.7 us)
Async XLA Ops:
  1.9 15.7 %collective-permute-start.5 = (f32[48,2048]{1,0:T(8,128)S(1)}, f32[48,2048]{1,0:T(8,128)S(1)}, u32[]{:S(2)}, u32[]{:S(2)}) collective-permute-start(f32[48,2048]{1,0:T(8,128)S(1)} %get-tuple-element.83), channel_id=1, source_target_pairs={{0,24},{8,16},{16,8},{24,0},{1,25},{9,17},{17,9},{25,1},{2,26},{10... | collective-permute-start | bytes 1179656 | tf_op jit(solution)/shard_map/ppermute | solution.py:525
  5.0 18.7 %collective-permute-start.6 = (f32[48,2048]{1,0:T(8,128)S(1)}, f32[48,2048]{1,0:T(8,128)S(1)}, u32[]{:S(2)}, u32[]{:S(2)}) collective-permute-start(f32[48,2048]{1,0:T(8,128)S(1)} %get-tuple-element.84), channel_id=1, source_target_pairs={{0,8},{8,0},{16,24},{24,16},{1,9},{9,1},{17,25},{25,17},{2,10},{10... | collective-permute-start | bytes 1179656 | tf_op jit(solution)/shard_map/ppermute | solution.py:525
  5.2 18.5 %collective-permute-start.7 = (f32[48,2048]{1,0:T(8,128)S(1)}, f32[48,2048]{1,0:T(8,128)S(1)}, u32[]{:S(2)}, u32[]{:S(2)}) collective-permute-start(f32[48,2048]{1,0:T(8,128)S(1)} %get-tuple-element.85), channel_id=1, source_target_pairs={{0,16},{8,24},{16,0},{24,8},{1,17},{9,25},{17,1},{25,9},{2,18},{10... | collective-permute-start | bytes 1179656 | tf_op jit(solution)/shard_map/ppermute | solution.py:525
  5.4 9.1 %collective-permute-start = (f32[32,2048]{1,0:T(8,128)S(1)}, f32[32,2048]{1,0:T(8,128)S(1)}, u32[]{:S(2)}, u32[]{:S(2)}) collective-permute-start(f32[32,2048]{1,0:T(8,128)S(1)} %get-tuple-element.76), channel_id=1, source_target_pairs={{1,2},{3,4},{5,6},{9,10},{11,12},{13,14},{17,18},{19,20},{21,22},{... | collective-permute-start | bytes 786440 | tf_op jit(solution)/shard_map/ppermute | solution.py:538
  10.1 4.3 %collective-permute-start.1 = (f32[32,2048]{1,0:T(8,128)S(1)}, f32[32,2048]{1,0:T(8,128)S(1)}, u32[]{:S(2)}, u32[]{:S(2)}) collective-permute-start(f32[32,2048]{1,0:T(8,128)S(1)} %get-tuple-element.77), channel_id=1, source_target_pairs={{0,1},{2,3},{4,5},{6,7},{8,9},{10,11},{12,13},{14,15},{16,17},{18,... | collective-permute-start | bytes 786440 | tf_op jit(solution)/shard_map/ppermute | solution.py:538
  15.2 13.0 %collective-permute-start.2 = (f32[16,2048]{1,0:T(8,128)S(1)}, f32[16,2048]{1,0:T(8,128)S(1)}, u32[]{:S(2)}, u32[]{:S(2)}) collective-permute-start(f32[16,2048]{1,0:T(8,128)S(1)} %get-tuple-element.79), channel_id=1, source_target_pairs={{0,24},{8,16},{16,8},{24,0},{1,25},{9,17},{17,9},{25,1},{2,26},{10... | collective-permute-start | bytes 393224 | tf_op jit(solution)/shard_map/ppermute | solution.py:525
  17.4 11.2 %collective-permute-start.3 = (f32[16,2048]{1,0:T(8,128)S(1)}, f32[16,2048]{1,0:T(8,128)S(1)}, u32[]{:S(2)}, u32[]{:S(2)}) collective-permute-start(f32[16,2048]{1,0:T(8,128)S(1)} %get-tuple-element.80), channel_id=1, source_target_pairs={{0,8},{8,0},{16,24},{24,16},{1,9},{9,1},{17,25},{25,17},{2,10},{10... | collective-permute-start | bytes 393224 | tf_op jit(solution)/shard_map/ppermute | solution.py:525
  17.6 11.0 %collective-permute-start.4 = (f32[16,2048]{1,0:T(8,128)S(1)}, f32[16,2048]{1,0:T(8,128)S(1)}, u32[]{:S(2)}, u32[]{:S(2)}) collective-permute-start(f32[16,2048]{1,0:T(8,128)S(1)} %get-tuple-element.81), channel_id=1, source_target_pairs={{0,16},{8,24},{16,0},{24,8},{1,17},{9,25},{17,1},{25,9},{2,18},{10... | collective-permute-start | bytes 393224 | tf_op jit(solution)/shard_map/ppermute | solution.py:525
  25.2 7.6 %collective-permute-start.13 = (f32[16,2048]{1,0:T(8,128)S(1)}, f32[16,2048]{1,0:T(8,128)S(1)}, u32[]{:S(2)}, u32[]{:S(2)}) collective-permute-start(f32[16,2048]{1,0:T(8,128)S(1)} %get-tuple-element.95), channel_id=1, source_target_pairs={{0,24},{8,16},{16,8},{24,0},{1,25},{9,17},{17,9},{25,1},{2,26},{10... | collective-permute-start | bytes 393224 | tf_op jit(solution)/shard_map/ppermute | solution.py:525
  25.5 8.4 %collective-permute-start.14 = (f32[16,2048]{1,0:T(8,128)S(1)}, f32[16,2048]{1,0:T(8,128)S(1)}, u32[]{:S(2)}, u32[]{:S(2)}) collective-permute-start(f32[16,2048]{1,0:T(8,128)S(1)} %get-tuple-element.96), channel_id=1, source_target_pairs={{0,8},{8,0},{16,24},{24,16},{1,9},{9,1},{17,25},{25,17},{2,10},{10... | collective-permute-start | bytes 393224 | tf_op jit(solution)/shard_map/ppermute | solution.py:525
  28.2 5.8 %collective-permute-start.15 = (f32[16,2048]{1,0:T(8,128)S(1)}, f32[16,2048]{1,0:T(8,128)S(1)}, u32[]{:S(2)}, u32[]{:S(2)}) collective-permute-start(f32[16,2048]{1,0:T(8,128)S(1)} %get-tuple-element.97), channel_id=1, source_target_pairs={{0,16},{8,24},{16,0},{24,8},{1,17},{9,25},{17,1},{25,9},{2,18},{10... | collective-permute-start | bytes 393224 | tf_op jit(solution)/shard_map/ppermute | solution.py:525
  30.2 9.9 %collective-permute-start.10 = (f32[16,2048]{1,0:T(8,128)S(1)}, f32[16,2048]{1,0:T(8,128)S(1)}, u32[]{:S(2)}, u32[]{:S(2)}) collective-permute-start(f32[16,2048]{1,0:T(8,128)S(1)} %get-tuple-element.89), channel_id=1, source_target_pairs={{0,16},{8,24},{16,0},{24,8},{1,17},{9,25},{17,1},{25,9},{2,18},{10... | collective-permute-start | bytes 393224 | tf_op jit(solution)/shard_map/ppermute | solution.py:525
  31.6 8.4 %collective-permute-start.8 = (f32[16,2048]{1,0:T(8,128)S(1)}, f32[16,2048]{1,0:T(8,128)S(1)}, u32[]{:S(2)}, u32[]{:S(2)}) collective-permute-start(f32[16,2048]{1,0:T(8,128)S(1)} %get-tuple-element.87), channel_id=1, source_target_pairs={{0,24},{8,16},{16,8},{24,0},{1,25},{9,17},{17,9},{25,1},{2,26},{10... | collective-permute-start | bytes 393224 | tf_op jit(solution)/shard_map/ppermute | solution.py:525
  32.8 7.2 %collective-permute-start.9 = (f32[16,2048]{1,0:T(8,128)S(1)}, f32[16,2048]{1,0:T(8,128)S(1)}, u32[]{:S(2)}, u32[]{:S(2)}) collective-permute-start(f32[16,2048]{1,0:T(8,128)S(1)} %get-tuple-element.88), channel_id=1, source_target_pairs={{0,8},{8,0},{16,24},{24,16},{1,9},{9,1},{17,25},{25,17},{2,10},{10... | collective-permute-start | bytes 393224 | tf_op jit(solution)/shard_map/ppermute | solution.py:525
  34.1 9.9 %collective-permute-start.16 = (f32[32,2048]{1,0:T(8,128)S(1)}, f32[32,2048]{1,0:T(8,128)S(1)}, u32[]{:S(2)}, u32[]{:S(2)}) collective-permute-start(f32[32,2048]{1,0:T(8,128)S(1)} %get-tuple-element.98), channel_id=1, source_target_pairs={{1,2},{3,4},{5,6},{9,10},{11,12},{13,14},{17,18},{19,20},{21,22},{... | collective-permute-start | bytes 786440 | tf_op jit(solution)/shard_map/ppermute | solution.py:538
  39.9 4.0 %collective-permute-start.17 = (f32[32,2048]{1,0:T(8,128)S(1)}, f32[32,2048]{1,0:T(8,128)S(1)}, u32[]{:S(2)}, u32[]{:S(2)}) collective-permute-start(f32[32,2048]{1,0:T(8,128)S(1)} %get-tuple-element.99), channel_id=1, source_target_pairs={{0,1},{2,3},{4,5},{6,7},{8,9},{10,11},{12,13},{14,15},{16,17},{18,... | collective-permute-start | bytes 786440 | tf_op jit(solution)/shard_map/ppermute | solution.py:538
  40.2 7.5 %collective-permute-start.11 = (f32[32,2048]{1,0:T(8,128)S(1)}, f32[32,2048]{1,0:T(8,128)S(1)}, u32[]{:S(2)}, u32[]{:S(2)}) collective-permute-start(f32[32,2048]{1,0:T(8,128)S(1)} %get-tuple-element.90), channel_id=1, source_target_pairs={{1,2},{3,4},{5,6},{0,16},{7,23},{9,10},{11,12},{13,14},{8,24},{15,... | collective-permute-start | bytes 786440 | tf_op jit(solution)/shard_map/ppermute | solution.py:538
  43.3 4.4 %collective-permute-start.12 = (f32[32,2048]{1,0:T(8,128)S(1)}, f32[32,2048]{1,0:T(8,128)S(1)}, u32[]{:S(2)}, u32[]{:S(2)}) collective-permute-start(f32[32,2048]{1,0:T(8,128)S(1)} %get-tuple-element.91), channel_id=1, source_target_pairs={{0,1},{2,3},{4,5},{6,7},{8,9},{10,11},{12,13},{14,15},{16,17},{18,... | collective-permute-start | bytes 786440 | tf_op jit(solution)/shard_map/ppermute | solution.py:538
  48.8 5.7 %collective-permute-start.18 = (f32[16,2048]{1,0:T(8,128)S(1)}, f32[16,2048]{1,0:T(8,128)S(1)}, u32[]{:S(2)}, u32[]{:S(2)}) collective-permute-start(f32[16,2048]{1,0:T(8,128)S(1)} %get-tuple-element.103), channel_id=1, source_target_pairs={{0,24},{8,16},{16,8},{24,0},{1,25},{9,17},{17,9},{25,1},{2,26},{10... | collective-permute-start | bytes 393224 | tf_op jit(solution)/shard_map/ppermute | solution.py:525
  50.3 8.5 %collective-permute-start.19 = (f32[16,2048]{1,0:T(8,128)S(1)}, f32[16,2048]{1,0:T(8,128)S(1)}, u32[]{:S(2)}, u32[]{:S(2)}) collective-permute-start(f32[16,2048]{1,0:T(8,128)S(1)} %get-tuple-element.104), channel_id=1, source_target_pairs={{0,8},{8,0},{16,24},{24,16},{1,9},{9,1},{17,25},{25,17},{2,10},{10... | collective-permute-start | bytes 393224 | tf_op jit(solution)/shard_map/ppermute | solution.py:525
  51.3 7.5 %collective-permute-start.20 = (f32[16,2048]{1,0:T(8,128)S(1)}, f32[16,2048]{1,0:T(8,128)S(1)}, u32[]{:S(2)}, u32[]{:S(2)}) collective-permute-start(f32[16,2048]{1,0:T(8,128)S(1)} %get-tuple-element.105), channel_id=1, source_target_pairs={{0,16},{8,24},{16,0},{24,8},{1,17},{9,25},{17,1},{25,9},{2,18},{10... | collective-permute-start | bytes 393224 | tf_op jit(solution)/shard_map/ppermute | solution.py:525
  52.0 10.1 %collective-permute-start.24 = (f32[16,2048]{1,0:T(8,128)S(1)}, f32[16,2048]{1,0:T(8,128)S(1)}, u32[]{:S(2)}, u32[]{:S(2)}) collective-permute-start(f32[16,2048]{1,0:T(8,128)S(1)} %get-tuple-element.115), channel_id=1, source_target_pairs={{0,24},{8,16},{16,8},{24,0},{1,25},{9,17},{17,9},{25,1},{2,26},{10... | collective-permute-start | bytes 393224 | tf_op jit(solution)/shard_map/ppermute | solution.py:525
  53.5 10.1 %collective-permute-start.25 = (f32[16,2048]{1,0:T(8,128)S(1)}, f32[16,2048]{1,0:T(8,128)S(1)}, u32[]{:S(2)}, u32[]{:S(2)}) collective-permute-start(f32[16,2048]{1,0:T(8,128)S(1)} %get-tuple-element.116), channel_id=1, source_target_pairs={{0,8},{8,0},{16,24},{24,16},{1,9},{9,1},{17,25},{25,17},{2,10},{10... | collective-permute-start | bytes 393224 | tf_op jit(solution)/shard_map/ppermute | solution.py:525
  54.5 9.0 %collective-permute-start.26 = (f32[16,2048]{1,0:T(8,128)S(1)}, f32[16,2048]{1,0:T(8,128)S(1)}, u32[]{:S(2)}, u32[]{:S(2)}) collective-permute-start(f32[16,2048]{1,0:T(8,128)S(1)} %get-tuple-element.117), channel_id=1, source_target_pairs={{0,16},{8,24},{16,0},{24,8},{1,17},{9,25},{17,1},{25,9},{2,18},{10... | collective-permute-start | bytes 393224 | tf_op jit(solution)/shard_map/ppermute | solution.py:525
  60.2 7.6 %collective-permute-start.21 = (f32[16,2048]{1,0:T(8,128)S(1)}, f32[16,2048]{1,0:T(8,128)S(1)}, u32[]{:S(2)}, u32[]{:S(2)}) collective-permute-start(f32[16,2048]{1,0:T(8,128)S(1)} %get-tuple-element.108), channel_id=1, source_target_pairs={{0,24},{8,16},{16,8},{24,0},{1,25},{9,17},{17,9},{25,1},{2,26},{10... | collective-permute-start | bytes 393224 | tf_op jit(solution)/shard_map/ppermute | solution.py:525
  62.1 6.3 %collective-permute-start.22 = (f32[16,2048]{1,0:T(8,128)S(1)}, f32[16,2048]{1,0:T(8,128)S(1)}, u32[]{:S(2)}, u32[]{:S(2)}) collective-permute-start(f32[16,2048]{1,0:T(8,128)S(1)} %get-tuple-element.109), channel_id=1, source_target_pairs={{0,8},{8,0},{16,24},{24,16},{1,9},{9,1},{17,25},{25,17},{2,10},{10... | collective-permute-start | bytes 393224 | tf_op jit(solution)/shard_map/ppermute | solution.py:525
  62.1 6.3 %collective-permute-start.23 = (f32[16,2048]{1,0:T(8,128)S(1)}, f32[16,2048]{1,0:T(8,128)S(1)}, u32[]{:S(2)}, u32[]{:S(2)}) collective-permute-start(f32[16,2048]{1,0:T(8,128)S(1)} %get-tuple-element.110), channel_id=1, source_target_pairs={{0,16},{8,24},{16,0},{24,8},{1,17},{9,25},{17,1},{25,9},{2,18},{10... | collective-permute-start | bytes 393224 | tf_op jit(solution)/shard_map/ppermute | solution.py:525
  65.7 7.6 %collective-permute-start.29 = (f32[16,2048]{1,0:T(8,128)S(1)}, f32[16,2048]{1,0:T(8,128)S(1)}, u32[]{:S(2)}, u32[]{:S(2)}) collective-permute-start(f32[16,2048]{1,0:T(8,128)S(1)} %get-tuple-element.124), channel_id=1, source_target_pairs={{0,24},{8,16},{16,8},{24,0},{1,25},{9,17},{17,9},{25,1},{2,26},{10... | collective-permute-start | bytes 393224 | tf_op jit(solution)/shard_map/ppermute | solution.py:525
  67.3 6.6 %collective-permute-start.30 = (f32[16,2048]{1,0:T(8,128)S(1)}, f32[16,2048]{1,0:T(8,128)S(1)}, u32[]{:S(2)}, u32[]{:S(2)}) collective-permute-start(f32[16,2048]{1,0:T(8,128)S(1)} %get-tuple-element.125), channel_id=1, source_target_pairs={{0,8},{8,0},{16,24},{24,16},{1,9},{9,1},{17,25},{25,17},{2,10},{10... | collective-permute-start | bytes 393224 | tf_op jit(solution)/shard_map/ppermute | solution.py:525
  67.9 6.0 %collective-permute-start.31 = (f32[16,2048]{1,0:T(8,128)S(1)}, f32[16,2048]{1,0:T(8,128)S(1)}, u32[]{:S(2)}, u32[]{:S(2)}) collective-permute-start(f32[16,2048]{1,0:T(8,128)S(1)} %get-tuple-element.126), channel_id=1, source_target_pairs={{0,16},{8,24},{16,0},{24,8},{1,17},{9,25},{17,1},{25,9},{2,18},{10... | collective-permute-start | bytes 393224 | tf_op jit(solution)/shard_map/ppermute | solution.py:525
  68.5 8.7 %collective-permute-start.27 = (f32[32,2048]{1,0:T(8,128)S(1)}, f32[32,2048]{1,0:T(8,128)S(1)}, u32[]{:S(2)}, u32[]{:S(2)}) collective-permute-start(f32[32,2048]{1,0:T(8,128)S(1)} %get-tuple-element.120), channel_id=1, source_target_pairs={{1,2},{3,4},{5,6},{9,10},{11,12},{13,14},{17,18},{19,20},{21,22},{... | collective-permute-start | bytes 786440 | tf_op jit(solution)/shard_map/ppermute | solution.py:538
  73.2 4.0 %collective-permute-start.28 = (f32[32,2048]{1,0:T(8,128)S(1)}, f32[32,2048]{1,0:T(8,128)S(1)}, u32[]{:S(2)}, u32[]{:S(2)}) collective-permute-start(f32[32,2048]{1,0:T(8,128)S(1)} %get-tuple-element.121), channel_id=1, source_target_pairs={{0,1},{2,3},{4,5},{6,7},{8,9},{10,11},{12,13},{14,15},{16,17},{18,... | collective-permute-start | bytes 786440 | tf_op jit(solution)/shard_map/ppermute | solution.py:538
  (15 other events, 123.6 us)

commit v8 on v7

--- a/solution.py
+++ b/solution.py
@@ -398,12 +398,12 @@
     pieces = sems.shape[0]
     piece = length // pieces
     copies = []
-    for at in range(0, length, STEP):
-        here = slice(at, at + STEP)
+    for at in range(0, length, STEP // 2):
+        here = slice(at, at + STEP // 2)
         sides = assembled([], odd, [], [(other_ref, sibling_ref)], here)
         outer = rows_of(estimate_ref[:, here], edges) * (outer_ref[:, here] + left_product(back_ref[...], sides))
         estimate = jnp.concatenate([outer[:radius], inner_ref[:, here], outer[radius:]], axis=0)
-        for tile in range(0, STEP, LANES):
+        for tile in range(0, STEP // 2, LANES):
             out_ref[at + tile : at + tile + LANES, :] = jnp.transpose(estimate[:, tile : tile + LANES])
             if (at + tile + LANES) % piece == 0:
                 k = (at + tile) // piece
@@ -665,7 +665,7 @@
         functools.partial(last_late_kernel, radius, count),
         shaped(length, columns),
         [VMEM] * 6,
-        [pltpu.VMEM((length, columns), F32), pltpu.SemaphoreType.DMA((pieces,))],
+        [pltpu.VMEM((length, columns), F32), pltpu.SemaphoreType.DMA((2 * pieces,))],
         HBM,
     )(end_late, *sides, *partial, estimate)
     return out.reshape(planes, rows, columns)

time: 78.8 us -> 78.8 us (level)
  no operation moved by 1% of the time
where the time goes in v8:
time: 78.8 us; the launch traced here: 78.5 us
  starting transfers between devices  42.2 us (54%)
  waiting for transfers between devices  19.9 us (25%)
  Pallas kernels  14.6 us (19%)
  local copies, waits for them, and re-layouts  1.64 us (2%)
    ppermute x24, starting transfers between devices, exchanged(): result.append(lax.ppermute(value, ('gz', 'bx'), pairs))  23.5 us
    ppermute x8, starting transfers between devices, from_sides(): lax.ppermute(value, ('gz', 'bx', 'by'), pairs + [(j, i) for i, j in pairs])  18.7 us
    ppermute x24, waiting for transfers between devices, exchanged(): result.append(lax.ppermute(value, ('gz', 'bx'), pairs))  11.8 us
    ppermute x8, waiting for transfers between devices, from_sides(): lax.ppermute(value, ('gz', 'bx', 'by'), pairs + [(j, i) for i, j in pairs])  8.08 us
    pallas_call x4, Pallas kernels, through_planes(): call(50, functools.partial(planes_kernel, sizes, first, seen_first), [sha...  5.75 us
    pallas_call x1, Pallas kernels, per_device(): call(1.3, functools.partial(start_kernel, parts, radius, count), [shaped(...  1.92 us
    unnamed x30, local copies, waits for them, and re-layouts  1.64 us
  transfers between devices with their start and end apart: 32, of which 10 were waited for; matrix products, arithmetic and copies ran while one was open for 0% of the time, Pallas kernels for 13%

profile of v8, /device:TPU:1, one launch (start us, length us, event | category | flops | bytes accessed | tf_op | source)
XLA Modules:
  0.0 78.5 jit_solution(2135285372055869279)
XLA Ops:
  0.0 1.9 %shard_map.47 = (f32[128,2048]{1,0:T(8,128)S(1)}, f32[32,2048]{1,0:T(8,128)S(1)}, f32[32,2048]{1,0:T(8,128)S(1)}, f32[48,2048]{1,0:T(8,128)S(1)}, f32[48,2048]{1...) custom-call(f32[1,65]{1,0:T(1,128)} %bitcast.7, f32[2048,128]{1,0:T(8,128)} %bitcast.9), custom_call_target="tpu_custom_call" | custom-call | flops 1495000064 | tf_op jit(solution)/shard_map/pallas_call | solution.py:546
  1.9 3.1 %collective-permute-start.5 = (f32[48,2048]{1,0:T(8,128)S(1)}, f32[48,2048]{1,0:T(8,128)S(1)}, u32[]{:S(2)}, u32[]{:S(2)}) collective-permute-start(f32[48,2048]{1,0:T(8,128)S(1)} %get-tuple-element.83), channel_id=1, source_target_pairs={{0,24},{8,16},{16,8},{24,0},{1,25},{9,17},{17,9},{25,1},{2,26},{10... | collective-permute-start | bytes 1179656 | tf_op jit(solution)/shard_map/ppermute | solution.py:525
  5.4 4.7 %collective-permute-start = (f32[32,2048]{1,0:T(8,128)S(1)}, f32[32,2048]{1,0:T(8,128)S(1)}, u32[]{:S(2)}, u32[]{:S(2)}) collective-permute-start(f32[32,2048]{1,0:T(8,128)S(1)} %get-tuple-element.76), channel_id=1, source_target_pairs={{1,2},{3,4},{5,6},{9,10},{11,12},{13,14},{17,18},{19,20},{21,22},{... | collective-permute-start | bytes 786440 | tf_op jit(solution)/shard_map/ppermute | solution.py:538
  10.9 0.9 %shard_map.46 = (bf16[64,576]{1,0:T(8,128)(2,1)S(1)}, bf16[192,576]{1,0:T(8,128)(2,1)S(1)}, bf16[128,192]{1,0:T(8,128)(2,1)S(1)}, bf16[128,192]{1,0:T(8,128)(2,1...) custom-call(f32[1,65]{1,0:T(1,128)S(1)} %bitcast.5, ...), custom_call_target="tpu_custom_call" | custom-call | flops 920000000 | tf_op jit(solution)/shard_map/pallas_call | solution.py:565
  11.8 2.6 %collective-permute-done.refs_2_.refs_7_ = f32[32,2048]{1,0:T(8,128)S(1)} collective-permute-done((f32[32,2048]{1,0:T(8,128)S(1)}, f32[32,2048]{1,0:T(8,128)S(1)}, u32[]{:S(2)}, u32[]{:S(2)}) %collective-permute-start) | collective-permute-done | bytes 262176 | tf_op jit(solution)/shard_map/ppermute | solution.py:538
  15.2 2.2 %collective-permute-start.2 = (f32[16,2048]{1,0:T(8,128)S(1)}, f32[16,2048]{1,0:T(8,128)S(1)}, u32[]{:S(2)}, u32[]{:S(2)}) collective-permute-start(f32[16,2048]{1,0:T(8,128)S(1)} %get-tuple-element.79), channel_id=1, source_target_pairs={{0,24},{8,16},{16,8},{24,0},{1,25},{9,17},{17,9},{25,1},{2,26},{10... | collective-permute-start | bytes 393224 | tf_op jit(solution)/shard_map/ppermute | solution.py:525
  17.9 5.8 %collective-permute-done.6.refs_10_.refs_6_ = f32[48,2048]{1,0:T(8,128)S(1)} collective-permute-done((f32[48,2048]{1,0:T(8,128)S(1)}, f32[48,2048]{1,0:T(8,128)S(1)}, u32[]{:S(2)}, u32[]{:S(2)}) %collective-permute-start.6) | collective-permute-done | bytes 393248 | tf_op jit(solution)/shard_map/ppermute | solution.py:525
  23.7 1.5 %shard_map.51 = (f32[16,2048]{1,0:T(8,128)S(1)}, f32[16,2048]{1,0:T(8,128)S(1)}, f32[16,2048]{1,0:T(8,128)S(1)}, f32[16,2048]{1,0:T(8,128)S(1)}, f32[1,1040,128]{2,1,0:T(8,128)S(1)}) custom-call(bf16[768,256]{1,0:T(8,128)(2,1)S(1)} %get-tuple-element.68.refs_0_, bf16[768,256]{1,0:T(8,128)(2,1)S(1)} %get-tuple-element.69.refs_1_, ...), custom_call_target="tpu_custom_call" | custom-call | flops 57500000256 | tf_op jit(solution)/shard_map/pallas_call | solution.py:598
  25.5 2.7 %collective-permute-start.14 = (f32[16,2048]{1,0:T(8,128)S(1)}, f32[16,2048]{1,0:T(8,128)S(1)}, u32[]{:S(2)}, u32[]{:S(2)}) collective-permute-start(f32[16,2048]{1,0:T(8,128)S(1)} %get-tuple-element.96), channel_id=1, source_target_pairs={{0,8},{8,0},{16,24},{24,16},{1,9},{9,1},{17,25},{25,17},{2,10},{10... | collective-permute-start | bytes 393224 | tf_op jit(solution)/shard_map/ppermute | solution.py:525
  28.6 1.5 %shard_map.49 = (f32[16,2048]{1,0:T(8,128)S(1)}, f32[16,2048]{1,0:T(8,128)S(1)}, f32[16,2048]{1,0:T(8,128)S(1)}, f32[16,2048]{1,0:T(8,128)S(1)}, f32[1,1040,128]{2,1,0:T(8,128)S(1)}) custom-call(bf16[768,256]{1,0:T(8,128)(2,1)S(1)} %get-tuple-element.68.refs_0_, bf16[768,256]{1,0:T(8,128)(2,1)S(1)} %get-tuple-element.69.refs_1_, ...), custom_call_target="tpu_custom_call" | custom-call | flops 57500000256 | tf_op jit(solution)/shard_map/pallas_call | solution.py:598
  30.2 1.5 %collective-permute-start.10 = (f32[16,2048]{1,0:T(8,128)S(1)}, f32[16,2048]{1,0:T(8,128)S(1)}, u32[]{:S(2)}, u32[]{:S(2)}) collective-permute-start(f32[16,2048]{1,0:T(8,128)S(1)} %get-tuple-element.89), channel_id=1, source_target_pairs={{0,16},{8,24},{16,0},{24,8},{1,17},{9,25},{17,1},{25,9},{2,18},{10... | collective-permute-start | bytes 393224 | tf_op jit(solution)/shard_map/ppermute | solution.py:525
  31.6 1.2 %collective-permute-start.8 = (f32[16,2048]{1,0:T(8,128)S(1)}, f32[16,2048]{1,0:T(8,128)S(1)}, u32[]{:S(2)}, u32[]{:S(2)}) collective-permute-start(f32[16,2048]{1,0:T(8,128)S(1)} %get-tuple-element.87), channel_id=1, source_target_pairs={{0,24},{8,16},{16,8},{24,0},{1,25},{9,17},{17,9},{25,1},{2,26},{10... | collective-permute-start | bytes 393224 | tf_op jit(solution)/shard_map/ppermute | solution.py:525
  32.9 1.1 %collective-permute-done.14.refs_2_.refs_8_ = f32[16,2048]{1,0:T(8,128)S(1)} collective-permute-done((f32[16,2048]{1,0:T(8,128)S(1)}, f32[16,2048]{1,0:T(8,128)S(1)}, u32[]{:S(2)}, u32[]{:S(2)}) %collective-permute-start.14) | collective-permute-done | bytes 131104 | tf_op jit(solution)/shard_map/ppermute | solution.py:525
  34.1 5.8 %collective-permute-start.16 = (f32[32,2048]{1,0:T(8,128)S(1)}, f32[32,2048]{1,0:T(8,128)S(1)}, u32[]{:S(2)}, u32[]{:S(2)}) collective-permute-start(f32[32,2048]{1,0:T(8,128)S(1)} %get-tuple-element.98), channel_id=1, source_target_pairs={{1,2},{3,4},{5,6},{9,10},{11,12},{13,14},{17,18},{19,20},{21,22},{... | collective-permute-start | bytes 786440 | tf_op jit(solution)/shard_map/ppermute | solution.py:538
  40.2 3.1 %collective-permute-start.11 = (f32[32,2048]{1,0:T(8,128)S(1)}, f32[32,2048]{1,0:T(8,128)S(1)}, u32[]{:S(2)}, u32[]{:S(2)}) collective-permute-start(f32[32,2048]{1,0:T(8,128)S(1)} %get-tuple-element.90), channel_id=1, source_target_pairs={{1,2},{3,4},{5,6},{0,16},{7,23},{9,10},{11,12},{13,14},{8,24},{15,... | collective-permute-start | bytes 786440 | tf_op jit(solution)/shard_map/ppermute | solution.py:538
  44.0 1.5 %shard_map.53 = (f32[128,2048]{1,0:T(8,128)S(1)}, f32[64,2048]{1,0:T(8,128)S(1)}, f32[128,2048]{1,0:T(8,128)S(1)}) custom-call(bf16[192,576]{1,0:T(8,128)(2,1)S(1)} %get-tuple-element.92.refs_0_, bf16[128,192]{1,0:T(8,128)(2,1)S(1)} %get-tuple-element.93.refs_1_, f32[16,2048]{1,0:T(8,128)S(1)} %get-tuple-element.86.refs_0_.refs_4_.refs_2_, ...), custom_call_target="tpu_custom_call" | custom-call | flops 2529999872 | tf_op jit(solution)/shard_map/pallas_call | solution.py:630
  45.5 2.2 %collective-permute-done.11.refs_2_ = f32[32,2048]{1,0:T(8,128)S(1)} collective-permute-done((f32[32,2048]{1,0:T(8,128)S(1)}, f32[32,2048]{1,0:T(8,128)S(1)}, u32[]{:S(2)}, u32[]{:S(2)}) %collective-permute-start.11) | collective-permute-done | bytes 262176 | tf_op jit(solution)/shard_map/ppermute | solution.py:538
  47.7 1.1 %shard_map.54 = (f32[128,2048]{1,0:T(8,128)S(1)}, f32[16,2048]{1,0:T(8,128)S(1)}, f32[16,2048]{1,0:T(8,128)S(1)}, f32[16,2048]{1,0:T(8,128)S(1)}, f32[16,2048]{1,0:T(8,128)S(1)}) custom-call(bf16[128,192]{1,0:T(8,128)(2,1)S(1)} %get-tuple-element.72.refs_0_, bf16[64,384]{1,0:T(8,128)(2,1)S(1)} %get-tuple-element.73.refs_1_, ...), custom_call_target="tpu_custom_call" | custom-call | flops 920000000 | tf_op jit(solution)/shard_map/pallas_call | solution.py:637
  48.8 1.5 %collective-permute-start.18 = (f32[16,2048]{1,0:T(8,128)S(1)}, f32[16,2048]{1,0:T(8,128)S(1)}, u32[]{:S(2)}, u32[]{:S(2)}) collective-permute-start(f32[16,2048]{1,0:T(8,128)S(1)} %get-tuple-element.103), channel_id=1, source_target_pairs={{0,24},{8,16},{16,8},{24,0},{1,25},{9,17},{17,9},{25,1},{2,26},{10... | collective-permute-start | bytes 393224 | tf_op jit(solution)/shard_map/ppermute | solution.py:525
  50.3 1.0 %collective-permute-start.19 = (f32[16,2048]{1,0:T(8,128)S(1)}, f32[16,2048]{1,0:T(8,128)S(1)}, u32[]{:S(2)}, u32[]{:S(2)}) collective-permute-start(f32[16,2048]{1,0:T(8,128)S(1)} %get-tuple-element.104), channel_id=1, source_target_pairs={{0,8},{8,0},{16,24},{24,16},{1,9},{9,1},{17,25},{25,17},{2,10},{10... | collective-permute-start | bytes 393224 | tf_op jit(solution)/shard_map/ppermute | solution.py:525
  52.0 1.5 %collective-permute-start.24 = (f32[16,2048]{1,0:T(8,128)S(1)}, f32[16,2048]{1,0:T(8,128)S(1)}, u32[]{:S(2)}, u32[]{:S(2)}) collective-permute-start(f32[16,2048]{1,0:T(8,128)S(1)} %get-tuple-element.115), channel_id=1, source_target_pairs={{0,24},{8,16},{16,8},{24,0},{1,25},{9,17},{17,9},{25,1},{2,26},{10... | collective-permute-start | bytes 393224 | tf_op jit(solution)/shard_map/ppermute | solution.py:525
  53.5 1.0 %collective-permute-start.25 = (f32[16,2048]{1,0:T(8,128)S(1)}, f32[16,2048]{1,0:T(8,128)S(1)}, u32[]{:S(2)}, u32[]{:S(2)}) collective-permute-start(f32[16,2048]{1,0:T(8,128)S(1)} %get-tuple-element.116), channel_id=1, source_target_pairs={{0,8},{8,0},{16,24},{24,16},{1,9},{9,1},{17,25},{25,17},{2,10},{10... | collective-permute-start | bytes 393224 | tf_op jit(solution)/shard_map/ppermute | solution.py:525
  54.5 1.0 %collective-permute-start.26 = (f32[16,2048]{1,0:T(8,128)S(1)}, f32[16,2048]{1,0:T(8,128)S(1)}, u32[]{:S(2)}, u32[]{:S(2)}) collective-permute-start(f32[16,2048]{1,0:T(8,128)S(1)} %get-tuple-element.117), channel_id=1, source_target_pairs={{0,16},{8,24},{16,0},{24,8},{1,17},{9,25},{17,1},{25,9},{2,18},{10... | collective-permute-start | bytes 393224 | tf_op jit(solution)/shard_map/ppermute | solution.py:525
  55.6 3.3 %collective-permute-done.19.refs_6_ = f32[16,2048]{1,0:T(8,128)S(1)} collective-permute-done((f32[16,2048]{1,0:T(8,128)S(1)}, f32[16,2048]{1,0:T(8,128)S(1)}, u32[]{:S(2)}, u32[]{:S(2)}) %collective-permute-start.19) | collective-permute-done | bytes 131104 | tf_op jit(solution)/shard_map/ppermute | solution.py:525
  58.8 1.4 %shard_map.55 = (f32[16,2048]{1,0:T(8,128)S(1)}, f32[16,2048]{1,0:T(8,128)S(1)}, f32[16,2048]{1,0:T(8,128)S(1)}, f32[16,2048]{1,0:T(8,128)S(1)}) custom-call(bf16[768,256]{1,0:T(8,128)(2,1)S(1)} %copy-done.10, bf16[768,256]{1,0:T(8,128)(2,1)S(1)} %copy-done.12, bf16[64,192]{1,0:T(8,128)(2,1)S(1)} %get-tuple-element.70.refs_2_, ...), custom_call_target="tpu_custom_call" | custom-call | flops 57500000256 | tf_op jit(solution)/shard_map/pallas_call | solution.py:598
  60.2 1.9 %collective-permute-start.21 = (f32[16,2048]{1,0:T(8,128)S(1)}, f32[16,2048]{1,0:T(8,128)S(1)}, u32[]{:S(2)}, u32[]{:S(2)}) collective-permute-start(f32[16,2048]{1,0:T(8,128)S(1)} %get-tuple-element.108), channel_id=1, source_target_pairs={{0,24},{8,16},{16,8},{24,0},{1,25},{9,17},{17,9},{25,1},{2,26},{10... | collective-permute-start | bytes 393224 | tf_op jit(solution)/shard_map/ppermute | solution.py:525
  62.1 0.8 %collective-permute-start.23 = (f32[16,2048]{1,0:T(8,128)S(1)}, f32[16,2048]{1,0:T(8,128)S(1)}, u32[]{:S(2)}, u32[]{:S(2)}) collective-permute-start(f32[16,2048]{1,0:T(8,128)S(1)} %get-tuple-element.110), channel_id=1, source_target_pairs={{0,16},{8,24},{16,0},{24,8},{1,17},{9,25},{17,1},{25,9},{2,18},{10... | collective-permute-start | bytes 393224 | tf_op jit(solution)/shard_map/ppermute | solution.py:525
  64.3 1.4 %shard_map.57 = (f32[16,2048]{1,0:T(8,128)S(1)}, f32[16,2048]{1,0:T(8,128)S(1)}, f32[16,2048]{1,0:T(8,128)S(1)}, f32[16,2048]{1,0:T(8,128)S(1)}) custom-call(bf16[768,256]{1,0:T(8,128)(2,1)S(1)} %copy-done.10, bf16[768,256]{1,0:T(8,128)(2,1)S(1)} %copy-done.12, bf16[64,192]{1,0:T(8,128)(2,1)S(1)} %get-tuple-element.70.refs_2_, ...), custom_call_target="tpu_custom_call" | custom-call | flops 57500000256 | tf_op jit(solution)/shard_map/pallas_call | solution.py:598
  65.7 1.6 %collective-permute-start.29 = (f32[16,2048]{1,0:T(8,128)S(1)}, f32[16,2048]{1,0:T(8,128)S(1)}, u32[]{:S(2)}, u32[]{:S(2)}) collective-permute-start(f32[16,2048]{1,0:T(8,128)S(1)} %get-tuple-element.124), channel_id=1, source_target_pairs={{0,24},{8,16},{16,8},{24,0},{1,25},{9,17},{17,9},{25,1},{2,26},{10... | collective-permute-start | bytes 393224 | tf_op jit(solution)/shard_map/ppermute | solution.py:525
  68.5 4.7 %collective-permute-start.27 = (f32[32,2048]{1,0:T(8,128)S(1)}, f32[32,2048]{1,0:T(8,128)S(1)}, u32[]{:S(2)}, u32[]{:S(2)}) collective-permute-start(f32[32,2048]{1,0:T(8,128)S(1)} %get-tuple-element.120), channel_id=1, source_target_pairs={{1,2},{3,4},{5,6},{9,10},{11,12},{13,14},{17,18},{19,20},{21,22},{... | collective-permute-start | bytes 786440 | tf_op jit(solution)/shard_map/ppermute | solution.py:538
  74.5 2.8 %collective-permute-done.27.refs_1_ = f32[32,2048]{1,0:T(8,128)S(1)} collective-permute-done((f32[32,2048]{1,0:T(8,128)S(1)}, f32[32,2048]{1,0:T(8,128)S(1)}, u32[]{:S(2)}, u32[]{:S(2)}) %collective-permute-start.27) | collective-permute-done | bytes 262176 | tf_op jit(solution)/shard_map/ppermute | solution.py:538
  77.2 1.3 %shard_map.60 = f32[2048,128]{1,0:T(8,128)} custom-call(bf16[64,192]{1,0:T(8,128)(2,1)S(1)} %get-tuple-element.67.refs_0_, f32[32,2048]{1,0:T(8,128)S(1)} %collective-permute-done.27.refs_1_, f32[32,2048]{1,0:T(8,128)S(1)} %collective-permute-done.28.refs_2_, f32[64,2048]{1,0:T(8,128)S(1)} %get-tuple-element.127.refs_3_, ...), custom_call_target="tpu_custom_call" | custom-call | flops 1724999936 | tf_op jit(solution)/shard_map/pallas_call | solution.py:663
  (77 shorter events, 8.7 us)
Async XLA Ops:
  1.9 15.7 %collective-permute-start.5 = (f32[48,2048]{1,0:T(8,128)S(1)}, f32[48,2048]{1,0:T(8,128)S(1)}, u32[]{:S(2)}, u32[]{:S(2)}) collective-permute-start(f32[48,2048]{1,0:T(8,128)S(1)} %get-tuple-element.83), channel_id=1, source_target_pairs={{0,24},{8,16},{16,8},{24,0},{1,25},{9,17},{17,9},{25,1},{2,26},{10... | collective-permute-start | bytes 1179656 | tf_op jit(solution)/shard_map/ppermute | solution.py:525
  5.0 18.7 %collective-permute-start.6 = (f32[48,2048]{1,0:T(8,128)S(1)}, f32[48,2048]{1,0:T(8,128)S(1)}, u32[]{:S(2)}, u32[]{:S(2)}) collective-permute-start(f32[48,2048]{1,0:T(8,128)S(1)} %get-tuple-element.84), channel_id=1, source_target_pairs={{0,8},{8,0},{16,24},{24,16},{1,9},{9,1},{17,25},{25,17},{2,10},{10... | collective-permute-start | bytes 1179656 | tf_op jit(solution)/shard_map/ppermute | solution.py:525
  5.2 18.5 %collective-permute-start.7 = (f32[48,2048]{1,0:T(8,128)S(1)}, f32[48,2048]{1,0:T(8,128)S(1)}, u32[]{:S(2)}, u32[]{:S(2)}) collective-permute-start(f32[48,2048]{1,0:T(8,128)S(1)} %get-tuple-element.85), channel_id=1, source_target_pairs={{0,16},{8,24},{16,0},{24,8},{1,17},{9,25},{17,1},{25,9},{2,18},{10... | collective-permute-start | bytes 1179656 | tf_op jit(solution)/shard_map/ppermute | solution.py:525
  5.4 9.1 %collective-permute-start = (f32[32,2048]{1,0:T(8,128)S(1)}, f32[32,2048]{1,0:T(8,128)S(1)}, u32[]{:S(2)}, u32[]{:S(2)}) collective-permute-start(f32[32,2048]{1,0:T(8,128)S(1)} %get-tuple-element.76), channel_id=1, source_target_pairs={{1,2},{3,4},{5,6},{9,10},{11,12},{13,14},{17,18},{19,20},{21,22},{... | collective-permute-start | bytes 786440 | tf_op jit(solution)/shard_map/ppermute | solution.py:538
  10.1 4.3 %collective-permute-start.1 = (f32[32,2048]{1,0:T(8,128)S(1)}, f32[32,2048]{1,0:T(8,128)S(1)}, u32[]{:S(2)}, u32[]{:S(2)}) collective-permute-start(f32[32,2048]{1,0:T(8,128)S(1)} %get-tuple-element.77), channel_id=1, source_target_pairs={{0,1},{2,3},{4,5},{6,7},{8,9},{10,11},{12,13},{14,15},{16,17},{18,... | collective-permute-start | bytes 786440 | tf_op jit(solution)/shard_map/ppermute | solution.py:538
  15.2 13.0 %collective-permute-start.2 = (f32[16,2048]{1,0:T(8,128)S(1)}, f32[16,2048]{1,0:T(8,128)S(1)}, u32[]{:S(2)}, u32[]{:S(2)}) collective-permute-start(f32[16,2048]{1,0:T(8,128)S(1)} %get-tuple-element.79), channel_id=1, source_target_pairs={{0,24},{8,16},{16,8},{24,0},{1,25},{9,17},{17,9},{25,1},{2,26},{10... | collective-permute-start | bytes 393224 | tf_op jit(solution)/shard_map/ppermute | solution.py:525
  17.4 11.2 %collective-permute-start.3 = (f32[16,2048]{1,0:T(8,128)S(1)}, f32[16,2048]{1,0:T(8,128)S(1)}, u32[]{:S(2)}, u32[]{:S(2)}) collective-permute-start(f32[16,2048]{1,0:T(8,128)S(1)} %get-tuple-element.80), channel_id=1, source_target_pairs={{0,8},{8,0},{16,24},{24,16},{1,9},{9,1},{17,25},{25,17},{2,10},{10... | collective-permute-start | bytes 393224 | tf_op jit(solution)/shard_map/ppermute | solution.py:525
  17.6 11.0 %collective-permute-start.4 = (f32[16,2048]{1,0:T(8,128)S(1)}, f32[16,2048]{1,0:T(8,128)S(1)}, u32[]{:S(2)}, u32[]{:S(2)}) collective-permute-start(f32[16,2048]{1,0:T(8,128)S(1)} %get-tuple-element.81), channel_id=1, source_target_pairs={{0,16},{8,24},{16,0},{24,8},{1,17},{9,25},{17,1},{25,9},{2,18},{10... | collective-permute-start | bytes 393224 | tf_op jit(solution)/shard_map/ppermute | solution.py:525
  25.2 7.6 %collective-permute-start.13 = (f32[16,2048]{1,0:T(8,128)S(1)}, f32[16,2048]{1,0:T(8,128)S(1)}, u32[]{:S(2)}, u32[]{:S(2)}) collective-permute-start(f32[16,2048]{1,0:T(8,128)S(1)} %get-tuple-element.95), channel_id=1, source_target_pairs={{0,24},{8,16},{16,8},{24,0},{1,25},{9,17},{17,9},{25,1},{2,26},{10... | collective-permute-start | bytes 393224 | tf_op jit(solution)/shard_map/ppermute | solution.py:525
  25.5 8.4 %collective-permute-start.14 = (f32[16,2048]{1,0:T(8,128)S(1)}, f32[16,2048]{1,0:T(8,128)S(1)}, u32[]{:S(2)}, u32[]{:S(2)}) collective-permute-start(f32[16,2048]{1,0:T(8,128)S(1)} %get-tuple-element.96), channel_id=1, source_target_pairs={{0,8},{8,0},{16,24},{24,16},{1,9},{9,1},{17,25},{25,17},{2,10},{10... | collective-permute-start | bytes 393224 | tf_op jit(solution)/shard_map/ppermute | solution.py:525
  28.2 5.8 %collective-permute-start.15 = (f32[16,2048]{1,0:T(8,128)S(1)}, f32[16,2048]{1,0:T(8,128)S(1)}, u32[]{:S(2)}, u32[]{:S(2)}) collective-permute-start(f32[16,2048]{1,0:T(8,128)S(1)} %get-tuple-element.97), channel_id=1, source_target_pairs={{0,16},{8,24},{16,0},{24,8},{1,17},{9,25},{17,1},{25,9},{2,18},{10... | collective-permute-start | bytes 393224 | tf_op jit(solution)/shard_map/ppermute | solution.py:525
  30.2 9.9 %collective-permute-start.10 = (f32[16,2048]{1,0:T(8,128)S(1)}, f32[16,2048]{1,0:T(8,128)S(1)}, u32[]{:S(2)}, u32[]{:S(2)}) collective-permute-start(f32[16,2048]{1,0:T(8,128)S(1)} %get-tuple-element.89), channel_id=1, source_target_pairs={{0,16},{8,24},{16,0},{24,8},{1,17},{9,25},{17,1},{25,9},{2,18},{10... | collective-permute-start | bytes 393224 | tf_op jit(solution)/shard_map/ppermute | solution.py:525
  31.6 8.4 %collective-permute-start.8 = (f32[16,2048]{1,0:T(8,128)S(1)}, f32[16,2048]{1,0:T(8,128)S(1)}, u32[]{:S(2)}, u32[]{:S(2)}) collective-permute-start(f32[16,2048]{1,0:T(8,128)S(1)} %get-tuple-element.87), channel_id=1, source_target_pairs={{0,24},{8,16},{16,8},{24,0},{1,25},{9,17},{17,9},{25,1},{2,26},{10... | collective-permute-start | bytes 393224 | tf_op jit(solution)/shard_map/ppermute | solution.py:525
  32.8 7.2 %collective-permute-start.9 = (f32[16,2048]{1,0:T(8,128)S(1)}, f32[16,2048]{1,0:T(8,128)S(1)}, u32[]{:S(2)}, u32[]{:S(2)}) collective-permute-start(f32[16,2048]{1,0:T(8,128)S(1)} %get-tuple-element.88), channel_id=1, source_target_pairs={{0,8},{8,0},{16,24},{24,16},{1,9},{9,1},{17,25},{25,17},{2,10},{10... | collective-permute-start | bytes 393224 | tf_op jit(solution)/shard_map/ppermute | solution.py:525
  34.1 9.9 %collective-permute-start.16 = (f32[32,2048]{1,0:T(8,128)S(1)}, f32[32,2048]{1,0:T(8,128)S(1)}, u32[]{:S(2)}, u32[]{:S(2)}) collective-permute-start(f32[32,2048]{1,0:T(8,128)S(1)} %get-tuple-element.98), channel_id=1, source_target_pairs={{1,2},{3,4},{5,6},{9,10},{11,12},{13,14},{17,18},{19,20},{21,22},{... | collective-permute-start | bytes 786440 | tf_op jit(solution)/shard_map/ppermute | solution.py:538
  39.9 4.0 %collective-permute-start.17 = (f32[32,2048]{1,0:T(8,128)S(1)}, f32[32,2048]{1,0:T(8,128)S(1)}, u32[]{:S(2)}, u32[]{:S(2)}) collective-permute-start(f32[32,2048]{1,0:T(8,128)S(1)} %get-tuple-element.99), channel_id=1, source_target_pairs={{0,1},{2,3},{4,5},{6,7},{8,9},{10,11},{12,13},{14,15},{16,17},{18,... | collective-permute-start | bytes 786440 | tf_op jit(solution)/shard_map/ppermute | solution.py:538
  40.2 7.5 %collective-permute-start.11 = (f32[32,2048]{1,0:T(8,128)S(1)}, f32[32,2048]{1,0:T(8,128)S(1)}, u32[]{:S(2)}, u32[]{:S(2)}) collective-permute-start(f32[32,2048]{1,0:T(8,128)S(1)} %get-tuple-element.90), channel_id=1, source_target_pairs={{1,2},{3,4},{5,6},{0,16},{7,23},{9,10},{11,12},{13,14},{8,24},{15,... | collective-permute-start | bytes 786440 | tf_op jit(solution)/shard_map/ppermute | solution.py:538
  43.3 4.4 %collective-permute-start.12 = (f32[32,2048]{1,0:T(8,128)S(1)}, f32[32,2048]{1,0:T(8,128)S(1)}, u32[]{:S(2)}, u32[]{:S(2)}) collective-permute-start(f32[32,2048]{1,0:T(8,128)S(1)} %get-tuple-element.91), channel_id=1, source_target_pairs={{0,1},{2,3},{4,5},{6,7},{8,9},{10,11},{12,13},{14,15},{16,17},{18,... | collective-permute-start | bytes 786440 | tf_op jit(solution)/shard_map/ppermute | solution.py:538
  48.8 5.7 %collective-permute-start.18 = (f32[16,2048]{1,0:T(8,128)S(1)}, f32[16,2048]{1,0:T(8,128)S(1)}, u32[]{:S(2)}, u32[]{:S(2)}) collective-permute-start(f32[16,2048]{1,0:T(8,128)S(1)} %get-tuple-element.103), channel_id=1, source_target_pairs={{0,24},{8,16},{16,8},{24,0},{1,25},{9,17},{17,9},{25,1},{2,26},{10... | collective-permute-start | bytes 393224 | tf_op jit(solution)/shard_map/ppermute | solution.py:525
  50.3 8.5 %collective-permute-start.19 = (f32[16,2048]{1,0:T(8,128)S(1)}, f32[16,2048]{1,0:T(8,128)S(1)}, u32[]{:S(2)}, u32[]{:S(2)}) collective-permute-start(f32[16,2048]{1,0:T(8,128)S(1)} %get-tuple-element.104), channel_id=1, source_target_pairs={{0,8},{8,0},{16,24},{24,16},{1,9},{9,1},{17,25},{25,17},{2,10},{10... | collective-permute-start | bytes 393224 | tf_op jit(solution)/shard_map/ppermute | solution.py:525
  51.3 7.5 %collective-permute-start.20 = (f32[16,2048]{1,0:T(8,128)S(1)}, f32[16,2048]{1,0:T(8,128)S(1)}, u32[]{:S(2)}, u32[]{:S(2)}) collective-permute-start(f32[16,2048]{1,0:T(8,128)S(1)} %get-tuple-element.105), channel_id=1, source_target_pairs={{0,16},{8,24},{16,0},{24,8},{1,17},{9,25},{17,1},{25,9},{2,18},{10... | collective-permute-start | bytes 393224 | tf_op jit(solution)/shard_map/ppermute | solution.py:525
  52.0 10.1 %collective-permute-start.24 = (f32[16,2048]{1,0:T(8,128)S(1)}, f32[16,2048]{1,0:T(8,128)S(1)}, u32[]{:S(2)}, u32[]{:S(2)}) collective-permute-start(f32[16,2048]{1,0:T(8,128)S(1)} %get-tuple-element.115), channel_id=1, source_target_pairs={{0,24},{8,16},{16,8},{24,0},{1,25},{9,17},{17,9},{25,1},{2,26},{10... | collective-permute-start | bytes 393224 | tf_op jit(solution)/shard_map/ppermute | solution.py:525
  53.5 10.1 %collective-permute-start.25 = (f32[16,2048]{1,0:T(8,128)S(1)}, f32[16,2048]{1,0:T(8,128)S(1)}, u32[]{:S(2)}, u32[]{:S(2)}) collective-permute-start(f32[16,2048]{1,0:T(8,128)S(1)} %get-tuple-element.116), channel_id=1, source_target_pairs={{0,8},{8,0},{16,24},{24,16},{1,9},{9,1},{17,25},{25,17},{2,10},{10... | collective-permute-start | bytes 393224 | tf_op jit(solution)/shard_map/ppermute | solution.py:525
  54.5 9.0 %collective-permute-start.26 = (f32[16,2048]{1,0:T(8,128)S(1)}, f32[16,2048]{1,0:T(8,128)S(1)}, u32[]{:S(2)}, u32[]{:S(2)}) collective-permute-start(f32[16,2048]{1,0:T(8,128)S(1)} %get-tuple-element.117), channel_id=1, source_target_pairs={{0,16},{8,24},{16,0},{24,8},{1,17},{9,25},{17,1},{25,9},{2,18},{10... | collective-permute-start | bytes 393224 | tf_op jit(solution)/shard_map/ppermute | solution.py:525
  60.2 7.6 %collective-permute-start.21 = (f32[16,2048]{1,0:T(8,128)S(1)}, f32[16,2048]{1,0:T(8,128)S(1)}, u32[]{:S(2)}, u32[]{:S(2)}) collective-permute-start(f32[16,2048]{1,0:T(8,128)S(1)} %get-tuple-element.108), channel_id=1, source_target_pairs={{0,24},{8,16},{16,8},{24,0},{1,25},{9,17},{17,9},{25,1},{2,26},{10... | collective-permute-start | bytes 393224 | tf_op jit(solution)/shard_map/ppermute | solution.py:525
  62.1 6.3 %collective-permute-start.22 = (f32[16,2048]{1,0:T(8,128)S(1)}, f32[16,2048]{1,0:T(8,128)S(1)}, u32[]{:S(2)}, u32[]{:S(2)}) collective-permute-start(f32[16,2048]{1,0:T(8,128)S(1)} %get-tuple-element.109), channel_id=1, source_target_pairs={{0,8},{8,0},{16,24},{24,16},{1,9},{9,1},{17,25},{25,17},{2,10},{10... | collective-permute-start | bytes 393224 | tf_op jit(solution)/shard_map/ppermute | solution.py:525
  62.1 6.3 %collective-permute-start.23 = (f32[16,2048]{1,0:T(8,128)S(1)}, f32[16,2048]{1,0:T(8,128)S(1)}, u32[]{:S(2)}, u32[]{:S(2)}) collective-permute-start(f32[16,2048]{1,0:T(8,128)S(1)} %get-tuple-element.110), channel_id=1, source_target_pairs={{0,16},{8,24},{16,0},{24,8},{1,17},{9,25},{17,1},{25,9},{2,18},{10... | collective-permute-start | bytes 393224 | tf_op jit(solution)/shard_map/ppermute | solution.py:525
  65.7 7.6 %collective-permute-start.29 = (f32[16,2048]{1,0:T(8,128)S(1)}, f32[16,2048]{1,0:T(8,128)S(1)}, u32[]{:S(2)}, u32[]{:S(2)}) collective-permute-start(f32[16,2048]{1,0:T(8,128)S(1)} %get-tuple-element.124), channel_id=1, source_target_pairs={{0,24},{8,16},{16,8},{24,0},{1,25},{9,17},{17,9},{25,1},{2,26},{10... | collective-permute-start | bytes 393224 | tf_op jit(solution)/shard_map/ppermute | solution.py:525
  67.3 6.6 %collective-permute-start.30 = (f32[16,2048]{1,0:T(8,128)S(1)}, f32[16,2048]{1,0:T(8,128)S(1)}, u32[]{:S(2)}, u32[]{:S(2)}) collective-permute-start(f32[16,2048]{1,0:T(8,128)S(1)} %get-tuple-element.125), channel_id=1, source_target_pairs={{0,8},{8,0},{16,24},{24,16},{1,9},{9,1},{17,25},{25,17},{2,10},{10... | collective-permute-start | bytes 393224 | tf_op jit(solution)/shard_map/ppermute | solution.py:525
  67.9 6.0 %collective-permute-start.31 = (f32[16,2048]{1,0:T(8,128)S(1)}, f32[16,2048]{1,0:T(8,128)S(1)}, u32[]{:S(2)}, u32[]{:S(2)}) collective-permute-start(f32[16,2048]{1,0:T(8,128)S(1)} %get-tuple-element.126), channel_id=1, source_target_pairs={{0,16},{8,24},{16,0},{24,8},{1,17},{9,25},{17,1},{25,9},{2,18},{10... | collective-permute-start | bytes 393224 | tf_op jit(solution)/shard_map/ppermute | solution.py:525
  68.5 8.7 %collective-permute-start.27 = (f32[32,2048]{1,0:T(8,128)S(1)}, f32[32,2048]{1,0:T(8,128)S(1)}, u32[]{:S(2)}, u32[]{:S(2)}) collective-permute-start(f32[32,2048]{1,0:T(8,128)S(1)} %get-tuple-element.120), channel_id=1, source_target_pairs={{1,2},{3,4},{5,6},{9,10},{11,12},{13,14},{17,18},{19,20},{21,22},{... | collective-permute-start | bytes 786440 | tf_op jit(solution)/shard_map/ppermute | solution.py:538
  73.2 4.0 %collective-permute-start.28 = (f32[32,2048]{1,0:T(8,128)S(1)}, f32[32,2048]{1,0:T(8,128)S(1)}, u32[]{:S(2)}, u32[]{:S(2)}) collective-permute-start(f32[32,2048]{1,0:T(8,128)S(1)} %get-tuple-element.121), channel_id=1, source_target_pairs={{0,1},{2,3},{4,5},{6,7},{8,9},{10,11},{12,13},{14,15},{16,17},{18,... | collective-permute-start | bytes 786440 | tf_op jit(solution)/shard_map/ppermute | solution.py:538
  (15 other events, 123.6 us)
